TPU v7x, 32 devices: a whole 2x2x4 slice. The times are simulated.
32 devices in a mesh: req: 8 (over z, x), head: 4 (over y, core).
Axes of the slice: x: 2, y: 2, z: 4, core: 2. Of those that a mesh axis runs over, the one named last changes fastest.
Arguments:
- hidden: bfloat16 [256, 2048], P('req', 'head'), may hold values from -6 to 6
- lengths: int32 [256], P('req'), may hold values from 1 to 384, as said below
- expert_ids: int32 [256, 8], P('req'), may hold values from 0 to 63, all different within a row
- route_weights: float32 [256, 8], P('req'), may hold values from 0.25 to 2.5
- w_qkv: bfloat16 [3, 2048, 2048], P(None, None, 'head'), may hold values from -0.125 to 0.125
- w_out: bfloat16 [2048, 2048], P('head'), may hold values from -0.125 to 0.125
- k_cache: bfloat16 [256, 384, 16, 128], P('req', None, 'head'), may hold values from -400 to 400
- v_cache: bfloat16 [256, 384, 16, 128], P('req', None, 'head'), may hold values from -12 to 12
- w_in: bfloat16 [2048, 64, 2048], P(None, 'head', 'req'), may hold values from -0.125 to 0.125
- w_down: bfloat16 [64, 1024, 2048], P('head', 'req'), may hold values from -0.1875 to 0.1875
Outputs:
- output: bfloat16 [256, 2048], P('req', 'head')
Inputs may be any that keep to these rules, and one draw needn't show every extreme that they name: `lengths`: some request has exactly 384 cached positions.
All inputs are finite; a program needn't handle non-finite values.
Results may differ from a plain program's by a relative error of at most 0.023.
Values may be sent and summed in bfloat16 or wider, within the bound.
No kernel may reach another device: no remote copies, remote signals or barrier semaphores. Data moves between devices by JAX's collectives and lax.ppermute only.
A program may use at most 128 MiB of HBM per device.

v0:
```python
import jax
import jax.numpy as jnp
from jax import lax
from jax.sharding import PartitionSpec as P

UNIT_BLOCK = 64
KEY_BLOCK = 128


rope_theta = 50000.0
norm_eps = 1e-05


def over_all(shard, axis, dim, work):
    return work(lax.all_gather(shard, axis, axis=dim, tiled=True), jnp.int32(0))


def rotate(values, positions):
    half_dim = values.shape[-1] // 2
    freqs = rope_theta ** (-jnp.arange(half_dim, dtype=jnp.float32) / half_dim)
    angles = positions.astype(jnp.float32)[:, None] * freqs[None, :]
    cosine = jnp.cos(angles)[:, None, :]
    sine = jnp.sin(angles)[:, None, :]
    first_half = values[..., :half_dim]
    second_half = values[..., half_dim:]
    return jnp.concatenate(
        [first_half * cosine - second_half * sine, second_half * cosine + first_half * sine],
        axis=-1,
    )


def rms_normed(values):
    return (
        values * lax.rsqrt(jnp.mean(values * values, axis=-1, keepdims=True) + norm_eps)
    ).astype(jnp.bfloat16)


def per_device(
    hidden, lengths, expert_ids, route_weights, w_qkv, w_out, k_cache, v_cache, w_in, w_down
):
    full_rows = lax.all_gather(hidden, "head", axis=1, tiled=True)
    hidden_f = full_rows.astype(jnp.float32)
    normed = rms_normed(hidden_f)
    req_local = hidden.shape[0]
    col_width = hidden.shape[1]
    heads_local = k_cache.shape[2]
    head_size = k_cache.shape[3]
    cache_len = k_cache.shape[1]
    projected = jnp.einsum("td,cdn->ctn", normed, w_qkv, preferred_element_type=jnp.float32)
    projected = projected.reshape(3, req_local, heads_local, head_size)
    query = rotate(projected[0], lengths).astype(jnp.bfloat16)
    key_new = rotate(projected[1], lengths).astype(jnp.bfloat16)
    value_new = projected[2].astype(jnp.bfloat16)
    score_scale = head_size ** (-0.5)
    block_count = (jnp.max(lengths) + KEY_BLOCK - 1) // KEY_BLOCK

    def score_block(block_idx, buffer):
        keys_block = lax.dynamic_slice_in_dim(k_cache, block_idx * KEY_BLOCK, KEY_BLOCK, 1)
        block_scores = (
            jnp.einsum("rhd,rlhd->rhl", query, keys_block, preferred_element_type=jnp.float32)
            * score_scale
        )
        return lax.dynamic_update_slice_in_dim(buffer, block_scores, block_idx * KEY_BLOCK, 2)

    buffer = jnp.full((req_local, heads_local, cache_len), -jnp.inf, jnp.float32)
    buffer = lax.fori_loop(0, block_count, score_block, buffer)
    positions = jnp.arange(cache_len, dtype=jnp.int32)
    scores = jnp.where(positions[None, None, :] < lengths[:, None, None], buffer, -jnp.inf)
    self_score = (
        jnp.einsum("rhd,rhd->rh", query, key_new, preferred_element_type=jnp.float32) * score_scale
    )
    row_top = jnp.maximum(jnp.max(scores, axis=-1), self_score)
    exponent = jnp.exp(scores - row_top[:, :, None])
    self_exp = jnp.exp(self_score - row_top)
    denominator = jnp.sum(exponent, axis=-1) + self_exp
    weights = (exponent / denominator[:, :, None]).astype(jnp.bfloat16)
    self_weight = (self_exp / denominator).astype(jnp.bfloat16)

    def value_block(block_idx, accum):
        weights_block = lax.dynamic_slice_in_dim(weights, block_idx * KEY_BLOCK, KEY_BLOCK, 2)
        values_block = lax.dynamic_slice_in_dim(v_cache, block_idx * KEY_BLOCK, KEY_BLOCK, 1)
        return accum + jnp.einsum(
            "rhl,rlhd->rhd", weights_block, values_block, preferred_element_type=jnp.float32
        )

    accum = lax.fori_loop(
        0, block_count, value_block, jnp.zeros((req_local, heads_local, head_size), jnp.float32)
    )
    accum = accum + self_weight.astype(jnp.float32)[:, :, None] * value_new.astype(jnp.float32)
    attended = accum.astype(jnp.bfloat16).reshape(req_local, heads_local * head_size)
    head_terms = jnp.dot(attended, w_out, preferred_element_type=jnp.float32)
    resid = hidden_f + lax.psum(head_terms.astype(jnp.bfloat16), "head").astype(jnp.float32)
    mixed = rms_normed(resid)
    experts_local = w_down.shape[0]
    units_local = w_down.shape[1]
    width = w_in.shape[0]
    expert_base = lax.axis_index("head") * experts_local + jnp.arange(
        experts_local, dtype=jnp.int32
    )
    w_in_flat = w_in.reshape(width, experts_local * 2 * units_local)
    w_down_flat = w_down.reshape(experts_local * units_local, width)

    def expert_hidden(pieces):
        token_rows, token_ids, token_weights = pieces
        row_count = token_rows.shape[0]
        matches = (token_ids[:, :, None] == expert_base[None, None, :]).astype(jnp.float32)
        combined = jnp.sum(token_weights[:, :, None] * matches, axis=1)
        gate_up = jnp.dot(token_rows, w_in_flat, preferred_element_type=jnp.float32)
        gate_up = gate_up.reshape(
            row_count, experts_local, units_local // UNIT_BLOCK, 2, UNIT_BLOCK
        )
        gate = gate_up[:, :, :, 0, :]
        upward = gate_up[:, :, :, 1, :]
        units = (combined[:, :, None, None] * (jax.nn.silu(gate) * upward)).astype(jnp.bfloat16)
        return units.reshape(row_count, experts_local * units_local)

    gathered = over_all(
        (mixed, expert_ids, route_weights.astype(jnp.bfloat16)),
        "req",
        0,
        lambda piece, start: expert_hidden((piece[0], piece[1], piece[2].astype(jnp.float32))),
    )
    token_sums = lax.psum_scatter(
        jnp.dot(gathered, w_down_flat, preferred_element_type=jnp.float32).astype(jnp.bfloat16),
        "req",
        scatter_dimension=0,
        tiled=True,
    )
    moe_share = lax.psum_scatter(token_sums, "head", scatter_dimension=1, tiled=True).astype(
        jnp.float32
    )
    resid_share = lax.dynamic_slice_in_dim(resid, lax.axis_index("head") * col_width, col_width, 1)
    return (resid_share + moe_share).astype(jnp.bfloat16)


def solution(mesh):
    in_specs = (
        P("req", "head"),
        P("req"),
        P("req", None),
        P("req", None),
        P(None, None, "head"),
        P("head", None),
        P("req", None, "head", None),
        P("req", None, "head", None),
        P(None, "head", "req"),
        P("head", "req", None),
    )
    out_specs = P("req", "head")
    return jax.shard_map(
        per_device, mesh=mesh, in_specs=in_specs, out_specs=out_specs, check_vma=False
    )
```

profile of v0, /device:TPU:0, one launch (start us, length us, event | category | flops | bytes accessed | tf_op | source)
XLA Modules:
  0.0 297.2 jit_solution(12377933692136148869)
XLA Ops:
  6.5 0.0 copy-start
  6.5 0.0 all-reduce.2.cloned.1.call-start
  6.5 1.5 fusion.24
  8.8 0.7 iota_compare_fusion
  9.5 6.7 %all_gather.12 = bf16[32,2048]{1,0:T(8,128)(2,1)S(1)} all-gather(bf16[32,512]{1,0:T(8,128)(2,1)} %param.14), channel_id=1, replica_groups=mesh['req'=8,'head'=4] {'head'}, dimensions={1}, use_global_device_ids=true | all-gather | bytes 163840 | tf_op jit(solution)/shard_map/all_gather | solution.py:41
  16.2 0.1 fusion.11
  16.4 4.0 %convolution_bitcast_fusion = f32[3,32,512]{2,1,0:T(8,128)S(1)} fusion(bf16[3,2048,512]{2,1,0:T(8,128)(2,1)} %param.18, bf16[32,2048]{1,0:T(8,128)(2,1)S(1)} %all_gather.12, f32[32]{0:T(128)S(1)} %add_rsqrt_fusion.1), kind=kOutput, calls=%fused_computation.17 | convolution fusion | flops 201523200 | bytes 6619264 | tf_op jit(solution)/shard_map/td,cdn->ctn/dot_general | solution.py:49
  20.5 0.1 multiply_cosine_fusion
  20.7 0.2 subtract_convert_fusion.1
  20.9 0.2 fusion.17
  21.1 12.4 %while.20 = (s32[]{:T(128)}, f32[32,4,384]{2,1,0:T(4,128)S(1)}, s32[]{:T(128)}, bf16[32,384,4,128]{3,2,1,0:T(4,128)(2,1)}, bf16[32,4,128]{2,1,0:T(4,128)(2,1)S(1...) while((s32[]{:T(128)}, f32[32,4,384]{2,1,0:T(4,128)S(1)}, s32[]{:T(128)}, ...), condition=%wide.region_3.4_spmd, body=%wide.region_2.3_spmd.sunk | while | flops 4210694 | bytes 12812443 | solution.py:66
  21.1 3.9 %constant_dynamic-slice_fusion.4 = bf16[32,128,4,128]{3,2,1,0:T(4,128)(2,1)S(1)} fusion(bf16[32,384,4,128]{3,2,1,0:T(4,128)(2,1)} %get-tuple-element.186, s32[]{:T(128)S(6)} %select_n.31), kind=kLoop, calls=%fused_computation.4.clone.1 | loop fusion | bytes 8388612 | tf_op jit(solution)/shard_map/while/body/dynamic_slice | solution.py:58
  25.0 2.2 fusion.38
  27.2 0.1 multiply_dynamic-update-slice_fusion.2
  27.3 3.9 %constant_dynamic-slice_fusion.4 = bf16[32,128,4,128]{3,2,1,0:T(4,128)(2,1)S(1)} fusion(bf16[32,384,4,128]{3,2,1,0:T(4,128)(2,1)} %get-tuple-element.186, s32[]{:T(128)S(6)} %select_n.31), kind=kLoop, calls=%fused_computation.4.clone.1 | loop fusion | bytes 8388612 | tf_op jit(solution)/shard_map/while/body/dynamic_slice | solution.py:58
  31.2 2.2 fusion.38
  33.5 0.1 multiply_dynamic-update-slice_fusion.2
  33.5 0.1 select_reduce_fusion
  33.7 0.2 fusion.16
  33.9 0.2 divide_convert_fusion
  34.1 10.4 %while.21 = (s32[]{:T(128)}, f32[32,4,128]{2,1,0:T(4,128)S(1)}, s32[]{:T(128)}, bf16[32,4,384]{2,1,0:T(4,128)(2,1)S(1)}, bf16[32,384,4,128]{3,2,1,0:T(4,128)(2,1...) while((s32[]{:T(128)}, f32[32,4,128]{2,1,0:T(4,128)S(1)}, s32[]{:T(128)}, ...), condition=%wide.region_7.8_spmd, body=%wide.region_6.7_spmd.sunk | while | flops 4210694 | bytes 12943515 | solution.py:86
  34.2 3.9 %constant_dynamic-slice_fusion.5 = bf16[32,128,4,128]{3,2,1,0:T(4,128)(2,1)S(1)} fusion(bf16[32,384,4,128]{3,2,1,0:T(4,128)(2,1)} %get-tuple-element.214, s32[]{:T(128)S(6)} %select_n.32), kind=kLoop, calls=%fused_computation.9.clone.1 | loop fusion | bytes 8388612 | tf_op jit(solution)/shard_map/while/body/dynamic_slice | solution.py:81
  38.1 1.2 fusion.41
  39.3 4.0 %constant_dynamic-slice_fusion.5 = bf16[32,128,4,128]{3,2,1,0:T(4,128)(2,1)S(1)} fusion(bf16[32,384,4,128]{3,2,1,0:T(4,128)(2,1)} %get-tuple-element.214, s32[]{:T(128)S(6)} %select_n.32), kind=kLoop, calls=%fused_computation.9.clone.1 | loop fusion | bytes 8388612 | tf_op jit(solution)/shard_map/while/body/dynamic_slice | solution.py:81
  43.3 1.2 fusion.41
  44.6 0.1 add_convert_fusion.1
  44.7 0.0 copy-done
  44.7 1.1 convolution_convert_fusion.1
  45.8 0.0 all-reduce.2.cloned.1.call-update
  45.9 0.0 all-gather.4.cloned.1.call-start
  45.9 44.5 %all-reduce.2.cloned.1.call-done = bf16[32,2048]{1,0:T(8,128)(2,1)} async-done(((bf16[32,2048]{1,0:T(8,128)(2,1)}), bf16[32,2048]{1,0:T(8,128)(2,1)}) %all-reduce.2.cloned.1.call-update) | async-done | bytes 131088 | tf_op jit(solution)/shard_map/psum | solution.py:92
  90.4 1.1 convert_add_fusion
  91.5 1.6 multiply_convert_fusion
  93.2 0.0 all-gather.4.cloned.1.call-update
  93.2 0.0 reduce-scatter.3.cloned.1.call-start
  93.2 16.0 %copy.43 = bf16[256,8,16,256]{3,1,2,0:T(8,128)(2,1)} copy(bf16[256,8,16,256]{3,2,1,0:T(8,128)(2,1)} %bitcast.64) | data formatting | bytes 33554432
  109.3 0.0 copy-start.3
  109.3 0.0 copy-start.2
  109.3 22.6 %copy.27 = bf16[4096,2048]{1,0:T(8,128)(2,1)} copy(bf16[4096,2048]{0,1:T(8,128)(2,1)} %bitcast.62) | data formatting | bytes 33554432 | tf_op jit(solution)/shard_map/dot_general | solution.py:108
  131.9 0.0 copy-done.3
  131.9 26.0 %all-gather.1 = bf16[8,32,8]{1,2,0:T(8,128)(2,1)S(1)} all-gather(bf16[1,32,8]{1,2,0:T(8,128)(2,1)S(1)} %convert_bitcast_fusion), channel_id=1, replica_groups=mesh['req'=8,'head'=4] {'req'}, dimensions={0}, use_global_device_ids=true | all-gather | bytes 4608 | tf_op jit(solution)/shard_map/all_gather | solution.py:15
  157.9 0.1 reshape.152
  158.0 0.0 copy-done.2
  158.0 30.6 %all-gather = s32[8,32,8]{1,2,0:T(8,128)S(1)} all-gather(s32[1,32,8]{1,2,0:T(8,128)S(1)} %bitcast.71), channel_id=1, replica_groups=mesh['req'=8,'head'=4] {'req'}, dimensions={0}, use_global_device_ids=true | all-gather | bytes 9216 | tf_op jit(solution)/shard_map/all_gather | solution.py:15
  188.6 0.1 reshape.149
  188.7 0.1 select_reduce_fusion.1
  188.8 0.0 all-gather.4.cloned.1.call-done
  188.8 9.6 %fusion.9 = f32[256,16,2,2,64]{0,4,3,2,1:T(8,128)S(1)} fusion(bf16[16,2,2,64,2048]{4,3,2,1,0:T(8,128)(2,1)} %bitcast.65, bf16[256,2048]{1,0:T(8,128)(2,1)} %all-gather.4.cloned.1.call-done), kind=kOutput, calls=%fused_computation.18 | convolution fusion | flops 4294967296 | bytes 22020096 | tf_op jit(solution)/shard_map/dot_general | solution.py:108
  198.3 0.7 fusion.8
  199.1 0.0 copy-start.1
  199.1 6.9 %convolution_convert_fusion = bf16[256,2048]{1,0:T(8,128)(2,1)} fusion(bf16[256,2048]{0,1:T(8,128)(2,1)S(1)} %bitcast.66, bf16[2048,2048]{1,0:T(8,128)(2,1)} %bitcast.63), kind=kOutput, calls=%fused_computation.10 | convolution fusion | flops 2148007936 | bytes 10485760 | tf_op jit(solution)/shard_map/dot_general | solution.py:124
  206.0 0.0 reduce-scatter.3.cloned.1.call-update
  206.0 0.0 reduce-scatter.5.cloned.1.call-start
  206.0 62.3 %reduce-scatter.3.cloned.1.call-done = bf16[32,2048]{1,0:T(8,128)(2,1)} async-done(((bf16[256,2048]{1,0:T(8,128)(2,1)}), bf16[32,2048]{1,0:T(8,128)(2,1)}) %reduce-scatter.3.cloned.1.call-update) | async-done | bytes 131088 | tf_op jit(solution)/shard_map/reduce_scatter | solution.py:123
  268.3 0.0 reduce-scatter.5.cloned.1.call-update
  268.4 20.9 %reduce-scatter.5.cloned.1.call-done = bf16[32,512]{1,0:T(8,128)(2,1)} async-done(((bf16[32,2048]{1,0:T(8,128)(2,1)}), bf16[32,512]{1,0:T(8,128)(2,1)}) %reduce-scatter.5.cloned.1.call-update) | async-done | bytes 32784 | tf_op jit(solution)/shard_map/reduce_scatter | solution.py:129
  289.2 1.4 add_convert_fusion
  290.6 0.0 copy-done.1
  (20 shorter events, 0.3 us)
Async XLA Ops:
  6.5 38.2 %copy-start = (bf16[512,2048]{1,0:T(8,128)(2,1)S(1)}, bf16[512,2048]{1,0:T(8,128)(2,1)}, u32[]{:S(2)}) copy-start(bf16[512,2048]{1,0:T(8,128)(2,1)} %param.19) | copy-start | bytes 6291460
  6.5 83.9 %all-reduce.2.cloned.1.call-start = ((), (), s32[]{:S(2)}) async-start(), calls=%async_computation.2 | async-start | bytes 262144 | tf_op jit(solution)/shard_map/psum | solution.py:92
  45.9 142.9 %all-gather.4.cloned.1.call-start = ((), (), s32[]{:S(2)}) async-start(), calls=%async_computation.3 | async-start | bytes 1179648 | tf_op jit(solution)/shard_map/all_gather | solution.py:15
  93.2 175.2 %reduce-scatter.3.cloned.1.call-start = ((), (), s32[]{:S(2)}) async-start(), calls=%async_computation.4 | async-start | bytes 1179648 | tf_op jit(solution)/shard_map/reduce_scatter | solution.py:123
  109.3 22.6 %copy-start.3 = (f32[32,8]{0,1:T(8,128)S(1)}, f32[32,8]{0,1:T(8,128)}, u32[]{:S(2)}) copy-start(f32[32,8]{0,1:T(8,128)} %param.17) | copy-start | bytes 3076
  109.3 48.7 %copy-start.2 = (s32[32,8]{0,1:T(8,128)S(1)}, s32[32,8]{0,1:T(8,128)}, u32[]{:S(2)}) copy-start(s32[32,8]{0,1:T(8,128)} %param.16) | copy-start | bytes 3076
  199.1 91.6 %copy-start.1 = (bf16[512,2048]{1,0:T(8,128)(2,1)S(1)}, bf16[512,2048]{1,0:T(8,128)(2,1)}, u32[]{:S(2)}) copy-start(bf16[512,2048]{1,0:T(8,128)(2,1)} %param.19) | copy-start | bytes 6291460
  206.0 83.3 %reduce-scatter.5.cloned.1.call-start = ((), (), s32[]{:S(2)}) async-start(), calls=%async_computation.5 | async-start | bytes 163840 | tf_op jit(solution)/shard_map/reduce_scatter | solution.py:129
Sparse Core Ops, SparseCore 0:
  46.0 44.4 all-reduce.1
  93.3 40.1 all-gather.3
  206.1 62.1 reduce-scatter.2
  270.6 18.5 reduce-scatter.4
where the time goes:
time: 298 us; the launch traced here: 297 us
  waiting for transfers between devices  128 us (43%)
  blocking collectives  63.3 us (21%)
  local copies, waits for them, and re-layouts  54.6 us (18%)
  matrix products  28.4 us (10%)
  between operations  14 us (5%)
  other arithmetic  8.66 us (3%)
    reduce_scatter x1, waiting for transfers between devices, per_device(): lax.psum_scatter(jnp.dot(gathered, w_down_flat, preferred_element_type=jn...  62.3 us
    all_gather x2, blocking collectives, over_all(): return work(lax.all_gather(shard, axis, axis=dim, tiled=True), jnp.int32(0))  56.6 us
    psum x1, waiting for transfers between devices, per_device(): lax.psum(head_terms.astype(jnp.bfloat16), 'head').astype(jnp.float32)  44.5 us
    dot_general x1, local copies, waits for them, and re-layouts, expert_hidden(): gate_up = jnp.dot(token_rows, w_in_flat, preferred_element_type=jnp.float32)  22.6 us
    reduce_scatter x1, waiting for transfers between devices, per_device(): lax.psum_scatter(token_sums, 'head', scatter_dimension=1, tiled=True)  20.9 us
    unnamed x10, local copies, waits for them, and re-layouts  16.1 us
    dot_general x1, matrix products, expert_hidden(): gate_up = jnp.dot(token_rows, w_in_flat, preferred_element_type=jnp.float32)  9.55 us
    dynamic_slice x2, local copies, waits for them, and re-layouts, value_block(): lax.dynamic_slice_in_dim(v_cache, block_idx * KEY_BLOCK, KEY_BLOCK, 1)  7.84 us
  transfers between devices with their start and end apart: 4, of which 3 were waited for; matrix products, arithmetic and copies ran while one was open for 13% of the time, Pallas kernels for 0%

commit v1 on v0

--- a/solution.py
+++ b/solution.py
@@ -9,10 +9,6 @@
 
 rope_theta = 50000.0
 norm_eps = 1e-05
-
-
-def over_all(shard, axis, dim, work):
-    return work(lax.all_gather(shard, axis, axis=dim, tiled=True), jnp.int32(0))
 
 
 def rotate(values, positions):
@@ -35,14 +31,12 @@
     ).astype(jnp.bfloat16)
 
 
-def per_device(
-    hidden, lengths, expert_ids, route_weights, w_qkv, w_out, k_cache, v_cache, w_in, w_down
-):
-    full_rows = lax.all_gather(hidden, "head", axis=1, tiled=True)
-    hidden_f = full_rows.astype(jnp.float32)
-    normed = rms_normed(hidden_f)
-    req_local = hidden.shape[0]
-    col_width = hidden.shape[1]
+def swap(value, axis, size, mask):
+    return lax.ppermute(value, axis, [(i, i ^ mask) for i in range(size)])
+
+
+def attention(normed, lengths, w_qkv, k_cache, v_cache):
+    req_local = normed.shape[0]
     heads_local = k_cache.shape[2]
     head_size = k_cache.shape[3]
     cache_len = k_cache.shape[1]
@@ -87,50 +81,112 @@
         0, block_count, value_block, jnp.zeros((req_local, heads_local, head_size), jnp.float32)
     )
     accum = accum + self_weight.astype(jnp.float32)[:, :, None] * value_new.astype(jnp.float32)
-    attended = accum.astype(jnp.bfloat16).reshape(req_local, heads_local * head_size)
+    return accum.astype(jnp.bfloat16).reshape(req_local, heads_local * head_size)
+
+
+def per_device(
+    hidden, lengths, expert_ids, route_weights, w_qkv, w_out, k_cache, v_cache, w_in, w_down
+):
+    req_size = lax.axis_size("req")
+    head_size = lax.axis_size("head")
+    me = lax.axis_index("head")
+    rows, cols = hidden.shape
+    experts_local, units_local, width = w_down.shape
+    even = range(0, head_size, 2)
+
+    pieces = [hidden] + [swap(hidden, "head", head_size, j) for j in range(1, head_size)]
+    stacked = jnp.stack(pieces)
+    full_rows = jnp.concatenate(
+        [lax.dynamic_index_in_dim(stacked, me ^ b, 0, False) for b in range(head_size)], axis=1
+    )
+    normed = rms_normed(full_rows.astype(jnp.float32))
+    attended = attention(normed, lengths, w_qkv, k_cache, v_cache)
     head_terms = jnp.dot(attended, w_out, preferred_element_type=jnp.float32)
-    resid = hidden_f + lax.psum(head_terms.astype(jnp.bfloat16), "head").astype(jnp.float32)
-    mixed = rms_normed(resid)
-    experts_local = w_down.shape[0]
-    units_local = w_down.shape[1]
-    width = w_in.shape[0]
-    expert_base = lax.axis_index("head") * experts_local + jnp.arange(
-        experts_local, dtype=jnp.int32
-    )
-    w_in_flat = w_in.reshape(width, experts_local * 2 * units_local)
-    w_down_flat = w_down.reshape(experts_local * units_local, width)
-
-    def expert_hidden(pieces):
-        token_rows, token_ids, token_weights = pieces
-        row_count = token_rows.shape[0]
-        matches = (token_ids[:, :, None] == expert_base[None, None, :]).astype(jnp.float32)
-        combined = jnp.sum(token_weights[:, :, None] * matches, axis=1)
-        gate_up = jnp.dot(token_rows, w_in_flat, preferred_element_type=jnp.float32)
-        gate_up = gate_up.reshape(
-            row_count, experts_local, units_local // UNIT_BLOCK, 2, UNIT_BLOCK
+    head_terms = head_terms.astype(jnp.bfloat16).reshape(rows, head_size, cols)
+
+    def block(array, j):
+        return lax.dynamic_index_in_dim(array, me ^ j, array.ndim - 2, False)
+
+    keep = jnp.concatenate([block(head_terms, j) for j in even], axis=1)
+    send = jnp.concatenate([block(head_terms, j + 1) for j in even], axis=1)
+    half = keep.astype(jnp.float32) + swap(send, "head", head_size, 1).astype(jnp.float32)
+    half = half.astype(jnp.bfloat16)
+    others = [swap(half, "head", head_size, j) for j in even if j]
+    total = half.astype(jnp.float32).reshape(rows, head_size // 2, cols)
+    for j, other in zip([j for j in even if j], others):
+        other = other.reshape(rows, head_size // 2, cols)
+        total = total + jnp.stack(
+            [other[:, t ^ (j // 2)] for t in range(head_size // 2)], axis=1
+        ).astype(jnp.float32)
+    own_x = jnp.stack([pieces[j] for j in even], axis=1)
+    resid = (own_x.astype(jnp.float32) + total).reshape(rows, head_size // 2 * cols)
+
+    every = jnp.arange(head_size * experts_local, dtype=jnp.int32)
+    matches = (expert_ids[:, :, None] == every[None, None, :]).astype(jnp.float32)
+    shares = jnp.sum(route_weights[:, :, None] * matches, axis=1).astype(jnp.bfloat16)
+    payload = jnp.concatenate([resid.astype(jnp.bfloat16), shares], axis=1)
+
+    steps = range(2, req_size, 2)
+    line = jnp.concatenate([payload] + [swap(payload, "req", req_size, k) for k in steps])
+    mine = jnp.concatenate([line, swap(line, "req", req_size, 1)])
+    states = mine[:, : resid.shape[1]]
+    share = mine[:, resid.shape[1] :]
+    other_states = swap(states, "head", head_size, 1)
+
+    tokens = states.shape[0]
+    square = jnp.sum(states.astype(jnp.float32) ** 2, axis=1) + jnp.sum(
+        other_states.astype(jnp.float32) ** 2, axis=1
+    )
+    scale = lax.rsqrt(square / width + norm_eps)
+    both = jnp.stack(
+        [
+            states.reshape(tokens, head_size // 2, cols),
+            other_states.reshape(tokens, head_size // 2, cols),
+        ],
+        axis=2,
+    ).reshape(tokens, head_size, cols)
+    ordered = jnp.concatenate([block(both, b) for b in range(head_size)], axis=1)
+    w_flat = w_in.transpose(1, 0, 2)
+    gate_up = jnp.einsum("td,edn->etn", ordered, w_flat, preferred_element_type=jnp.float32)
+    gate_up = gate_up * scale[None, :, None]
+    gate_up = gate_up.reshape(experts_local, tokens, units_local // UNIT_BLOCK, 2, UNIT_BLOCK)
+    local = lax.dynamic_slice_in_dim(share, me * experts_local, experts_local, 1)
+    units = local.T.astype(jnp.float32)[:, :, None, None] * (
+        jax.nn.silu(gate_up[:, :, :, 0]) * gate_up[:, :, :, 1]
+    )
+    units = units.astype(jnp.bfloat16).reshape(experts_local, tokens, units_local)
+    w_blocks = w_down.reshape(experts_local, units_local, head_size, cols)
+
+    def down(blocks):
+        return jnp.concatenate(
+            [
+                jnp.einsum(
+                    "etu,eun->tn", units, block(w_blocks, j), preferred_element_type=jnp.float32
+                ).astype(jnp.bfloat16)
+                for j in blocks
+            ],
+            axis=1,
         )
-        gate = gate_up[:, :, :, 0, :]
-        upward = gate_up[:, :, :, 1, :]
-        units = (combined[:, :, None, None] * (jax.nn.silu(gate) * upward)).astype(jnp.bfloat16)
-        return units.reshape(row_count, experts_local * units_local)
-
-    gathered = over_all(
-        (mixed, expert_ids, route_weights.astype(jnp.bfloat16)),
-        "req",
-        0,
-        lambda piece, start: expert_hidden((piece[0], piece[1], piece[2].astype(jnp.float32))),
-    )
-    token_sums = lax.psum_scatter(
-        jnp.dot(gathered, w_down_flat, preferred_element_type=jnp.float32).astype(jnp.bfloat16),
-        "req",
-        scatter_dimension=0,
-        tiled=True,
-    )
-    moe_share = lax.psum_scatter(token_sums, "head", scatter_dimension=1, tiled=True).astype(
-        jnp.float32
-    )
-    resid_share = lax.dynamic_slice_in_dim(resid, lax.axis_index("head") * col_width, col_width, 1)
-    return (resid_share + moe_share).astype(jnp.bfloat16)
+
+    sent = swap(down([j + 1 for j in even]), "head", head_size, 1)
+    summed = down(even).astype(jnp.float32) + sent.astype(jnp.float32)
+    summed = summed.astype(jnp.bfloat16).reshape(2, tokens // 2, head_size // 2, cols)
+    total = summed[0, :, 0].astype(jnp.float32)
+    for j in even:
+        for k in range(2):
+            if j or k:
+                pairs = [
+                    (r * head_size + h, (r ^ k) * head_size + (h ^ j))
+                    for r in range(req_size)
+                    for h in range(head_size)
+                ]
+                got = lax.ppermute(summed[k, :, j // 2], ("req", "head"), pairs)
+                total = total + got.astype(jnp.float32)
+    chunks = total.astype(jnp.bfloat16).reshape(req_size // 2, rows, cols)
+    out = chunks[0].astype(jnp.float32)
+    for k in steps:
+        out = out + swap(chunks[k // 2], "req", req_size, k).astype(jnp.float32)
+    return (out + resid[:, :cols]).astype(jnp.bfloat16)
 
 
 def solution(mesh):

time: 298 us -> 160 us (0.54)
  waiting for transfers between devices: 128 us -> 19.6 us
  blocking collectives: 63.3 us -> 0 us
  starting transfers between devices: 0.13 us -> 31 us
  between operations: 14 us -> 1.23 us
  local copies, waits for them, and re-layouts: 54.6 us -> 63.1 us
  matrix products: 28.4 us -> 32.7 us
    reduce_scatter x2 -> x0, waiting for transfers between devices: 83.2 us -> none  [the longest x1 62.3 us: per_device(): lax.psum_scatter(jnp.dot(gathered, w_down_flat, preferred_element_type=jn...]
    all_gather x3 -> x0, blocking collectives: 63.3 us -> none  [the longest x2 56.6 us: over_all(): return work(lax.all_gather(shard, axis, axis=dim, tiled=True), jnp.int32(0))]
    psum x1 -> x0, waiting for transfers between devices: 44.5 us -> none  [per_device(): lax.psum(head_terms.astype(jnp.bfloat16), 'head').astype(jnp.float32)]
    ppermute x0 -> x17, starting transfers between devices: none -> 31 us  [the longest x14 27.5 us: swap(): return lax.ppermute(value, axis, [(i, i ^ mask) for i in range(size)])]
    dynamic_slice x0 -> x2, local copies, waits for them, and re-layouts: none -> 27.3 us  [block(): return lax.dynamic_index_in_dim(array, me ^ j, array.ndim - 2, False)]
    dot_general x1 -> x0, local copies, waits for them, and re-layouts: 22.6 us -> none  [expert_hidden(): gate_up = jnp.dot(token_rows, w_in_flat, preferred_element_type=jnp.float32)]
    ppermute x0 -> x17, waiting for transfers between devices: none -> 19.6 us  [the longest x14 13.4 us: swap(): return lax.ppermute(value, axis, [(i, i ^ mask) for i in range(size)])]
    reshape x0 -> x4, local copies, waits for them, and re-layouts: none -> 15 us  [the longest x1 14.5 us: per_device(): w_blocks = w_down.reshape(experts_local, units_local, head_size, cols)]
  transfers between devices with their start and end apart: 4 -> 17, of which waited for: 3 -> 8; matrix products, arithmetic and copies ran while one was open for 13% -> 30% of each run, Pallas kernels for 0% -> 0%
where the time goes in v1:
time: 160 us; the launch traced here: 159 us
  local copies, waits for them, and re-layouts  63.1 us (39%)
  matrix products  32.7 us (20%)
  starting transfers between devices  31 us (19%)
  waiting for transfers between devices  19.6 us (12%)
  other arithmetic  10.8 us (7%)
    ppermute x14, starting transfers between devices, swap(): return lax.ppermute(value, axis, [(i, i ^ mask) for i in range(size)])  27.5 us
    dynamic_slice x2, local copies, waits for them, and re-layouts, block(): return lax.dynamic_index_in_dim(array, me ^ j, array.ndim - 2, False)  27.3 us
    dot_general x1, matrix products, per_device(): jnp.einsum('td,edn->etn', ordered, w_flat, preferred_element_type=jnp.flo...  18.5 us
    reshape x1, local copies, waits for them, and re-layouts, per_device(): w_blocks = w_down.reshape(experts_local, units_local, head_size, cols)  14.5 us
    ppermute x14, waiting for transfers between devices, swap(): return lax.ppermute(value, axis, [(i, i ^ mask) for i in range(size)])  13.4 us
    dynamic_slice x2, local copies, waits for them, and re-layouts, value_block(): lax.dynamic_slice_in_dim(v_cache, block_idx * KEY_BLOCK, KEY_BLOCK, 1)  7.76 us
    dynamic_slice x2, local copies, waits for them, and re-layouts, score_block(): lax.dynamic_slice_in_dim(k_cache, block_idx * KEY_BLOCK, KEY_BLOCK, 1)  7.76 us
    ppermute x3, waiting for transfers between devices, per_device(): got = lax.ppermute(summed[k, :, j // 2], ('req', 'head'), pairs)  6.2 us
  transfers between devices with their start and end apart: 17, of which 8 were waited for; matrix products, arithmetic and copies ran while one was open for 30% of the time, Pallas kernels for 0%

profile of v1, /device:TPU:0, one launch (start us, length us, event | category | flops | bytes accessed | tf_op | source)
XLA Modules:
  0.0 158.8 jit_solution(1021756618278386390)
XLA Ops:
  0.0 3.0 %collective-permute-start = (bf16[32,512]{1,0:T(8,128)(2,1)}, bf16[32,512]{1,0:T(8,128)(2,1)S(1)}, u32[]{:S(2)}, u32[]{:S(2)}) collective-permute-start(bf16[32,512]{1,0:T(8,128)(2,1)} %param.14), channel_id=1, source_target_pairs={{0,2},{1,3},{2,0},{3,1},{4,6},{5,7},{6,4},{7,5},{8,10},{9,11},{10,... | collective-permute-start | bytes 98312 | tf_op jit(solution)/shard_map/ppermute | solution.py:35
  3.0 0.2 collective-permute-start.1
  3.2 1.4 fusion.54
  4.6 0.7 iota_compare_fusion.1
  5.3 0.8 copy.55
  6.1 0.8 copy.56
  7.9 0.8 pad_maximum_fusion.3
  8.9 4.0 %convolution_bitcast_fusion = f32[3,32,512]{2,1,0:T(8,128)S(1)} fusion(bf16[3,2048,512]{2,1,0:T(8,128)(2,1)} %param.18, f32[32]{0:T(128)S(1)} %add_rsqrt_fusion.1, bf16[32,512]{1,0:T(8,128)(2,1)S(1)} %get-tuple-element.109, bf16[32,512]{1,0:T(8,128)(2,1)S(1)} %get-tuple-element.110, bf16[32,512]{1,0:T(8,128)(2,1)S(1)} %get-tuple-element.111, ...), kind=kOutput, calls=%fused_computation.35 | convolution fusion | flops 201981952 | bytes 6619264 | tf_op jit(solution)/shard_map/td,cdn->ctn/dot_general | solution.py:43
  13.2 0.2 fusion.41
  13.4 12.4 %while.20 = (s32[]{:T(128)}, f32[32,4,384]{2,1,0:T(4,128)S(1)}, s32[]{:T(128)}, bf16[32,384,4,128]{3,2,1,0:T(4,128)(2,1)}, bf16[32,4,128]{2,1,0:T(4,128)(2,1)S(1...) while((s32[]{:T(128)}, f32[32,4,384]{2,1,0:T(4,128)S(1)}, s32[]{:T(128)}, ...), condition=%wide.region_3.4_spmd, body=%wide.region_2.3_spmd.sunk | while | flops 4210694 | bytes 12812435 | solution.py:60
  13.5 3.9 %constant_dynamic-slice_fusion.12 = bf16[32,128,4,128]{3,2,1,0:T(4,128)(2,1)S(1)} fusion(bf16[32,384,4,128]{3,2,1,0:T(4,128)(2,1)} %get-tuple-element.217, s32[]{:T(128)S(6)} %select_n.63), kind=kLoop, calls=%fused_computation.4.clone.1 | loop fusion | bytes 8388612 | tf_op jit(solution)/shard_map/while/body/dynamic_slice | solution.py:52
  17.4 2.2 %fusion.69 = f32[32,4,1,128]{3,2,1,0:T(1,128)S(1)} fusion(bf16[32,128,4,128]{3,2,1,0:T(4,128)(2,1)S(1)} %constant_dynamic-slice_fusion.12, bf16[32,4,128,1]{2,1,0,3:T(4,128)(2,1)S(1)} %bitcast.165), kind=kOutput, calls=%fused_computation.clone.1 | convolution fusion | flops 4194304 | bytes 4292608 | tf_op jit(solution)/shard_map/while/body/rhd,rlhd->rhl/dot_general | solution.py:54
  19.7 3.9 %constant_dynamic-slice_fusion.12 = bf16[32,128,4,128]{3,2,1,0:T(4,128)(2,1)S(1)} fusion(bf16[32,384,4,128]{3,2,1,0:T(4,128)(2,1)} %get-tuple-element.217, s32[]{:T(128)S(6)} %select_n.63), kind=kLoop, calls=%fused_computation.4.clone.1 | loop fusion | bytes 8388612 | tf_op jit(solution)/shard_map/while/body/dynamic_slice | solution.py:52
  23.6 2.2 %fusion.69 = f32[32,4,1,128]{3,2,1,0:T(1,128)S(1)} fusion(bf16[32,128,4,128]{3,2,1,0:T(4,128)(2,1)S(1)} %constant_dynamic-slice_fusion.12, bf16[32,4,128,1]{2,1,0,3:T(4,128)(2,1)S(1)} %bitcast.165), kind=kOutput, calls=%fused_computation.clone.1 | convolution fusion | flops 4194304 | bytes 4292608 | tf_op jit(solution)/shard_map/while/body/rhd,rlhd->rhl/dot_general | solution.py:54
  26.0 0.2 fusion.39
  26.3 0.2 divide_convert_fusion
  26.5 10.5 %while.21 = (s32[]{:T(128)}, f32[32,4,128]{2,1,0:T(4,128)S(1)}, s32[]{:T(128)}, bf16[32,4,384]{2,1,0:T(4,128)(2,1)S(1)}, bf16[32,384,4,128]{3,2,1,0:T(4,128)(2,1...) while((s32[]{:T(128)}, f32[32,4,128]{2,1,0:T(4,128)S(1)}, s32[]{:T(128)}, ...), condition=%wide.region_7.8_spmd, body=%wide.region_6.7_spmd.sunk | while | flops 4210694 | bytes 12943507 | solution.py:80
  26.6 3.9 %constant_dynamic-slice_fusion.13 = bf16[32,128,4,128]{3,2,1,0:T(4,128)(2,1)S(1)} fusion(bf16[32,384,4,128]{3,2,1,0:T(4,128)(2,1)} %get-tuple-element.245, s32[]{:T(128)S(6)} %select_n.64), kind=kLoop, calls=%fused_computation.9.clone.1 | loop fusion | bytes 8388612 | tf_op jit(solution)/shard_map/while/body/dynamic_slice | solution.py:75
  30.5 1.2 fusion.72
  31.7 3.9 %constant_dynamic-slice_fusion.13 = bf16[32,128,4,128]{3,2,1,0:T(4,128)(2,1)S(1)} fusion(bf16[32,384,4,128]{3,2,1,0:T(4,128)(2,1)} %get-tuple-element.245, s32[]{:T(128)S(6)} %select_n.64), kind=kLoop, calls=%fused_computation.9.clone.1 | loop fusion | bytes 8388612 | tf_op jit(solution)/shard_map/while/body/dynamic_slice | solution.py:75
  35.6 1.2 fusion.72
  37.1 0.5 convolution_convert_fusion
  37.7 0.3 constant_dynamic-slice_fusion.9
  38.0 0.4 collective-permute-start.3
  38.4 0.9 collective-permute-done.3
  39.4 2.0 %collective-permute-start.4 = (bf16[32,1024]{1,0:T(8,128)(2,1)S(1)}, bf16[32,1024]{1,0:T(8,128)(2,1)S(1)}, u32[]{:S(2)}, u32[]{:S(2)}) collective-permute-start(bf16[32,1024]{1,0:T(8,128)(2,1)S(1)} %add_convert_fusion.1), channel_id=1, source_target_pairs={{0,2},{1,3},{2,0},{3,1},{4,6},{5,7},{6,4},{7,5},{8,10},{9,11},{10,... | collective-permute-start | bytes 196616 | tf_op jit(solution)/shard_map/ppermute | solution.py:35
  41.4 2.4 %collective-permute-done.4 = bf16[32,1024]{1,0:T(8,128)(2,1)S(1)} collective-permute-done((bf16[32,1024]{1,0:T(8,128)(2,1)S(1)}, bf16[32,1024]{1,0:T(8,128)(2,1)S(1)}, u32[]{:S(2)}, u32[]{:S(2)}) %collective-permute-start.4) | collective-permute-done | bytes 65568 | tf_op jit(solution)/shard_map/ppermute | solution.py:35
  44.2 14.4 %collective-permute-start.6 = (bf16[32,1088]{1,0:T(8,128)(2,1)S(1)}, bf16[32,1088]{1,0:T(8,128)(2,1)S(1)}, u32[]{:S(2)}, u32[]{:S(2)}) collective-permute-start(bf16[32,1088]{1,0:T(8,128)(2,1)S(1)} %get-tuple-element.116), channel_id=1, source_target_pairs={{0,16},{4,20},{8,24},{12,28},{16,0},{20,4},{24,8},{28,12},{1,17},{... | collective-permute-start | bytes 208904 | tf_op jit(solution)/shard_map/ppermute | solution.py:35
  58.6 1.5 collective-permute-start.7
  60.1 14.5 %reshape.156 = bf16[16,128,4,512]{3,2,1,0:T(4,128)(2,1)} reshape(bf16[16,128,2048]{2,1,0:T(8,128)(2,1)} %param.23) | data formatting | bytes 16777216 | tf_op jit(solution)/shard_map/reshape | solution.py:158
  74.7 1.8 %collective-permute-start.8 = (bf16[128,1088]{1,0:T(8,128)(2,1)S(1)}, bf16[128,1088]{1,0:T(8,128)(2,1)S(1)}, u32[]{:S(2)}, u32[]{:S(2)}) collective-permute-start(bf16[128,1088]{1,0:T(8,128)(2,1)S(1)} %pad_maximum_fusion.2), channel_id=1, source_target_pairs={{0,4},{4,0},{8,12},{12,8},{16,20},{20,16},{24,28},{28,24},{1,5},{5... | collective-permute-start | bytes 835592 | tf_op jit(solution)/shard_map/ppermute | solution.py:35
  76.5 5.6 %collective-permute-done.8 = bf16[128,1088]{1,0:T(8,128)(2,1)S(1)} collective-permute-done((bf16[128,1088]{1,0:T(8,128)(2,1)S(1)}, bf16[128,1088]{1,0:T(8,128)(2,1)S(1)}, u32[]{:S(2)}, u32[]{:S(2)}) %collective-permute-start.8) | collective-permute-done | bytes 278560 | tf_op jit(solution)/shard_map/ppermute | solution.py:35
  82.3 27.0 %constant_dynamic-slice_fusion.5 = (bf16[16,128,1,512]{3,2,1,0:T(2,128)(2,1)}, bf16[16,128,1,512]{3,2,1,0:T(2,128)(2,1)}, bf16[16,128,1,512]{3,2,1,0:T(2,128)(2,1)}, bf16[16,128,1,512]{3,2,1,0:T(2,128)(2,1)}) fusion(bf16[16,128,4,512]{3,2,1,0:T(4,128)(2,1)} %reshape.156, s32[]{:T(128)S(6)} %select_n.49, s32[]{:T(128)S(6)} %select_n.50, s32[]{:T(128)S(6)} %select_n.51, ...), kind=kLoop, calls=%fused_computation.120 | loop fusion | bytes 16777232 | tf_op jit(solution)/shard_map/jit(dynamic_index_in_dim)/dynamic_slice | solution.py:108
  109.3 0.4 stack_reshape.6
  109.8 0.2 multiply_reduce_fusion.1
  110.0 0.4 stack_reshape.7
  110.4 1.5 pad_maximum_fusion
  111.9 0.2 copy.58
  112.2 0.2 multiply_reduce_fusion
  112.4 18.5 %broadcast_multiply_fusion = f32[256,16,256]{0,2,1:T(8,128)} fusion(f32[256]{0:T(256)S(1)} %add_rsqrt_fusion, bf16[16,2048,256]{2,0,1:T(8,128)(2,1)} %bitcast.168, bf16[256,512]{1,0:T(8,128)(2,1)S(1)} %get-tuple-element.92, bf16[256,512]{1,0:T(8,128)(2,1)S(1)} %get-tuple-element.93, bf16[256,512]{1,0:T(8,128)(2,1)S(1)} %get-tuple-element.94, ...), kind=kOutput, calls=%fused_computation.26 | convolution fusion | flops 4300210176 | bytes 22021120 | tf_op jit(solution)/shard_map/td,edn->etn/dot_general | solution.py:150
  130.8 3.1 %fusion.10 = bf16[16,256,2,1,64]{1,4,2,0,3:T(8,128)(2,1)S(1)} fusion(f32[16,256,2,2,64]{1,4,3,2,0:T(8,128)} %bitcast.146, f32[16,256]{1,0:T(8,128)S(1)} %copy.57), kind=kLoop, calls=%fused_computation.16 | loop fusion | flops 3670016 | bytes 5259264 | tf_op jit(solution)/shard_map/convert_element_type | solution.py:157
  133.9 0.4 copy-done.5
  134.3 0.7 fusion.22
  135.0 0.5 copy-done.4
  135.6 0.7 fusion.21
  136.4 0.5 collective-permute-start.10
  137.0 0.7 fusion.24
  137.7 0.4 copy-done.2
  138.1 0.7 fusion.23
  138.9 0.2 add_convert_fusion
  139.1 0.4 reshape.157
  139.4 0.7 fusion.50
  140.3 2.5 %collective-permute-start.13 = (bf16[128,512]{1,0:T(8,128)(2,1)S(1)}, bf16[128,512]{1,0:T(8,128)(2,1)S(1)}, u32[]{:S(2)}, u32[]{:S(2)}) collective-permute-start(bf16[128,512]{1,0:T(8,128)(2,1)S(1)} %bitcast.160), channel_id=1, source_target_pairs={{0,6},{1,7},{2,4},{3,5},{4,2},{5,3},{6,0},{7,1},{8,14},{9,15},{10,... | collective-permute-start | bytes 393224 | tf_op jit(solution)/shard_map/ppermute | solution.py:183
  142.8 0.5 collective-permute-start.11
  143.3 0.5 collective-permute-start.12
  143.8 3.7 %collective-permute-done.13 = bf16[128,512]{1,0:T(8,128)(2,1)S(1)} collective-permute-done((bf16[128,512]{1,0:T(8,128)(2,1)S(1)}, bf16[128,512]{1,0:T(8,128)(2,1)S(1)}, u32[]{:S(2)}, u32[]{:S(2)}) %collective-permute-start.13) | collective-permute-done | bytes 131104 | tf_op jit(solution)/shard_map/ppermute | solution.py:183
  147.5 2.5 %collective-permute-done.11 = bf16[128,512]{1,0:T(8,128)(2,1)S(1)} collective-permute-done((bf16[128,512]{1,0:T(8,128)(2,1)S(1)}, bf16[128,512]{1,0:T(8,128)(2,1)S(1)}, u32[]{:S(2)}, u32[]{:S(2)}) %collective-permute-start.11) | collective-permute-done | bytes 131104 | tf_op jit(solution)/shard_map/ppermute | solution.py:183
  150.1 0.6 collective-permute-start.14
  150.7 2.6 %collective-permute-start.16 = (bf16[32,512]{1,0:T(8,128)(2,1)S(1)}, bf16[32,512]{1,0:T(8,128)(2,1)S(1)}, u32[]{:S(2)}, u32[]{:S(2)}) collective-permute-start(bf16[32,512]{1,0:T(8,128)(2,1)S(1)} %get-tuple-element.102), channel_id=1, source_target_pairs={{0,24},{4,28},{8,16},{12,20},{16,8},{20,12},{24,0},{28,4},{1,25},{... | collective-permute-start | bytes 98312 | tf_op jit(solution)/shard_map/ppermute | solution.py:35
  153.3 0.4 collective-permute-start.15
  153.7 0.4 collective-permute-done.14
  154.1 2.5 %collective-permute-done.16 = bf16[32,512]{1,0:T(8,128)(2,1)S(1)} collective-permute-done((bf16[32,512]{1,0:T(8,128)(2,1)S(1)}, bf16[32,512]{1,0:T(8,128)(2,1)S(1)}, u32[]{:S(2)}, u32[]{:S(2)}) %collective-permute-start.16) | collective-permute-done | bytes 32800 | tf_op jit(solution)/shard_map/ppermute | solution.py:35
  156.6 1.6 collective-permute-done.15
  158.2 0.6 fusion.40
  (77 shorter events, 2.5 us)
Async XLA Ops:
  0.0 37.1 %copy-start = (bf16[512,2048]{1,0:T(8,128)(2,1)S(1)}, bf16[512,2048]{1,0:T(8,128)(2,1)}, u32[]{:S(2)}) copy-start(bf16[512,2048]{1,0:T(8,128)(2,1)} %param.19) | copy-start | bytes 6291460
  0.0 7.9 %collective-permute-start = (bf16[32,512]{1,0:T(8,128)(2,1)}, bf16[32,512]{1,0:T(8,128)(2,1)S(1)}, u32[]{:S(2)}, u32[]{:S(2)}) collective-permute-start(bf16[32,512]{1,0:T(8,128)(2,1)} %param.14), channel_id=1, source_target_pairs={{0,2},{1,3},{2,0},{3,1},{4,6},{5,7},{6,4},{7,5},{8,10},{9,11},{10,... | collective-permute-start | bytes 98312 | tf_op jit(solution)/shard_map/ppermute | solution.py:35
  3.0 4.9 %collective-permute-start.2 = (bf16[32,512]{1,0:T(8,128)(2,1)}, bf16[32,512]{1,0:T(8,128)(2,1)S(1)}, u32[]{:S(2)}, u32[]{:S(2)}) collective-permute-start(bf16[32,512]{1,0:T(8,128)(2,1)} %param.14), channel_id=1, source_target_pairs={{0,3},{1,2},{2,1},{3,0},{4,7},{5,6},{6,5},{7,4},{8,11},{9,10},{10,... | collective-permute-start | bytes 98312 | tf_op jit(solution)/shard_map/ppermute | solution.py:35
  3.0 5.0 %collective-permute-start.1 = (bf16[32,512]{1,0:T(8,128)(2,1)}, bf16[32,512]{1,0:T(8,128)(2,1)S(1)}, u32[]{:S(2)}, u32[]{:S(2)}) collective-permute-start(bf16[32,512]{1,0:T(8,128)(2,1)} %param.14), channel_id=1, source_target_pairs={{0,1},{1,0},{2,3},{3,2},{4,5},{5,4},{6,7},{7,6},{8,9},{9,8},{10,11... | collective-permute-start | bytes 98312 | tf_op jit(solution)/shard_map/ppermute | solution.py:35
  26.5 14.9 %copy-start.6 = (bf16[32,512]{1,0:T(8,128)(2,1)S(1)}, bf16[32,512]{1,0:T(8,128)(2,1)}, u32[]{:S(2)}) copy-start(bf16[32,512]{1,0:T(8,128)(2,1)} %param.14) | copy-start | bytes 98308
  38.0 1.3 collective-permute-start.3
  39.4 4.4 %collective-permute-start.4 = (bf16[32,1024]{1,0:T(8,128)(2,1)S(1)}, bf16[32,1024]{1,0:T(8,128)(2,1)S(1)}, u32[]{:S(2)}, u32[]{:S(2)}) collective-permute-start(bf16[32,1024]{1,0:T(8,128)(2,1)S(1)} %add_convert_fusion.1), channel_id=1, source_target_pairs={{0,2},{1,3},{2,0},{3,1},{4,6},{5,7},{6,4},{7,5},{8,10},{9,11},{10,... | collective-permute-start | bytes 196616 | tf_op jit(solution)/shard_map/ppermute | solution.py:35
  44.2 30.4 %collective-permute-start.6 = (bf16[32,1088]{1,0:T(8,128)(2,1)S(1)}, bf16[32,1088]{1,0:T(8,128)(2,1)S(1)}, u32[]{:S(2)}, u32[]{:S(2)}) collective-permute-start(bf16[32,1088]{1,0:T(8,128)(2,1)S(1)} %get-tuple-element.116), channel_id=1, source_target_pairs={{0,16},{4,20},{8,24},{12,28},{16,0},{20,4},{24,8},{28,12},{1,17},{... | collective-permute-start | bytes 208904 | tf_op jit(solution)/shard_map/ppermute | solution.py:35
  58.6 16.1 %collective-permute-start.5 = (bf16[32,1088]{1,0:T(8,128)(2,1)S(1)}, bf16[32,1088]{1,0:T(8,128)(2,1)S(1)}, u32[]{:S(2)}, u32[]{:S(2)}) collective-permute-start(bf16[32,1088]{1,0:T(8,128)(2,1)S(1)} %get-tuple-element.116), channel_id=1, source_target_pairs={{0,8},{4,12},{8,0},{12,4},{16,24},{20,28},{24,16},{28,20},{1,9},{5... | collective-permute-start | bytes 208904 | tf_op jit(solution)/shard_map/ppermute | solution.py:35
  58.6 16.1 %collective-permute-start.7 = (bf16[32,1088]{1,0:T(8,128)(2,1)S(1)}, bf16[32,1088]{1,0:T(8,128)(2,1)S(1)}, u32[]{:S(2)}, u32[]{:S(2)}) collective-permute-start(bf16[32,1088]{1,0:T(8,128)(2,1)S(1)} %get-tuple-element.116), channel_id=1, source_target_pairs={{0,24},{4,28},{8,16},{12,20},{16,8},{20,12},{24,0},{28,4},{1,25},{... | collective-permute-start | bytes 208904 | tf_op jit(solution)/shard_map/ppermute | solution.py:35
  74.7 7.4 %collective-permute-start.8 = (bf16[128,1088]{1,0:T(8,128)(2,1)S(1)}, bf16[128,1088]{1,0:T(8,128)(2,1)S(1)}, u32[]{:S(2)}, u32[]{:S(2)}) collective-permute-start(bf16[128,1088]{1,0:T(8,128)(2,1)S(1)} %pad_maximum_fusion.2), channel_id=1, source_target_pairs={{0,4},{4,0},{8,12},{12,8},{16,20},{20,16},{24,28},{28,24},{1,5},{5... | collective-permute-start | bytes 835592 | tf_op jit(solution)/shard_map/ppermute | solution.py:35
  82.2 27.8 %collective-permute-start.9 = (bf16[256,1024]{1,0:T(8,128)(2,1)S(1)}, bf16[256,1024]{1,0:T(8,128)(2,1)S(1)}, u32[]{:S(2)}, u32[]{:S(2)}) collective-permute-start(bf16[256,1024]{1,0:T(8,128)(2,1)S(1)} %slice.106), channel_id=1, source_target_pairs={{0,1},{1,0},{2,3},{3,2},{4,5},{5,4},{6,7},{7,6},{8,9},{9,8},{10,11... | collective-permute-start | bytes 1572872 | tf_op jit(solution)/shard_map/ppermute | solution.py:35
  130.8 3.5 %copy-start.5 = (bf16[16,128,1,512]{3,2,1,0:T(2,128)(2,1)S(1)}, bf16[16,128,1,512]{3,2,1,0:T(2,128)(2,1)}, u32[]{:S(2)}) copy-start(bf16[16,128,1,512]{3,2,1,0:T(2,128)(2,1)} %get-tuple-element.88) | copy-start | bytes 6291460
  130.8 4.7 %copy-start.4 = (bf16[16,128,1,512]{3,2,1,0:T(2,128)(2,1)S(1)}, bf16[16,128,1,512]{3,2,1,0:T(2,128)(2,1)}, u32[]{:S(2)}) copy-start(bf16[16,128,1,512]{3,2,1,0:T(2,128)(2,1)} %get-tuple-element.90) | copy-start | bytes 6291460
  133.9 3.0 %copy-start.3 = (bf16[16,128,1,512]{3,2,1,0:T(2,128)(2,1)S(1)}, bf16[16,128,1,512]{3,2,1,0:T(2,128)(2,1)}, u32[]{:S(2)}) copy-start(bf16[16,128,1,512]{3,2,1,0:T(2,128)(2,1)} %get-tuple-element.87) | copy-start | bytes 6291460
  135.0 3.1 %copy-start.2 = (bf16[16,128,1,512]{3,2,1,0:T(2,128)(2,1)S(1)}, bf16[16,128,1,512]{3,2,1,0:T(2,128)(2,1)}, u32[]{:S(2)}) copy-start(bf16[16,128,1,512]{3,2,1,0:T(2,128)(2,1)} %get-tuple-element.89) | copy-start | bytes 6291460
  136.4 2.5 %collective-permute-start.10 = (bf16[256,1024]{1,0:T(8,128)(2,1)S(1)}, bf16[256,1024]{1,0:T(8,128)(2,1)S(1)}, u32[]{:S(2)}, u32[]{:S(2)}) collective-permute-start(bf16[256,1024]{1,0:T(8,128)(2,1)S(1)} %pad_maximum_fusion.1), channel_id=1, source_target_pairs={{0,1},{1,0},{2,3},{3,2},{4,5},{5,4},{6,7},{7,6},{8,9},{9,8},{10,11... | collective-permute-start | bytes 1572872 | tf_op jit(solution)/shard_map/ppermute | solution.py:35
  138.1 20.7 %copy-start.1 = (bf16[512,2048]{1,0:T(8,128)(2,1)S(1)}, bf16[512,2048]{1,0:T(8,128)(2,1)}, u32[]{:S(2)}) copy-start(bf16[512,2048]{1,0:T(8,128)(2,1)} %param.19) | copy-start | bytes 6291460
  140.3 7.3 %collective-permute-start.13 = (bf16[128,512]{1,0:T(8,128)(2,1)S(1)}, bf16[128,512]{1,0:T(8,128)(2,1)S(1)}, u32[]{:S(2)}, u32[]{:S(2)}) collective-permute-start(bf16[128,512]{1,0:T(8,128)(2,1)S(1)} %bitcast.160), channel_id=1, source_target_pairs={{0,6},{1,7},{2,4},{3,5},{4,2},{5,3},{6,0},{7,1},{8,14},{9,15},{10,... | collective-permute-start | bytes 393224 | tf_op jit(solution)/shard_map/ppermute | solution.py:183
  142.8 7.2 %collective-permute-start.11 = (bf16[128,512]{1,0:T(8,128)(2,1)S(1)}, bf16[128,512]{1,0:T(8,128)(2,1)S(1)}, u32[]{:S(2)}, u32[]{:S(2)}) collective-permute-start(bf16[128,512]{1,0:T(8,128)(2,1)S(1)} %bitcast.159), channel_id=1, source_target_pairs={{0,4},{1,5},{2,6},{3,7},{4,0},{5,1},{6,2},{7,3},{8,12},{9,13},{10,... | collective-permute-start | bytes 393224 | tf_op jit(solution)/shard_map/ppermute | solution.py:183
  143.3 6.7 %collective-permute-start.12 = (bf16[128,512]{1,0:T(8,128)(2,1)S(1)}, bf16[128,512]{1,0:T(8,128)(2,1)S(1)}, u32[]{:S(2)}, u32[]{:S(2)}) collective-permute-start(bf16[128,512]{1,0:T(8,128)(2,1)S(1)} %bitcast.158), channel_id=1, source_target_pairs={{0,2},{1,3},{2,0},{3,1},{4,6},{5,7},{6,4},{7,5},{8,10},{9,11},{10,... | collective-permute-start | bytes 393224 | tf_op jit(solution)/shard_map/ppermute | solution.py:183
  150.1 4.0 %collective-permute-start.14 = (bf16[32,512]{1,0:T(8,128)(2,1)S(1)}, bf16[32,512]{1,0:T(8,128)(2,1)S(1)}, u32[]{:S(2)}, u32[]{:S(2)}) collective-permute-start(bf16[32,512]{1,0:T(8,128)(2,1)S(1)} %get-tuple-element.101), channel_id=1, source_target_pairs={{0,8},{4,12},{8,0},{12,4},{16,24},{20,28},{24,16},{28,20},{1,9},{5... | collective-permute-start | bytes 98312 | tf_op jit(solution)/shard_map/ppermute | solution.py:35
  150.7 6.0 %collective-permute-start.16 = (bf16[32,512]{1,0:T(8,128)(2,1)S(1)}, bf16[32,512]{1,0:T(8,128)(2,1)S(1)}, u32[]{:S(2)}, u32[]{:S(2)}) collective-permute-start(bf16[32,512]{1,0:T(8,128)(2,1)S(1)} %get-tuple-element.102), channel_id=1, source_target_pairs={{0,24},{4,28},{8,16},{12,20},{16,8},{20,12},{24,0},{28,4},{1,25},{... | collective-permute-start | bytes 98312 | tf_op jit(solution)/shard_map/ppermute | solution.py:35
  153.3 4.9 %collective-permute-start.15 = (bf16[32,512]{1,0:T(8,128)(2,1)S(1)}, bf16[32,512]{1,0:T(8,128)(2,1)S(1)}, u32[]{:S(2)}, u32[]{:S(2)}) collective-permute-start(bf16[32,512]{1,0:T(8,128)(2,1)S(1)} %get-tuple-element.103), channel_id=1, source_target_pairs={{0,16},{4,20},{8,24},{12,28},{16,0},{20,4},{24,8},{28,12},{1,17},{... | collective-permute-start | bytes 98312 | tf_op jit(solution)/shard_map/ppermute | solution.py:35

commit v2 on v1

--- a/solution.py
+++ b/solution.py
@@ -1,87 +1,205 @@
+import functools
 import jax
 import jax.numpy as jnp
 from jax import lax
+from jax.experimental import pallas as pl
+from jax.experimental.pallas import tpu as pltpu
 from jax.sharding import PartitionSpec as P
 
 UNIT_BLOCK = 64
-KEY_BLOCK = 128
 
 
 rope_theta = 50000.0
 norm_eps = 1e-05
-
-
-def rotate(values, positions):
-    half_dim = values.shape[-1] // 2
-    freqs = rope_theta ** (-jnp.arange(half_dim, dtype=jnp.float32) / half_dim)
-    angles = positions.astype(jnp.float32)[:, None] * freqs[None, :]
-    cosine = jnp.cos(angles)[:, None, :]
-    sine = jnp.sin(angles)[:, None, :]
-    first_half = values[..., :half_dim]
-    second_half = values[..., half_dim:]
-    return jnp.concatenate(
-        [first_half * cosine - second_half * sine, second_half * cosine + first_half * sine],
-        axis=-1,
-    )
-
-
-def rms_normed(values):
-    return (
-        values * lax.rsqrt(jnp.mean(values * values, axis=-1, keepdims=True) + norm_eps)
+LANES = 128
+SUBLANES = 8
+CHUNK = 64
+GROUP = 8
+MASKED = -1e30
+
+
+def attention_kernel(
+    head_count, lengths_ref, me_ref, cos_ref, sin_ref, *refs
+):
+    pieces = refs[:head_count]
+    (
+        w_qkv_ref, w_out_ref, k_ref, v_ref, keep_ref, send_ref,
+        w_qkv_s, w_out_s, k_s, v_s, query_s, key_s, value_s, attended_s,
+        qkv_sem, out_sem, k_sem, v_sem,
+    ) = refs[head_count:]
+    rows, cols = pieces[0].shape
+    heads_local = cols // LANES
+    chunk_rows = CHUNK * heads_local
+    me = me_ref[0]
+
+    def qkv_copy(c, j):
+        first = pl.multiple_of((me ^ j) * cols, cols)
+        return pltpu.make_async_copy(
+            w_qkv_ref.at[c, pl.ds(first, cols)], w_qkv_s.at[c, j], qkv_sem.at[c, j]
+        )
+
+    def out_copy(j):
+        first = pl.multiple_of((me ^ j) * cols, cols)
+        return pltpu.make_async_copy(
+            w_out_ref.at[:, pl.ds(first, cols)], w_out_s.at[j], out_sem.at[j]
+        )
+
+    def cache_copy(source, target, sem, r):
+        used = pl.multiple_of((lengths_ref[r] + 7) // 8 * (8 * heads_local), 8 * heads_local)
+        return pltpu.make_async_copy(
+            source.at[r, pl.ds(0, used)], target.at[r, pl.ds(0, used)], sem.at[r]
+        )
+
+    for c in range(3):
+        for j in range(head_count):
+            qkv_copy(c, j).start()
+
+    @pl.loop(0, rows)
+    def _(r):
+        cache_copy(k_ref, k_s, k_sem, r).start()
+        last = pl.multiple_of((lengths_ref[r] - 1) // CHUNK * chunk_rows, chunk_rows)
+        v_s[r, pl.ds(last, chunk_rows)] = jnp.zeros((chunk_rows, LANES), jnp.bfloat16)
+        cache_copy(v_ref, v_s, v_sem, r).start()
+
+    for j in range(head_count):
+        out_copy(j).start()
+
+    states = [piece[...].astype(jnp.float32) for piece in pieces]
+    square = sum(jnp.sum(state * state, axis=1, keepdims=True) for state in states)
+    scale = lax.rsqrt(square / (cols * head_count) + norm_eps)
+    normed = [(state * scale).astype(jnp.bfloat16) for state in states]
+    cosine, sine = cos_ref[...], sin_ref[...]
+    if heads_local < SUBLANES:
+        query_s[...] = jnp.zeros_like(query_s)
+        key_s[...] = jnp.zeros_like(key_s)
+        value_s[...] = jnp.zeros_like(value_s)
+    for c, target in enumerate((query_s, key_s, value_s)):
+        projected = jnp.zeros((rows, cols), jnp.float32)
+        for j in range(head_count):
+            qkv_copy(c, j).wait()
+            projected += jnp.dot(normed[j], w_qkv_s[c, j], preferred_element_type=jnp.float32)
+        for h in range(heads_local):
+            part = projected[:, h * LANES : (h + 1) * LANES]
+            if c < 2:
+                part = part * cosine + pltpu.roll(part, LANES // 2, 1) * sine
+            target[:, h, :] = part.astype(jnp.bfloat16).astype(jnp.float32)
+
+    column = lax.broadcasted_iota(jnp.int32, (SUBLANES, chunk_rows), 1)
+    row = lax.broadcasted_iota(jnp.int32, (SUBLANES, chunk_rows), 0)
+    same_head = column % heads_local == row
+    score_scale = LANES**-0.5
+
+    @pl.loop(0, rows // GROUP)
+    def _(g):
+        requests = [g * GROUP + i for i in range(GROUP)]
+        lengths = [lengths_ref[r] for r in requests]
+        queries = [query_s[r].astype(jnp.bfloat16) for r in requests]
+        top = [
+            jnp.sum(query_s[r] * key_s[r], axis=1, keepdims=True) * score_scale for r in requests
+        ]
+        total = [jnp.ones((SUBLANES, 1), jnp.float32)] * GROUP
+        accum = [value_s[r] for r in requests]
+        longest = functools.reduce(jnp.maximum, lengths)
+        for r in requests:
+            cache_copy(k_ref, k_s, k_sem, r).wait()
+            cache_copy(v_ref, v_s, v_sem, r).wait()
+
+        def step(c, carry):
+            top, total, accum = carry
+            starts = [
+                pl.multiple_of(jnp.minimum(c, (n - 1) // CHUNK) * chunk_rows, chunk_rows)
+                for n in lengths
+            ]
+            scores = [
+                lax.dot_general(
+                    queries[i],
+                    k_s[r, pl.ds(starts[i], chunk_rows)],
+                    (((1,), (1,)), ((), ())),
+                    preferred_element_type=jnp.float32,
+                )
+                for i, r in enumerate(requests)
+            ]
+            scores = [
+                jnp.where(
+                    same_head & (column < (n - c * CHUNK) * heads_local), s * score_scale, MASKED
+                )
+                for n, s in zip(lengths, scores)
+            ]
+            new_top = [
+                jnp.maximum(t, jnp.max(s, axis=1, keepdims=True)) for t, s in zip(top, scores)
+            ]
+            weights = [jnp.exp(s - t) for s, t in zip(scores, new_top)]
+            fade = [jnp.exp(a - b) for a, b in zip(top, new_top)]
+            total = [
+                t * f + jnp.sum(w, axis=1, keepdims=True) for t, f, w in zip(total, fade, weights)
+            ]
+            accum = [
+                a * f
+                + jnp.dot(
+                    w.astype(jnp.bfloat16),
+                    v_s[r, pl.ds(starts[i], chunk_rows)],
+                    preferred_element_type=jnp.float32,
+                )
+                for i, (r, a, f, w) in enumerate(zip(requests, accum, fade, weights))
+            ]
+            return new_top, total, accum
+
+        top, total, accum = lax.fori_loop(
+            0, (longest + CHUNK - 1) // CHUNK, step, (top, total, accum)
+        )
+        for r, t, a in zip(requests, total, accum):
+            attended_s[r] = a / t
+
+    attended = jnp.concatenate(
+        [attended_s[:, h, :] for h in range(heads_local)], axis=1
     ).astype(jnp.bfloat16)
+    for j in range(head_count):
+        out_copy(j).wait()
+        target = send_ref if j % 2 else keep_ref
+        target[:, j // 2 * cols : (j // 2 + 1) * cols] = jnp.dot(
+            attended, w_out_s[j], preferred_element_type=jnp.float32
+        ).astype(jnp.bfloat16)
+
+
+def attention(pieces, me, lengths, cosine, sine, w_qkv, w_out, k_cache, v_cache):
+    head_count = len(pieces)
+    rows, cols = pieces[0].shape
+    cache_len, heads_local, head_dim = k_cache.shape[1:]
+    flat = (rows, cache_len * heads_local, head_dim)
+    vmem = pl.BlockSpec(memory_space=pltpu.VMEM)
+    smem = pl.BlockSpec(memory_space=pltpu.SMEM)
+    anywhere = pl.BlockSpec(memory_space=pl.ANY)
+    half = jax.ShapeDtypeStruct((rows, head_count // 2 * cols), jnp.bfloat16)
+    return pl.pallas_call(
+        functools.partial(attention_kernel, head_count),
+        out_shape=(half, half),
+        in_specs=[smem, smem, vmem, vmem] + [vmem] * head_count + [anywhere] * 4,
+        out_specs=(vmem, vmem),
+        scratch_shapes=[
+            pltpu.VMEM((3, head_count, cols, cols), jnp.bfloat16),
+            pltpu.VMEM((head_count, cols, cols), jnp.bfloat16),
+            pltpu.VMEM(flat, jnp.bfloat16),
+            pltpu.VMEM(flat, jnp.bfloat16),
+        ]
+        + [pltpu.VMEM((rows, SUBLANES, LANES), jnp.float32)] * 4
+        + [
+            pltpu.SemaphoreType.DMA((3, head_count)),
+            pltpu.SemaphoreType.DMA((head_count,)),
+            pltpu.SemaphoreType.DMA((rows,)),
+            pltpu.SemaphoreType.DMA((rows,)),
+        ],
+        compiler_params=pltpu.CompilerParams(vmem_limit_bytes=44 * 2**20),
+        cost_estimate=pl.CostEstimate(
+            flops=2 * rows * 4 * cols * head_count * cols,
+            bytes_accessed=8 * cols * cols * head_count + 4 * rows * cache_len * cols // 2,
+            transcendentals=0,
+        ),
+        name="attention",
+    )(lengths, me, cosine, sine, *pieces, w_qkv, w_out, k_cache.reshape(flat), v_cache.reshape(flat))
 
 
 def swap(value, axis, size, mask):
     return lax.ppermute(value, axis, [(i, i ^ mask) for i in range(size)])
-
-
-def attention(normed, lengths, w_qkv, k_cache, v_cache):
-    req_local = normed.shape[0]
-    heads_local = k_cache.shape[2]
-    head_size = k_cache.shape[3]
-    cache_len = k_cache.shape[1]
-    projected = jnp.einsum("td,cdn->ctn", normed, w_qkv, preferred_element_type=jnp.float32)
-    projected = projected.reshape(3, req_local, heads_local, head_size)
-    query = rotate(projected[0], lengths).astype(jnp.bfloat16)
-    key_new = rotate(projected[1], lengths).astype(jnp.bfloat16)
-    value_new = projected[2].astype(jnp.bfloat16)
-    score_scale = head_size ** (-0.5)
-    block_count = (jnp.max(lengths) + KEY_BLOCK - 1) // KEY_BLOCK
-
-    def score_block(block_idx, buffer):
-        keys_block = lax.dynamic_slice_in_dim(k_cache, block_idx * KEY_BLOCK, KEY_BLOCK, 1)
-        block_scores = (
-            jnp.einsum("rhd,rlhd->rhl", query, keys_block, preferred_element_type=jnp.float32)
-            * score_scale
-        )
-        return lax.dynamic_update_slice_in_dim(buffer, block_scores, block_idx * KEY_BLOCK, 2)
-
-    buffer = jnp.full((req_local, heads_local, cache_len), -jnp.inf, jnp.float32)
-    buffer = lax.fori_loop(0, block_count, score_block, buffer)
-    positions = jnp.arange(cache_len, dtype=jnp.int32)
-    scores = jnp.where(positions[None, None, :] < lengths[:, None, None], buffer, -jnp.inf)
-    self_score = (
-        jnp.einsum("rhd,rhd->rh", query, key_new, preferred_element_type=jnp.float32) * score_scale
-    )
-    row_top = jnp.maximum(jnp.max(scores, axis=-1), self_score)
-    exponent = jnp.exp(scores - row_top[:, :, None])
-    self_exp = jnp.exp(self_score - row_top)
-    denominator = jnp.sum(exponent, axis=-1) + self_exp
-    weights = (exponent / denominator[:, :, None]).astype(jnp.bfloat16)
-    self_weight = (self_exp / denominator).astype(jnp.bfloat16)
-
-    def value_block(block_idx, accum):
-        weights_block = lax.dynamic_slice_in_dim(weights, block_idx * KEY_BLOCK, KEY_BLOCK, 2)
-        values_block = lax.dynamic_slice_in_dim(v_cache, block_idx * KEY_BLOCK, KEY_BLOCK, 1)
-        return accum + jnp.einsum(
-            "rhl,rlhd->rhd", weights_block, values_block, preferred_element_type=jnp.float32
-        )
-
-    accum = lax.fori_loop(
-        0, block_count, value_block, jnp.zeros((req_local, heads_local, head_size), jnp.float32)
-    )
-    accum = accum + self_weight.astype(jnp.float32)[:, :, None] * value_new.astype(jnp.float32)
-    return accum.astype(jnp.bfloat16).reshape(req_local, heads_local * head_size)
 
 
 def per_device(
@@ -94,21 +212,25 @@
     experts_local, units_local, width = w_down.shape
     even = range(0, head_size, 2)
 
-    pieces = [hidden] + [swap(hidden, "head", head_size, j) for j in range(1, head_size)]
-    stacked = jnp.stack(pieces)
-    full_rows = jnp.concatenate(
-        [lax.dynamic_index_in_dim(stacked, me ^ b, 0, False) for b in range(head_size)], axis=1
-    )
-    normed = rms_normed(full_rows.astype(jnp.float32))
-    attended = attention(normed, lengths, w_qkv, k_cache, v_cache)
-    head_terms = jnp.dot(attended, w_out, preferred_element_type=jnp.float32)
-    head_terms = head_terms.astype(jnp.bfloat16).reshape(rows, head_size, cols)
-
     def block(array, j):
         return lax.dynamic_index_in_dim(array, me ^ j, array.ndim - 2, False)
 
-    keep = jnp.concatenate([block(head_terms, j) for j in even], axis=1)
-    send = jnp.concatenate([block(head_terms, j + 1) for j in even], axis=1)
+    pieces = [hidden] + [swap(hidden, "head", head_size, j) for j in range(1, head_size)]
+    half_dim = k_cache.shape[3] // 2
+    freqs = rope_theta ** (-jnp.arange(half_dim, dtype=jnp.float32) / half_dim)
+    angles = lengths.astype(jnp.float32)[:, None] * freqs[None, :]
+    cosine, sine = jnp.cos(angles), jnp.sin(angles)
+    keep, send = attention(
+        pieces,
+        me[None].astype(jnp.int32),
+        lengths,
+        jnp.concatenate([cosine, cosine], axis=1),
+        jnp.concatenate([-sine, sine], axis=1),
+        w_qkv,
+        w_out,
+        k_cache,
+        v_cache,
+    )
     half = keep.astype(jnp.float32) + swap(send, "head", head_size, 1).astype(jnp.float32)
     half = half.astype(jnp.bfloat16)
     others = [swap(half, "head", head_size, j) for j in even if j]

time: 160 us -> 134 us (0.84)
  starting transfers between devices: 31 us -> 16.5 us
  Pallas kernels: 0 us -> 14.4 us
  matrix products: 32.7 us -> 21.4 us
  local copies, waits for them, and re-layouts: 63.1 us -> 52.9 us
  other arithmetic: 10.8 us -> 5.92 us
  waiting for transfers between devices: 19.6 us -> 21.9 us
    dynamic_slice x6 -> x0, local copies, waits for them, and re-layouts: 15.6 us -> none  [the longest x2 7.76 us: value_block(): lax.dynamic_slice_in_dim(v_cache, block_idx * KEY_BLOCK, KEY_BLOCK, 1)]
    ppermute x14, starting transfers between devices: 27.5 us -> 13 us  [swap(): return lax.ppermute(value, axis, [(i, i ^ mask) for i in range(size)])]
    pallas_call x0 -> x1, Pallas kernels: none -> 14.4 us  [attention(): pl.pallas_call(functools.partial(attention_kernel, head_count), out_shape...]
    dot_general x6 -> x0, matrix products: 11.3 us -> none  [the longest x2 4.49 us: score_block(): jnp.einsum('rhd,rlhd->rhl', query, keys_block, preferred_element_type=jnp...]
    unnamed x23 -> x25, local copies, waits for them, and re-layouts: 3.02 us -> 8.76 us
    ppermute x14, waiting for transfers between devices: 13.4 us -> 15.8 us  [swap(): return lax.ppermute(value, axis, [(i, i ^ mask) for i in range(size)])]
    dynamic_slice x2 -> x1, local copies, waits for them, and re-layouts: 27.3 us -> 27.2 us  [block(): return lax.dynamic_index_in_dim(array, me ^ j, array.ndim - 2, False)]
  transfers between devices with their start and end apart: 17 -> 17, of which waited for: 8 -> 10; matrix products, arithmetic and copies ran while one was open for 30% -> 35% of each run, Pallas kernels for 0% -> 0%
where the time goes in v2:
time: 134 us; the launch traced here: 133 us
  local copies, waits for them, and re-layouts  52.9 us (39%)
  waiting for transfers between devices  21.9 us (16%)
  matrix products  21.4 us (16%)
  starting transfers between devices  16.5 us (12%)
  Pallas kernels  14.4 us (11%)
  other arithmetic  5.92 us (4%)
    dynamic_slice x1, local copies, waits for them, and re-layouts, block(): return lax.dynamic_index_in_dim(array, me ^ j, array.ndim - 2, False)  27.2 us
    dot_general x1, matrix products, per_device(): jnp.einsum('td,edn->etn', ordered, w_flat, preferred_element_type=jnp.flo...  18.4 us
    ppermute x14, waiting for transfers between devices, swap(): return lax.ppermute(value, axis, [(i, i ^ mask) for i in range(size)])  15.8 us
    reshape x1, local copies, waits for them, and re-layouts, per_device(): w_blocks = w_down.reshape(experts_local, units_local, head_size, cols)  14.5 us
    pallas_call x1, Pallas kernels, attention(): pl.pallas_call(functools.partial(attention_kernel, head_count), out_shape...  14.4 us
    ppermute x14, starting transfers between devices, swap(): return lax.ppermute(value, axis, [(i, i ^ mask) for i in range(size)])  13 us
    unnamed x25, local copies, waits for them, and re-layouts  8.76 us
    ppermute x3, waiting for transfers between devices, per_device(): got = lax.ppermute(summed[k, :, j // 2], ('req', 'head'), pairs)  6.1 us
  transfers between devices with their start and end apart: 17, of which 10 were waited for; matrix products, arithmetic and copies ran while one was open for 35% of the time, Pallas kernels for 0%

profile of v2, /device:TPU:0, one launch (start us, length us, event | category | flops | bytes accessed | tf_op | source)
XLA Modules:
  0.0 133.3 jit_solution(111119381548117949)
XLA Ops:
  0.0 0.5 collective-permute-start.1
  0.5 2.5 %collective-permute-start = (bf16[32,512]{1,0:T(8,128)(2,1)}, bf16[32,512]{1,0:T(8,128)(2,1)S(1)}, u32[]{:S(2)}, u32[]{:S(2)}) collective-permute-start(bf16[32,512]{1,0:T(8,128)(2,1)} %refs_0_.1), channel_id=1, source_target_pairs={{0,2},{1,3},{2,0},{3,1},{4,6},{5,7},{6,4},{7,5},{8,10},{9,11},{10,... | collective-permute-start | bytes 98312 | tf_op jit(solution)/shard_map/ppermute | solution.py:202
  3.0 0.1 collective-permute-start.2
  3.1 0.7 convert_element_type.114
  3.8 0.1 fusion.29
  3.9 0.1 pad_maximum_fusion.4
  4.0 0.8 copy.42
  4.8 0.8 copy.43
  5.6 1.0 collective-permute-done.2.refs_3_
  6.5 2.8 %copy-done = bf16[3,2048,512]{2,1,0:T(8,128)(2,1)S(1)} copy-done((bf16[3,2048,512]{2,1,0:T(8,128)(2,1)S(1)}, bf16[3,2048,512]{2,1,0:T(8,128)(2,1)}, u32[]{:S(2)}) %copy-start) | copy-done | bytes 6291480
  9.3 1.6 %copy-done.1 = bf16[512,2048]{1,0:T(8,128)(2,1)S(1)} copy-done((bf16[512,2048]{1,0:T(8,128)(2,1)S(1)}, bf16[512,2048]{1,0:T(8,128)(2,1)}, u32[]{:S(2)}) %copy-start.1) | copy-done | bytes 2097176
  10.9 0.8 copy-done.2
  11.7 0.7 copy-done.3
  12.3 14.4 %attention.1 = (bf16[32,1024]{1,0:T(8,128)(2,1)S(1)}, bf16[32,1024]{1,0:T(8,128)(2,1)S(1)}) custom-call(s32[32]{0:T(128)S(1)} %copy-done.3, s32[1]{0:T(128)} %bitcast.2.me_ref, f32[32,128]{1,0:T(8,128)S(1)} %get-tuple-element.33.cos_ref, f32[32,128]{1,0:T(8,128)S(1)} %get-tuple-element.34.sin_ref, bf16[32,512]{1,0:T(8,128)(2,1)S(1)} %copy-done.2, ...), custom_call_target="tpu_custom_call" | custom-call | flops 268435456 | bytes 20971520 | tf_op jit(solution)/shard_map/attention/pallas_call | solution.py:173
  26.8 0.3 collective-permute-start.3
  27.1 0.2 select_reduce_fusion
  27.2 0.9 collective-permute-done.3
  28.1 0.9 collective-permute-start.4
  29.0 3.4 %collective-permute-done.4 = bf16[32,1024]{1,0:T(8,128)(2,1)S(1)} collective-permute-done((bf16[32,1024]{1,0:T(8,128)(2,1)S(1)}, bf16[32,1024]{1,0:T(8,128)(2,1)S(1)}, u32[]{:S(2)}, u32[]{:S(2)}) %collective-permute-start.4) | collective-permute-done | bytes 65568 | tf_op jit(solution)/shard_map/ppermute | solution.py:202
  32.5 0.1 fusion.34
  32.6 0.2 maximum_convert_fusion
  32.8 0.1 collective-permute-start.6
  32.9 1.6 %collective-permute-start.5 = (bf16[32,1088]{1,0:T(8,128)(2,1)S(1)}, bf16[32,1088]{1,0:T(8,128)(2,1)S(1)}, u32[]{:S(2)}, u32[]{:S(2)}) collective-permute-start(bf16[32,1088]{1,0:T(8,128)(2,1)S(1)} %get-tuple-element.26), channel_id=1, source_target_pairs={{0,8},{4,12},{8,0},{12,4},{16,24},{20,28},{24,16},{28,20},{1,9},{5... | collective-permute-start | bytes 208904 | tf_op jit(solution)/shard_map/ppermute | solution.py:202
  34.5 2.7 %collective-permute-start.7 = (bf16[32,1088]{1,0:T(8,128)(2,1)S(1)}, bf16[32,1088]{1,0:T(8,128)(2,1)S(1)}, u32[]{:S(2)}, u32[]{:S(2)}) collective-permute-start(bf16[32,1088]{1,0:T(8,128)(2,1)S(1)} %get-tuple-element.26), channel_id=1, source_target_pairs={{0,24},{4,28},{8,16},{12,20},{16,8},{20,12},{24,0},{28,4},{1,25},{... | collective-permute-start | bytes 208904 | tf_op jit(solution)/shard_map/ppermute | solution.py:202
  37.3 14.5 %reshape.70 = bf16[16,128,4,512]{3,2,1,0:T(4,128)(2,1)} reshape(bf16[16,128,2048]{2,1,0:T(8,128)(2,1)} %param.19) | data formatting | bytes 16777216 | tf_op jit(solution)/shard_map/reshape | solution.py:280
  51.9 0.1 collective-permute-start.8
  52.0 7.1 %collective-permute-done.8 = bf16[128,1088]{1,0:T(8,128)(2,1)S(1)} collective-permute-done((bf16[128,1088]{1,0:T(8,128)(2,1)S(1)}, bf16[128,1088]{1,0:T(8,128)(2,1)S(1)}, u32[]{:S(2)}, u32[]{:S(2)}) %collective-permute-start.8) | collective-permute-done | bytes 278560 | tf_op jit(solution)/shard_map/ppermute | solution.py:202
  59.2 0.1 collective-permute-start.9
  59.3 27.2 %constant_dynamic-slice_fusion.3 = (bf16[16,128,1,512]{3,2,1,0:T(2,128)(2,1)}, bf16[16,128,1,512]{3,2,1,0:T(2,128)(2,1)}, bf16[16,128,1,512]{3,2,1,0:T(2,128)(2,1)}, bf16[16,128,1,512]{3,2,1,0:T(2,128)(2,1)}) fusion(bf16[16,128,4,512]{3,2,1,0:T(4,128)(2,1)} %reshape.70, s32[]{:T(128)S(6)} %select_n.22, s32[]{:T(128)S(6)} %select_n.23, s32[]{:T(128)S(6)} %select_n.24, ...), kind=kLoop, calls=%fused_computation.72 | loop fusion | bytes 16777232 | tf_op jit(solution)/shard_map/jit(dynamic_index_in_dim)/dynamic_slice | solution.py:216
  86.5 0.4 stack_reshape.6
  86.8 0.1 convert_bitcast_fusion
  87.0 0.1 copy.45
  87.1 0.2 multiply_reduce_fusion.1
  87.2 0.4 stack_reshape.7
  87.7 0.1 pad_maximum_fusion
  87.8 0.1 dynamic-slice_bitcast_fusion.3
  87.9 0.2 multiply_reduce_fusion
  88.1 18.4 %broadcast_multiply_fusion = f32[256,16,256]{0,2,1:T(8,128)} fusion(f32[256]{0:T(256)S(1)} %add_rsqrt_fusion, bf16[16,2048,256]{2,0,1:T(8,128)(2,1)} %bitcast.119, bf16[256,512]{1,0:T(8,128)(2,1)S(1)} %get-tuple-element.16, bf16[256,512]{1,0:T(8,128)(2,1)S(1)} %get-tuple-element.17, bf16[256,512]{1,0:T(8,128)(2,1)S(1)} %get-tuple-element.18, ...), kind=kOutput, calls=%fused_computation.15 | convolution fusion | flops 4300210176 | bytes 22021120 | tf_op jit(solution)/shard_map/td,edn->etn/dot_general | solution.py:272
  106.5 3.1 %fusion.4 = bf16[16,256,2,1,64]{1,4,2,0,3:T(8,128)(2,1)S(1)} fusion(f32[16,256,2,2,64]{1,4,3,2,0:T(8,128)} %bitcast.107, f32[16,256]{1,0:T(8,128)S(1)} %copy.44), kind=kLoop, calls=%fused_computation.5 | loop fusion | flops 3670016 | bytes 5259264 | tf_op jit(solution)/shard_map/convert_element_type | solution.py:279
  109.7 0.3 copy-done.7
  110.0 0.7 fusion.16
  110.7 0.5 copy-done.6
  111.3 0.7 fusion.15
  112.1 0.5 collective-permute-start.10
  112.7 0.7 fusion.18
  113.4 0.4 copy-done.4
  113.8 0.7 fusion.17
  114.6 0.2 add_convert_fusion
  114.8 0.4 reshape.71
  115.2 0.7 fusion.32
  116.0 0.6 collective-permute-start.13
  116.6 1.7 %collective-permute-start.11 = (bf16[128,512]{1,0:T(8,128)(2,1)S(1)}, bf16[128,512]{1,0:T(8,128)(2,1)S(1)}, u32[]{:S(2)}, u32[]{:S(2)}) collective-permute-start(bf16[128,512]{1,0:T(8,128)(2,1)S(1)} %bitcast.117), channel_id=1, source_target_pairs={{0,4},{1,5},{2,6},{3,7},{4,0},{5,1},{6,2},{7,3},{8,12},{9,13},{10,... | collective-permute-start | bytes 393224 | tf_op jit(solution)/shard_map/ppermute | solution.py:305
  118.3 1.2 collective-permute-start.12
  119.5 3.7 %collective-permute-done.13 = bf16[128,512]{1,0:T(8,128)(2,1)S(1)} collective-permute-done((bf16[128,512]{1,0:T(8,128)(2,1)S(1)}, bf16[128,512]{1,0:T(8,128)(2,1)S(1)}, u32[]{:S(2)}, u32[]{:S(2)}) %collective-permute-start.13) | collective-permute-done | bytes 131104 | tf_op jit(solution)/shard_map/ppermute | solution.py:305
  123.3 1.7 %collective-permute-done.11 = bf16[128,512]{1,0:T(8,128)(2,1)S(1)} collective-permute-done((bf16[128,512]{1,0:T(8,128)(2,1)S(1)}, bf16[128,512]{1,0:T(8,128)(2,1)S(1)}, u32[]{:S(2)}, u32[]{:S(2)}) %collective-permute-start.11) | collective-permute-done | bytes 131104 | tf_op jit(solution)/shard_map/ppermute | solution.py:305
  125.0 0.7 collective-permute-done.12
  125.6 0.1 fusion.27
  125.7 0.7 collective-permute-start.14
  126.5 1.4 %collective-permute-start.16 = (bf16[32,512]{1,0:T(8,128)(2,1)S(1)}, bf16[32,512]{1,0:T(8,128)(2,1)S(1)}, u32[]{:S(2)}, u32[]{:S(2)}) collective-permute-start(bf16[32,512]{1,0:T(8,128)(2,1)S(1)} %get-tuple-element.24), channel_id=1, source_target_pairs={{0,24},{4,28},{8,16},{12,20},{16,8},{20,12},{24,0},{28,4},{1,25},{... | collective-permute-start | bytes 98312 | tf_op jit(solution)/shard_map/ppermute | solution.py:202
  127.8 1.4 %collective-permute-start.15 = (bf16[32,512]{1,0:T(8,128)(2,1)S(1)}, bf16[32,512]{1,0:T(8,128)(2,1)S(1)}, u32[]{:S(2)}, u32[]{:S(2)}) collective-permute-start(bf16[32,512]{1,0:T(8,128)(2,1)S(1)} %get-tuple-element.25), channel_id=1, source_target_pairs={{0,16},{4,20},{8,24},{12,28},{16,0},{20,4},{24,8},{28,12},{1,17},{... | collective-permute-start | bytes 98312 | tf_op jit(solution)/shard_map/ppermute | solution.py:202
  129.3 0.4 collective-permute-done.14
  129.7 2.5 %collective-permute-done.16 = bf16[32,512]{1,0:T(8,128)(2,1)S(1)} collective-permute-done((bf16[32,512]{1,0:T(8,128)(2,1)S(1)}, bf16[32,512]{1,0:T(8,128)(2,1)S(1)}, u32[]{:S(2)}, u32[]{:S(2)}) %collective-permute-start.16) | collective-permute-done | bytes 32800 | tf_op jit(solution)/shard_map/ppermute | solution.py:202
  132.2 0.5 collective-permute-done.15
  132.7 0.6 fusion.28
  (39 shorter events, 0.6 us)
Async XLA Ops:
  0.0 5.5 %collective-permute-start.1 = (bf16[32,512]{1,0:T(8,128)(2,1)}, bf16[32,512]{1,0:T(8,128)(2,1)S(1)}, u32[]{:S(2)}, u32[]{:S(2)}) collective-permute-start(bf16[32,512]{1,0:T(8,128)(2,1)} %refs_0_.1), channel_id=1, source_target_pairs={{0,1},{1,0},{2,3},{3,2},{4,5},{5,4},{6,7},{7,6},{8,9},{9,8},{10,11... | collective-permute-start | bytes 98312 | tf_op jit(solution)/shard_map/ppermute | solution.py:202
  0.5 5.1 %collective-permute-start = (bf16[32,512]{1,0:T(8,128)(2,1)}, bf16[32,512]{1,0:T(8,128)(2,1)S(1)}, u32[]{:S(2)}, u32[]{:S(2)}) collective-permute-start(bf16[32,512]{1,0:T(8,128)(2,1)} %refs_0_.1), channel_id=1, source_target_pairs={{0,2},{1,3},{2,0},{3,1},{4,6},{5,7},{6,4},{7,5},{8,10},{9,11},{10,... | collective-permute-start | bytes 98312 | tf_op jit(solution)/shard_map/ppermute | solution.py:202
  3.0 3.6 %collective-permute-start.2 = (bf16[32,512]{1,0:T(8,128)(2,1)}, bf16[32,512]{1,0:T(8,128)(2,1)S(1)}, u32[]{:S(2)}, u32[]{:S(2)}) collective-permute-start(bf16[32,512]{1,0:T(8,128)(2,1)} %refs_0_.1), channel_id=1, source_target_pairs={{0,3},{1,2},{2,1},{3,0},{4,7},{5,6},{6,5},{7,4},{8,11},{9,10},{10,... | collective-permute-start | bytes 98312 | tf_op jit(solution)/shard_map/ppermute | solution.py:202
  6.5 2.8 %copy-start = (bf16[3,2048,512]{2,1,0:T(8,128)(2,1)S(1)}, bf16[3,2048,512]{2,1,0:T(8,128)(2,1)}, u32[]{:S(2)}) copy-start(bf16[3,2048,512]{2,1,0:T(8,128)(2,1)} %refs_4_.1) | copy-start | bytes 18874372
  9.3 1.6 %copy-start.1 = (bf16[512,2048]{1,0:T(8,128)(2,1)S(1)}, bf16[512,2048]{1,0:T(8,128)(2,1)}, u32[]{:S(2)}) copy-start(bf16[512,2048]{1,0:T(8,128)(2,1)} %refs_5_.1) | copy-start | bytes 6291460
  10.9 0.8 copy-start.2
  11.7 0.7 copy-start.3
  26.8 1.3 collective-permute-start.3
  28.1 4.3 %collective-permute-start.4 = (bf16[32,1024]{1,0:T(8,128)(2,1)S(1)}, bf16[32,1024]{1,0:T(8,128)(2,1)S(1)}, u32[]{:S(2)}, u32[]{:S(2)}) collective-permute-start(bf16[32,1024]{1,0:T(8,128)(2,1)S(1)} %add_convert_fusion.1), channel_id=1, source_target_pairs={{0,2},{1,3},{2,0},{3,1},{4,6},{5,7},{6,4},{7,5},{8,10},{9,11},{10,... | collective-permute-start | bytes 196616 | tf_op jit(solution)/shard_map/ppermute | solution.py:202
  32.8 19.0 %collective-permute-start.6 = (bf16[32,1088]{1,0:T(8,128)(2,1)S(1)}, bf16[32,1088]{1,0:T(8,128)(2,1)S(1)}, u32[]{:S(2)}, u32[]{:S(2)}) collective-permute-start(bf16[32,1088]{1,0:T(8,128)(2,1)S(1)} %get-tuple-element.26), channel_id=1, source_target_pairs={{0,16},{4,20},{8,24},{12,28},{16,0},{20,4},{24,8},{28,12},{1,17},{... | collective-permute-start | bytes 208904 | tf_op jit(solution)/shard_map/ppermute | solution.py:202
  32.9 18.9 %collective-permute-start.5 = (bf16[32,1088]{1,0:T(8,128)(2,1)S(1)}, bf16[32,1088]{1,0:T(8,128)(2,1)S(1)}, u32[]{:S(2)}, u32[]{:S(2)}) collective-permute-start(bf16[32,1088]{1,0:T(8,128)(2,1)S(1)} %get-tuple-element.26), channel_id=1, source_target_pairs={{0,8},{4,12},{8,0},{12,4},{16,24},{20,28},{24,16},{28,20},{1,9},{5... | collective-permute-start | bytes 208904 | tf_op jit(solution)/shard_map/ppermute | solution.py:202
  34.5 17.3 %collective-permute-start.7 = (bf16[32,1088]{1,0:T(8,128)(2,1)S(1)}, bf16[32,1088]{1,0:T(8,128)(2,1)S(1)}, u32[]{:S(2)}, u32[]{:S(2)}) collective-permute-start(bf16[32,1088]{1,0:T(8,128)(2,1)S(1)} %get-tuple-element.26), channel_id=1, source_target_pairs={{0,24},{4,28},{8,16},{12,20},{16,8},{20,12},{24,0},{28,4},{1,25},{... | collective-permute-start | bytes 208904 | tf_op jit(solution)/shard_map/ppermute | solution.py:202
  51.9 7.2 %collective-permute-start.8 = (bf16[128,1088]{1,0:T(8,128)(2,1)S(1)}, bf16[128,1088]{1,0:T(8,128)(2,1)S(1)}, u32[]{:S(2)}, u32[]{:S(2)}) collective-permute-start(bf16[128,1088]{1,0:T(8,128)(2,1)S(1)} %pad_maximum_fusion.2), channel_id=1, source_target_pairs={{0,4},{4,0},{8,12},{12,8},{16,20},{20,16},{24,28},{28,24},{1,5},{5... | collective-permute-start | bytes 835592 | tf_op jit(solution)/shard_map/ppermute | solution.py:202
  59.2 28.1 %collective-permute-start.9 = (bf16[256,1024]{1,0:T(8,128)(2,1)S(1)}, bf16[256,1024]{1,0:T(8,128)(2,1)S(1)}, u32[]{:S(2)}, u32[]{:S(2)}) collective-permute-start(bf16[256,1024]{1,0:T(8,128)(2,1)S(1)} %slice.67), channel_id=1, source_target_pairs={{0,1},{1,0},{2,3},{3,2},{4,5},{5,4},{6,7},{7,6},{8,9},{9,8},{10,11... | collective-permute-start | bytes 1572872 | tf_op jit(solution)/shard_map/ppermute | solution.py:202
  106.5 3.5 %copy-start.7 = (bf16[16,128,1,512]{3,2,1,0:T(2,128)(2,1)S(1)}, bf16[16,128,1,512]{3,2,1,0:T(2,128)(2,1)}, u32[]{:S(2)}) copy-start(bf16[16,128,1,512]{3,2,1,0:T(2,128)(2,1)} %get-tuple-element.12) | copy-start | bytes 6291460
  106.5 4.7 %copy-start.6 = (bf16[16,128,1,512]{3,2,1,0:T(2,128)(2,1)S(1)}, bf16[16,128,1,512]{3,2,1,0:T(2,128)(2,1)}, u32[]{:S(2)}) copy-start(bf16[16,128,1,512]{3,2,1,0:T(2,128)(2,1)} %get-tuple-element.14) | copy-start | bytes 6291460
  109.7 3.0 %copy-start.5 = (bf16[16,128,1,512]{3,2,1,0:T(2,128)(2,1)S(1)}, bf16[16,128,1,512]{3,2,1,0:T(2,128)(2,1)}, u32[]{:S(2)}) copy-start(bf16[16,128,1,512]{3,2,1,0:T(2,128)(2,1)} %get-tuple-element.11) | copy-start | bytes 6291460
  110.7 3.1 %copy-start.4 = (bf16[16,128,1,512]{3,2,1,0:T(2,128)(2,1)S(1)}, bf16[16,128,1,512]{3,2,1,0:T(2,128)(2,1)}, u32[]{:S(2)}) copy-start(bf16[16,128,1,512]{3,2,1,0:T(2,128)(2,1)} %get-tuple-element.13) | copy-start | bytes 6291460
  112.1 2.5 %collective-permute-start.10 = (bf16[256,1024]{1,0:T(8,128)(2,1)S(1)}, bf16[256,1024]{1,0:T(8,128)(2,1)S(1)}, u32[]{:S(2)}, u32[]{:S(2)}) collective-permute-start(bf16[256,1024]{1,0:T(8,128)(2,1)S(1)} %pad_maximum_fusion.1), channel_id=1, source_target_pairs={{0,1},{1,0},{2,3},{3,2},{4,5},{5,4},{6,7},{7,6},{8,9},{9,8},{10,11... | collective-permute-start | bytes 1572872 | tf_op jit(solution)/shard_map/ppermute | solution.py:202
  116.0 7.3 %collective-permute-start.13 = (bf16[128,512]{1,0:T(8,128)(2,1)S(1)}, bf16[128,512]{1,0:T(8,128)(2,1)S(1)}, u32[]{:S(2)}, u32[]{:S(2)}) collective-permute-start(bf16[128,512]{1,0:T(8,128)(2,1)S(1)} %bitcast.118), channel_id=1, source_target_pairs={{0,6},{1,7},{2,4},{3,5},{4,2},{5,3},{6,0},{7,1},{8,14},{9,15},{10,... | collective-permute-start | bytes 393224 | tf_op jit(solution)/shard_map/ppermute | solution.py:305
  116.6 8.4 %collective-permute-start.11 = (bf16[128,512]{1,0:T(8,128)(2,1)S(1)}, bf16[128,512]{1,0:T(8,128)(2,1)S(1)}, u32[]{:S(2)}, u32[]{:S(2)}) collective-permute-start(bf16[128,512]{1,0:T(8,128)(2,1)S(1)} %bitcast.117), channel_id=1, source_target_pairs={{0,4},{1,5},{2,6},{3,7},{4,0},{5,1},{6,2},{7,3},{8,12},{9,13},{10,... | collective-permute-start | bytes 393224 | tf_op jit(solution)/shard_map/ppermute | solution.py:305
  118.3 7.3 %collective-permute-start.12 = (bf16[128,512]{1,0:T(8,128)(2,1)S(1)}, bf16[128,512]{1,0:T(8,128)(2,1)S(1)}, u32[]{:S(2)}, u32[]{:S(2)}) collective-permute-start(bf16[128,512]{1,0:T(8,128)(2,1)S(1)} %bitcast.116), channel_id=1, source_target_pairs={{0,2},{1,3},{2,0},{3,1},{4,6},{5,7},{6,4},{7,5},{8,10},{9,11},{10,... | collective-permute-start | bytes 393224 | tf_op jit(solution)/shard_map/ppermute | solution.py:305
  125.7 4.0 %collective-permute-start.14 = (bf16[32,512]{1,0:T(8,128)(2,1)S(1)}, bf16[32,512]{1,0:T(8,128)(2,1)S(1)}, u32[]{:S(2)}, u32[]{:S(2)}) collective-permute-start(bf16[32,512]{1,0:T(8,128)(2,1)S(1)} %get-tuple-element.23), channel_id=1, source_target_pairs={{0,8},{4,12},{8,0},{12,4},{16,24},{20,28},{24,16},{28,20},{1,9},{5... | collective-permute-start | bytes 98312 | tf_op jit(solution)/shard_map/ppermute | solution.py:202
  126.5 5.7 %collective-permute-start.16 = (bf16[32,512]{1,0:T(8,128)(2,1)S(1)}, bf16[32,512]{1,0:T(8,128)(2,1)S(1)}, u32[]{:S(2)}, u32[]{:S(2)}) collective-permute-start(bf16[32,512]{1,0:T(8,128)(2,1)S(1)} %get-tuple-element.24), channel_id=1, source_target_pairs={{0,24},{4,28},{8,16},{12,20},{16,8},{20,12},{24,0},{28,4},{1,25},{... | collective-permute-start | bytes 98312 | tf_op jit(solution)/shard_map/ppermute | solution.py:202
  127.8 4.9 %collective-permute-start.15 = (bf16[32,512]{1,0:T(8,128)(2,1)S(1)}, bf16[32,512]{1,0:T(8,128)(2,1)S(1)}, u32[]{:S(2)}, u32[]{:S(2)}) collective-permute-start(bf16[32,512]{1,0:T(8,128)(2,1)S(1)} %get-tuple-element.25), channel_id=1, source_target_pairs={{0,16},{4,20},{8,24},{12,28},{16,0},{20,4},{24,8},{28,12},{1,17},{... | collective-permute-start | bytes 98312 | tf_op jit(solution)/shard_map/ppermute | solution.py:202

commit v3 on v2

--- a/solution.py
+++ b/solution.py
@@ -5,9 +5,6 @@
 from jax.experimental import pallas as pl
 from jax.experimental.pallas import tpu as pltpu
 from jax.sharding import PartitionSpec as P
-
-UNIT_BLOCK = 64
-
 
 rope_theta = 50000.0
 norm_eps = 1e-05
@@ -198,6 +195,183 @@
     )(lengths, me, cosine, sine, *pieces, w_qkv, w_out, k_cache.reshape(flat), v_cache.reshape(flat))
 
 
+RELAYOUT_ROWS = 128
+RELAYOUT_STEP = 16
+
+
+def relayout_kernel(j, me_ref, w_ref, out_ref, in_s, in_sem):
+    experts, cols, _ = out_ref.shape
+    base = (me_ref[0] ^ j) * cols
+    step = min(RELAYOUT_ROWS, cols)
+    copies = [
+        pltpu.make_async_copy(
+            w_ref.at[pl.ds(pl.multiple_of(base + i * step, step), step)], in_s.at[i], in_sem.at[i]
+        )
+        for i in range(cols // step)
+    ]
+    for copy in copies:
+        copy.start()
+    for i, copy in enumerate(copies):
+        copy.wait()
+
+        @pl.loop(0, step // RELAYOUT_STEP, unroll=True)
+        def _(s):
+            first = pl.multiple_of(s * RELAYOUT_STEP, RELAYOUT_STEP)
+            part = in_s[i, pl.ds(first, RELAYOUT_STEP)]
+            out_ref[:, pl.ds(pl.multiple_of(i * step + first, RELAYOUT_STEP), RELAYOUT_STEP), :] = (
+                jnp.swapaxes(part, 0, 1)
+            )
+
+
+def by_expert(j, me, w_in, head_count):
+    width, experts, columns = w_in.shape
+    cols = width // head_count
+    step = min(RELAYOUT_ROWS, cols)
+    return pl.pallas_call(
+        functools.partial(relayout_kernel, j),
+        out_shape=pltpu.VMEM((experts, cols, columns), jnp.bfloat16),
+        in_specs=[pl.BlockSpec(memory_space=pltpu.SMEM), pl.BlockSpec(memory_space=pl.ANY)],
+        out_specs=pl.BlockSpec(memory_space=pltpu.VMEM),
+        scratch_shapes=[
+            pltpu.VMEM((cols // step, step, experts, columns), jnp.bfloat16),
+            pltpu.SemaphoreType.DMA((cols // step,)),
+        ],
+        compiler_params=pltpu.CompilerParams(vmem_limit_bytes=16 * 2**20),
+        cost_estimate=pl.CostEstimate(
+            flops=0, bytes_accessed=4 * cols * experts * columns, transcendentals=0
+        ),
+        name=f"by_expert_{j}",
+    )(me, w_in)
+
+
+def down_copy(w_ref, scratch, sem, me, j, t):
+    cols = scratch.shape[2]
+    first = pl.multiple_of((me ^ j) * cols, cols)
+    return pltpu.make_async_copy(w_ref.at[:, pl.ds(first, cols)], scratch.at[t], sem.at[t])
+
+
+def experts_kernel(head_count, me_ref, mine_ref, other_ref, *refs):
+    weights = refs[:head_count]
+    w_down_ref, units_ref, send_ref, down_s, down_sem = refs[head_count:]
+    me = me_ref[0]
+    blocks = head_count // 2
+    for t in range(blocks):
+        down_copy(w_down_ref, down_s, down_sem, me, 2 * t + 1, t).start()
+    experts, cols, columns = weights[0].shape
+    tokens = mine_ref.shape[0]
+    states = [
+        (other_ref if j % 2 else mine_ref)[:, j // 2 * cols : (j // 2 + 1) * cols]
+        for j in range(head_count)
+    ]
+    shares = mine_ref[:, blocks * cols :]
+    square = sum(
+        jnp.sum(jnp.square(state.astype(jnp.float32)), axis=1, keepdims=True) for state in states
+    )
+    scale = lax.rsqrt(square / (head_count * cols) + norm_eps)
+    per_step = max(1, 2 * LANES // columns)
+    first_half = lax.broadcasted_iota(jnp.int32, (tokens, LANES), 1) < LANES // 2
+    source = lax.broadcasted_iota(jnp.int32, (LANES, LANES), 0)
+    lane = lax.broadcasted_iota(jnp.int32, (LANES, LANES), 1)
+
+    @pl.loop(0, experts // per_step)
+    def _(p):
+        products = [
+            sum(
+                jnp.dot(state, w[p * per_step + i], preferred_element_type=jnp.float32)
+                for state, w in zip(states, weights)
+            )
+            for i in range(per_step)
+        ]
+        product = products[0] if per_step == 1 else jnp.concatenate(products, axis=1)
+        expert = me * experts + p * per_step + lane * per_step // LANES
+        share = jnp.dot(
+            shares, (source == expert).astype(jnp.bfloat16), preferred_element_type=jnp.float32
+        )
+        a, b = product[:, :LANES], product[:, LANES:]
+        gate = jnp.where(first_half, a, pltpu.roll(b, LANES // 2, 1)) * scale
+        upward = jnp.where(first_half, pltpu.roll(a, LANES // 2, 1), b) * scale
+        units = share * (gate / (1.0 + jnp.exp(-gate)) * upward)
+        units_ref[:, pl.ds(pl.multiple_of(p * LANES, LANES), LANES)] = units.astype(jnp.bfloat16)
+
+    units = units_ref[...]
+    for t in range(blocks):
+        down_copy(w_down_ref, down_s, down_sem, me, 2 * t + 1, t).wait()
+        send_ref[:, t * cols : (t + 1) * cols] = jnp.dot(
+            units, down_s[t], preferred_element_type=jnp.float32
+        ).astype(jnp.bfloat16)
+
+
+def experts_part(me, mine, other, weights, w_down):
+    head_count = len(weights)
+    experts, cols, columns = weights[0].shape
+    tokens = mine.shape[0]
+    total_units = w_down.shape[0]
+    vmem = pl.BlockSpec(memory_space=pltpu.VMEM)
+    return pl.pallas_call(
+        functools.partial(experts_kernel, head_count),
+        out_shape=(
+            jax.ShapeDtypeStruct((tokens, total_units), jnp.bfloat16),
+            jax.ShapeDtypeStruct((tokens, head_count // 2 * cols), jnp.bfloat16),
+        ),
+        in_specs=[pl.BlockSpec(memory_space=pltpu.SMEM)]
+        + [vmem] * (2 + head_count)
+        + [pl.BlockSpec(memory_space=pl.ANY)],
+        out_specs=(vmem, vmem),
+        scratch_shapes=[
+            pltpu.VMEM((head_count // 2, total_units, cols), jnp.bfloat16),
+            pltpu.SemaphoreType.DMA((head_count // 2,)),
+        ],
+        compiler_params=pltpu.CompilerParams(vmem_limit_bytes=16 * 2**20),
+        cost_estimate=pl.CostEstimate(
+            flops=2 * tokens * head_count * cols * experts * columns,
+            bytes_accessed=2 * head_count * cols * experts * columns,
+            transcendentals=0,
+        ),
+        name="experts",
+    )(me, mine, other, *[pltpu.with_memory_space_constraint(w, pltpu.VMEM) for w in weights], w_down)
+
+
+def down_kernel(head_count, me_ref, units_ref, w_down_ref, keep_ref, down_s, down_sem):
+    me = me_ref[0]
+    cols = down_s.shape[2]
+    blocks = head_count // 2
+    for t in range(blocks):
+        down_copy(w_down_ref, down_s, down_sem, me, 2 * t, t).start()
+    units = units_ref[...]
+    for t in range(blocks):
+        down_copy(w_down_ref, down_s, down_sem, me, 2 * t, t).wait()
+        keep_ref[:, t * cols : (t + 1) * cols] = jnp.dot(
+            units, down_s[t], preferred_element_type=jnp.float32
+        ).astype(jnp.bfloat16)
+
+
+def down_part(me, units, w_down, head_count):
+    tokens, total_units = units.shape
+    cols = w_down.shape[1] // head_count
+    vmem = pl.BlockSpec(memory_space=pltpu.VMEM)
+    return pl.pallas_call(
+        functools.partial(down_kernel, head_count),
+        out_shape=jax.ShapeDtypeStruct((tokens, head_count // 2 * cols), jnp.bfloat16),
+        in_specs=[
+            pl.BlockSpec(memory_space=pltpu.SMEM),
+            vmem,
+            pl.BlockSpec(memory_space=pl.ANY),
+        ],
+        out_specs=vmem,
+        scratch_shapes=[
+            pltpu.VMEM((head_count // 2, total_units, cols), jnp.bfloat16),
+            pltpu.SemaphoreType.DMA((head_count // 2,)),
+        ],
+        compiler_params=pltpu.CompilerParams(vmem_limit_bytes=16 * 2**20),
+        cost_estimate=pl.CostEstimate(
+            flops=2 * tokens * total_units * head_count // 2 * cols,
+            bytes_accessed=2 * total_units * head_count // 2 * cols,
+            transcendentals=0,
+        ),
+        name="down",
+    )(me, units, w_down)
+
+
 def swap(value, axis, size, mask):
     return lax.ppermute(value, axis, [(i, i ^ mask) for i in range(size)])
 
@@ -208,12 +382,10 @@
     req_size = lax.axis_size("req")
     head_size = lax.axis_size("head")
     me = lax.axis_index("head")
+    me_ref = me[None].astype(jnp.int32)
     rows, cols = hidden.shape
     experts_local, units_local, width = w_down.shape
     even = range(0, head_size, 2)
-
-    def block(array, j):
-        return lax.dynamic_index_in_dim(array, me ^ j, array.ndim - 2, False)
 
     pieces = [hidden] + [swap(hidden, "head", head_size, j) for j in range(1, head_size)]
     half_dim = k_cache.shape[3] // 2
@@ -222,7 +394,7 @@
     cosine, sine = jnp.cos(angles), jnp.sin(angles)
     keep, send = attention(
         pieces,
-        me[None].astype(jnp.int32),
+        me_ref,
         lengths,
         jnp.concatenate([cosine, cosine], axis=1),
         jnp.concatenate([-sine, sine], axis=1),
@@ -246,52 +418,20 @@
     every = jnp.arange(head_size * experts_local, dtype=jnp.int32)
     matches = (expert_ids[:, :, None] == every[None, None, :]).astype(jnp.float32)
     shares = jnp.sum(route_weights[:, :, None] * matches, axis=1).astype(jnp.bfloat16)
+    shares = jnp.pad(shares, ((0, 0), (0, -shares.shape[1] % LANES)))
     payload = jnp.concatenate([resid.astype(jnp.bfloat16), shares], axis=1)
 
     steps = range(2, req_size, 2)
     line = jnp.concatenate([payload] + [swap(payload, "req", req_size, k) for k in steps])
     mine = jnp.concatenate([line, swap(line, "req", req_size, 1)])
-    states = mine[:, : resid.shape[1]]
-    share = mine[:, resid.shape[1] :]
-    other_states = swap(states, "head", head_size, 1)
-
-    tokens = states.shape[0]
-    square = jnp.sum(states.astype(jnp.float32) ** 2, axis=1) + jnp.sum(
-        other_states.astype(jnp.float32) ** 2, axis=1
-    )
-    scale = lax.rsqrt(square / width + norm_eps)
-    both = jnp.stack(
-        [
-            states.reshape(tokens, head_size // 2, cols),
-            other_states.reshape(tokens, head_size // 2, cols),
-        ],
-        axis=2,
-    ).reshape(tokens, head_size, cols)
-    ordered = jnp.concatenate([block(both, b) for b in range(head_size)], axis=1)
-    w_flat = w_in.transpose(1, 0, 2)
-    gate_up = jnp.einsum("td,edn->etn", ordered, w_flat, preferred_element_type=jnp.float32)
-    gate_up = gate_up * scale[None, :, None]
-    gate_up = gate_up.reshape(experts_local, tokens, units_local // UNIT_BLOCK, 2, UNIT_BLOCK)
-    local = lax.dynamic_slice_in_dim(share, me * experts_local, experts_local, 1)
-    units = local.T.astype(jnp.float32)[:, :, None, None] * (
-        jax.nn.silu(gate_up[:, :, :, 0]) * gate_up[:, :, :, 1]
-    )
-    units = units.astype(jnp.bfloat16).reshape(experts_local, tokens, units_local)
-    w_blocks = w_down.reshape(experts_local, units_local, head_size, cols)
-
-    def down(blocks):
-        return jnp.concatenate(
-            [
-                jnp.einsum(
-                    "etu,eun->tn", units, block(w_blocks, j), preferred_element_type=jnp.float32
-                ).astype(jnp.bfloat16)
-                for j in blocks
-            ],
-            axis=1,
-        )
-
-    sent = swap(down([j + 1 for j in even]), "head", head_size, 1)
-    summed = down(even).astype(jnp.float32) + sent.astype(jnp.float32)
+    other_states = swap(mine[:, : resid.shape[1]], "head", head_size, 1)
+    weights = [by_expert(j, me_ref, w_in, head_size) for j in range(head_size)]
+    w_down_flat = w_down.reshape(experts_local * units_local, width)
+    units, send = experts_part(me_ref, mine, other_states, weights, w_down_flat)
+    sent = swap(send, "head", head_size, 1)
+    tokens = mine.shape[0]
+    summed = down_part(me_ref, units, w_down_flat, head_size)
+    summed = summed.astype(jnp.float32) + sent.astype(jnp.float32)
     summed = summed.astype(jnp.bfloat16).reshape(2, tokens // 2, head_size // 2, cols)
     total = summed[0, :, 0].astype(jnp.float32)
     for j in even:

time: 134 us -> 94 us (0.70)
  local copies, waits for them, and re-layouts: 52.9 us -> 15.6 us
  matrix products: 21.4 us -> 0 us
  Pallas kernels: 14.4 us -> 32.7 us
  other arithmetic: 5.92 us -> 2.19 us
  starting transfers between devices: 16.5 us -> 19.4 us
  waiting for transfers between devices: 21.9 us -> 24.1 us
    dynamic_slice x1 -> x0, local copies, waits for them, and re-layouts: 27.2 us -> none  [block(): return lax.dynamic_index_in_dim(array, me ^ j, array.ndim - 2, False)]
    dot_general x5 -> x0, matrix products: 21.4 us -> none  [the longest x1 18.4 us: per_device(): jnp.einsum('td,edn->etn', ordered, w_flat, preferred_element_type=jnp.flo...]
    pallas_call x0 -> x6, Pallas kernels: none -> 18.7 us  [the longest x1 11.3 us: experts_part(): pl.pallas_call(functools.partial(experts_kernel, head_count), out_shape=(...]
    reshape x1 -> x0, local copies, waits for them, and re-layouts: 14.5 us -> none  [per_device(): w_blocks = w_down.reshape(experts_local, units_local, head_size, cols)]
    unnamed x25 -> x23, local copies, waits for them, and re-layouts: 8.76 us -> 14.3 us
    convert_element_type x2 -> x0, other arithmetic: 3.21 us -> none  [the longest x1 3.12 us: per_device(): units.astype(jnp.bfloat16).reshape(experts_local, tokens, units_local)]
    ppermute x14, starting transfers between devices: 13 us -> 15.9 us  [swap(): return lax.ppermute(value, axis, [(i, i ^ mask) for i in range(size)])]
    ppermute x14, waiting for transfers between devices: 15.8 us -> 18.4 us  [swap(): return lax.ppermute(value, axis, [(i, i ^ mask) for i in range(size)])]
  transfers between devices with their start and end apart: 17 -> 17, of which waited for: 10 -> 11; matrix products, arithmetic and copies ran while one was open for 35% -> 3% of each run, Pallas kernels for 0% -> 8%
where the time goes in v3:
time: 94 us; the launch traced here: 94.3 us
  Pallas kernels  32.7 us (35%)
  waiting for transfers between devices  24.1 us (26%)
  starting transfers between devices  19.4 us (21%)
  local copies, waits for them, and re-layouts  15.6 us (17%)
  other arithmetic  2.19 us (2%)
    ppermute x14, waiting for transfers between devices, swap(): return lax.ppermute(value, axis, [(i, i ^ mask) for i in range(size)])  18.4 us
    ppermute x14, starting transfers between devices, swap(): return lax.ppermute(value, axis, [(i, i ^ mask) for i in range(size)])  15.9 us
    unnamed x23, local copies, waits for them, and re-layouts  14.3 us
    pallas_call x1, Pallas kernels, attention(): pl.pallas_call(functools.partial(attention_kernel, head_count), out_shape...  14 us
    pallas_call x1, Pallas kernels, experts_part(): pl.pallas_call(functools.partial(experts_kernel, head_count), out_shape=(...  11.3 us
    ppermute x3, waiting for transfers between devices, per_device(): got = lax.ppermute(summed[k, :, j // 2], ('req', 'head'), pairs)  5.66 us
    pallas_call x4, Pallas kernels, by_expert(): pl.pallas_call(functools.partial(relayout_kernel, j), out_shape=pltpu.VME...  5.21 us
    ppermute x3, starting transfers between devices, per_device(): got = lax.ppermute(summed[k, :, j // 2], ('req', 'head'), pairs)  3.55 us
  transfers between devices with their start and end apart: 17, of which 11 were waited for; matrix products, arithmetic and copies ran while one was open for 3% of the time, Pallas kernels for 8%

profile of v3, /device:TPU:0, one launch (start us, length us, event | category | flops | bytes accessed | tf_op | source)
XLA Modules:
  0.0 94.3 jit_solution(4897831461915980730)
XLA Ops:
  0.0 0.5 collective-permute-start.1
  0.5 2.5 %collective-permute-start = (bf16[32,512]{1,0:T(8,128)(2,1)}, bf16[32,512]{1,0:T(8,128)(2,1)S(1)}, u32[]{:S(2)}, u32[]{:S(2)}) collective-permute-start(bf16[32,512]{1,0:T(8,128)(2,1)} %refs_0_.1), channel_id=1, source_target_pairs={{0,2},{1,3},{2,0},{3,1},{4,6},{5,7},{6,4},{7,5},{8,10},{9,11},{10,... | collective-permute-start | bytes 98312 | tf_op jit(solution)/shard_map/ppermute | solution.py:376
  3.0 0.1 collective-permute-start.2
  3.1 0.7 convert_element_type.82
  3.8 0.1 fusion.4
  3.9 0.1 pad_maximum_fusion.2
  4.0 0.8 copy.19
  4.8 0.8 copy.20
  5.5 0.0 collective-permute-done.1.refs_1_
  5.5 0.0 collective-permute-done.refs_2_
  5.6 1.0 %collective-permute-done.2.refs_3_ = bf16[32,512]{1,0:T(8,128)(2,1)S(1)} collective-permute-done((bf16[32,512]{1,0:T(8,128)(2,1)}, bf16[32,512]{1,0:T(8,128)(2,1)S(1)}, u32[]{:S(2)}, u32[]{:S(2)}) %collective-permute-start.2) | collective-permute-done | bytes 32800 | tf_op jit(solution)/shard_map/ppermute | solution.py:376
  6.5 2.8 %copy-done.1 = bf16[3,2048,512]{2,1,0:T(8,128)(2,1)S(1)} copy-done((bf16[3,2048,512]{2,1,0:T(8,128)(2,1)S(1)}, bf16[3,2048,512]{2,1,0:T(8,128)(2,1)}, u32[]{:S(2)}) %copy-start.1) | copy-done | bytes 6291480
  9.3 1.6 %copy-done.2 = bf16[512,2048]{1,0:T(8,128)(2,1)S(1)} copy-done((bf16[512,2048]{1,0:T(8,128)(2,1)S(1)}, bf16[512,2048]{1,0:T(8,128)(2,1)}, u32[]{:S(2)}) %copy-start.2) | copy-done | bytes 2097176
  10.9 0.8 copy-done.3
  11.7 0.7 copy-done.4
  12.3 14.0 %attention.1 = (bf16[32,1024]{1,0:T(8,128)(2,1)S(1)}, bf16[32,1024]{1,0:T(8,128)(2,1)S(1)}) custom-call(s32[32]{0:T(128)S(1)} %copy-done.4, s32[1]{0:T(128)} %bitcast.me_ref, f32[32,128]{1,0:T(8,128)S(1)} %get-tuple-element.29.cos_ref, f32[32,128]{1,0:T(8,128)S(1)} %get-tuple-element.30.sin_ref, bf16[32,512]{1,0:T(8,128)(2,1)S(1)} %copy-done.3, ...), custom_call_target="tpu_custom_call" | custom-call | flops 268435456 | bytes 20971520 | tf_op jit(solution)/shard_map/attention/pallas_call | solution.py:170
  26.3 0.3 collective-permute-start.3
  26.6 0.2 select_reduce_fusion
  26.8 0.9 collective-permute-done.3
  27.6 0.9 collective-permute-start.4
  28.6 3.4 %collective-permute-done.4 = bf16[32,1024]{1,0:T(8,128)(2,1)S(1)} collective-permute-done((bf16[32,1024]{1,0:T(8,128)(2,1)S(1)}, bf16[32,1024]{1,0:T(8,128)(2,1)S(1)}, u32[]{:S(2)}, u32[]{:S(2)}) %collective-permute-start.4) | collective-permute-done | bytes 65568 | tf_op jit(solution)/shard_map/ppermute | solution.py:376
  32.0 0.1 fusion.8
  32.1 0.2 maximum_convert_fusion
  32.4 0.3 collective-permute-start.6
  32.7 1.1 %collective-permute-start.5 = (bf16[32,1152]{1,0:T(8,128)(2,1)S(1)}, bf16[32,1152]{1,0:T(8,128)(2,1)S(1)}, u32[]{:S(2)}, u32[]{:S(2)}) collective-permute-start(bf16[32,1152]{1,0:T(8,128)(2,1)S(1)} %get-tuple-element.22), channel_id=1, source_target_pairs={{0,8},{4,12},{8,0},{12,4},{16,24},{20,28},{24,16},{28,20},{1,9},{5... | collective-permute-start | bytes 221192 | tf_op jit(solution)/shard_map/ppermute | solution.py:376
  33.8 3.0 %collective-permute-start.7 = (bf16[32,1152]{1,0:T(8,128)(2,1)S(1)}, bf16[32,1152]{1,0:T(8,128)(2,1)S(1)}, u32[]{:S(2)}, u32[]{:S(2)}) collective-permute-start(bf16[32,1152]{1,0:T(8,128)(2,1)S(1)} %get-tuple-element.22), channel_id=1, source_target_pairs={{0,24},{4,28},{8,16},{12,20},{16,8},{20,12},{24,0},{28,4},{1,25},{... | collective-permute-start | bytes 221192 | tf_op jit(solution)/shard_map/ppermute | solution.py:376
  36.8 3.7 %collective-permute-done.6 = bf16[32,1152]{1,0:T(8,128)(2,1)S(1)} collective-permute-done((bf16[32,1152]{1,0:T(8,128)(2,1)S(1)}, bf16[32,1152]{1,0:T(8,128)(2,1)S(1)}, u32[]{:S(2)}, u32[]{:S(2)}) %collective-permute-start.6) | collective-permute-done | bytes 73760 | tf_op jit(solution)/shard_map/ppermute | solution.py:376
  40.5 0.0 collective-permute-done.5
  40.5 0.0 collective-permute-done.7
  40.6 2.9 %collective-permute-start.8 = (bf16[128,1152]{1,0:T(8,128)(2,1)S(1)}, bf16[128,1152]{1,0:T(8,128)(2,1)S(1)}, u32[]{:S(2)}, u32[]{:S(2)}) collective-permute-start(bf16[128,1152]{1,0:T(8,128)(2,1)S(1)} %pad_maximum_fusion), channel_id=1, source_target_pairs={{0,4},{4,0},{8,12},{12,8},{16,20},{20,16},{24,28},{28,24},{1,5},{5... | collective-permute-start | bytes 884744 | tf_op jit(solution)/shard_map/ppermute | solution.py:376
  43.6 5.2 %collective-permute-done.8 = bf16[128,1152]{1,0:T(8,128)(2,1)S(1)} collective-permute-done((bf16[128,1152]{1,0:T(8,128)(2,1)S(1)}, bf16[128,1152]{1,0:T(8,128)(2,1)S(1)}, u32[]{:S(2)}, u32[]{:S(2)}) %collective-permute-start.8) | collective-permute-done | bytes 294944 | tf_op jit(solution)/shard_map/ppermute | solution.py:376
  48.8 0.1 slice.54
  48.9 0.1 collective-permute-start.9
  49.0 0.0 copy-start
  49.0 5.8 %copy-done = bf16[2048,16,256]{2,1,0:T(8,128)(2,1)S(1)} copy-done((bf16[2048,16,256]{2,1,0:T(8,128)(2,1)S(1)}, bf16[2048,16,256]{2,1,0:T(8,128)(2,1)}, u32[]{:S(2)}) %copy-start) | copy-done | bytes 16777240
  54.7 1.3 %by_expert_1.1.refs_1_ = bf16[16,512,256]{2,1,0:T(8,128)(2,1)S(1)} custom-call(s32[1]{0:T(128)} %bitcast.me_ref, bf16[2048,16,256]{2,1,0:T(8,128)(2,1)S(1)} %copy-done), custom_call_target="tpu_custom_call" | custom-call | bytes 8388608 | tf_op jit(solution)/shard_map/by_expert_1/pallas_call | solution.py:230
  56.0 1.3 %by_expert_0.1.refs_0_ = bf16[16,512,256]{2,1,0:T(8,128)(2,1)S(1)} custom-call(s32[1]{0:T(128)} %bitcast.me_ref, bf16[2048,16,256]{2,1,0:T(8,128)(2,1)S(1)} %copy-done), custom_call_target="tpu_custom_call" | custom-call | bytes 8388608 | tf_op jit(solution)/shard_map/by_expert_0/pallas_call | solution.py:230
  57.3 0.0 slice-start
  57.4 1.3 %by_expert_3.1.refs_3_ = bf16[16,512,256]{2,1,0:T(8,128)(2,1)S(1)} custom-call(s32[1]{0:T(128)} %bitcast.me_ref, bf16[2048,16,256]{2,1,0:T(8,128)(2,1)S(1)} %copy-done), custom_call_target="tpu_custom_call" | custom-call | bytes 8388608 | tf_op jit(solution)/shard_map/by_expert_3/pallas_call | solution.py:230
  58.7 0.0 slice-start.1
  58.7 1.3 %by_expert_2.1.refs_2_ = bf16[16,512,256]{2,1,0:T(8,128)(2,1)S(1)} custom-call(s32[1]{0:T(128)} %bitcast.me_ref, bf16[2048,16,256]{2,1,0:T(8,128)(2,1)S(1)} %copy-done), custom_call_target="tpu_custom_call" | custom-call | bytes 8388608 | tf_op jit(solution)/shard_map/by_expert_2/pallas_call | solution.py:230
  60.0 0.0 collective-permute-done.9.other_ref
  60.0 1.1 %slice-done.1 = s8[4194304]{0:T(1024)(128)(4,1)S(1)} async-done(((s8[8388608]{0:T(1024)(128)(4,1)}), s8[4194304]{0:T(1024)(128)(4,1)S(1)}, s32[]{:S(2)}) %slice-start.1) | async-done | bytes 4194328
  61.1 11.3 %experts.1 = (bf16[256,2048]{1,0:T(8,128)(2,1)S(1)}, bf16[256,1024]{1,0:T(8,128)(2,1)S(1)}) custom-call(s32[1]{0:T(128)} %bitcast.me_ref, bf16[256,1152]{1,0:T(8,128)(2,1)S(1)} %constant_dynamic-update-slice_fusion.mine_ref, bf16[256,1024]{1,0:T(8,128)(2,1)S(1)} %collective-permute-done.9.other_ref, bf16[16,512,256]{2,1,0:T(8,128)(2,1)S(1)} %by_expert_0.1.refs_0_, ...), custom_call_target="tpu_custom_call" | custom-call | flops 4294967296 | bytes 16777216 | tf_op jit(solution)/shard_map/experts/pallas_call | solution.py:310
  72.4 0.5 collective-permute-start.10
  72.9 2.2 %down.1 = bf16[256,1024]{1,0:T(8,128)(2,1)S(1)} custom-call(s32[1]{0:T(128)} %bitcast.me_ref, bf16[256,2048]{1,0:T(8,128)(2,1)S(1)} %get-tuple-element.11.units_ref, bf16[2048,2048]{1,0:T(8,128)(2,1)S(1)} %bitcast.28), custom_call_target="tpu_custom_call" | custom-call | flops 1073741824 | bytes 4194304 | tf_op jit(solution)/shard_map/down/pallas_call | solution.py:352
  75.2 0.0 collective-permute-done.10
  75.2 0.2 add_convert_fusion
  75.4 0.4 reshape.47
  75.8 0.7 fusion.6
  76.6 2.1 %collective-permute-start.13 = (bf16[128,512]{1,0:T(8,128)(2,1)S(1)}, bf16[128,512]{1,0:T(8,128)(2,1)S(1)}, u32[]{:S(2)}, u32[]{:S(2)}) collective-permute-start(bf16[128,512]{1,0:T(8,128)(2,1)S(1)} %bitcast.38), channel_id=1, source_target_pairs={{0,6},{1,7},{2,4},{3,5},{4,2},{5,3},{6,0},{7,1},{8,14},{9,15},{10,... | collective-permute-start | bytes 393224 | tf_op jit(solution)/shard_map/ppermute | solution.py:445
  78.7 0.2 collective-permute-start.11
  78.9 1.2 %collective-permute-start.12 = (bf16[128,512]{1,0:T(8,128)(2,1)S(1)}, bf16[128,512]{1,0:T(8,128)(2,1)S(1)}, u32[]{:S(2)}, u32[]{:S(2)}) collective-permute-start(bf16[128,512]{1,0:T(8,128)(2,1)S(1)} %bitcast.36), channel_id=1, source_target_pairs={{0,2},{1,3},{2,0},{3,1},{4,6},{5,7},{6,4},{7,5},{8,10},{9,11},{10,... | collective-permute-start | bytes 393224 | tf_op jit(solution)/shard_map/ppermute | solution.py:445
  80.1 3.8 %collective-permute-done.13 = bf16[128,512]{1,0:T(8,128)(2,1)S(1)} collective-permute-done((bf16[128,512]{1,0:T(8,128)(2,1)S(1)}, bf16[128,512]{1,0:T(8,128)(2,1)S(1)}, u32[]{:S(2)}, u32[]{:S(2)}) %collective-permute-start.13) | collective-permute-done | bytes 131104 | tf_op jit(solution)/shard_map/ppermute | solution.py:445
  83.9 1.2 %collective-permute-done.11 = bf16[128,512]{1,0:T(8,128)(2,1)S(1)} collective-permute-done((bf16[128,512]{1,0:T(8,128)(2,1)S(1)}, bf16[128,512]{1,0:T(8,128)(2,1)S(1)}, u32[]{:S(2)}, u32[]{:S(2)}) %collective-permute-start.11) | collective-permute-done | bytes 131104 | tf_op jit(solution)/shard_map/ppermute | solution.py:445
  85.1 0.7 collective-permute-done.12
  85.8 0.1 fusion.2
  85.9 1.4 %collective-permute-start.14 = (bf16[32,512]{1,0:T(8,128)(2,1)S(1)}, bf16[32,512]{1,0:T(8,128)(2,1)S(1)}, u32[]{:S(2)}, u32[]{:S(2)}) collective-permute-start(bf16[32,512]{1,0:T(8,128)(2,1)S(1)} %get-tuple-element.19), channel_id=1, source_target_pairs={{0,8},{4,12},{8,0},{12,4},{16,24},{20,28},{24,16},{28,20},{1,9},{5... | collective-permute-start | bytes 98312 | tf_op jit(solution)/shard_map/ppermute | solution.py:376
  87.3 1.6 %collective-permute-start.16 = (bf16[32,512]{1,0:T(8,128)(2,1)S(1)}, bf16[32,512]{1,0:T(8,128)(2,1)S(1)}, u32[]{:S(2)}, u32[]{:S(2)}) collective-permute-start(bf16[32,512]{1,0:T(8,128)(2,1)S(1)} %get-tuple-element.20), channel_id=1, source_target_pairs={{0,24},{4,28},{8,16},{12,20},{16,8},{20,12},{24,0},{28,4},{1,25},{... | collective-permute-start | bytes 98312 | tf_op jit(solution)/shard_map/ppermute | solution.py:376
  88.9 0.6 collective-permute-start.15
  89.4 0.4 collective-permute-done.14
  89.9 3.1 %collective-permute-done.16 = bf16[32,512]{1,0:T(8,128)(2,1)S(1)} collective-permute-done((bf16[32,512]{1,0:T(8,128)(2,1)S(1)}, bf16[32,512]{1,0:T(8,128)(2,1)S(1)}, u32[]{:S(2)}, u32[]{:S(2)}) %collective-permute-start.16) | collective-permute-done | bytes 32800 | tf_op jit(solution)/shard_map/ppermute | solution.py:376
  93.0 0.7 collective-permute-done.15
  93.7 0.6 fusion.3
  (24 shorter events, 0.3 us)
Async XLA Ops:
  0.0 5.5 %collective-permute-start.1 = (bf16[32,512]{1,0:T(8,128)(2,1)}, bf16[32,512]{1,0:T(8,128)(2,1)S(1)}, u32[]{:S(2)}, u32[]{:S(2)}) collective-permute-start(bf16[32,512]{1,0:T(8,128)(2,1)} %refs_0_.1), channel_id=1, source_target_pairs={{0,1},{1,0},{2,3},{3,2},{4,5},{5,4},{6,7},{7,6},{8,9},{9,8},{10,11... | collective-permute-start | bytes 98312 | tf_op jit(solution)/shard_map/ppermute | solution.py:376
  0.5 5.1 %collective-permute-start = (bf16[32,512]{1,0:T(8,128)(2,1)}, bf16[32,512]{1,0:T(8,128)(2,1)S(1)}, u32[]{:S(2)}, u32[]{:S(2)}) collective-permute-start(bf16[32,512]{1,0:T(8,128)(2,1)} %refs_0_.1), channel_id=1, source_target_pairs={{0,2},{1,3},{2,0},{3,1},{4,6},{5,7},{6,4},{7,5},{8,10},{9,11},{10,... | collective-permute-start | bytes 98312 | tf_op jit(solution)/shard_map/ppermute | solution.py:376
  3.0 3.6 %collective-permute-start.2 = (bf16[32,512]{1,0:T(8,128)(2,1)}, bf16[32,512]{1,0:T(8,128)(2,1)S(1)}, u32[]{:S(2)}, u32[]{:S(2)}) collective-permute-start(bf16[32,512]{1,0:T(8,128)(2,1)} %refs_0_.1), channel_id=1, source_target_pairs={{0,3},{1,2},{2,1},{3,0},{4,7},{5,6},{6,5},{7,4},{8,11},{9,10},{10,... | collective-permute-start | bytes 98312 | tf_op jit(solution)/shard_map/ppermute | solution.py:376
  6.5 2.8 %copy-start.1 = (bf16[3,2048,512]{2,1,0:T(8,128)(2,1)S(1)}, bf16[3,2048,512]{2,1,0:T(8,128)(2,1)}, u32[]{:S(2)}) copy-start(bf16[3,2048,512]{2,1,0:T(8,128)(2,1)} %refs_4_.1) | copy-start | bytes 18874372
  9.3 1.6 %copy-start.2 = (bf16[512,2048]{1,0:T(8,128)(2,1)S(1)}, bf16[512,2048]{1,0:T(8,128)(2,1)}, u32[]{:S(2)}) copy-start(bf16[512,2048]{1,0:T(8,128)(2,1)} %refs_5_.1) | copy-start | bytes 6291460
  10.9 0.8 copy-start.3
  11.7 0.7 copy-start.4
  26.3 1.3 %collective-permute-start.3 = (bf16[32,1024]{1,0:T(8,128)(2,1)S(1)}, bf16[32,1024]{1,0:T(8,128)(2,1)S(1)}, u32[]{:S(2)}, u32[]{:S(2)}) collective-permute-start(bf16[32,1024]{1,0:T(8,128)(2,1)S(1)} %get-tuple-element.10), channel_id=1, source_target_pairs={{0,1},{1,0},{2,3},{3,2},{4,5},{5,4},{6,7},{7,6},{8,9},{9,8},{10,11... | collective-permute-start | bytes 196616 | tf_op jit(solution)/shard_map/ppermute | solution.py:376
  27.6 4.3 %collective-permute-start.4 = (bf16[32,1024]{1,0:T(8,128)(2,1)S(1)}, bf16[32,1024]{1,0:T(8,128)(2,1)S(1)}, u32[]{:S(2)}, u32[]{:S(2)}) collective-permute-start(bf16[32,1024]{1,0:T(8,128)(2,1)S(1)} %add_convert_fusion.1), channel_id=1, source_target_pairs={{0,2},{1,3},{2,0},{3,1},{4,6},{5,7},{6,4},{7,5},{8,10},{9,11},{10,... | collective-permute-start | bytes 196616 | tf_op jit(solution)/shard_map/ppermute | solution.py:376
  32.4 8.2 %collective-permute-start.6 = (bf16[32,1152]{1,0:T(8,128)(2,1)S(1)}, bf16[32,1152]{1,0:T(8,128)(2,1)S(1)}, u32[]{:S(2)}, u32[]{:S(2)}) collective-permute-start(bf16[32,1152]{1,0:T(8,128)(2,1)S(1)} %get-tuple-element.22), channel_id=1, source_target_pairs={{0,16},{4,20},{8,24},{12,28},{16,0},{20,4},{24,8},{28,12},{1,17},{... | collective-permute-start | bytes 221192 | tf_op jit(solution)/shard_map/ppermute | solution.py:376
  32.7 7.8 %collective-permute-start.5 = (bf16[32,1152]{1,0:T(8,128)(2,1)S(1)}, bf16[32,1152]{1,0:T(8,128)(2,1)S(1)}, u32[]{:S(2)}, u32[]{:S(2)}) collective-permute-start(bf16[32,1152]{1,0:T(8,128)(2,1)S(1)} %get-tuple-element.22), channel_id=1, source_target_pairs={{0,8},{4,12},{8,0},{12,4},{16,24},{20,28},{24,16},{28,20},{1,9},{5... | collective-permute-start | bytes 221192 | tf_op jit(solution)/shard_map/ppermute | solution.py:376
  33.8 6.7 %collective-permute-start.7 = (bf16[32,1152]{1,0:T(8,128)(2,1)S(1)}, bf16[32,1152]{1,0:T(8,128)(2,1)S(1)}, u32[]{:S(2)}, u32[]{:S(2)}) collective-permute-start(bf16[32,1152]{1,0:T(8,128)(2,1)S(1)} %get-tuple-element.22), channel_id=1, source_target_pairs={{0,24},{4,28},{8,16},{12,20},{16,8},{20,12},{24,0},{28,4},{1,25},{... | collective-permute-start | bytes 221192 | tf_op jit(solution)/shard_map/ppermute | solution.py:376
  40.6 8.2 %collective-permute-start.8 = (bf16[128,1152]{1,0:T(8,128)(2,1)S(1)}, bf16[128,1152]{1,0:T(8,128)(2,1)S(1)}, u32[]{:S(2)}, u32[]{:S(2)}) collective-permute-start(bf16[128,1152]{1,0:T(8,128)(2,1)S(1)} %pad_maximum_fusion), channel_id=1, source_target_pairs={{0,4},{4,0},{8,12},{12,8},{16,20},{20,16},{24,28},{28,24},{1,5},{5... | collective-permute-start | bytes 884744 | tf_op jit(solution)/shard_map/ppermute | solution.py:376
  48.9 11.1 %collective-permute-start.9 = (bf16[256,1024]{1,0:T(8,128)(2,1)S(1)}, bf16[256,1024]{1,0:T(8,128)(2,1)S(1)}, u32[]{:S(2)}, u32[]{:S(2)}) collective-permute-start(bf16[256,1024]{1,0:T(8,128)(2,1)S(1)} %slice.54), channel_id=1, source_target_pairs={{0,1},{1,0},{2,3},{3,2},{4,5},{5,4},{6,7},{7,6},{8,9},{9,8},{10,11... | collective-permute-start | bytes 1572872 | tf_op jit(solution)/shard_map/ppermute | solution.py:376
  49.0 5.8 %copy-start = (bf16[2048,16,256]{2,1,0:T(8,128)(2,1)S(1)}, bf16[2048,16,256]{2,1,0:T(8,128)(2,1)}, u32[]{:S(2)}) copy-start(bf16[2048,16,256]{2,1,0:T(8,128)(2,1)} %w_ref.7) | copy-start | bytes 50331652
  57.3 2.7 %slice-start = ((s8[8388608]{0:T(1024)(128)(4,1)}), s8[4194304]{0:T(1024)(128)(4,1)S(1)}, s32[]{:S(2)}) async-start(s8[8388608]{0:T(1024)(128)(4,1)} %bitcast.25), calls=%async_computation | async-start | bytes 8388608
  58.7 2.4 %slice-start.1 = ((s8[8388608]{0:T(1024)(128)(4,1)}), s8[4194304]{0:T(1024)(128)(4,1)S(1)}, s32[]{:S(2)}) async-start(s8[8388608]{0:T(1024)(128)(4,1)} %bitcast.25), calls=%async_computation.1 | async-start | bytes 8388608
  72.4 2.8 %collective-permute-start.10 = (bf16[256,1024]{1,0:T(8,128)(2,1)S(1)}, bf16[256,1024]{1,0:T(8,128)(2,1)S(1)}, u32[]{:S(2)}, u32[]{:S(2)}) collective-permute-start(bf16[256,1024]{1,0:T(8,128)(2,1)S(1)} %get-tuple-element.12), channel_id=1, source_target_pairs={{0,1},{1,0},{2,3},{3,2},{4,5},{5,4},{6,7},{7,6},{8,9},{9,8},{10,11... | collective-permute-start | bytes 1572872 | tf_op jit(solution)/shard_map/ppermute | solution.py:376
  76.6 7.3 %collective-permute-start.13 = (bf16[128,512]{1,0:T(8,128)(2,1)S(1)}, bf16[128,512]{1,0:T(8,128)(2,1)S(1)}, u32[]{:S(2)}, u32[]{:S(2)}) collective-permute-start(bf16[128,512]{1,0:T(8,128)(2,1)S(1)} %bitcast.38), channel_id=1, source_target_pairs={{0,6},{1,7},{2,4},{3,5},{4,2},{5,3},{6,0},{7,1},{8,14},{9,15},{10,... | collective-permute-start | bytes 393224 | tf_op jit(solution)/shard_map/ppermute | solution.py:445
  78.7 6.5 %collective-permute-start.11 = (bf16[128,512]{1,0:T(8,128)(2,1)S(1)}, bf16[128,512]{1,0:T(8,128)(2,1)S(1)}, u32[]{:S(2)}, u32[]{:S(2)}) collective-permute-start(bf16[128,512]{1,0:T(8,128)(2,1)S(1)} %bitcast.37), channel_id=1, source_target_pairs={{0,4},{1,5},{2,6},{3,7},{4,0},{5,1},{6,2},{7,3},{8,12},{9,13},{10,... | collective-permute-start | bytes 393224 | tf_op jit(solution)/shard_map/ppermute | solution.py:445
  78.9 6.9 %collective-permute-start.12 = (bf16[128,512]{1,0:T(8,128)(2,1)S(1)}, bf16[128,512]{1,0:T(8,128)(2,1)S(1)}, u32[]{:S(2)}, u32[]{:S(2)}) collective-permute-start(bf16[128,512]{1,0:T(8,128)(2,1)S(1)} %bitcast.36), channel_id=1, source_target_pairs={{0,2},{1,3},{2,0},{3,1},{4,6},{5,7},{6,4},{7,5},{8,10},{9,11},{10,... | collective-permute-start | bytes 393224 | tf_op jit(solution)/shard_map/ppermute | solution.py:445
  85.9 4.0 %collective-permute-start.14 = (bf16[32,512]{1,0:T(8,128)(2,1)S(1)}, bf16[32,512]{1,0:T(8,128)(2,1)S(1)}, u32[]{:S(2)}, u32[]{:S(2)}) collective-permute-start(bf16[32,512]{1,0:T(8,128)(2,1)S(1)} %get-tuple-element.19), channel_id=1, source_target_pairs={{0,8},{4,12},{8,0},{12,4},{16,24},{20,28},{24,16},{28,20},{1,9},{5... | collective-permute-start | bytes 98312 | tf_op jit(solution)/shard_map/ppermute | solution.py:376
  87.3 5.7 %collective-permute-start.16 = (bf16[32,512]{1,0:T(8,128)(2,1)S(1)}, bf16[32,512]{1,0:T(8,128)(2,1)S(1)}, u32[]{:S(2)}, u32[]{:S(2)}) collective-permute-start(bf16[32,512]{1,0:T(8,128)(2,1)S(1)} %get-tuple-element.20), channel_id=1, source_target_pairs={{0,24},{4,28},{8,16},{12,20},{16,8},{20,12},{24,0},{28,4},{1,25},{... | collective-permute-start | bytes 98312 | tf_op jit(solution)/shard_map/ppermute | solution.py:376
  88.9 4.8 %collective-permute-start.15 = (bf16[32,512]{1,0:T(8,128)(2,1)S(1)}, bf16[32,512]{1,0:T(8,128)(2,1)S(1)}, u32[]{:S(2)}, u32[]{:S(2)}) collective-permute-start(bf16[32,512]{1,0:T(8,128)(2,1)S(1)} %get-tuple-element.21), channel_id=1, source_target_pairs={{0,16},{4,20},{8,24},{12,28},{16,0},{20,4},{24,8},{28,12},{1,17},{... | collective-permute-start | bytes 98312 | tf_op jit(solution)/shard_map/ppermute | solution.py:376

commit v4 on v3

--- a/solution.py
+++ b/solution.py
@@ -15,6 +15,19 @@
 MASKED = -1e30
 
 
+VMEM = pl.BlockSpec(memory_space=pltpu.VMEM)
+SMEM = pl.BlockSpec(memory_space=pltpu.SMEM)
+ANY = pl.BlockSpec(memory_space=pl.ANY)
+
+
+def in_hbm(array):
+    return pltpu.with_memory_space_constraint(array, pltpu.HBM)
+
+
+def in_vmem(array):
+    return pltpu.with_memory_space_constraint(array, pltpu.VMEM)
+
+
 def attention_kernel(
     head_count, lengths_ref, me_ref, cos_ref, sin_ref, *refs
 ):
@@ -22,7 +35,7 @@
     (
         w_qkv_ref, w_out_ref, k_ref, v_ref, keep_ref, send_ref,
         w_qkv_s, w_out_s, k_s, v_s, query_s, key_s, value_s, attended_s,
-        qkv_sem, out_sem, k_sem, v_sem,
+        own_s, qkv_sem, out_sem, k_sem, v_sem, own_sem,
     ) = refs[head_count:]
     rows, cols = pieces[0].shape
     heads_local = cols // LANES
@@ -47,6 +60,8 @@
             source.at[r, pl.ds(0, used)], target.at[r, pl.ds(0, used)], sem.at[r]
         )
 
+    own_copy = pltpu.make_async_copy(pieces[0], own_s, own_sem)
+    own_copy.start()
     for c in range(3):
         for j in range(head_count):
             qkv_copy(c, j).start()
@@ -61,7 +76,8 @@
     for j in range(head_count):
         out_copy(j).start()
 
-    states = [piece[...].astype(jnp.float32) for piece in pieces]
+    own_copy.wait()
+    states = [piece[...].astype(jnp.float32) for piece in (own_s, *pieces[1:])]
     square = sum(jnp.sum(state * state, axis=1, keepdims=True) for state in states)
     scale = lax.rsqrt(square / (cols * head_count) + norm_eps)
     normed = [(state * scale).astype(jnp.bfloat16) for state in states]
@@ -163,15 +179,12 @@
     rows, cols = pieces[0].shape
     cache_len, heads_local, head_dim = k_cache.shape[1:]
     flat = (rows, cache_len * heads_local, head_dim)
-    vmem = pl.BlockSpec(memory_space=pltpu.VMEM)
-    smem = pl.BlockSpec(memory_space=pltpu.SMEM)
-    anywhere = pl.BlockSpec(memory_space=pl.ANY)
     half = jax.ShapeDtypeStruct((rows, head_count // 2 * cols), jnp.bfloat16)
     return pl.pallas_call(
         functools.partial(attention_kernel, head_count),
         out_shape=(half, half),
-        in_specs=[smem, smem, vmem, vmem] + [vmem] * head_count + [anywhere] * 4,
-        out_specs=(vmem, vmem),
+        in_specs=[SMEM, SMEM, VMEM, VMEM, ANY] + [VMEM] * (head_count - 1) + [ANY] * 4,
+        out_specs=(VMEM, VMEM),
         scratch_shapes=[
             pltpu.VMEM((3, head_count, cols, cols), jnp.bfloat16),
             pltpu.VMEM((head_count, cols, cols), jnp.bfloat16),
@@ -180,10 +193,12 @@
         ]
         + [pltpu.VMEM((rows, SUBLANES, LANES), jnp.float32)] * 4
         + [
+            pltpu.VMEM((rows, cols), jnp.bfloat16),
             pltpu.SemaphoreType.DMA((3, head_count)),
             pltpu.SemaphoreType.DMA((head_count,)),
             pltpu.SemaphoreType.DMA((rows,)),
             pltpu.SemaphoreType.DMA((rows,)),
+            pltpu.SemaphoreType.DMA(()),
         ],
         compiler_params=pltpu.CompilerParams(vmem_limit_bytes=44 * 2**20),
         cost_estimate=pl.CostEstimate(
@@ -192,56 +207,114 @@
             transcendentals=0,
         ),
         name="attention",
-    )(lengths, me, cosine, sine, *pieces, w_qkv, w_out, k_cache.reshape(flat), v_cache.reshape(flat))
+    )(in_hbm(lengths), me, cosine, sine, in_hbm(pieces[0]), *pieces[1:], in_hbm(w_qkv), in_hbm(w_out), in_hbm(k_cache.reshape(flat)), in_hbm(v_cache.reshape(flat)))
 
 
 RELAYOUT_ROWS = 128
 RELAYOUT_STEP = 16
 
-
-def relayout_kernel(j, me_ref, w_ref, out_ref, in_s, in_sem):
-    experts, cols, _ = out_ref.shape
-    base = (me_ref[0] ^ j) * cols
-    step = min(RELAYOUT_ROWS, cols)
-    copies = [
-        pltpu.make_async_copy(
-            w_ref.at[pl.ds(pl.multiple_of(base + i * step, step), step)], in_s.at[i], in_sem.at[i]
-        )
-        for i in range(cols // step)
-    ]
+def relayout_kernel(js, me_ref, w_ref, *refs):
+    out_ref, token_ref, in_s, in_sem = refs[-4:]
+    token_ref[...] = jnp.zeros_like(token_ref)
+    experts, _, cols, _ = out_ref.shape
+    step = in_s.shape[1]
+    per_block = cols // step
+    copies = []
+    for at, j in enumerate(js):
+        base = (me_ref[0] ^ j) * cols
+        for i in range(per_block):
+            slot = at * per_block + i
+            first = pl.multiple_of(base + i * step, step)
+            copies.append(
+                pltpu.make_async_copy(
+                    w_ref.at[pl.ds(first, step)], in_s.at[slot], in_sem.at[slot]
+                )
+            )
     for copy in copies:
         copy.start()
-    for i, copy in enumerate(copies):
+    for slot, copy in enumerate(copies):
+        j, i = js[slot // per_block], slot % per_block
         copy.wait()
-
-        @pl.loop(0, step // RELAYOUT_STEP, unroll=True)
-        def _(s):
-            first = pl.multiple_of(s * RELAYOUT_STEP, RELAYOUT_STEP)
-            part = in_s[i, pl.ds(first, RELAYOUT_STEP)]
-            out_ref[:, pl.ds(pl.multiple_of(i * step + first, RELAYOUT_STEP), RELAYOUT_STEP), :] = (
-                jnp.swapaxes(part, 0, 1)
+        for s in range(step // RELAYOUT_STEP):
+            part = in_s[slot, pl.ds(s * RELAYOUT_STEP, RELAYOUT_STEP)]
+            out_ref[:, j, pl.ds(i * step + s * RELAYOUT_STEP, RELAYOUT_STEP), :] = jnp.swapaxes(
+                part, 0, 1
             )
 
 
-def by_expert(j, me, w_in, head_count):
+def by_expert(js, me, w_in, head_count, buffer, after):
     width, experts, columns = w_in.shape
     cols = width // head_count
     step = min(RELAYOUT_ROWS, cols)
+    slots = len(js) * cols // step
+    held = [] if buffer is None else [in_vmem(buffer)]
     return pl.pallas_call(
-        functools.partial(relayout_kernel, j),
-        out_shape=pltpu.VMEM((experts, cols, columns), jnp.bfloat16),
-        in_specs=[pl.BlockSpec(memory_space=pltpu.SMEM), pl.BlockSpec(memory_space=pl.ANY)],
-        out_specs=pl.BlockSpec(memory_space=pltpu.VMEM),
+        functools.partial(relayout_kernel, js),
+        out_shape=(
+            pltpu.VMEM((experts, head_count, cols, columns), jnp.bfloat16),
+            jax.ShapeDtypeStruct((SUBLANES, LANES), jnp.float32),
+        ),
+        in_specs=[SMEM, ANY] + [VMEM] * len(held) + [ANY],
+        out_specs=(VMEM, VMEM),
+        input_output_aliases={2: 0} if held else {},
         scratch_shapes=[
-            pltpu.VMEM((cols // step, step, experts, columns), jnp.bfloat16),
-            pltpu.SemaphoreType.DMA((cols // step,)),
+            pltpu.VMEM((slots, step, experts, columns), jnp.bfloat16),
+            pltpu.SemaphoreType.DMA((slots,)),
         ],
         compiler_params=pltpu.CompilerParams(vmem_limit_bytes=16 * 2**20),
         cost_estimate=pl.CostEstimate(
-            flops=0, bytes_accessed=4 * cols * experts * columns, transcendentals=0
-        ),
-        name=f"by_expert_{j}",
-    )(me, w_in)
+            flops=0, bytes_accessed=4 * len(js) * cols * experts * columns, transcendentals=0
+        ),
+        name=f"by_expert_{js[0]}",
+    )(me, in_hbm(w_in), *held, after)
+
+
+def payload_kernel(head_count, *refs):
+    blocks = head_count // 2
+    pieces, (half_ref, *others), shares_ref = refs[:blocks], refs[blocks : 2 * blocks], refs[2 * blocks]
+    payload_ref, resid_ref = refs[-2:]
+    cols = pieces[0].shape[1]
+    for t in range(blocks):
+        total = pieces[t][...].astype(jnp.float32)
+        for at, source in enumerate((half_ref, *others)):
+            place = (t ^ at) * cols
+            total += source[:, place : place + cols].astype(jnp.float32)
+        payload_ref[:, t * cols : (t + 1) * cols] = total.astype(jnp.bfloat16)
+        if t == 0:
+            resid_ref[...] = total
+    payload_ref[:, blocks * cols :] = shares_ref[...]
+
+
+def payload_part(pieces, half, others, shares, after):
+    blocks = len(pieces)
+    rows, cols = pieces[0].shape
+    return pl.pallas_call(
+        functools.partial(payload_kernel, 2 * blocks),
+        out_shape=(
+            jax.ShapeDtypeStruct((rows, blocks * cols + shares.shape[1]), jnp.bfloat16),
+            jax.ShapeDtypeStruct((rows, cols), jnp.float32),
+        ),
+        in_specs=[VMEM] * (2 * blocks + 1) + [ANY],
+        out_specs=(VMEM, VMEM),
+        name="payload",
+    )(*pieces, half, *others, shares, after)
+
+
+def stack_kernel(count, *refs):
+    rows = refs[0].shape[0]
+    for i in range(count):
+        refs[-1][i * rows : (i + 1) * rows, :] = refs[i][...]
+
+
+def stack_part(parts, after):
+    rows, columns = parts[0].shape
+    return pl.pallas_call(
+        functools.partial(stack_kernel, len(parts)),
+        out_shape=jax.ShapeDtypeStruct((len(parts) * rows, columns), jnp.bfloat16),
+        in_specs=[VMEM] * len(parts) + [ANY],
+        out_specs=VMEM,
+        name="stack",
+    )(*parts, after)
 
 
 def down_copy(w_ref, scratch, sem, me, j, t):
@@ -250,35 +323,38 @@
     return pltpu.make_async_copy(w_ref.at[:, pl.ds(first, cols)], scratch.at[t], sem.at[t])
 
 
-def experts_kernel(head_count, me_ref, mine_ref, other_ref, *refs):
-    weights = refs[:head_count]
-    w_down_ref, units_ref, send_ref, down_s, down_sem = refs[head_count:]
+def experts_kernel(me_ref, mine_0, mine_1, other_0, other_1, w_ref, w_down_ref, *refs):
+    units_ref, send_ref, states_s, down_s, down_sem = refs
     me = me_ref[0]
+    experts, head_count, cols, columns = w_ref.shape
     blocks = head_count // 2
     for t in range(blocks):
         down_copy(w_down_ref, down_s, down_sem, me, 2 * t + 1, t).start()
-    experts, cols, columns = weights[0].shape
-    tokens = mine_ref.shape[0]
-    states = [
-        (other_ref if j % 2 else mine_ref)[:, j // 2 * cols : (j // 2 + 1) * cols]
-        for j in range(head_count)
-    ]
-    shares = mine_ref[:, blocks * cols :]
-    square = sum(
-        jnp.sum(jnp.square(state.astype(jnp.float32)), axis=1, keepdims=True) for state in states
-    )
-    scale = lax.rsqrt(square / (head_count * cols) + norm_eps)
+    tokens = states_s.shape[0]
+    square = []
+    for at, pair in enumerate(((mine_0, other_0), (mine_1, other_1))):
+        first = at * tokens // 2
+        total = 0.0
+        for j in range(head_count):
+            part = pair[j % 2][:, j // 2 * cols : (j // 2 + 1) * cols]
+            states_s[first : first + tokens // 2, j * cols : (j + 1) * cols] = part
+            total += jnp.sum(jnp.square(part.astype(jnp.float32)), axis=1, keepdims=True)
+        square.append(total)
+    scale = lax.rsqrt(jnp.concatenate(square, axis=0) / (head_count * cols) + norm_eps)
+    shares = jnp.concatenate([mine_0[:, blocks * cols :], mine_1[:, blocks * cols :]], axis=0)
     per_step = max(1, 2 * LANES // columns)
     first_half = lax.broadcasted_iota(jnp.int32, (tokens, LANES), 1) < LANES // 2
     source = lax.broadcasted_iota(jnp.int32, (LANES, LANES), 0)
     lane = lax.broadcasted_iota(jnp.int32, (LANES, LANES), 1)
 
-    @pl.loop(0, experts // per_step)
+    @pl.loop(0, experts // per_step, unroll=2)
     def _(p):
+        states = states_s[...]
         products = [
-            sum(
-                jnp.dot(state, w[p * per_step + i], preferred_element_type=jnp.float32)
-                for state, w in zip(states, weights)
+            jnp.dot(
+                states,
+                w_ref[p * per_step + i].reshape(head_count * cols, columns),
+                preferred_element_type=jnp.float32,
             )
             for i in range(per_step)
         ]
@@ -302,33 +378,30 @@
 
 
 def experts_part(me, mine, other, weights, w_down):
-    head_count = len(weights)
-    experts, cols, columns = weights[0].shape
-    tokens = mine.shape[0]
+    experts, head_count, cols, columns = weights.shape
+    tokens = 2 * mine[0].shape[0]
     total_units = w_down.shape[0]
-    vmem = pl.BlockSpec(memory_space=pltpu.VMEM)
     return pl.pallas_call(
-        functools.partial(experts_kernel, head_count),
+        experts_kernel,
         out_shape=(
             jax.ShapeDtypeStruct((tokens, total_units), jnp.bfloat16),
             jax.ShapeDtypeStruct((tokens, head_count // 2 * cols), jnp.bfloat16),
         ),
-        in_specs=[pl.BlockSpec(memory_space=pltpu.SMEM)]
-        + [vmem] * (2 + head_count)
-        + [pl.BlockSpec(memory_space=pl.ANY)],
-        out_specs=(vmem, vmem),
+        in_specs=[SMEM] + [VMEM] * 5 + [ANY],
+        out_specs=(VMEM, VMEM),
         scratch_shapes=[
+            pltpu.VMEM((tokens, head_count * cols), jnp.bfloat16),
             pltpu.VMEM((head_count // 2, total_units, cols), jnp.bfloat16),
             pltpu.SemaphoreType.DMA((head_count // 2,)),
         ],
-        compiler_params=pltpu.CompilerParams(vmem_limit_bytes=16 * 2**20),
+        compiler_params=pltpu.CompilerParams(vmem_limit_bytes=20 * 2**20),
         cost_estimate=pl.CostEstimate(
             flops=2 * tokens * head_count * cols * experts * columns,
             bytes_accessed=2 * head_count * cols * experts * columns,
             transcendentals=0,
         ),
         name="experts",
-    )(me, mine, other, *[pltpu.with_memory_space_constraint(w, pltpu.VMEM) for w in weights], w_down)
+    )(me, *mine, *other, in_vmem(weights), in_hbm(w_down))
 
 
 def down_kernel(head_count, me_ref, units_ref, w_down_ref, keep_ref, down_s, down_sem):
@@ -348,16 +421,11 @@
 def down_part(me, units, w_down, head_count):
     tokens, total_units = units.shape
     cols = w_down.shape[1] // head_count
-    vmem = pl.BlockSpec(memory_space=pltpu.VMEM)
     return pl.pallas_call(
         functools.partial(down_kernel, head_count),
         out_shape=jax.ShapeDtypeStruct((tokens, head_count // 2 * cols), jnp.bfloat16),
-        in_specs=[
-            pl.BlockSpec(memory_space=pltpu.SMEM),
-            vmem,
-            pl.BlockSpec(memory_space=pl.ANY),
-        ],
-        out_specs=vmem,
+        in_specs=[SMEM, VMEM, ANY],
+        out_specs=VMEM,
         scratch_shapes=[
             pltpu.VMEM((head_count // 2, total_units, cols), jnp.bfloat16),
             pltpu.SemaphoreType.DMA((head_count // 2,)),
@@ -369,7 +437,7 @@
             transcendentals=0,
         ),
         name="down",
-    )(me, units, w_down)
+    )(me, units, in_hbm(w_down))
 
 
 def swap(value, axis, size, mask):
@@ -406,30 +474,29 @@
     half = keep.astype(jnp.float32) + swap(send, "head", head_size, 1).astype(jnp.float32)
     half = half.astype(jnp.bfloat16)
     others = [swap(half, "head", head_size, j) for j in even if j]
-    total = half.astype(jnp.float32).reshape(rows, head_size // 2, cols)
-    for j, other in zip([j for j in even if j], others):
-        other = other.reshape(rows, head_size // 2, cols)
-        total = total + jnp.stack(
-            [other[:, t ^ (j // 2)] for t in range(head_size // 2)], axis=1
-        ).astype(jnp.float32)
-    own_x = jnp.stack([pieces[j] for j in even], axis=1)
-    resid = (own_x.astype(jnp.float32) + total).reshape(rows, head_size // 2 * cols)
+    buffer, token = by_expert((0,), me_ref, w_in, head_size, None, half)
 
     every = jnp.arange(head_size * experts_local, dtype=jnp.int32)
     matches = (expert_ids[:, :, None] == every[None, None, :]).astype(jnp.float32)
     shares = jnp.sum(route_weights[:, :, None] * matches, axis=1).astype(jnp.bfloat16)
     shares = jnp.pad(shares, ((0, 0), (0, -shares.shape[1] % LANES)))
-    payload = jnp.concatenate([resid.astype(jnp.bfloat16), shares], axis=1)
+    payload, resid = payload_part([pieces[j] for j in even], half, others, shares, token)
 
     steps = range(2, req_size, 2)
-    line = jnp.concatenate([payload] + [swap(payload, "req", req_size, k) for k in steps])
-    mine = jnp.concatenate([line, swap(line, "req", req_size, 1)])
-    other_states = swap(mine[:, : resid.shape[1]], "head", head_size, 1)
-    weights = [by_expert(j, me_ref, w_in, head_size) for j in range(head_size)]
+    line = [payload] + [swap(payload, "req", req_size, k) for k in steps]
+    buffer, token = by_expert((1, 2), me_ref, w_in, head_size, buffer, payload)
+    line = stack_part(line, token)
+    crossed = swap(line, "req", req_size, 1)
+    line_other = swap(line, "head", head_size, 1)
+    rest = tuple(range(3, head_size))
+    buffer, _ = by_expert(rest, me_ref, w_in, head_size, buffer, line)
+    crossed_other = swap(crossed, "head", head_size, 1)
     w_down_flat = w_down.reshape(experts_local * units_local, width)
-    units, send = experts_part(me_ref, mine, other_states, weights, w_down_flat)
+    units, send = experts_part(
+        me_ref, (line, crossed), (line_other, crossed_other), buffer, w_down_flat
+    )
     sent = swap(send, "head", head_size, 1)
-    tokens = mine.shape[0]
+    tokens = units.shape[0]
     summed = down_part(me_ref, units, w_down_flat, head_size)
     summed = summed.astype(jnp.float32) + sent.astype(jnp.float32)
     summed = summed.astype(jnp.bfloat16).reshape(2, tokens // 2, head_size // 2, cols)
@@ -448,7 +515,7 @@
     out = chunks[0].astype(jnp.float32)
     for k in steps:
         out = out + swap(chunks[k // 2], "req", req_size, k).astype(jnp.float32)
-    return (out + resid[:, :cols]).astype(jnp.bfloat16)
+    return (out + resid).astype(jnp.bfloat16)
 
 
 def solution(mesh):

time: 94 us -> 121 us (1.29)
  local copies, waits for them, and re-layouts: 15.6 us -> 40.8 us
  waiting for transfers between devices: 24.1 us -> 19.6 us
  Pallas kernels: 32.7 us -> 35.9 us
  starting transfers between devices: 19.4 us -> 22.4 us
    unnamed x23 -> x45, local copies, waits for them, and re-layouts: 14.3 us -> 39.1 us
    ppermute x14 -> x15, waiting for transfers between devices: 18.4 us -> 13.9 us  [swap(): return lax.ppermute(value, axis, [(i, i ^ mask) for i in range(size)])]
    pallas_call x5 -> x6, Pallas kernels: 16.5 us -> 21 us  [the longest x3 9.01 us: by_expert(): pl.pallas_call(functools.partial(relayout_kernel, js), out_shape=(pltpu.V...]
    ppermute x14 -> x15, starting transfers between devices: 15.9 us -> 18.8 us  [swap(): return lax.ppermute(value, axis, [(i, i ^ mask) for i in range(size)])]
    pallas_call x1, Pallas kernels: 14 us -> 11.8 us  [attention(): pl.pallas_call(functools.partial(attention_kernel, head_count), out_shape...]
  transfers between devices with their start and end apart: 17 -> 18, of which waited for: 11 -> 9; matrix products, arithmetic and copies ran while one was open for 3% -> 1% of each run, Pallas kernels for 8% -> 10%
where the time goes in v4:
time: 121 us
  local copies, waits for them, and re-layouts  40.8 us (34%)
  Pallas kernels  35.9 us (30%)
  starting transfers between devices  22.4 us (19%)
  waiting for transfers between devices  19.6 us (16%)
  other arithmetic  1.96 us (2%)
    unnamed x45, local copies, waits for them, and re-layouts  39.1 us
    ppermute x15, starting transfers between devices, swap(): return lax.ppermute(value, axis, [(i, i ^ mask) for i in range(size)])  18.8 us
    ppermute x15, waiting for transfers between devices, swap(): return lax.ppermute(value, axis, [(i, i ^ mask) for i in range(size)])  13.9 us
    pallas_call x1, Pallas kernels, attention(): pl.pallas_call(functools.partial(attention_kernel, head_count), out_shape...  11.8 us
    pallas_call x3, Pallas kernels, by_expert(): pl.pallas_call(functools.partial(relayout_kernel, js), out_shape=(pltpu.V...  9.01 us
    pallas_call x1, Pallas kernels, experts_part(): pl.pallas_call(experts_kernel, out_shape=(jax.ShapeDtypeStruct((tokens, t...  8.65 us
    ppermute x3, waiting for transfers between devices, per_device(): got = lax.ppermute(summed[k, :, j // 2], ('req', 'head'), pairs)  5.69 us
    ppermute x3, starting transfers between devices, per_device(): got = lax.ppermute(summed[k, :, j // 2], ('req', 'head'), pairs)  3.55 us
  transfers between devices with their start and end apart: 18, of which 9 were waited for; matrix products, arithmetic and copies ran while one was open for 1% of the time, Pallas kernels for 10%

profile of v4, /device:TPU:0, one launch (start us, length us, event | category | flops | bytes accessed | tf_op | source)
XLA Modules:
  0.0 120.9 jit_solution(17870074674650610249)
XLA Ops:
  0.0 2.4 %collective-permute-start.2 = (bf16[32,512]{1,0:T(8,128)(2,1)}, bf16[32,512]{1,0:T(8,128)(2,1)S(1)}, u32[]{:S(2)}, u32[]{:S(2)}) collective-permute-start(bf16[32,512]{1,0:T(8,128)(2,1)} %refs_0_.3), channel_id=1, source_target_pairs={{0,3},{1,2},{2,1},{3,0},{4,7},{5,6},{6,5},{7,4},{8,11},{9,10},{10,... | collective-permute-start | bytes 98312 | tf_op jit(solution)/shard_map/ppermute | solution.py:444
  2.4 0.7 collective-permute-start.1
  3.1 0.7 convert_element_type.60
  3.8 0.1 fusion.3
  3.9 0.1 pad_maximum_fusion
  4.0 0.5 collective-permute-done.2.refs_3_
  4.5 2.7 %collective-permute-done.refs_2_.refs_1_ = bf16[32,512]{1,0:T(8,128)(2,1)S(1)} collective-permute-done((bf16[32,512]{1,0:T(8,128)(2,1)}, bf16[32,512]{1,0:T(8,128)(2,1)S(1)}, u32[]{:S(2)}, u32[]{:S(2)}) %collective-permute-start) | collective-permute-done | bytes 32800 | tf_op jit(solution)/shard_map/ppermute | solution.py:444
  7.2 11.8 %attention.1 = (bf16[32,1024]{1,0:T(8,128)(2,1)S(1)}, bf16[32,1024]{1,0:T(8,128)(2,1)S(1)}) custom-call(s32[32]{0:T(128)} %lengths_ref.1, s32[1]{0:T(128)} %bitcast.me_ref, f32[32,128]{1,0:T(8,128)S(1)} %get-tuple-element.37.cos_ref, f32[32,128]{1,0:T(8,128)S(1)} %get-tuple-element.38.sin_ref, bf16[32,512]{1,0:T(8,128)(2,1)} %refs_0_.3, ...), custom_call_target="tpu_custom_call" | custom-call | flops 268435456 | bytes 20971520 | tf_op jit(solution)/shard_map/attention/pallas_call | solution.py:183
  19.1 0.1 collective-permute-start.3
  19.2 0.1 copy.19
  19.2 0.1 copy.20
  19.3 1.1 collective-permute-done.3
  20.4 0.4 collective-permute-start.4
  20.9 0.2 select_reduce_fusion
  21.0 0.6 pad.4.refs_4_
  21.6 2.4 %by_expert_0.1 = (bf16[16,4,512,256]{3,2,1,0:T(8,128)(2,1)S(1)}, f32[8,128]{1,0:T(8,128)S(1)}) custom-call(s32[1]{0:T(128)} %bitcast.me_ref, bf16[2048,16,256]{2,1,0:T(8,128)(2,1)} %w_ref.5, bf16[32,1024]{1,0:T(8,128)(2,1)S(1)} %add_convert_fusion.1.refs_0_.refs_2_), custom_call_target="tpu_custom_call" | custom-call | bytes 8388608 | tf_op jit(solution)/shard_map/by_expert_0/pallas_call | solution.py:251
  24.1 5.7 %copy-done = bf16[16,4,512,256]{3,2,1,0:T(8,128)(2,1)} copy-done((bf16[16,4,512,256]{3,2,1,0:T(8,128)(2,1)}, bf16[16,4,512,256]{3,2,1,0:T(8,128)(2,1)S(1)}, u32[]{:S(2)}) %copy-start) | copy-done | bytes 16777240
  29.8 0.6 copy-done.12
  30.4 0.6 copy-done.17
  31.1 1.6 %payload.1 = (bf16[32,1152]{1,0:T(8,128)(2,1)}, f32[32,512]{1,0:T(8,128)}) custom-call(bf16[32,512]{1,0:T(8,128)(2,1)} %refs_0_.3, bf16[32,512]{1,0:T(8,128)(2,1)} %copy-done.10, bf16[32,1024]{1,0:T(8,128)(2,1)} %copy-done.8, bf16[32,1024]{1,0:T(8,128)(2,1)} %copy-done.17, bf16[32,128]{1,0:T(8,128)(2,1)} %pad.4.refs_4_, f32[8,128]{1,0:T(8,128)} %copy-done.12), custom_call_target="tpu_custom_call" | custom-call | tf_op jit(solution)/shard_map/payload/pallas_call | solution.py:291
  32.7 4.2 %collective-permute-start.7 = (bf16[32,1152]{1,0:T(8,128)(2,1)}, bf16[32,1152]{1,0:T(8,128)(2,1)S(1)}, u32[]{:S(2)}, u32[]{:S(2)}) collective-permute-start(bf16[32,1152]{1,0:T(8,128)(2,1)} %get-tuple-element.19.refs_1_.refs_0_), channel_id=1, source_target_pairs={{0,24},{4,28},{8,16},{12,20},{16,8},{20,12},{24,0},{28,4},{1,25},{... | collective-permute-start | bytes 221192 | tf_op jit(solution)/shard_map/ppermute | solution.py:444
  36.9 0.0 collective-permute-start.6
  36.9 0.6 collective-permute-start.5
  37.4 5.8 %copy-done.1 = bf16[16,4,512,256]{3,2,1,0:T(8,128)(2,1)S(1)} copy-done((bf16[16,4,512,256]{3,2,1,0:T(8,128)(2,1)S(1)}, bf16[16,4,512,256]{3,2,1,0:T(8,128)(2,1)}, u32[]{:S(2)}) %copy-start.1) | copy-done | bytes 16777240
  43.2 0.9 copy-done.9
  44.1 3.7 %by_expert_1.1 = (bf16[16,4,512,256]{3,2,1,0:T(8,128)(2,1)S(1)}, f32[8,128]{1,0:T(8,128)S(1)}) custom-call(s32[1]{0:T(128)} %bitcast.me_ref, bf16[2048,16,256]{2,1,0:T(8,128)(2,1)} %w_ref.5, bf16[16,4,512,256]{3,2,1,0:T(8,128)(2,1)S(1)} %copy-done.1, bf16[32,1152]{1,0:T(8,128)(2,1)S(1)} %copy-done.9), custom_call_target="tpu_custom_call", output_to_operand_aliasing={{0}: (2, {})} | custom-call | bytes 16777216 | tf_op jit(solution)/shard_map/by_expert_1/pallas_call | solution.py:251
  47.8 5.7 %copy-done.2 = bf16[16,4,512,256]{3,2,1,0:T(8,128)(2,1)} copy-done((bf16[16,4,512,256]{3,2,1,0:T(8,128)(2,1)}, bf16[16,4,512,256]{3,2,1,0:T(8,128)(2,1)S(1)}, u32[]{:S(2)}) %copy-start.2) | copy-done | bytes 16777240
  53.6 0.6 copy-done.11
  54.2 0.0 collective-permute-done.7.refs_3_
  54.2 0.0 collective-permute-done.5.refs_1_
  54.2 0.6 copy-done.13
  54.8 0.0 copy-done.14
  54.8 0.0 copy-done.15
  54.9 1.7 %stack.1.refs_1_.mine_0 = bf16[128,1152]{1,0:T(8,128)(2,1)} custom-call(bf16[32,1152]{1,0:T(8,128)(2,1)} %get-tuple-element.19.refs_1_.refs_0_, bf16[32,1152]{1,0:T(8,128)(2,1)} %copy-done.15, bf16[32,1152]{1,0:T(8,128)(2,1)} %copy-done.14, bf16[32,1152]{1,0:T(8,128)(2,1)} %copy-done.13, f32[8,128]{1,0:T(8,128)} %copy-done.11), custom_call_target="tpu_custom_call" | custom-call | tf_op jit(solution)/shard_map/stack/pallas_call | solution.py:311
  56.6 6.3 %collective-permute-start.8 = (bf16[128,1152]{1,0:T(8,128)(2,1)}, bf16[128,1152]{1,0:T(8,128)(2,1)S(1)}, u32[]{:S(2)}, u32[]{:S(2)}) collective-permute-start(bf16[128,1152]{1,0:T(8,128)(2,1)} %stack.1.refs_1_.mine_0), channel_id=1, source_target_pairs={{0,4},{4,0},{8,12},{12,8},{16,20},{20,16},{24,28},{28,24},{1,5},{5... | collective-permute-start | bytes 884744 | tf_op jit(solution)/shard_map/ppermute | solution.py:444
  62.9 0.0 collective-permute-start.9
  62.9 6.4 %collective-permute-done.8.mine_1 = bf16[128,1152]{1,0:T(8,128)(2,1)S(1)} collective-permute-done((bf16[128,1152]{1,0:T(8,128)(2,1)}, bf16[128,1152]{1,0:T(8,128)(2,1)S(1)}, u32[]{:S(2)}, u32[]{:S(2)}) %collective-permute-start.8) | collective-permute-done | bytes 294944 | tf_op jit(solution)/shard_map/ppermute | solution.py:444
  69.3 0.0 collective-permute-start.10
  69.3 5.8 %copy-done.3 = bf16[16,4,512,256]{3,2,1,0:T(8,128)(2,1)S(1)} copy-done((bf16[16,4,512,256]{3,2,1,0:T(8,128)(2,1)S(1)}, bf16[16,4,512,256]{3,2,1,0:T(8,128)(2,1)}, u32[]{:S(2)}) %copy-start.3) | copy-done | bytes 16777240
  75.1 1.0 copy-done.6
  76.1 2.8 %by_expert_3.1 = (bf16[16,4,512,256]{3,2,1,0:T(8,128)(2,1)S(1)}, f32[8,128]{1,0:T(8,128)}) custom-call(s32[1]{0:T(128)} %bitcast.me_ref, bf16[2048,16,256]{2,1,0:T(8,128)(2,1)} %w_ref.5, bf16[16,4,512,256]{3,2,1,0:T(8,128)(2,1)S(1)} %copy-done.3, bf16[128,1152]{1,0:T(8,128)(2,1)S(1)} %copy-done.6), custom_call_target="tpu_custom_call", output_to_operand_aliasing={{0}: (2, {})} | custom-call | bytes 8388608 | tf_op jit(solution)/shard_map/by_expert_3/pallas_call | solution.py:251
  78.9 5.7 %copy-done.4 = bf16[16,4,512,256]{3,2,1,0:T(8,128)(2,1)} copy-done((bf16[16,4,512,256]{3,2,1,0:T(8,128)(2,1)}, bf16[16,4,512,256]{3,2,1,0:T(8,128)(2,1)S(1)}, u32[]{:S(2)}) %copy-start.4) | copy-done | bytes 16777240
  84.7 0.0 collective-permute-done.9.other_0
  84.7 0.0 collective-permute-done.10.other_1
  84.7 5.8 %copy-done.5 = bf16[16,4,512,256]{3,2,1,0:T(8,128)(2,1)S(1)} copy-done((bf16[16,4,512,256]{3,2,1,0:T(8,128)(2,1)S(1)}, bf16[16,4,512,256]{3,2,1,0:T(8,128)(2,1)}, u32[]{:S(2)}) %copy-start.5) | copy-done | bytes 16777240
  90.5 8.6 %experts.1 = (bf16[256,2048]{1,0:T(8,128)(2,1)S(1)}, bf16[256,1024]{1,0:T(8,128)(2,1)S(1)}) custom-call(s32[1]{0:T(128)} %bitcast.me_ref, bf16[128,1152]{1,0:T(8,128)(2,1)S(1)} %copy-done.7, bf16[128,1152]{1,0:T(8,128)(2,1)S(1)} %collective-permute-done.8.mine_1, bf16[128,1152]{1,0:T(8,128)(2,1)S(1)} %collective-permute-done.9.other_0, ...), custom_call_target="tpu_custom_call" | custom-call | flops 4294967296 | bytes 16777216 | tf_op jit(solution)/shard_map/experts/pallas_call | solution.py:384
  99.1 0.6 collective-permute-start.11
  99.7 3.0 %down.1 = bf16[256,1024]{1,0:T(8,128)(2,1)S(1)} custom-call(s32[1]{0:T(128)} %bitcast.me_ref, bf16[256,2048]{1,0:T(8,128)(2,1)S(1)} %get-tuple-element.24.units_ref, bf16[2048,2048]{1,0:T(8,128)(2,1)} %bitcast.19), custom_call_target="tpu_custom_call" | custom-call | flops 1073741824 | bytes 4194304 | tf_op jit(solution)/shard_map/down/pallas_call | solution.py:424
  102.8 0.2 add_convert_fusion
  103.0 0.4 reshape.35
  103.3 0.7 fusion.4
  104.2 2.8 %collective-permute-start.14 = (bf16[128,512]{1,0:T(8,128)(2,1)S(1)}, bf16[128,512]{1,0:T(8,128)(2,1)S(1)}, u32[]{:S(2)}, u32[]{:S(2)}) collective-permute-start(bf16[128,512]{1,0:T(8,128)(2,1)S(1)} %bitcast.24), channel_id=1, source_target_pairs={{0,6},{1,7},{2,4},{3,5},{4,2},{5,3},{6,0},{7,1},{8,14},{9,15},{10,... | collective-permute-start | bytes 393224 | tf_op jit(solution)/shard_map/ppermute | solution.py:512
  106.9 0.3 collective-permute-start.12
  107.2 0.5 collective-permute-start.13
  107.7 3.8 %collective-permute-done.14 = bf16[128,512]{1,0:T(8,128)(2,1)S(1)} collective-permute-done((bf16[128,512]{1,0:T(8,128)(2,1)S(1)}, bf16[128,512]{1,0:T(8,128)(2,1)S(1)}, u32[]{:S(2)}, u32[]{:S(2)}) %collective-permute-start.14) | collective-permute-done | bytes 131104 | tf_op jit(solution)/shard_map/ppermute | solution.py:512
  111.5 1.9 %collective-permute-done.12 = bf16[128,512]{1,0:T(8,128)(2,1)S(1)} collective-permute-done((bf16[128,512]{1,0:T(8,128)(2,1)S(1)}, bf16[128,512]{1,0:T(8,128)(2,1)S(1)}, u32[]{:S(2)}, u32[]{:S(2)}) %collective-permute-start.12) | collective-permute-done | bytes 131104 | tf_op jit(solution)/shard_map/ppermute | solution.py:512
  113.4 0.1 fusion.2
  113.5 0.3 collective-permute-start.15
  113.9 1.5 %collective-permute-start.17 = (bf16[32,512]{1,0:T(8,128)(2,1)S(1)}, bf16[32,512]{1,0:T(8,128)(2,1)S(1)}, u32[]{:S(2)}, u32[]{:S(2)}) collective-permute-start(bf16[32,512]{1,0:T(8,128)(2,1)S(1)} %get-tuple-element.32), channel_id=1, source_target_pairs={{0,24},{4,28},{8,16},{12,20},{16,8},{20,12},{24,0},{28,4},{1,25},{... | collective-permute-start | bytes 98312 | tf_op jit(solution)/shard_map/ppermute | solution.py:444
  115.3 1.7 %collective-permute-start.16 = (bf16[32,512]{1,0:T(8,128)(2,1)S(1)}, bf16[32,512]{1,0:T(8,128)(2,1)S(1)}, u32[]{:S(2)}, u32[]{:S(2)}) collective-permute-start(bf16[32,512]{1,0:T(8,128)(2,1)S(1)} %get-tuple-element.33), channel_id=1, source_target_pairs={{0,16},{4,20},{8,24},{12,28},{16,0},{20,4},{24,8},{28,12},{1,17},{... | collective-permute-start | bytes 98312 | tf_op jit(solution)/shard_map/ppermute | solution.py:444
  117.1 0.4 collective-permute-done.15
  117.5 2.1 %collective-permute-done.17 = bf16[32,512]{1,0:T(8,128)(2,1)S(1)} collective-permute-done((bf16[32,512]{1,0:T(8,128)(2,1)S(1)}, bf16[32,512]{1,0:T(8,128)(2,1)S(1)}, u32[]{:S(2)}, u32[]{:S(2)}) %collective-permute-start.17) | collective-permute-done | bytes 32800 | tf_op jit(solution)/shard_map/ppermute | solution.py:444
  119.6 0.7 collective-permute-done.16
  120.3 0.6 add_convert_fusion.2
  (38 shorter events, 0.2 us)
Async XLA Ops:
  0.0 4.5 %collective-permute-start.2 = (bf16[32,512]{1,0:T(8,128)(2,1)}, bf16[32,512]{1,0:T(8,128)(2,1)S(1)}, u32[]{:S(2)}, u32[]{:S(2)}) collective-permute-start(bf16[32,512]{1,0:T(8,128)(2,1)} %refs_0_.3), channel_id=1, source_target_pairs={{0,3},{1,2},{2,1},{3,0},{4,7},{5,6},{6,5},{7,4},{8,11},{9,10},{10,... | collective-permute-start | bytes 98312 | tf_op jit(solution)/shard_map/ppermute | solution.py:444
  2.4 2.1 %collective-permute-start.1 = (bf16[32,512]{1,0:T(8,128)(2,1)}, bf16[32,512]{1,0:T(8,128)(2,1)S(1)}, u32[]{:S(2)}, u32[]{:S(2)}) collective-permute-start(bf16[32,512]{1,0:T(8,128)(2,1)} %refs_0_.3), channel_id=1, source_target_pairs={{0,1},{1,0},{2,3},{3,2},{4,5},{5,4},{6,7},{7,6},{8,9},{9,8},{10,11... | collective-permute-start | bytes 98312 | tf_op jit(solution)/shard_map/ppermute | solution.py:444
  3.1 4.1 %collective-permute-start = (bf16[32,512]{1,0:T(8,128)(2,1)}, bf16[32,512]{1,0:T(8,128)(2,1)S(1)}, u32[]{:S(2)}, u32[]{:S(2)}) collective-permute-start(bf16[32,512]{1,0:T(8,128)(2,1)} %refs_0_.3), channel_id=1, source_target_pairs={{0,2},{1,3},{2,0},{3,1},{4,6},{5,7},{6,4},{7,5},{8,10},{9,11},{10,... | collective-permute-start | bytes 98312 | tf_op jit(solution)/shard_map/ppermute | solution.py:444
  7.2 11.9 %copy-start.10 = (bf16[32,512]{1,0:T(8,128)(2,1)}, bf16[32,512]{1,0:T(8,128)(2,1)S(1)}, u32[]{:S(2)}) copy-start(bf16[32,512]{1,0:T(8,128)(2,1)S(1)} %collective-permute-done.refs_2_.refs_1_) | copy-start | bytes 98308
  7.2 11.9 %copy-start.18 = (s32[32,8]{0,1:T(8,128)S(1)}, s32[32,8]{0,1:T(8,128)}, u32[]{:S(2)}) copy-start(s32[32,8]{0,1:T(8,128)} %param.12) | copy-start | bytes 3076
  7.2 12.0 %copy-start.19 = (f32[32,8]{0,1:T(8,128)S(1)}, f32[32,8]{0,1:T(8,128)}, u32[]{:S(2)}) copy-start(f32[32,8]{0,1:T(8,128)} %param.13) | copy-start | bytes 3076
  19.1 1.3 %collective-permute-start.3 = (bf16[32,1024]{1,0:T(8,128)(2,1)S(1)}, bf16[32,1024]{1,0:T(8,128)(2,1)S(1)}, u32[]{:S(2)}, u32[]{:S(2)}) collective-permute-start(bf16[32,1024]{1,0:T(8,128)(2,1)S(1)} %get-tuple-element.17), channel_id=1, source_target_pairs={{0,1},{1,0},{2,3},{3,2},{4,5},{5,4},{6,7},{7,6},{8,9},{9,8},{10,11... | collective-permute-start | bytes 196616 | tf_op jit(solution)/shard_map/ppermute | solution.py:444
  20.4 10.0 %copy-start.8 = (bf16[32,1024]{1,0:T(8,128)(2,1)}, bf16[32,1024]{1,0:T(8,128)(2,1)S(1)}, u32[]{:S(2)}) copy-start(bf16[32,1024]{1,0:T(8,128)(2,1)S(1)} %add_convert_fusion.1.refs_0_.refs_2_) | copy-start | bytes 196612
  20.4 10.0 %collective-permute-start.4 = (bf16[32,1024]{1,0:T(8,128)(2,1)S(1)}, bf16[32,1024]{1,0:T(8,128)(2,1)S(1)}, u32[]{:S(2)}, u32[]{:S(2)}) collective-permute-start(bf16[32,1024]{1,0:T(8,128)(2,1)S(1)} %add_convert_fusion.1.refs_0_.refs_2_), channel_id=1, source_target_pairs={{0,2},{1,3},{2,0},{3,1},{4,6},{5,7},{6,4},{7,5},{8,10},{9,11},{10,... | collective-permute-start | bytes 196616 | tf_op jit(solution)/shard_map/ppermute | solution.py:444
  24.1 5.8 %copy-start = (bf16[16,4,512,256]{3,2,1,0:T(8,128)(2,1)}, bf16[16,4,512,256]{3,2,1,0:T(8,128)(2,1)S(1)}, u32[]{:S(2)}) copy-start(bf16[16,4,512,256]{3,2,1,0:T(8,128)(2,1)S(1)} %get-tuple-element.20.refs_0_) | copy-start | bytes 50331652
  29.8 0.6 copy-start.12
  30.4 0.6 copy-start.17
  32.7 21.5 %collective-permute-start.7 = (bf16[32,1152]{1,0:T(8,128)(2,1)}, bf16[32,1152]{1,0:T(8,128)(2,1)S(1)}, u32[]{:S(2)}, u32[]{:S(2)}) collective-permute-start(bf16[32,1152]{1,0:T(8,128)(2,1)} %get-tuple-element.19.refs_1_.refs_0_), channel_id=1, source_target_pairs={{0,24},{4,28},{8,16},{12,20},{16,8},{20,12},{24,0},{28,4},{1,25},{... | collective-permute-start | bytes 221192 | tf_op jit(solution)/shard_map/ppermute | solution.py:444
  36.9 17.3 %collective-permute-start.6 = (bf16[32,1152]{1,0:T(8,128)(2,1)}, bf16[32,1152]{1,0:T(8,128)(2,1)S(1)}, u32[]{:S(2)}, u32[]{:S(2)}) collective-permute-start(bf16[32,1152]{1,0:T(8,128)(2,1)} %get-tuple-element.19.refs_1_.refs_0_), channel_id=1, source_target_pairs={{0,16},{4,20},{8,24},{12,28},{16,0},{20,4},{24,8},{28,12},{1,17},{... | collective-permute-start | bytes 221192 | tf_op jit(solution)/shard_map/ppermute | solution.py:444
  36.9 17.3 %collective-permute-start.5 = (bf16[32,1152]{1,0:T(8,128)(2,1)}, bf16[32,1152]{1,0:T(8,128)(2,1)S(1)}, u32[]{:S(2)}, u32[]{:S(2)}) collective-permute-start(bf16[32,1152]{1,0:T(8,128)(2,1)} %get-tuple-element.19.refs_1_.refs_0_), channel_id=1, source_target_pairs={{0,8},{4,12},{8,0},{12,4},{16,24},{20,28},{24,16},{28,20},{1,9},{5... | collective-permute-start | bytes 221192 | tf_op jit(solution)/shard_map/ppermute | solution.py:444
  37.4 5.8 %copy-start.1 = (bf16[16,4,512,256]{3,2,1,0:T(8,128)(2,1)S(1)}, bf16[16,4,512,256]{3,2,1,0:T(8,128)(2,1)}, u32[]{:S(2)}) copy-start(bf16[16,4,512,256]{3,2,1,0:T(8,128)(2,1)} %copy-done) | copy-start | bytes 50331652
  43.2 0.9 copy-start.9
  47.8 5.8 %copy-start.2 = (bf16[16,4,512,256]{3,2,1,0:T(8,128)(2,1)}, bf16[16,4,512,256]{3,2,1,0:T(8,128)(2,1)S(1)}, u32[]{:S(2)}) copy-start(bf16[16,4,512,256]{3,2,1,0:T(8,128)(2,1)S(1)} %get-tuple-element.22.refs_0_) | copy-start | bytes 50331652
  53.6 0.6 copy-start.11
  54.2 0.6 copy-start.13
  54.2 0.7 copy-start.14
  54.2 0.7 copy-start.15
  56.6 12.8 %collective-permute-start.8 = (bf16[128,1152]{1,0:T(8,128)(2,1)}, bf16[128,1152]{1,0:T(8,128)(2,1)S(1)}, u32[]{:S(2)}, u32[]{:S(2)}) collective-permute-start(bf16[128,1152]{1,0:T(8,128)(2,1)} %stack.1.refs_1_.mine_0), channel_id=1, source_target_pairs={{0,4},{4,0},{8,12},{12,8},{16,20},{20,16},{24,28},{28,24},{1,5},{5... | collective-permute-start | bytes 884744 | tf_op jit(solution)/shard_map/ppermute | solution.py:444
  62.9 21.8 %collective-permute-start.9 = (bf16[128,1152]{1,0:T(8,128)(2,1)}, bf16[128,1152]{1,0:T(8,128)(2,1)S(1)}, u32[]{:S(2)}, u32[]{:S(2)}) collective-permute-start(bf16[128,1152]{1,0:T(8,128)(2,1)} %stack.1.refs_1_.mine_0), channel_id=1, source_target_pairs={{0,1},{1,0},{2,3},{3,2},{4,5},{5,4},{6,7},{7,6},{8,9},{9,8},{10,11... | collective-permute-start | bytes 884744 | tf_op jit(solution)/shard_map/ppermute | solution.py:444
  69.3 15.4 %collective-permute-start.10 = (bf16[128,1152]{1,0:T(8,128)(2,1)S(1)}, bf16[128,1152]{1,0:T(8,128)(2,1)S(1)}, u32[]{:S(2)}, u32[]{:S(2)}) collective-permute-start(bf16[128,1152]{1,0:T(8,128)(2,1)S(1)} %collective-permute-done.8.mine_1), channel_id=1, source_target_pairs={{0,1},{1,0},{2,3},{3,2},{4,5},{5,4},{6,7},{7,6},{8,9},{9,8},{10,11... | collective-permute-start | bytes 884744 | tf_op jit(solution)/shard_map/ppermute | solution.py:444
  69.3 5.8 %copy-start.3 = (bf16[16,4,512,256]{3,2,1,0:T(8,128)(2,1)S(1)}, bf16[16,4,512,256]{3,2,1,0:T(8,128)(2,1)}, u32[]{:S(2)}) copy-start(bf16[16,4,512,256]{3,2,1,0:T(8,128)(2,1)} %copy-done.2) | copy-start | bytes 50331652
  75.1 1.0 copy-start.6
  76.1 8.6 %copy-start.7 = (bf16[128,1152]{1,0:T(8,128)(2,1)S(1)}, bf16[128,1152]{1,0:T(8,128)(2,1)}, u32[]{:S(2)}) copy-start(bf16[128,1152]{1,0:T(8,128)(2,1)} %stack.1.refs_1_.mine_0) | copy-start | bytes 884740
  78.9 5.8 %copy-start.4 = (bf16[16,4,512,256]{3,2,1,0:T(8,128)(2,1)}, bf16[16,4,512,256]{3,2,1,0:T(8,128)(2,1)S(1)}, u32[]{:S(2)}) copy-start(bf16[16,4,512,256]{3,2,1,0:T(8,128)(2,1)S(1)} %get-tuple-element.23.w_ref) | copy-start | bytes 50331652
  84.7 5.8 %copy-start.5 = (bf16[16,4,512,256]{3,2,1,0:T(8,128)(2,1)S(1)}, bf16[16,4,512,256]{3,2,1,0:T(8,128)(2,1)}, u32[]{:S(2)}) copy-start(bf16[16,4,512,256]{3,2,1,0:T(8,128)(2,1)} %copy-done.4) | copy-start | bytes 50331652
  99.1 21.1 %copy-start.16 = (f32[32,512]{1,0:T(8,128)S(1)}, f32[32,512]{1,0:T(8,128)}, u32[]{:S(2)}) copy-start(f32[32,512]{1,0:T(8,128)} %get-tuple-element.26) | copy-start | bytes 196612
  99.1 3.6 %collective-permute-start.11 = (bf16[256,1024]{1,0:T(8,128)(2,1)S(1)}, bf16[256,1024]{1,0:T(8,128)(2,1)S(1)}, u32[]{:S(2)}, u32[]{:S(2)}) collective-permute-start(bf16[256,1024]{1,0:T(8,128)(2,1)S(1)} %get-tuple-element.25), channel_id=1, source_target_pairs={{0,1},{1,0},{2,3},{3,2},{4,5},{5,4},{6,7},{7,6},{8,9},{9,8},{10,11... | collective-permute-start | bytes 1572872 | tf_op jit(solution)/shard_map/ppermute | solution.py:444
  104.2 7.3 %collective-permute-start.14 = (bf16[128,512]{1,0:T(8,128)(2,1)S(1)}, bf16[128,512]{1,0:T(8,128)(2,1)S(1)}, u32[]{:S(2)}, u32[]{:S(2)}) collective-permute-start(bf16[128,512]{1,0:T(8,128)(2,1)S(1)} %bitcast.24), channel_id=1, source_target_pairs={{0,6},{1,7},{2,4},{3,5},{4,2},{5,3},{6,0},{7,1},{8,14},{9,15},{10,... | collective-permute-start | bytes 393224 | tf_op jit(solution)/shard_map/ppermute | solution.py:512
  106.9 6.5 %collective-permute-start.12 = (bf16[128,512]{1,0:T(8,128)(2,1)S(1)}, bf16[128,512]{1,0:T(8,128)(2,1)S(1)}, u32[]{:S(2)}, u32[]{:S(2)}) collective-permute-start(bf16[128,512]{1,0:T(8,128)(2,1)S(1)} %bitcast.23), channel_id=1, source_target_pairs={{0,4},{1,5},{2,6},{3,7},{4,0},{5,1},{6,2},{7,3},{8,12},{9,13},{10,... | collective-permute-start | bytes 393224 | tf_op jit(solution)/shard_map/ppermute | solution.py:512
  107.2 6.2 %collective-permute-start.13 = (bf16[128,512]{1,0:T(8,128)(2,1)S(1)}, bf16[128,512]{1,0:T(8,128)(2,1)S(1)}, u32[]{:S(2)}, u32[]{:S(2)}) collective-permute-start(bf16[128,512]{1,0:T(8,128)(2,1)S(1)} %bitcast.22), channel_id=1, source_target_pairs={{0,2},{1,3},{2,0},{3,1},{4,6},{5,7},{6,4},{7,5},{8,10},{9,11},{10,... | collective-permute-start | bytes 393224 | tf_op jit(solution)/shard_map/ppermute | solution.py:512
  113.5 4.0 %collective-permute-start.15 = (bf16[32,512]{1,0:T(8,128)(2,1)S(1)}, bf16[32,512]{1,0:T(8,128)(2,1)S(1)}, u32[]{:S(2)}, u32[]{:S(2)}) collective-permute-start(bf16[32,512]{1,0:T(8,128)(2,1)S(1)} %get-tuple-element.31), channel_id=1, source_target_pairs={{0,8},{4,12},{8,0},{12,4},{16,24},{20,28},{24,16},{28,20},{1,9},{5... | collective-permute-start | bytes 98312 | tf_op jit(solution)/shard_map/ppermute | solution.py:444
  113.9 5.7 %collective-permute-start.17 = (bf16[32,512]{1,0:T(8,128)(2,1)S(1)}, bf16[32,512]{1,0:T(8,128)(2,1)S(1)}, u32[]{:S(2)}, u32[]{:S(2)}) collective-permute-start(bf16[32,512]{1,0:T(8,128)(2,1)S(1)} %get-tuple-element.32), channel_id=1, source_target_pairs={{0,24},{4,28},{8,16},{12,20},{16,8},{20,12},{24,0},{28,4},{1,25},{... | collective-permute-start | bytes 98312 | tf_op jit(solution)/shard_map/ppermute | solution.py:444
  115.3 5.0 %collective-permute-start.16 = (bf16[32,512]{1,0:T(8,128)(2,1)S(1)}, bf16[32,512]{1,0:T(8,128)(2,1)S(1)}, u32[]{:S(2)}, u32[]{:S(2)}) collective-permute-start(bf16[32,512]{1,0:T(8,128)(2,1)S(1)} %get-tuple-element.33), channel_id=1, source_target_pairs={{0,16},{4,20},{8,24},{12,28},{16,0},{20,4},{24,8},{28,12},{1,17},{... | collective-permute-start | bytes 98312 | tf_op jit(solution)/shard_map/ppermute | solution.py:444

commit v5 on v4

--- a/solution.py
+++ b/solution.py
@@ -296,6 +296,7 @@
         ),
         in_specs=[VMEM] * (2 * blocks + 1) + [ANY],
         out_specs=(VMEM, VMEM),
+        compiler_params=pltpu.CompilerParams(vmem_limit_bytes=8 * 2**20),
         name="payload",
     )(*pieces, half, *others, shares, after)
 
@@ -313,6 +314,7 @@
         out_shape=jax.ShapeDtypeStruct((len(parts) * rows, columns), jnp.bfloat16),
         in_specs=[VMEM] * len(parts) + [ANY],
         out_specs=VMEM,
+        compiler_params=pltpu.CompilerParams(vmem_limit_bytes=8 * 2**20),
         name="stack",
     )(*parts, after)
 

time: 121 us -> 77.7 us (0.64)
  local copies, waits for them, and re-layouts: 40.8 us -> 1.36 us
  starting transfers between devices: 22.4 us -> 16.3 us
  waiting for transfers between devices: 19.6 us -> 22.5 us
    unnamed x45 -> x11, local copies, waits for them, and re-layouts: 39.1 us -> 0.23 us
    ppermute x15, starting transfers between devices: 18.8 us -> 12.7 us  [swap(): return lax.ppermute(value, axis, [(i, i ^ mask) for i in range(size)])]
    pallas_call x1, Pallas kernels: 11.8 us -> 14.6 us  [attention(): pl.pallas_call(functools.partial(attention_kernel, head_count), out_shape...]
    ppermute x15, waiting for transfers between devices: 13.9 us -> 16.4 us  [swap(): return lax.ppermute(value, axis, [(i, i ^ mask) for i in range(size)])]
    pallas_call x1, Pallas kernels: 1.73 us -> 0.02 us  [stack_part(): pl.pallas_call(functools.partial(stack_kernel, len(parts)), out_shape=jax...]
    pallas_call x1, Pallas kernels: 1.59 us -> 0.03 us  [payload_part(): pl.pallas_call(functools.partial(payload_kernel, 2 * blocks), out_shape=(...]
  transfers between devices with their start and end apart: 18 -> 18, of which waited for: 9 -> 11; matrix products, arithmetic and copies ran while one was open for 1% -> 2% of each run, Pallas kernels for 10% -> 15%
where the time goes in v5:
time: 77.7 us; the launch traced here: 77.8 us
  Pallas kernels  35.4 us (46%)
  waiting for transfers between devices  22.5 us (29%)
  starting transfers between devices  16.3 us (21%)
  other arithmetic  1.96 us (3%)
  local copies, waits for them, and re-layouts  1.36 us (2%)
    ppermute x15, waiting for transfers between devices, swap(): return lax.ppermute(value, axis, [(i, i ^ mask) for i in range(size)])  16.4 us
    pallas_call x1, Pallas kernels, attention(): pl.pallas_call(functools.partial(attention_kernel, head_count), out_shape...  14.6 us
    ppermute x15, starting transfers between devices, swap(): return lax.ppermute(value, axis, [(i, i ^ mask) for i in range(size)])  12.7 us
    pallas_call x3, Pallas kernels, by_expert(): pl.pallas_call(functools.partial(relayout_kernel, js), out_shape=(pltpu.V...  8.97 us
    pallas_call x1, Pallas kernels, experts_part(): pl.pallas_call(experts_kernel, out_shape=(jax.ShapeDtypeStruct((tokens, t...  8.76 us
    ppermute x3, waiting for transfers between devices, per_device(): got = lax.ppermute(summed[k, :, j // 2], ('req', 'head'), pairs)  6.14 us
    ppermute x3, starting transfers between devices, per_device(): got = lax.ppermute(summed[k, :, j // 2], ('req', 'head'), pairs)  3.55 us
    pallas_call x1, Pallas kernels, down_part(): pl.pallas_call(functools.partial(down_kernel, head_count), out_shape=jax....  3.02 us
  transfers between devices with their start and end apart: 18, of which 11 were waited for; matrix products, arithmetic and copies ran while one was open for 2% of the time, Pallas kernels for 15%

profile of v5, /device:TPU:0, one launch (start us, length us, event | category | flops | bytes accessed | tf_op | source)
XLA Modules:
  0.0 77.8 jit_solution(10648747897774625992)
XLA Ops:
  0.0 2.4 %collective-permute-start.2 = (bf16[32,512]{1,0:T(8,128)(2,1)}, bf16[32,512]{1,0:T(8,128)(2,1)S(1)}, u32[]{:S(2)}, u32[]{:S(2)}) collective-permute-start(bf16[32,512]{1,0:T(8,128)(2,1)} %refs_0_.3), channel_id=1, source_target_pairs={{0,3},{1,2},{2,1},{3,0},{4,7},{5,6},{6,5},{7,4},{8,11},{9,10},{10,... | collective-permute-start | bytes 98312 | tf_op jit(solution)/shard_map/ppermute | solution.py:446
  2.4 0.7 collective-permute-start.1
  3.1 0.0 collective-permute-start
  3.1 0.7 convert_element_type.60
  3.8 0.1 fusion.3
  3.9 0.1 pad_maximum_fusion
  4.0 0.5 collective-permute-done.2.refs_3_
  4.5 0.0 collective-permute-done.1.refs_1_
  4.5 2.7 %collective-permute-done.refs_2_.refs_1_ = bf16[32,512]{1,0:T(8,128)(2,1)S(1)} collective-permute-done((bf16[32,512]{1,0:T(8,128)(2,1)}, bf16[32,512]{1,0:T(8,128)(2,1)S(1)}, u32[]{:S(2)}, u32[]{:S(2)}) %collective-permute-start) | collective-permute-done | bytes 32800 | tf_op jit(solution)/shard_map/ppermute | solution.py:446
  7.2 0.0 copy-start.1
  7.2 0.0 copy-start.2
  7.2 14.6 %attention.1 = (bf16[32,1024]{1,0:T(8,128)(2,1)S(1)}, bf16[32,1024]{1,0:T(8,128)(2,1)S(1)}) custom-call(s32[32]{0:T(128)} %lengths_ref.1, s32[1]{0:T(128)} %bitcast.me_ref, f32[32,128]{1,0:T(8,128)S(1)} %get-tuple-element.37.cos_ref, f32[32,128]{1,0:T(8,128)S(1)} %get-tuple-element.38.sin_ref, bf16[32,512]{1,0:T(8,128)(2,1)} %refs_0_.3, ...), custom_call_target="tpu_custom_call" | custom-call | flops 268435456 | bytes 20971520 | tf_op jit(solution)/shard_map/attention/pallas_call | solution.py:183
  21.8 0.0 copy-start
  21.9 0.1 collective-permute-start.3
  21.9 0.0 copy-done.1
  21.9 0.1 copy.19
  22.0 0.0 copy-done.2
  22.0 0.1 copy.20
  22.1 1.1 %collective-permute-done.3 = bf16[32,1024]{1,0:T(8,128)(2,1)S(1)} collective-permute-done((bf16[32,1024]{1,0:T(8,128)(2,1)S(1)}, bf16[32,1024]{1,0:T(8,128)(2,1)S(1)}, u32[]{:S(2)}, u32[]{:S(2)}) %collective-permute-start.3) | collective-permute-done | bytes 65568 | tf_op jit(solution)/shard_map/ppermute | solution.py:446
  23.2 0.4 collective-permute-start.4
  23.6 0.2 select_reduce_fusion
  23.8 2.5 %by_expert_0.1 = (bf16[16,4,512,256]{3,2,1,0:T(8,128)(2,1)S(1)}, f32[8,128]{1,0:T(8,128)S(1)}) custom-call(s32[1]{0:T(128)} %bitcast.me_ref, bf16[2048,16,256]{2,1,0:T(8,128)(2,1)} %w_ref.5, bf16[32,1024]{1,0:T(8,128)(2,1)S(1)} %add_convert_fusion.1.refs_0_.refs_2_), custom_call_target="tpu_custom_call" | custom-call | bytes 8388608 | tf_op jit(solution)/shard_map/by_expert_0/pallas_call | solution.py:251
  26.3 1.3 %collective-permute-done.4.refs_3_ = bf16[32,1024]{1,0:T(8,128)(2,1)S(1)} collective-permute-done((bf16[32,1024]{1,0:T(8,128)(2,1)S(1)}, bf16[32,1024]{1,0:T(8,128)(2,1)S(1)}, u32[]{:S(2)}, u32[]{:S(2)}) %collective-permute-start.4) | collective-permute-done | bytes 65568 | tf_op jit(solution)/shard_map/ppermute | solution.py:446
  27.5 0.0 copy-done
  27.6 0.1 collective-permute-start.7
  27.6 2.2 %collective-permute-start.6 = (bf16[32,1152]{1,0:T(8,128)(2,1)S(1)}, bf16[32,1152]{1,0:T(8,128)(2,1)S(1)}, u32[]{:S(2)}, u32[]{:S(2)}) collective-permute-start(bf16[32,1152]{1,0:T(8,128)(2,1)S(1)} %get-tuple-element.19.refs_1_.refs_0_), channel_id=1, source_target_pairs={{0,16},{4,20},{8,24},{12,28},{16,0},{20,4},{24,8},{28,12},{1,17},{... | collective-permute-start | bytes 221192 | tf_op jit(solution)/shard_map/ppermute | solution.py:446
  29.8 2.2 %collective-permute-start.5 = (bf16[32,1152]{1,0:T(8,128)(2,1)S(1)}, bf16[32,1152]{1,0:T(8,128)(2,1)S(1)}, u32[]{:S(2)}, u32[]{:S(2)}) collective-permute-start(bf16[32,1152]{1,0:T(8,128)(2,1)S(1)} %get-tuple-element.19.refs_1_.refs_0_), channel_id=1, source_target_pairs={{0,8},{4,12},{8,0},{12,4},{16,24},{20,28},{24,16},{28,20},{1,9},{5... | collective-permute-start | bytes 221192 | tf_op jit(solution)/shard_map/ppermute | solution.py:446
  32.0 3.7 %by_expert_1.1 = (bf16[16,4,512,256]{3,2,1,0:T(8,128)(2,1)S(1)}, f32[8,128]{1,0:T(8,128)S(1)}) custom-call(s32[1]{0:T(128)} %bitcast.me_ref, bf16[2048,16,256]{2,1,0:T(8,128)(2,1)} %w_ref.5, bf16[16,4,512,256]{3,2,1,0:T(8,128)(2,1)S(1)} %get-tuple-element.20.refs_0_, ...), custom_call_target="tpu_custom_call", output_to_operand_aliasing={{0}: (2, {})} | custom-call | bytes 16777216 | tf_op jit(solution)/shard_map/by_expert_1/pallas_call | solution.py:251
  35.7 0.0 collective-permute-done.7.refs_3_
  35.8 0.2 collective-permute-done.6.refs_2_
  35.9 0.0 collective-permute-done.5.refs_1_
  36.0 0.6 collective-permute-start.8
  36.5 0.0 collective-permute-start.9
  36.5 6.4 %collective-permute-done.8.mine_1 = bf16[128,1152]{1,0:T(8,128)(2,1)S(1)} collective-permute-done((bf16[128,1152]{1,0:T(8,128)(2,1)S(1)}, bf16[128,1152]{1,0:T(8,128)(2,1)S(1)}, u32[]{:S(2)}, u32[]{:S(2)}) %collective-permute-start.8) | collective-permute-done | bytes 294944 | tf_op jit(solution)/shard_map/ppermute | solution.py:446
  43.0 0.0 collective-permute-start.10
  43.0 2.8 %by_expert_3.1 = (bf16[16,4,512,256]{3,2,1,0:T(8,128)(2,1)S(1)}, f32[8,128]{1,0:T(8,128)}) custom-call(s32[1]{0:T(128)} %bitcast.me_ref, bf16[2048,16,256]{2,1,0:T(8,128)(2,1)} %w_ref.5, bf16[16,4,512,256]{3,2,1,0:T(8,128)(2,1)S(1)} %get-tuple-element.22.refs_0_, bf16[128,1152]{1,0:T(8,128)(2,1)S(1)} %stack.1.refs_1_.mine_0), custom_call_target="tpu_custom_call", output_to_operand_aliasing={{0}: (2, {})} | custom-call | bytes 8388608 | tf_op jit(solution)/shard_map/by_expert_3/pallas_call | solution.py:251
  45.8 0.0 collective-permute-done.9.other_0
  45.8 0.0 collective-permute-done.10.other_1
  45.8 8.8 %experts.1 = (bf16[256,2048]{1,0:T(8,128)(2,1)S(1)}, bf16[256,1024]{1,0:T(8,128)(2,1)S(1)}) custom-call(s32[1]{0:T(128)} %bitcast.me_ref, bf16[128,1152]{1,0:T(8,128)(2,1)S(1)} %stack.1.refs_1_.mine_0, bf16[128,1152]{1,0:T(8,128)(2,1)S(1)} %collective-permute-done.8.mine_1, bf16[128,1152]{1,0:T(8,128)(2,1)S(1)} %collective-permute-done.9.other_0, ...), custom_call_target="tpu_custom_call" | custom-call | flops 4294967296 | bytes 16777216 | tf_op jit(solution)/shard_map/experts/pallas_call | solution.py:386
  54.6 0.6 collective-permute-start.11
  55.1 3.0 %down.1 = bf16[256,1024]{1,0:T(8,128)(2,1)S(1)} custom-call(s32[1]{0:T(128)} %bitcast.me_ref, bf16[256,2048]{1,0:T(8,128)(2,1)S(1)} %get-tuple-element.24.units_ref, bf16[2048,2048]{1,0:T(8,128)(2,1)} %bitcast.19), custom_call_target="tpu_custom_call" | custom-call | flops 1073741824 | bytes 4194304 | tf_op jit(solution)/shard_map/down/pallas_call | solution.py:426
  58.2 0.0 collective-permute-done.11
  58.2 0.2 add_convert_fusion
  58.4 0.4 reshape.35
  58.8 0.7 fusion.4
  59.6 2.6 %collective-permute-start.14 = (bf16[128,512]{1,0:T(8,128)(2,1)S(1)}, bf16[128,512]{1,0:T(8,128)(2,1)S(1)}, u32[]{:S(2)}, u32[]{:S(2)}) collective-permute-start(bf16[128,512]{1,0:T(8,128)(2,1)S(1)} %bitcast.24), channel_id=1, source_target_pairs={{0,6},{1,7},{2,4},{3,5},{4,2},{5,3},{6,0},{7,1},{8,14},{9,15},{10,... | collective-permute-start | bytes 393224 | tf_op jit(solution)/shard_map/ppermute | solution.py:514
  62.1 0.9 %collective-permute-start.12 = (bf16[128,512]{1,0:T(8,128)(2,1)S(1)}, bf16[128,512]{1,0:T(8,128)(2,1)S(1)}, u32[]{:S(2)}, u32[]{:S(2)}) collective-permute-start(bf16[128,512]{1,0:T(8,128)(2,1)S(1)} %bitcast.23), channel_id=1, source_target_pairs={{0,4},{1,5},{2,6},{3,7},{4,0},{5,1},{6,2},{7,3},{8,12},{9,13},{10,... | collective-permute-start | bytes 393224 | tf_op jit(solution)/shard_map/ppermute | solution.py:514
  63.1 0.1 collective-permute-start.13
  63.1 3.8 %collective-permute-done.14 = bf16[128,512]{1,0:T(8,128)(2,1)S(1)} collective-permute-done((bf16[128,512]{1,0:T(8,128)(2,1)S(1)}, bf16[128,512]{1,0:T(8,128)(2,1)S(1)}, u32[]{:S(2)}, u32[]{:S(2)}) %collective-permute-start.14) | collective-permute-done | bytes 131104 | tf_op jit(solution)/shard_map/ppermute | solution.py:514
  66.9 2.4 %collective-permute-done.12 = bf16[128,512]{1,0:T(8,128)(2,1)S(1)} collective-permute-done((bf16[128,512]{1,0:T(8,128)(2,1)S(1)}, bf16[128,512]{1,0:T(8,128)(2,1)S(1)}, u32[]{:S(2)}, u32[]{:S(2)}) %collective-permute-start.12) | collective-permute-done | bytes 131104 | tf_op jit(solution)/shard_map/ppermute | solution.py:514
  69.3 0.0 collective-permute-done.13
  69.3 0.1 fusion.2
  69.4 0.1 collective-permute-start.15
  69.4 2.9 %collective-permute-start.17 = (bf16[32,512]{1,0:T(8,128)(2,1)S(1)}, bf16[32,512]{1,0:T(8,128)(2,1)S(1)}, u32[]{:S(2)}, u32[]{:S(2)}) collective-permute-start(bf16[32,512]{1,0:T(8,128)(2,1)S(1)} %get-tuple-element.32), channel_id=1, source_target_pairs={{0,24},{4,28},{8,16},{12,20},{16,8},{20,12},{24,0},{28,4},{1,25},{... | collective-permute-start | bytes 98312 | tf_op jit(solution)/shard_map/ppermute | solution.py:446
  72.3 0.6 collective-permute-start.16
  72.9 0.8 collective-permute-done.15
  73.7 1.9 %collective-permute-done.17 = bf16[32,512]{1,0:T(8,128)(2,1)S(1)} collective-permute-done((bf16[32,512]{1,0:T(8,128)(2,1)S(1)}, bf16[32,512]{1,0:T(8,128)(2,1)S(1)}, u32[]{:S(2)}, u32[]{:S(2)}) %collective-permute-start.17) | collective-permute-done | bytes 32800 | tf_op jit(solution)/shard_map/ppermute | solution.py:446
  75.6 1.5 %collective-permute-done.16 = bf16[32,512]{1,0:T(8,128)(2,1)S(1)} collective-permute-done((bf16[32,512]{1,0:T(8,128)(2,1)S(1)}, bf16[32,512]{1,0:T(8,128)(2,1)S(1)}, u32[]{:S(2)}, u32[]{:S(2)}) %collective-permute-start.16) | collective-permute-done | bytes 32800 | tf_op jit(solution)/shard_map/ppermute | solution.py:446
  77.1 0.6 add_convert_fusion.2
  (9 shorter events, 0.2 us)
Async XLA Ops:
  0.0 4.5 %collective-permute-start.2 = (bf16[32,512]{1,0:T(8,128)(2,1)}, bf16[32,512]{1,0:T(8,128)(2,1)S(1)}, u32[]{:S(2)}, u32[]{:S(2)}) collective-permute-start(bf16[32,512]{1,0:T(8,128)(2,1)} %refs_0_.3), channel_id=1, source_target_pairs={{0,3},{1,2},{2,1},{3,0},{4,7},{5,6},{6,5},{7,4},{8,11},{9,10},{10,... | collective-permute-start | bytes 98312 | tf_op jit(solution)/shard_map/ppermute | solution.py:446
  2.4 2.1 %collective-permute-start.1 = (bf16[32,512]{1,0:T(8,128)(2,1)}, bf16[32,512]{1,0:T(8,128)(2,1)S(1)}, u32[]{:S(2)}, u32[]{:S(2)}) collective-permute-start(bf16[32,512]{1,0:T(8,128)(2,1)} %refs_0_.3), channel_id=1, source_target_pairs={{0,1},{1,0},{2,3},{3,2},{4,5},{5,4},{6,7},{7,6},{8,9},{9,8},{10,11... | collective-permute-start | bytes 98312 | tf_op jit(solution)/shard_map/ppermute | solution.py:446
  3.1 4.1 %collective-permute-start = (bf16[32,512]{1,0:T(8,128)(2,1)}, bf16[32,512]{1,0:T(8,128)(2,1)S(1)}, u32[]{:S(2)}, u32[]{:S(2)}) collective-permute-start(bf16[32,512]{1,0:T(8,128)(2,1)} %refs_0_.3), channel_id=1, source_target_pairs={{0,2},{1,3},{2,0},{3,1},{4,6},{5,7},{6,4},{7,5},{8,10},{9,11},{10,... | collective-permute-start | bytes 98312 | tf_op jit(solution)/shard_map/ppermute | solution.py:446
  7.2 14.7 %copy-start.1 = (s32[32,8]{0,1:T(8,128)S(1)}, s32[32,8]{0,1:T(8,128)}, u32[]{:S(2)}) copy-start(s32[32,8]{0,1:T(8,128)} %param.12) | copy-start | bytes 3076
  7.2 14.8 %copy-start.2 = (f32[32,8]{0,1:T(8,128)S(1)}, f32[32,8]{0,1:T(8,128)}, u32[]{:S(2)}) copy-start(f32[32,8]{0,1:T(8,128)} %param.13) | copy-start | bytes 3076
  21.8 5.7 %copy-start = (bf16[32,512]{1,0:T(8,128)(2,1)S(1)}, bf16[32,512]{1,0:T(8,128)(2,1)}, u32[]{:S(2)}) copy-start(bf16[32,512]{1,0:T(8,128)(2,1)} %refs_0_.3) | copy-start | bytes 98308
  21.9 1.3 %collective-permute-start.3 = (bf16[32,1024]{1,0:T(8,128)(2,1)S(1)}, bf16[32,1024]{1,0:T(8,128)(2,1)S(1)}, u32[]{:S(2)}, u32[]{:S(2)}) collective-permute-start(bf16[32,1024]{1,0:T(8,128)(2,1)S(1)} %get-tuple-element.17), channel_id=1, source_target_pairs={{0,1},{1,0},{2,3},{3,2},{4,5},{5,4},{6,7},{7,6},{8,9},{9,8},{10,11... | collective-permute-start | bytes 196616 | tf_op jit(solution)/shard_map/ppermute | solution.py:446
  23.2 4.3 %collective-permute-start.4 = (bf16[32,1024]{1,0:T(8,128)(2,1)S(1)}, bf16[32,1024]{1,0:T(8,128)(2,1)S(1)}, u32[]{:S(2)}, u32[]{:S(2)}) collective-permute-start(bf16[32,1024]{1,0:T(8,128)(2,1)S(1)} %add_convert_fusion.1.refs_0_.refs_2_), channel_id=1, source_target_pairs={{0,2},{1,3},{2,0},{3,1},{4,6},{5,7},{6,4},{7,5},{8,10},{9,11},{10,... | collective-permute-start | bytes 196616 | tf_op jit(solution)/shard_map/ppermute | solution.py:446
  27.6 8.2 %collective-permute-start.7 = (bf16[32,1152]{1,0:T(8,128)(2,1)S(1)}, bf16[32,1152]{1,0:T(8,128)(2,1)S(1)}, u32[]{:S(2)}, u32[]{:S(2)}) collective-permute-start(bf16[32,1152]{1,0:T(8,128)(2,1)S(1)} %get-tuple-element.19.refs_1_.refs_0_), channel_id=1, source_target_pairs={{0,24},{4,28},{8,16},{12,20},{16,8},{20,12},{24,0},{28,4},{1,25},{... | collective-permute-start | bytes 221192 | tf_op jit(solution)/shard_map/ppermute | solution.py:446
  27.6 8.3 %collective-permute-start.6 = (bf16[32,1152]{1,0:T(8,128)(2,1)S(1)}, bf16[32,1152]{1,0:T(8,128)(2,1)S(1)}, u32[]{:S(2)}, u32[]{:S(2)}) collective-permute-start(bf16[32,1152]{1,0:T(8,128)(2,1)S(1)} %get-tuple-element.19.refs_1_.refs_0_), channel_id=1, source_target_pairs={{0,16},{4,20},{8,24},{12,28},{16,0},{20,4},{24,8},{28,12},{1,17},{... | collective-permute-start | bytes 221192 | tf_op jit(solution)/shard_map/ppermute | solution.py:446
  29.8 6.1 %collective-permute-start.5 = (bf16[32,1152]{1,0:T(8,128)(2,1)S(1)}, bf16[32,1152]{1,0:T(8,128)(2,1)S(1)}, u32[]{:S(2)}, u32[]{:S(2)}) collective-permute-start(bf16[32,1152]{1,0:T(8,128)(2,1)S(1)} %get-tuple-element.19.refs_1_.refs_0_), channel_id=1, source_target_pairs={{0,8},{4,12},{8,0},{12,4},{16,24},{20,28},{24,16},{28,20},{1,9},{5... | collective-permute-start | bytes 221192 | tf_op jit(solution)/shard_map/ppermute | solution.py:446
  36.0 7.0 %collective-permute-start.8 = (bf16[128,1152]{1,0:T(8,128)(2,1)S(1)}, bf16[128,1152]{1,0:T(8,128)(2,1)S(1)}, u32[]{:S(2)}, u32[]{:S(2)}) collective-permute-start(bf16[128,1152]{1,0:T(8,128)(2,1)S(1)} %stack.1.refs_1_.mine_0), channel_id=1, source_target_pairs={{0,4},{4,0},{8,12},{12,8},{16,20},{20,16},{24,28},{28,24},{1,5},{5... | collective-permute-start | bytes 884744 | tf_op jit(solution)/shard_map/ppermute | solution.py:446
  36.5 9.2 %collective-permute-start.9 = (bf16[128,1152]{1,0:T(8,128)(2,1)S(1)}, bf16[128,1152]{1,0:T(8,128)(2,1)S(1)}, u32[]{:S(2)}, u32[]{:S(2)}) collective-permute-start(bf16[128,1152]{1,0:T(8,128)(2,1)S(1)} %stack.1.refs_1_.mine_0), channel_id=1, source_target_pairs={{0,1},{1,0},{2,3},{3,2},{4,5},{5,4},{6,7},{7,6},{8,9},{9,8},{10,11... | collective-permute-start | bytes 884744 | tf_op jit(solution)/shard_map/ppermute | solution.py:446
  43.0 2.8 %collective-permute-start.10 = (bf16[128,1152]{1,0:T(8,128)(2,1)S(1)}, bf16[128,1152]{1,0:T(8,128)(2,1)S(1)}, u32[]{:S(2)}, u32[]{:S(2)}) collective-permute-start(bf16[128,1152]{1,0:T(8,128)(2,1)S(1)} %collective-permute-done.8.mine_1), channel_id=1, source_target_pairs={{0,1},{1,0},{2,3},{3,2},{4,5},{5,4},{6,7},{7,6},{8,9},{9,8},{10,11... | collective-permute-start | bytes 884744 | tf_op jit(solution)/shard_map/ppermute | solution.py:446
  54.6 3.6 %collective-permute-start.11 = (bf16[256,1024]{1,0:T(8,128)(2,1)S(1)}, bf16[256,1024]{1,0:T(8,128)(2,1)S(1)}, u32[]{:S(2)}, u32[]{:S(2)}) collective-permute-start(bf16[256,1024]{1,0:T(8,128)(2,1)S(1)} %get-tuple-element.25), channel_id=1, source_target_pairs={{0,1},{1,0},{2,3},{3,2},{4,5},{5,4},{6,7},{7,6},{8,9},{9,8},{10,11... | collective-permute-start | bytes 1572872 | tf_op jit(solution)/shard_map/ppermute | solution.py:446
  59.6 7.3 %collective-permute-start.14 = (bf16[128,512]{1,0:T(8,128)(2,1)S(1)}, bf16[128,512]{1,0:T(8,128)(2,1)S(1)}, u32[]{:S(2)}, u32[]{:S(2)}) collective-permute-start(bf16[128,512]{1,0:T(8,128)(2,1)S(1)} %bitcast.24), channel_id=1, source_target_pairs={{0,6},{1,7},{2,4},{3,5},{4,2},{5,3},{6,0},{7,1},{8,14},{9,15},{10,... | collective-permute-start | bytes 393224 | tf_op jit(solution)/shard_map/ppermute | solution.py:514
  62.1 7.1 %collective-permute-start.12 = (bf16[128,512]{1,0:T(8,128)(2,1)S(1)}, bf16[128,512]{1,0:T(8,128)(2,1)S(1)}, u32[]{:S(2)}, u32[]{:S(2)}) collective-permute-start(bf16[128,512]{1,0:T(8,128)(2,1)S(1)} %bitcast.23), channel_id=1, source_target_pairs={{0,4},{1,5},{2,6},{3,7},{4,0},{5,1},{6,2},{7,3},{8,12},{9,13},{10,... | collective-permute-start | bytes 393224 | tf_op jit(solution)/shard_map/ppermute | solution.py:514
  63.1 6.2 %collective-permute-start.13 = (bf16[128,512]{1,0:T(8,128)(2,1)S(1)}, bf16[128,512]{1,0:T(8,128)(2,1)S(1)}, u32[]{:S(2)}, u32[]{:S(2)}) collective-permute-start(bf16[128,512]{1,0:T(8,128)(2,1)S(1)} %bitcast.22), channel_id=1, source_target_pairs={{0,2},{1,3},{2,0},{3,1},{4,6},{5,7},{6,4},{7,5},{8,10},{9,11},{10,... | collective-permute-start | bytes 393224 | tf_op jit(solution)/shard_map/ppermute | solution.py:514
  69.4 4.3 %collective-permute-start.15 = (bf16[32,512]{1,0:T(8,128)(2,1)S(1)}, bf16[32,512]{1,0:T(8,128)(2,1)S(1)}, u32[]{:S(2)}, u32[]{:S(2)}) collective-permute-start(bf16[32,512]{1,0:T(8,128)(2,1)S(1)} %get-tuple-element.31), channel_id=1, source_target_pairs={{0,8},{4,12},{8,0},{12,4},{16,24},{20,28},{24,16},{28,20},{1,9},{5... | collective-permute-start | bytes 98312 | tf_op jit(solution)/shard_map/ppermute | solution.py:446
  69.4 6.2 %collective-permute-start.17 = (bf16[32,512]{1,0:T(8,128)(2,1)S(1)}, bf16[32,512]{1,0:T(8,128)(2,1)S(1)}, u32[]{:S(2)}, u32[]{:S(2)}) collective-permute-start(bf16[32,512]{1,0:T(8,128)(2,1)S(1)} %get-tuple-element.32), channel_id=1, source_target_pairs={{0,24},{4,28},{8,16},{12,20},{16,8},{20,12},{24,0},{28,4},{1,25},{... | collective-permute-start | bytes 98312 | tf_op jit(solution)/shard_map/ppermute | solution.py:446
  72.3 4.8 %collective-permute-start.16 = (bf16[32,512]{1,0:T(8,128)(2,1)S(1)}, bf16[32,512]{1,0:T(8,128)(2,1)S(1)}, u32[]{:S(2)}, u32[]{:S(2)}) collective-permute-start(bf16[32,512]{1,0:T(8,128)(2,1)S(1)} %get-tuple-element.33), channel_id=1, source_target_pairs={{0,16},{4,20},{8,24},{12,28},{16,0},{20,4},{24,8},{28,12},{1,17},{... | collective-permute-start | bytes 98312 | tf_op jit(solution)/shard_map/ppermute | solution.py:446

commit v6 on v5

v6 whole, which is shorter than its diff:
```python
import functools
import jax
import jax.numpy as jnp
from jax import lax
from jax.experimental import pallas as pl
from jax.experimental.pallas import tpu as pltpu
from jax.sharding import PartitionSpec as P

rope_theta = 50000.0
norm_eps = 1e-05
LANES = 128
SUBLANES = 8
CHUNK = 128
GROUP = 8
MASKED = -1e30


VMEM = pl.BlockSpec(memory_space=pltpu.VMEM)
SMEM = pl.BlockSpec(memory_space=pltpu.SMEM)
ANY = pl.BlockSpec(memory_space=pl.ANY)


def in_hbm(array):
    return pltpu.with_memory_space_constraint(array, pltpu.HBM)


def in_vmem(array):
    return pltpu.with_memory_space_constraint(array, pltpu.VMEM)


def used_rows(length, heads_local):
    return pl.multiple_of((length + 7) // 8 * (8 * heads_local), 8 * heads_local)


def fetch_kernel(lengths_ref, me_ref, own_ref, w_ref, own_out_ref, w_out_ref, blank_ref, sem, own_sem):
    head_count, cols = w_out_ref.shape[1:3]
    chunk_rows = CHUNK * cols // LANES
    me = me_ref[0]
    copies = [pltpu.make_async_copy(own_ref, own_out_ref, own_sem)]
    for c in range(w_ref.shape[0]):
        for j in range(head_count):
            first = pl.multiple_of((me ^ j) * cols, cols)
            copies.append(
                pltpu.make_async_copy(
                    w_ref.at[c, pl.ds(first, cols)], w_out_ref.at[c, j], sem.at[c, j]
                )
            )
    for copy in copies:
        copy.start()

    @pl.loop(0, blank_ref.shape[0])
    def _(r):
        last = pl.multiple_of((lengths_ref[r] - 1) // CHUNK * chunk_rows, chunk_rows)
        blank_ref[r, pl.ds(last, chunk_rows)] = jnp.zeros((chunk_rows, LANES), jnp.bfloat16)

    for copy in copies:
        copy.wait()


def fetch(me, lengths, hidden, w_qkv, v_shape, head_count):
    cols = w_qkv.shape[2]
    return pl.pallas_call(
        fetch_kernel,
        out_shape=(
            pltpu.VMEM(hidden.shape, jnp.bfloat16),
            pltpu.VMEM((w_qkv.shape[0], head_count, cols, cols), jnp.bfloat16),
            pltpu.VMEM(v_shape, jnp.bfloat16),
        ),
        in_specs=[SMEM, SMEM, ANY, ANY],
        out_specs=(VMEM, VMEM, VMEM),
        scratch_shapes=[
            pltpu.SemaphoreType.DMA((w_qkv.shape[0], head_count)),
            pltpu.SemaphoreType.DMA(()),
        ],
        compiler_params=pltpu.CompilerParams(vmem_limit_bytes=8 * 2**20),
        cost_estimate=pl.CostEstimate(
            flops=0, bytes_accessed=4 * w_qkv.size, transcendentals=0
        ),
        name="fetch",
    )(in_hbm(lengths), me, in_hbm(hidden), in_hbm(w_qkv))


def attention_kernel(head_count, lengths_ref, me_ref, cos_ref, sin_ref, *refs):
    pieces = refs[:head_count]
    (
        w_qkv_ref, _, w_out_ref, k_ref, v_ref, keep_ref, send_ref, v_s,
        w_out_s, k_s, query_s, key_s, value_s, attended_s, out_sem, k_sem, v_sem,
    ) = refs[head_count:]
    rows, cols = pieces[0].shape
    heads_local = cols // LANES
    chunk_rows = CHUNK * heads_local
    me = me_ref[0]

    def out_copy(j):
        first = pl.multiple_of((me ^ j) * cols, cols)
        return pltpu.make_async_copy(
            w_out_ref.at[:, pl.ds(first, cols)], w_out_s.at[j], out_sem.at[j]
        )

    def cache_copy(source, target, sem, r):
        used = used_rows(lengths_ref[r], heads_local)
        return pltpu.make_async_copy(
            source.at[r, pl.ds(0, used)], target.at[r, pl.ds(0, used)], sem.at[r]
        )

    @pl.loop(0, rows, unroll=4)
    def _(r):
        cache_copy(k_ref, k_s, k_sem, r).start()
        cache_copy(v_ref, v_s, v_sem, r).start()

    for j in range(head_count):
        out_copy(j).start()

    if heads_local < SUBLANES:
        query_s[...] = jnp.zeros_like(query_s)
        key_s[...] = jnp.zeros_like(key_s)
        value_s[...] = jnp.zeros_like(value_s)
    states = jnp.concatenate([piece[...] for piece in pieces], axis=1)
    square = jnp.sum(jnp.square(states.astype(jnp.float32)), axis=1, keepdims=True)
    scale = lax.rsqrt(square / (cols * head_count) + norm_eps)
    cosine, sine = cos_ref[...], sin_ref[...]
    for c, target in enumerate((query_s, key_s, value_s)):
        projected = scale * jnp.dot(
            states,
            w_qkv_ref[c].reshape(head_count * cols, cols),
            preferred_element_type=jnp.float32,
        )
        for h in range(heads_local):
            part = projected[:, h * LANES : (h + 1) * LANES]
            if c < 2:
                part = part * cosine + pltpu.roll(part, LANES // 2, 1) * sine
            target[:, h, :] = part.astype(jnp.bfloat16).astype(jnp.float32)

    column = lax.broadcasted_iota(jnp.int32, (2 * SUBLANES, chunk_rows), 1)
    row = lax.broadcasted_iota(jnp.int32, (2 * SUBLANES, chunk_rows), 0)
    same_head = column % heads_local == row % SUBLANES
    upper = row < SUBLANES
    score_scale = LANES**-0.5
    blank = jnp.zeros((SUBLANES, LANES), jnp.float32)

    def diagonal(a, b):
        return jnp.concatenate(
            [jnp.concatenate([a, blank], axis=1), jnp.concatenate([blank, b], axis=1)], axis=0
        )

    @pl.loop(0, rows // GROUP)
    def _(g):
        requests = [g * GROUP + i for i in range(GROUP)]
        pairs = list(zip(requests[::2], requests[1::2]))
        lengths = [lengths_ref[r] for r in requests]
        spans = list(zip(lengths[::2], lengths[1::2]))
        queries = [diagonal(query_s[a], query_s[b]).astype(jnp.bfloat16) for a, b in pairs]
        own = [
            jnp.sum(query_s[r] * key_s[r], axis=1, keepdims=True) * score_scale for r in requests
        ]
        own = [jnp.concatenate([a, b], axis=0) for a, b in zip(own[::2], own[1::2])]
        values = [diagonal(value_s[a], value_s[b]) for a, b in pairs]
        longest = functools.reduce(jnp.maximum, lengths)
        for r in requests:
            cache_copy(k_ref, k_s, k_sem, r).wait()
            cache_copy(v_ref, v_s, v_sem, r).wait()

        def with_chunks(count):
            def both(ref, c, pair, span):
                parts = []
                for r, length in zip(pair, span):
                    first = jnp.minimum(c, (length - 1) // CHUNK) * chunk_rows if c else 0
                    parts.append(ref[r, pl.ds(pl.multiple_of(first, chunk_rows), chunk_rows)])
                return jnp.concatenate(parts, axis=1)

            scores = [
                [
                    lax.dot_general(
                        query,
                        both(k_s, c, pair, span),
                        (((1,), (1,)), ((), ())),
                        preferred_element_type=jnp.float32,
                    )
                    for c in range(count)
                ]
                for query, pair, span in zip(queries, pairs, spans)
            ]
            limits = [
                jnp.where(upper, span[0] * heads_local, span[1] * heads_local) for span in spans
            ]
            scores = [
                [
                    jnp.where(
                        same_head & (column < limit - c * chunk_rows), score * score_scale, MASKED
                    )
                    for c, score in enumerate(parts)
                ]
                for limit, parts in zip(limits, scores)
            ]
            tops = [
                jnp.maximum(
                    mine, jnp.max(functools.reduce(jnp.maximum, parts), axis=1, keepdims=True)
                )
                for mine, parts in zip(own, scores)
            ]
            weights = [[jnp.exp(part - top) for part in parts] for top, parts in zip(tops, scores)]
            faded = [jnp.exp(mine - top) for mine, top in zip(own, tops)]
            totals = [
                fade + jnp.sum(functools.reduce(jnp.add, parts), axis=1, keepdims=True)
                for fade, parts in zip(faded, weights)
            ]
            sums = [
                fade * value
                + sum(
                    jnp.dot(
                        part.astype(jnp.bfloat16),
                        both(v_s, c, pair, span),
                        preferred_element_type=jnp.float32,
                    )
                    for c, part in enumerate(parts)
                )
                for pair, span, fade, value, parts in zip(pairs, spans, faded, values, weights)
            ]
            for (a, b), total, summed in zip(pairs, totals, sums):
                summed = summed / total
                attended_s[a] = summed[:SUBLANES, :LANES]
                attended_s[b] = summed[SUBLANES:, LANES:]

        for count in range(1, k_s.shape[1] // chunk_rows + 1):
            pl.when((longest + CHUNK - 1) // CHUNK == count)(
                functools.partial(with_chunks, count)
            )

    attended = jnp.concatenate(
        [attended_s[:, h, :] for h in range(heads_local)], axis=1
    ).astype(jnp.bfloat16)
    for j in range(head_count):
        out_copy(j).wait()
        target = send_ref if j % 2 else keep_ref
        target[:, j // 2 * cols : (j // 2 + 1) * cols] = jnp.dot(
            attended, w_out_s[j], preferred_element_type=jnp.float32
        ).astype(jnp.bfloat16)


def attention(pieces, me, lengths, cosine, sine, w_qkv, room, w_out, k_cache, v_cache):
    head_count = len(pieces)
    rows, cols = pieces[0].shape
    half = jax.ShapeDtypeStruct((rows, head_count // 2 * cols), jnp.bfloat16)
    return pl.pallas_call(
        functools.partial(attention_kernel, head_count),
        out_shape=(half, half, pltpu.VMEM(room.shape, jnp.bfloat16)),
        in_specs=[SMEM, SMEM] + [VMEM] * (head_count + 4) + [ANY] * 3,
        out_specs=(VMEM, VMEM, VMEM),
        input_output_aliases={head_count + 5: 2},
        scratch_shapes=[
            pltpu.VMEM((head_count, cols, cols), jnp.bfloat16),
            pltpu.VMEM(k_cache.shape, jnp.bfloat16),
        ]
        + [pltpu.VMEM((rows, SUBLANES, LANES), jnp.float32)] * 4
        + [
            pltpu.SemaphoreType.DMA((head_count,)),
            pltpu.SemaphoreType.DMA((rows,)),
            pltpu.SemaphoreType.DMA((rows,)),
        ],
        compiler_params=pltpu.CompilerParams(vmem_limit_bytes=20 * 2**20),
        cost_estimate=pl.CostEstimate(
            flops=2 * rows * 4 * cols * head_count * cols,
            bytes_accessed=2 * cols * cols * head_count + k_cache.size // 2,
            transcendentals=0,
        ),
        name="attention",
    )(
        in_hbm(lengths), me, cosine, sine, *map(in_vmem, pieces), in_vmem(w_qkv), in_vmem(room),
        in_hbm(w_out), in_hbm(k_cache), in_hbm(v_cache),
    )[:2]


RELAYOUT_ROWS = 128
RELAYOUT_STEP = 16

def relayout_kernel(js, me_ref, w_ref, *refs):
    out_ref, token_ref, in_s, in_sem = refs[-4:]
    token_ref[...] = jnp.zeros_like(token_ref)
    experts, _, cols, _ = out_ref.shape
    step = in_s.shape[1]
    per_block = cols // step
    copies = []
    for at, j in enumerate(js):
        base = (me_ref[0] ^ j) * cols
        for i in range(per_block):
            slot = at * per_block + i
            first = pl.multiple_of(base + i * step, step)
            copies.append(
                pltpu.make_async_copy(
                    w_ref.at[pl.ds(first, step)], in_s.at[slot], in_sem.at[slot]
                )
            )
    for copy in copies:
        copy.start()
    for slot, copy in enumerate(copies):
        j, i = js[slot // per_block], slot % per_block
        copy.wait()
        for s in range(step // RELAYOUT_STEP):
            part = in_s[slot, pl.ds(s * RELAYOUT_STEP, RELAYOUT_STEP)]
            out_ref[:, j, pl.ds(i * step + s * RELAYOUT_STEP, RELAYOUT_STEP), :] = jnp.swapaxes(
                part, 0, 1
            )


def by_expert(js, me, w_in, head_count, buffer, after):
    width, experts, columns = w_in.shape
    cols = width // head_count
    step = min(RELAYOUT_ROWS, cols)
    slots = len(js) * cols // step
    held = [] if buffer is None else [in_vmem(buffer)]
    return pl.pallas_call(
        functools.partial(relayout_kernel, js),
        out_shape=(
            pltpu.VMEM((experts, head_count, cols, columns), jnp.bfloat16),
            jax.ShapeDtypeStruct((SUBLANES, LANES), jnp.float32),
        ),
        in_specs=[SMEM, ANY] + [VMEM] * len(held) + [ANY],
        out_specs=(VMEM, VMEM),
        input_output_aliases={2: 0} if held else {},
        scratch_shapes=[
            pltpu.VMEM((slots, step, experts, columns), jnp.bfloat16),
            pltpu.SemaphoreType.DMA((slots,)),
        ],
        compiler_params=pltpu.CompilerParams(vmem_limit_bytes=16 * 2**20),
        cost_estimate=pl.CostEstimate(
            flops=0, bytes_accessed=4 * len(js) * cols * experts * columns, transcendentals=0
        ),
        name=f"by_expert_{js[0]}",
    )(me, in_hbm(w_in), *held, after)


def payload_kernel(head_count, *refs):
    blocks = head_count // 2
    pieces, (half_ref, *others), shares_ref = refs[:blocks], refs[blocks : 2 * blocks], refs[2 * blocks]
    payload_ref, resid_ref = refs[-2:]
    cols = pieces[0].shape[1]
    for t in range(blocks):
        total = pieces[t][...].astype(jnp.float32)
        for at, source in enumerate((half_ref, *others)):
            place = (t ^ at) * cols
            total += source[:, place : place + cols].astype(jnp.float32)
        payload_ref[:, t * cols : (t + 1) * cols] = total.astype(jnp.bfloat16)
        if t == 0:
            resid_ref[...] = total
    payload_ref[:, blocks * cols :] = shares_ref[...]


def payload_part(pieces, half, others, shares, after):
    blocks = len(pieces)
    rows, cols = pieces[0].shape
    return pl.pallas_call(
        functools.partial(payload_kernel, 2 * blocks),
        out_shape=(
            jax.ShapeDtypeStruct((rows, blocks * cols + shares.shape[1]), jnp.bfloat16),
            jax.ShapeDtypeStruct((rows, cols), jnp.float32),
        ),
        in_specs=[VMEM] * (2 * blocks + 1) + [ANY],
        out_specs=(VMEM, VMEM),
        compiler_params=pltpu.CompilerParams(vmem_limit_bytes=8 * 2**20),
        name="payload",
    )(*pieces, half, *others, shares, after)


def stack_kernel(count, *refs):
    rows = refs[0].shape[0]
    for i in range(count):
        refs[-1][i * rows : (i + 1) * rows, :] = refs[i][...]


def stack_part(parts, after):
    rows, columns = parts[0].shape
    return pl.pallas_call(
        functools.partial(stack_kernel, len(parts)),
        out_shape=jax.ShapeDtypeStruct((len(parts) * rows, columns), jnp.bfloat16),
        in_specs=[VMEM] * len(parts) + [ANY],
        out_specs=VMEM,
        compiler_params=pltpu.CompilerParams(vmem_limit_bytes=8 * 2**20),
        name="stack",
    )(*parts, after)


def fetch_down_kernel(me_ref, w_ref, _, out_ref, token_ref, sem):
    token_ref[...] = jnp.zeros_like(token_ref)
    head_count, _, cols = out_ref.shape
    copies = []
    for j in range(head_count):
        first = pl.multiple_of((me_ref[0] ^ j) * cols, cols)
        copies.append(
            pltpu.make_async_copy(w_ref.at[:, pl.ds(first, cols)], out_ref.at[j], sem.at[j])
        )
        copies[-1].start()
    for copy in copies:
        copy.wait()


def fetch_down(me, w_down, head_count, after):
    total_units, width = w_down.shape
    return pl.pallas_call(
        fetch_down_kernel,
        out_shape=(
            pltpu.VMEM((head_count, total_units, width // head_count), jnp.bfloat16),
            jax.ShapeDtypeStruct((SUBLANES, LANES), jnp.float32),
        ),
        in_specs=[SMEM, ANY, ANY],
        out_specs=(VMEM, VMEM),
        scratch_shapes=[pltpu.SemaphoreType.DMA((head_count,))],
        compiler_params=pltpu.CompilerParams(vmem_limit_bytes=8 * 2**20),
        cost_estimate=pl.CostEstimate(
            flops=0, bytes_accessed=4 * w_down.size, transcendentals=0
        ),
        name="fetch_down",
    )(me, in_hbm(w_down), after)


def down_blocks(units, w_ref, first, out_ref):
    cols = w_ref.shape[2]
    for t in range(w_ref.shape[0] // 2):
        out_ref[:, t * cols : (t + 1) * cols] = jnp.dot(
            units, w_ref[2 * t + first], preferred_element_type=jnp.float32
        ).astype(jnp.bfloat16)


def experts_kernel(me_ref, mine_ref, other_ref, w_ref, w_down_ref, _, units_ref, send_ref, states_s):
    me = me_ref[0]
    experts, head_count, cols, columns = w_ref.shape
    blocks = head_count // 2
    tokens = states_s.shape[0]
    square = 0.0
    for j in range(head_count):
        part = (mine_ref, other_ref)[j % 2][:, j // 2 * cols : (j // 2 + 1) * cols]
        states_s[:, j * cols : (j + 1) * cols] = part
        square += jnp.sum(jnp.square(part.astype(jnp.float32)), axis=1, keepdims=True)
    scale = lax.rsqrt(square / (head_count * cols) + norm_eps)
    shares = mine_ref[:, blocks * cols :]
    per_step = max(1, 2 * LANES // columns)
    first_half = lax.broadcasted_iota(jnp.int32, (tokens, LANES), 1) < LANES // 2
    source = lax.broadcasted_iota(jnp.int32, (LANES, LANES), 0)
    lane = lax.broadcasted_iota(jnp.int32, (LANES, LANES), 1)

    @pl.loop(0, experts // per_step, unroll=4)
    def _(p):
        states = states_s[...]
        products = [
            jnp.dot(
                states,
                w_ref[p * per_step + i].reshape(head_count * cols, columns),
                preferred_element_type=jnp.float32,
            )
            for i in range(per_step)
        ]
        product = products[0] if per_step == 1 else jnp.concatenate(products, axis=1)
        expert = me * experts + p * per_step + lane * per_step // LANES
        share = jnp.dot(
            shares, (source == expert).astype(jnp.bfloat16), preferred_element_type=jnp.float32
        )
        a, b = product[:, :LANES], product[:, LANES:]
        gate = jnp.where(first_half, a, pltpu.roll(b, LANES // 2, 1)) * scale
        upward = jnp.where(first_half, pltpu.roll(a, LANES // 2, 1), b) * scale
        units = share * (gate / (1.0 + jnp.exp(-gate)) * upward)
        units_ref[:, pl.ds(pl.multiple_of(p * LANES, LANES), LANES)] = units.astype(jnp.bfloat16)

    down_blocks(units_ref[...], w_down_ref, 1, send_ref)


def experts_part(me, mine, other, weights, w_down, after):
    experts, head_count, cols, columns = weights.shape
    tokens = mine.shape[0]
    total_units = w_down.shape[1]
    return pl.pallas_call(
        experts_kernel,
        out_shape=(
            jax.ShapeDtypeStruct((tokens, total_units), jnp.bfloat16),
            jax.ShapeDtypeStruct((tokens, head_count // 2 * cols), jnp.bfloat16),
        ),
        in_specs=[SMEM] + [VMEM] * 4 + [ANY],
        out_specs=(VMEM, VMEM),
        scratch_shapes=[pltpu.VMEM((tokens, head_count * cols), jnp.bfloat16)],
        compiler_params=pltpu.CompilerParams(vmem_limit_bytes=16 * 2**20),
        cost_estimate=pl.CostEstimate(
            flops=2 * tokens * head_count * cols * experts * columns,
            bytes_accessed=2 * head_count * cols * experts * columns,
            transcendentals=0,
        ),
        name="experts",
    )(me, mine, other, in_vmem(weights), in_vmem(w_down), after)


def down_kernel(units_ref, w_ref, keep_ref):
    down_blocks(units_ref[...], w_ref, 0, keep_ref)


def down_part(units, w_down):
    head_count, total_units, cols = w_down.shape
    tokens = units.shape[0]
    return pl.pallas_call(
        down_kernel,
        out_shape=jax.ShapeDtypeStruct((tokens, head_count // 2 * cols), jnp.bfloat16),
        in_specs=[VMEM, VMEM],
        out_specs=VMEM,
        compiler_params=pltpu.CompilerParams(vmem_limit_bytes=16 * 2**20),
        cost_estimate=pl.CostEstimate(
            flops=2 * tokens * total_units * head_count // 2 * cols,
            bytes_accessed=2 * total_units * head_count // 2 * cols,
            transcendentals=0,
        ),
        name="down",
    )(units, in_vmem(w_down))


def hold_kernel(value_ref, after_ref, out_ref):
    pass


def hold(value, after):
    return pl.pallas_call(
        hold_kernel,
        out_shape=jax.ShapeDtypeStruct(value.shape, value.dtype),
        in_specs=[ANY, ANY],
        out_specs=ANY,
        input_output_aliases={0: 0},
        compiler_params=pltpu.CompilerParams(vmem_limit_bytes=2**20),
        name="hold",
    )(value, after)


def sum_kernel(keep_ref, sent_ref, *outs):
    cols = outs[0].shape[1]
    for t, out in enumerate(outs):
        part = slice(t * cols, (t + 1) * cols)
        total = keep_ref[:, part].astype(jnp.float32) + sent_ref[:, part].astype(jnp.float32)
        out[...] = total.astype(out.dtype)


def sum_part(keep, sent, cols, first_type):
    tokens, columns = keep.shape
    blocks = columns // cols
    return pl.pallas_call(
        sum_kernel,
        out_shape=[
            jax.ShapeDtypeStruct((tokens, cols), jnp.bfloat16 if t else first_type)
            for t in range(blocks)
        ],
        in_specs=[VMEM, VMEM],
        out_specs=[VMEM] * blocks,
        compiler_params=pltpu.CompilerParams(vmem_limit_bytes=8 * 2**20),
        name="sum",
    )(keep, sent)


def swap(value, axis, size, mask):
    return lax.ppermute(value, axis, [(i, i ^ mask) for i in range(size)])


def per_device(
    hidden, lengths, expert_ids, route_weights, w_qkv, w_out, k_cache, v_cache, w_in, w_down
):
    req_size = lax.axis_size("req")
    head_size = lax.axis_size("head")
    me = lax.axis_index("head")
    me_ref = me[None].astype(jnp.int32)
    rows, cols = hidden.shape
    experts_local, units_local, width = w_down.shape
    even = range(0, head_size, 2)

    pieces = [hidden] + [swap(hidden, "head", head_size, j) for j in range(1, head_size)]
    half_dim = k_cache.shape[3] // 2
    freqs = rope_theta ** (-jnp.arange(half_dim, dtype=jnp.float32) / half_dim)
    angles = lengths.astype(jnp.float32)[:, None] * freqs[None, :]
    cosine, sine = jnp.cos(angles), jnp.sin(angles)
    flat = (rows, k_cache.shape[1] * k_cache.shape[2], k_cache.shape[3])
    own, w_near, room = fetch(me_ref, lengths, hidden, w_qkv, flat, head_size)
    keep, send = attention(
        [own] + pieces[1:],
        me_ref,
        lengths,
        jnp.concatenate([cosine, cosine], axis=1),
        jnp.concatenate([-sine, sine], axis=1),
        w_near,
        room,
        w_out,
        k_cache.reshape(flat),
        v_cache.reshape(flat),
    )
    half = keep.astype(jnp.float32) + swap(send, "head", head_size, 1).astype(jnp.float32)
    half = half.astype(jnp.bfloat16)
    others = [swap(half, "head", head_size, j) for j in even if j]
    early, late = range(head_size // 2), range(head_size // 2, head_size)
    buffer, token = by_expert(tuple(early), me_ref, w_in, head_size, None, half)

    every = jnp.arange(head_size * experts_local, dtype=jnp.int32)
    matches = (expert_ids[:, :, None] == every[None, None, :]).astype(jnp.float32)
    shares = jnp.sum(route_weights[:, :, None] * matches, axis=1).astype(jnp.bfloat16)
    shares = jnp.pad(shares, ((0, 0), (0, -shares.shape[1] % LANES)))
    payload, resid = payload_part([pieces[j] for j in even], half, others, shares, token)

    steps = range(2, req_size, 2)
    line = [payload] + [swap(payload, "req", req_size, k) for k in steps]
    w_down_flat = w_down.reshape(experts_local * units_local, width)
    buffer, token = by_expert(tuple(late), me_ref, w_in, head_size, buffer, payload)
    w_down_near, token = fetch_down(me_ref, w_down_flat, head_size, token)
    line = stack_part(line, token)
    crossed = swap(line, "req", req_size, 1)
    line_other = swap(line, "head", head_size, 1)
    units, send = experts_part(me_ref, line, line_other, buffer, w_down_near, token)
    crossed = hold(crossed, send)
    crossed_other = swap(crossed, "head", head_size, 1)
    keep = down_part(units, w_down_near)
    line_sums = sum_part(keep, swap(send, "head", head_size, 1), cols, jnp.float32)
    total = line_sums[0]
    got = [swap(line_sums[j // 2], "head", head_size, j) for j in even if j]
    units, send = experts_part(me_ref, crossed, crossed_other, buffer, w_down_near, line_sums[-1])
    keep = down_part(units, w_down_near)
    crossed_sums = sum_part(keep, swap(send, "head", head_size, 1), cols, jnp.bfloat16)
    for j in even:
        pairs = [
            (r * head_size + h, (r ^ 1) * head_size + (h ^ j))
            for r in range(req_size)
            for h in range(head_size)
        ]
        got.append(lax.ppermute(crossed_sums[j // 2], ("req", "head"), pairs))
    for part in got:
        total = total + part.astype(jnp.float32)
    chunks = total.astype(jnp.bfloat16).reshape(req_size // 2, rows, cols)
    out = chunks[0].astype(jnp.float32)
    for k in steps:
        out = out + swap(chunks[k // 2], "req", req_size, k).astype(jnp.float32)
    return (out + resid).astype(jnp.bfloat16)


def solution(mesh):
    in_specs = (
        P("req", "head"),
        P("req"),
        P("req", None),
        P("req", None),
        P(None, None, "head"),
        P("head", None),
        P("req", None, "head", None),
        P("req", None, "head", None),
        P(None, "head", "req"),
        P("head", "req", None),
    )
    out_specs = P("req", "head")
    return jax.shard_map(
        per_device, mesh=mesh, in_specs=in_specs, out_specs=out_specs, check_vma=False
    )
```

time: 77.7 us -> 72.3 us (0.931); the launches traced: 77.8 us -> 71.5 us
  waiting for transfers between devices: 22.5 us -> 16.6 us
  starting transfers between devices: 16.3 us -> 17.7 us
  local copies, waits for them, and re-layouts: 1.36 us -> 0.19 us
    pallas_call x1 -> x7, Pallas kernels: 3.02 us -> 8.66 us  [the longest x1 3.57 us: fetch(): pl.pallas_call(fetch_kernel, out_shape=(pltpu.VMEM(hidden.shape, jnp.bflo...]
    pallas_call x1, Pallas kernels: 14.6 us -> 9.8 us  [attention(): pl.pallas_call(functools.partial(attention_kernel, head_count), out_shape...]
    ppermute x15 -> x17, waiting for transfers between devices: 16.4 us -> 11.7 us  [swap(): return lax.ppermute(value, axis, [(i, i ^ mask) for i in range(size)])]
    ppermute x15 -> x17, starting transfers between devices: 12.7 us -> 14.8 us  [swap(): return lax.ppermute(value, axis, [(i, i ^ mask) for i in range(size)])]
    pallas_call x3 -> x2, Pallas kernels: 8.97 us -> 7.44 us  [by_expert(): pl.pallas_call(functools.partial(relayout_kernel, js), out_shape=(pltpu.V...]
    ppermute x3 -> x2, waiting for transfers between devices: 6.14 us -> 4.86 us  [per_device(): got.append(lax.ppermute(crossed_sums[j // 2], ('req', 'head'), pairs))]
    ppermute x3 -> x2, starting transfers between devices: 3.55 us -> 2.91 us  [per_device(): got.append(lax.ppermute(crossed_sums[j // 2], ('req', 'head'), pairs))]
    pallas_call x1 -> x2, Pallas kernels: 8.76 us -> 9.01 us  [experts_part(): pl.pallas_call(experts_kernel, out_shape=(jax.ShapeDtypeStruct((tokens, t...]
  transfers between devices with their start and end apart: 18 -> 19, of which waited for: 11 -> 11; matrix products, arithmetic and copies ran while one was open for 2% -> 2% of each run, Pallas kernels for 15% -> 29%
where the time goes in v6:
time: 72.3 us; the launch traced here: 71.5 us
  Pallas kernels  35 us (48%)
  starting transfers between devices  17.7 us (24%)
  waiting for transfers between devices  16.6 us (23%)
  other arithmetic  1.77 us (2%)
    ppermute x17, starting transfers between devices, swap(): return lax.ppermute(value, axis, [(i, i ^ mask) for i in range(size)])  14.8 us
    ppermute x17, waiting for transfers between devices, swap(): return lax.ppermute(value, axis, [(i, i ^ mask) for i in range(size)])  11.7 us
    pallas_call x1, Pallas kernels, attention(): pl.pallas_call(functools.partial(attention_kernel, head_count), out_shape...  9.8 us
    pallas_call x2, Pallas kernels, experts_part(): pl.pallas_call(experts_kernel, out_shape=(jax.ShapeDtypeStruct((tokens, t...  9.01 us
    pallas_call x2, Pallas kernels, by_expert(): pl.pallas_call(functools.partial(relayout_kernel, js), out_shape=(pltpu.V...  7.44 us
    ppermute x2, waiting for transfers between devices, per_device(): got.append(lax.ppermute(crossed_sums[j // 2], ('req', 'head'), pairs))  4.86 us
    pallas_call x1, Pallas kernels, fetch(): pl.pallas_call(fetch_kernel, out_shape=(pltpu.VMEM(hidden.shape, jnp.bflo...  3.57 us
    pallas_call x1, Pallas kernels, fetch_down(): pl.pallas_call(fetch_down_kernel, out_shape=(pltpu.VMEM((head_count, tota...  3.55 us
  transfers between devices with their start and end apart: 19, of which 11 were waited for; matrix products, arithmetic and copies ran while one was open for 2% of the time, Pallas kernels for 29%

profile of v6, /device:TPU:0, one launch (start us, length us, event | category | flops | bytes accessed | tf_op | source)
XLA Modules:
  0.0 71.5 jit_solution(13326370366160636900)
XLA Ops:
  0.0 0.5 collective-permute-start.1
  0.5 2.5 %collective-permute-start = (bf16[32,512]{1,0:T(8,128)(2,1)}, bf16[32,512]{1,0:T(8,128)(2,1)S(1)}, u32[]{:S(2)}, u32[]{:S(2)}) collective-permute-start(bf16[32,512]{1,0:T(8,128)(2,1)} %refs_0_.1), channel_id=1, source_target_pairs={{0,2},{1,3},{2,0},{3,1},{4,6},{5,7},{6,4},{7,5},{8,10},{9,11},{10,... | collective-permute-start | bytes 98312 | tf_op jit(solution)/shard_map/ppermute | solution.py:551
  3.0 0.1 collective-permute-start.2
  3.1 0.7 convert_element_type.45
  3.8 0.1 fusion
  3.9 0.1 pad_maximum_fusion
  4.0 3.6 %fetch.1 = (bf16[32,512]{1,0:T(8,128)(2,1)S(1)}, bf16[3,4,512,512]{3,2,1,0:T(8,128)(2,1)S(1)}, bf16[32,1536,128]{2,1,0:T(8,128)(2,1)S(1)}) custom-call(s32[32]{0:T(128)} %lengths_ref.3, s32[1]{0:T(128)} %bitcast.me_ref, bf16[32,512]{1,0:T(8,128)(2,1)} %refs_0_.1, bf16[3,2048,512]{2,1,0:T(8,128)(2,1)} %w_ref.3), custom_call_target="tpu_custom_call" | custom-call | bytes 12582912 | tf_op jit(solution)/shard_map/fetch/pallas_call | solution.py:62
  7.6 0.0 collective-permute-done.1.refs_1_
  7.6 0.0 collective-permute-done.refs_2_.refs_1_
  7.6 0.0 collective-permute-done.2.refs_3_
  7.6 0.0 copy-start.1
  7.6 0.0 copy-start.2
  7.6 9.8 %attention.1 = (bf16[32,1024]{1,0:T(8,128)(2,1)S(1)}, bf16[32,1024]{1,0:T(8,128)(2,1)S(1)}, bf16[32,1536,128]{2,1,0:T(8,128)(2,1)S(1)}) custom-call(s32[32]{0:T(128)} %lengths_ref.3, s32[1]{0:T(128)} %bitcast.me_ref, f32[32,128]{1,0:T(8,128)S(1)} %get-tuple-element.53.cos_ref, ...), custom_call_target="tpu_custom_call", output_to_operand_aliasing={{2}: (9, {})} | custom-call | flops 268435456 | bytes 5242880 | tf_op jit(solution)/shard_map/attention/pallas_call | solution.py:244
  17.4 0.0 copy-start
  17.5 0.2 collective-permute-start.3
  17.6 0.0 copy-done.1
  17.6 0.1 copy.16
  17.7 0.0 copy-done.2
  17.7 0.1 copy.17
  17.8 1.0 %collective-permute-done.3 = bf16[32,1024]{1,0:T(8,128)(2,1)S(1)} collective-permute-done((bf16[32,1024]{1,0:T(8,128)(2,1)S(1)}, bf16[32,1024]{1,0:T(8,128)(2,1)S(1)}, u32[]{:S(2)}, u32[]{:S(2)}) %collective-permute-start.3) | collective-permute-done | bytes 65568 | tf_op jit(solution)/shard_map/ppermute | solution.py:551
  18.8 1.8 %collective-permute-start.4 = (bf16[32,1024]{1,0:T(8,128)(2,1)S(1)}, bf16[32,1024]{1,0:T(8,128)(2,1)S(1)}, u32[]{:S(2)}, u32[]{:S(2)}) collective-permute-start(bf16[32,1024]{1,0:T(8,128)(2,1)S(1)} %add_convert_fusion.1.refs_0_.refs_2_), channel_id=1, source_target_pairs={{0,2},{1,3},{2,0},{3,1},{4,6},{5,7},{6,4},{7,5},{8,10},{9,11},{10,... | collective-permute-start | bytes 196616 | tf_op jit(solution)/shard_map/ppermute | solution.py:551
  20.6 0.2 select_reduce_fusion
  20.7 3.7 %by_expert_0.1 = (bf16[16,4,512,256]{3,2,1,0:T(8,128)(2,1)S(1)}, f32[8,128]{1,0:T(8,128)S(1)}) custom-call(s32[1]{0:T(128)} %bitcast.me_ref, bf16[2048,16,256]{2,1,0:T(8,128)(2,1)} %w_ref.5, bf16[32,1024]{1,0:T(8,128)(2,1)S(1)} %add_convert_fusion.1.refs_0_.refs_2_), custom_call_target="tpu_custom_call" | custom-call | bytes 16777216 | tf_op jit(solution)/shard_map/by_expert_0/pallas_call | solution.py:311
  24.5 0.0 collective-permute-done.4.refs_3_
  24.5 0.0 copy-done
  24.5 2.4 %collective-permute-start.7 = (bf16[32,1152]{1,0:T(8,128)(2,1)S(1)}, bf16[32,1152]{1,0:T(8,128)(2,1)S(1)}, u32[]{:S(2)}, u32[]{:S(2)}) collective-permute-start(bf16[32,1152]{1,0:T(8,128)(2,1)S(1)} %get-tuple-element.32.refs_1_.refs_0_), channel_id=1, source_target_pairs={{0,24},{4,28},{8,16},{12,20},{16,8},{20,12},{24,0},{28,4},{1,25},{... | collective-permute-start | bytes 221192 | tf_op jit(solution)/shard_map/ppermute | solution.py:551
  26.9 0.1 collective-permute-start.6
  27.0 2.0 %collective-permute-start.5 = (bf16[32,1152]{1,0:T(8,128)(2,1)S(1)}, bf16[32,1152]{1,0:T(8,128)(2,1)S(1)}, u32[]{:S(2)}, u32[]{:S(2)}) collective-permute-start(bf16[32,1152]{1,0:T(8,128)(2,1)S(1)} %get-tuple-element.32.refs_1_.refs_0_), channel_id=1, source_target_pairs={{0,8},{4,12},{8,0},{12,4},{16,24},{20,28},{24,16},{28,20},{1,9},{5... | collective-permute-start | bytes 221192 | tf_op jit(solution)/shard_map/ppermute | solution.py:551
  29.0 3.7 %by_expert_2.1 = (bf16[16,4,512,256]{3,2,1,0:T(8,128)(2,1)S(1)}, f32[8,128]{1,0:T(8,128)S(1)}) custom-call(s32[1]{0:T(128)} %bitcast.me_ref, bf16[2048,16,256]{2,1,0:T(8,128)(2,1)} %w_ref.5, bf16[16,4,512,256]{3,2,1,0:T(8,128)(2,1)S(1)} %get-tuple-element.33.refs_0_, ...), custom_call_target="tpu_custom_call", output_to_operand_aliasing={{0}: (2, {})} | custom-call | bytes 16777216 | tf_op jit(solution)/shard_map/by_expert_2/pallas_call | solution.py:311
  32.7 3.6 %fetch_down.1 = (bf16[4,2048,512]{2,1,0:T(8,128)(2,1)S(1)}, f32[8,128]{1,0:T(8,128)S(1)}) custom-call(s32[1]{0:T(128)} %bitcast.me_ref, bf16[2048,2048]{1,0:T(8,128)(2,1)} %bitcast.6, f32[8,128]{1,0:T(8,128)S(1)} %get-tuple-element.34._), custom_call_target="tpu_custom_call" | custom-call | bytes 16777216 | tf_op jit(solution)/shard_map/fetch_down/pallas_call | solution.py:398
  36.3 0.0 collective-permute-done.7.refs_3_
  36.3 0.0 collective-permute-done.6.refs_2_
  36.3 0.0 collective-permute-done.5.refs_1_
  36.3 0.1 collective-permute-start.8
  36.4 0.6 collective-permute-start.11
  37.0 1.0 %collective-permute-done.8.other_ref = bf16[128,1152]{1,0:T(8,128)(2,1)S(1)} collective-permute-done((bf16[128,1152]{1,0:T(8,128)(2,1)S(1)}, bf16[128,1152]{1,0:T(8,128)(2,1)S(1)}, u32[]{:S(2)}, u32[]{:S(2)}) %collective-permute-start.8) | collective-permute-done | bytes 294944 | tf_op jit(solution)/shard_map/ppermute | solution.py:551
  38.0 4.5 %experts.2 = (bf16[128,2048]{1,0:T(8,128)(2,1)S(1)}, bf16[128,1024]{1,0:T(8,128)(2,1)S(1)}) custom-call(s32[1]{0:T(128)} %bitcast.me_ref, bf16[128,1152]{1,0:T(8,128)(2,1)S(1)} %stack.1.mine_ref, bf16[128,1152]{1,0:T(8,128)(2,1)S(1)} %collective-permute-done.8.other_ref, bf16[16,4,512,256]{3,2,1,0:T(8,128)(2,1)S(1)} %get-tuple-element.36.w_ref, ...), custom_call_target="tpu_custom_call" | custom-call | flops 2147483648 | bytes 16777216 | tf_op jit(solution)/shard_map/experts/pallas_call | solution.py:469
  42.5 3.3 %collective-permute-done.11.value_ref = bf16[128,1152]{1,0:T(8,128)(2,1)S(1)} collective-permute-done((bf16[128,1152]{1,0:T(8,128)(2,1)S(1)}, bf16[128,1152]{1,0:T(8,128)(2,1)S(1)}, u32[]{:S(2)}, u32[]{:S(2)}) %collective-permute-start.11) | collective-permute-done | bytes 294944 | tf_op jit(solution)/shard_map/ppermute | solution.py:551
  45.8 0.0 collective-permute-start.12
  45.8 0.5 collective-permute-start.9
  46.4 0.7 down.2.keep_ref
  47.1 0.7 %collective-permute-done.9.sent_ref = bf16[128,1024]{1,0:T(8,128)(2,1)S(1)} collective-permute-done((bf16[128,1024]{1,0:T(8,128)(2,1)S(1)}, bf16[128,1024]{1,0:T(8,128)(2,1)S(1)}, u32[]{:S(2)}, u32[]{:S(2)}) %collective-permute-start.9) | collective-permute-done | bytes 262176 | tf_op jit(solution)/shard_map/ppermute | solution.py:551
  47.8 0.1 sum.2
  47.9 0.0 collective-permute-done.12.other_ref
  47.9 4.5 %experts.3 = (bf16[128,2048]{1,0:T(8,128)(2,1)S(1)}, bf16[128,1024]{1,0:T(8,128)(2,1)S(1)}) custom-call(s32[1]{0:T(128)} %bitcast.me_ref, bf16[128,1152]{1,0:T(8,128)(2,1)S(1)} %hold.1.mine_ref, bf16[128,1152]{1,0:T(8,128)(2,1)S(1)} %collective-permute-done.12.other_ref, bf16[16,4,512,256]{3,2,1,0:T(8,128)(2,1)S(1)} %get-tuple-element.36.w_ref, ...), custom_call_target="tpu_custom_call" | custom-call | flops 2147483648 | bytes 16777216 | tf_op jit(solution)/shard_map/experts/pallas_call | solution.py:469
  52.4 0.2 collective-permute-start.13
  52.6 0.4 collective-permute-start.10
  53.0 0.7 %down.3.keep_ref = bf16[128,1024]{1,0:T(8,128)(2,1)S(1)} custom-call(bf16[128,2048]{1,0:T(8,128)(2,1)S(1)} %get-tuple-element.42.units_ref, bf16[4,2048,512]{2,1,0:T(8,128)(2,1)S(1)} %get-tuple-element.37.w_down_ref.w_ref), custom_call_target="tpu_custom_call" | custom-call | flops 536870912 | bytes 4194304 | tf_op jit(solution)/shard_map/down/pallas_call | solution.py:495
  53.7 0.3 collective-permute-done.13.sent_ref
  54.0 0.1 sum.3
  54.1 0.6 collective-permute-start.14
  54.6 2.3 %collective-permute-start.15 = (bf16[128,512]{1,0:T(8,128)(2,1)S(1)}, bf16[128,512]{1,0:T(8,128)(2,1)S(1)}, u32[]{:S(2)}, u32[]{:S(2)}) collective-permute-start(bf16[128,512]{1,0:T(8,128)(2,1)S(1)} %get-tuple-element.45), channel_id=1, source_target_pairs={{0,6},{1,7},{2,4},{3,5},{4,2},{5,3},{6,0},{7,1},{8,14},{9,15},{10,... | collective-permute-start | bytes 393224 | tf_op jit(solution)/shard_map/ppermute | solution.py:620
  57.0 1.4 %collective-permute-done.10 = bf16[128,512]{1,0:T(8,128)(2,1)S(1)} collective-permute-done((bf16[128,512]{1,0:T(8,128)(2,1)S(1)}, bf16[128,512]{1,0:T(8,128)(2,1)S(1)}, u32[]{:S(2)}, u32[]{:S(2)}) %collective-permute-start.10) | collective-permute-done | bytes 131104 | tf_op jit(solution)/shard_map/ppermute | solution.py:551
  58.4 2.1 %collective-permute-done.14 = bf16[128,512]{1,0:T(8,128)(2,1)S(1)} collective-permute-done((bf16[128,512]{1,0:T(8,128)(2,1)S(1)}, bf16[128,512]{1,0:T(8,128)(2,1)S(1)}, u32[]{:S(2)}, u32[]{:S(2)}) %collective-permute-start.14) | collective-permute-done | bytes 131104 | tf_op jit(solution)/shard_map/ppermute | solution.py:620
  60.5 2.8 %collective-permute-done.15 = bf16[128,512]{1,0:T(8,128)(2,1)S(1)} collective-permute-done((bf16[128,512]{1,0:T(8,128)(2,1)S(1)}, bf16[128,512]{1,0:T(8,128)(2,1)S(1)}, u32[]{:S(2)}, u32[]{:S(2)}) %collective-permute-start.15) | collective-permute-done | bytes 131104 | tf_op jit(solution)/shard_map/ppermute | solution.py:620
  63.2 0.1 add_convert_fusion
  63.3 0.9 %collective-permute-start.16 = (bf16[32,512]{1,0:T(8,128)(2,1)S(1)}, bf16[32,512]{1,0:T(8,128)(2,1)S(1)}, u32[]{:S(2)}, u32[]{:S(2)}) collective-permute-start(bf16[32,512]{1,0:T(8,128)(2,1)S(1)} %get-tuple-element.47), channel_id=1, source_target_pairs={{0,8},{4,12},{8,0},{12,4},{16,24},{20,28},{24,16},{28,20},{1,9},{5... | collective-permute-start | bytes 98312 | tf_op jit(solution)/shard_map/ppermute | solution.py:551
  64.2 1.8 %collective-permute-start.18 = (bf16[32,512]{1,0:T(8,128)(2,1)S(1)}, bf16[32,512]{1,0:T(8,128)(2,1)S(1)}, u32[]{:S(2)}, u32[]{:S(2)}) collective-permute-start(bf16[32,512]{1,0:T(8,128)(2,1)S(1)} %get-tuple-element.48), channel_id=1, source_target_pairs={{0,24},{4,28},{8,16},{12,20},{16,8},{20,12},{24,0},{28,4},{1,25},{... | collective-permute-start | bytes 98312 | tf_op jit(solution)/shard_map/ppermute | solution.py:551
  66.0 0.9 %collective-permute-start.17 = (bf16[32,512]{1,0:T(8,128)(2,1)S(1)}, bf16[32,512]{1,0:T(8,128)(2,1)S(1)}, u32[]{:S(2)}, u32[]{:S(2)}) collective-permute-start(bf16[32,512]{1,0:T(8,128)(2,1)S(1)} %get-tuple-element.49), channel_id=1, source_target_pairs={{0,16},{4,20},{8,24},{12,28},{16,0},{20,4},{24,8},{28,12},{1,17},{... | collective-permute-start | bytes 98312 | tf_op jit(solution)/shard_map/ppermute | solution.py:551
  66.9 0.4 collective-permute-done.16
  67.3 2.6 %collective-permute-done.18 = bf16[32,512]{1,0:T(8,128)(2,1)S(1)} collective-permute-done((bf16[32,512]{1,0:T(8,128)(2,1)S(1)}, bf16[32,512]{1,0:T(8,128)(2,1)S(1)}, u32[]{:S(2)}, u32[]{:S(2)}) %collective-permute-start.18) | collective-permute-done | bytes 32800 | tf_op jit(solution)/shard_map/ppermute | solution.py:551
  69.9 0.9 %collective-permute-done.17 = bf16[32,512]{1,0:T(8,128)(2,1)S(1)} collective-permute-done((bf16[32,512]{1,0:T(8,128)(2,1)S(1)}, bf16[32,512]{1,0:T(8,128)(2,1)S(1)}, u32[]{:S(2)}, u32[]{:S(2)}) %collective-permute-start.17) | collective-permute-done | bytes 32800 | tf_op jit(solution)/shard_map/ppermute | solution.py:551
  70.8 0.6 add_convert_fusion.2
  (7 shorter events, 0.1 us)
Async XLA Ops:
  0.0 7.6 %collective-permute-start.1 = (bf16[32,512]{1,0:T(8,128)(2,1)}, bf16[32,512]{1,0:T(8,128)(2,1)S(1)}, u32[]{:S(2)}, u32[]{:S(2)}) collective-permute-start(bf16[32,512]{1,0:T(8,128)(2,1)} %refs_0_.1), channel_id=1, source_target_pairs={{0,1},{1,0},{2,3},{3,2},{4,5},{5,4},{6,7},{7,6},{8,9},{9,8},{10,11... | collective-permute-start | bytes 98312 | tf_op jit(solution)/shard_map/ppermute | solution.py:551
  0.5 7.1 %collective-permute-start = (bf16[32,512]{1,0:T(8,128)(2,1)}, bf16[32,512]{1,0:T(8,128)(2,1)S(1)}, u32[]{:S(2)}, u32[]{:S(2)}) collective-permute-start(bf16[32,512]{1,0:T(8,128)(2,1)} %refs_0_.1), channel_id=1, source_target_pairs={{0,2},{1,3},{2,0},{3,1},{4,6},{5,7},{6,4},{7,5},{8,10},{9,11},{10,... | collective-permute-start | bytes 98312 | tf_op jit(solution)/shard_map/ppermute | solution.py:551
  3.0 4.6 %collective-permute-start.2 = (bf16[32,512]{1,0:T(8,128)(2,1)}, bf16[32,512]{1,0:T(8,128)(2,1)S(1)}, u32[]{:S(2)}, u32[]{:S(2)}) collective-permute-start(bf16[32,512]{1,0:T(8,128)(2,1)} %refs_0_.1), channel_id=1, source_target_pairs={{0,3},{1,2},{2,1},{3,0},{4,7},{5,6},{6,5},{7,4},{8,11},{9,10},{10,... | collective-permute-start | bytes 98312 | tf_op jit(solution)/shard_map/ppermute | solution.py:551
  7.6 10.0 %copy-start.1 = (s32[32,8]{0,1:T(8,128)S(1)}, s32[32,8]{0,1:T(8,128)}, u32[]{:S(2)}) copy-start(s32[32,8]{0,1:T(8,128)} %param.12) | copy-start | bytes 3076
  7.6 10.1 %copy-start.2 = (f32[32,8]{0,1:T(8,128)S(1)}, f32[32,8]{0,1:T(8,128)}, u32[]{:S(2)}) copy-start(f32[32,8]{0,1:T(8,128)} %param.13) | copy-start | bytes 3076
  17.4 7.0 %copy-start = (bf16[32,512]{1,0:T(8,128)(2,1)S(1)}, bf16[32,512]{1,0:T(8,128)(2,1)}, u32[]{:S(2)}) copy-start(bf16[32,512]{1,0:T(8,128)(2,1)} %refs_0_.1) | copy-start | bytes 98308
  17.5 1.3 %collective-permute-start.3 = (bf16[32,1024]{1,0:T(8,128)(2,1)S(1)}, bf16[32,1024]{1,0:T(8,128)(2,1)S(1)}, u32[]{:S(2)}, u32[]{:S(2)}) collective-permute-start(bf16[32,1024]{1,0:T(8,128)(2,1)S(1)} %get-tuple-element.30), channel_id=1, source_target_pairs={{0,1},{1,0},{2,3},{3,2},{4,5},{5,4},{6,7},{7,6},{8,9},{9,8},{10,11... | collective-permute-start | bytes 196616 | tf_op jit(solution)/shard_map/ppermute | solution.py:551
  18.8 5.7 %collective-permute-start.4 = (bf16[32,1024]{1,0:T(8,128)(2,1)S(1)}, bf16[32,1024]{1,0:T(8,128)(2,1)S(1)}, u32[]{:S(2)}, u32[]{:S(2)}) collective-permute-start(bf16[32,1024]{1,0:T(8,128)(2,1)S(1)} %add_convert_fusion.1.refs_0_.refs_2_), channel_id=1, source_target_pairs={{0,2},{1,3},{2,0},{3,1},{4,6},{5,7},{6,4},{7,5},{8,10},{9,11},{10,... | collective-permute-start | bytes 196616 | tf_op jit(solution)/shard_map/ppermute | solution.py:551
  24.5 11.7 %collective-permute-start.7 = (bf16[32,1152]{1,0:T(8,128)(2,1)S(1)}, bf16[32,1152]{1,0:T(8,128)(2,1)S(1)}, u32[]{:S(2)}, u32[]{:S(2)}) collective-permute-start(bf16[32,1152]{1,0:T(8,128)(2,1)S(1)} %get-tuple-element.32.refs_1_.refs_0_), channel_id=1, source_target_pairs={{0,24},{4,28},{8,16},{12,20},{16,8},{20,12},{24,0},{28,4},{1,25},{... | collective-permute-start | bytes 221192 | tf_op jit(solution)/shard_map/ppermute | solution.py:551
  26.9 9.4 %collective-permute-start.6 = (bf16[32,1152]{1,0:T(8,128)(2,1)S(1)}, bf16[32,1152]{1,0:T(8,128)(2,1)S(1)}, u32[]{:S(2)}, u32[]{:S(2)}) collective-permute-start(bf16[32,1152]{1,0:T(8,128)(2,1)S(1)} %get-tuple-element.32.refs_1_.refs_0_), channel_id=1, source_target_pairs={{0,16},{4,20},{8,24},{12,28},{16,0},{20,4},{24,8},{28,12},{1,17},{... | collective-permute-start | bytes 221192 | tf_op jit(solution)/shard_map/ppermute | solution.py:551
  27.0 9.3 %collective-permute-start.5 = (bf16[32,1152]{1,0:T(8,128)(2,1)S(1)}, bf16[32,1152]{1,0:T(8,128)(2,1)S(1)}, u32[]{:S(2)}, u32[]{:S(2)}) collective-permute-start(bf16[32,1152]{1,0:T(8,128)(2,1)S(1)} %get-tuple-element.32.refs_1_.refs_0_), channel_id=1, source_target_pairs={{0,8},{4,12},{8,0},{12,4},{16,24},{20,28},{24,16},{28,20},{1,9},{5... | collective-permute-start | bytes 221192 | tf_op jit(solution)/shard_map/ppermute | solution.py:551
  36.3 1.6 %collective-permute-start.8 = (bf16[128,1152]{1,0:T(8,128)(2,1)S(1)}, bf16[128,1152]{1,0:T(8,128)(2,1)S(1)}, u32[]{:S(2)}, u32[]{:S(2)}) collective-permute-start(bf16[128,1152]{1,0:T(8,128)(2,1)S(1)} %stack.1.mine_ref), channel_id=1, source_target_pairs={{0,1},{1,0},{2,3},{3,2},{4,5},{5,4},{6,7},{7,6},{8,9},{9,8},{10,11... | collective-permute-start | bytes 884744 | tf_op jit(solution)/shard_map/ppermute | solution.py:551
  36.4 9.4 %collective-permute-start.11 = (bf16[128,1152]{1,0:T(8,128)(2,1)S(1)}, bf16[128,1152]{1,0:T(8,128)(2,1)S(1)}, u32[]{:S(2)}, u32[]{:S(2)}) collective-permute-start(bf16[128,1152]{1,0:T(8,128)(2,1)S(1)} %stack.1.mine_ref), channel_id=1, source_target_pairs={{0,4},{4,0},{8,12},{12,8},{16,20},{20,16},{24,28},{28,24},{1,5},{5... | collective-permute-start | bytes 884744 | tf_op jit(solution)/shard_map/ppermute | solution.py:551
  45.8 2.0 %collective-permute-start.12 = (bf16[128,1152]{1,0:T(8,128)(2,1)S(1)}, bf16[128,1152]{1,0:T(8,128)(2,1)S(1)}, u32[]{:S(2)}, u32[]{:S(2)}) collective-permute-start(bf16[128,1152]{1,0:T(8,128)(2,1)S(1)} %hold.1.mine_ref), channel_id=1, source_target_pairs={{0,1},{1,0},{2,3},{3,2},{4,5},{5,4},{6,7},{7,6},{8,9},{9,8},{10,11... | collective-permute-start | bytes 884744 | tf_op jit(solution)/shard_map/ppermute | solution.py:551
  45.8 2.0 %collective-permute-start.9 = (bf16[128,1024]{1,0:T(8,128)(2,1)S(1)}, bf16[128,1024]{1,0:T(8,128)(2,1)S(1)}, u32[]{:S(2)}, u32[]{:S(2)}) collective-permute-start(bf16[128,1024]{1,0:T(8,128)(2,1)S(1)} %get-tuple-element.39.after_ref), channel_id=1, source_target_pairs={{0,1},{1,0},{2,3},{3,2},{4,5},{5,4},{6,7},{7,6},{8,9},{9,8},{10,11... | collective-permute-start | bytes 786440 | tf_op jit(solution)/shard_map/ppermute | solution.py:551
  52.4 1.6 %collective-permute-start.13 = (bf16[128,1024]{1,0:T(8,128)(2,1)S(1)}, bf16[128,1024]{1,0:T(8,128)(2,1)S(1)}, u32[]{:S(2)}, u32[]{:S(2)}) collective-permute-start(bf16[128,1024]{1,0:T(8,128)(2,1)S(1)} %get-tuple-element.43), channel_id=1, source_target_pairs={{0,1},{1,0},{2,3},{3,2},{4,5},{5,4},{6,7},{7,6},{8,9},{9,8},{10,11... | collective-permute-start | bytes 786440 | tf_op jit(solution)/shard_map/ppermute | solution.py:551
  52.6 5.8 %collective-permute-start.10 = (bf16[128,512]{1,0:T(8,128)(2,1)S(1)}, bf16[128,512]{1,0:T(8,128)(2,1)S(1)}, u32[]{:S(2)}, u32[]{:S(2)}) collective-permute-start(bf16[128,512]{1,0:T(8,128)(2,1)S(1)} %get-tuple-element.41._), channel_id=1, source_target_pairs={{0,2},{1,3},{2,0},{3,1},{4,6},{5,7},{6,4},{7,5},{8,10},{9,11},{10,... | collective-permute-start | bytes 393224 | tf_op jit(solution)/shard_map/ppermute | solution.py:551
  54.1 6.4 %collective-permute-start.14 = (bf16[128,512]{1,0:T(8,128)(2,1)S(1)}, bf16[128,512]{1,0:T(8,128)(2,1)S(1)}, u32[]{:S(2)}, u32[]{:S(2)}) collective-permute-start(bf16[128,512]{1,0:T(8,128)(2,1)S(1)} %get-tuple-element.44), channel_id=1, source_target_pairs={{0,4},{1,5},{2,6},{3,7},{4,0},{5,1},{6,2},{7,3},{8,12},{9,13},{10,... | collective-permute-start | bytes 393224 | tf_op jit(solution)/shard_map/ppermute | solution.py:620
  54.6 8.6 %collective-permute-start.15 = (bf16[128,512]{1,0:T(8,128)(2,1)S(1)}, bf16[128,512]{1,0:T(8,128)(2,1)S(1)}, u32[]{:S(2)}, u32[]{:S(2)}) collective-permute-start(bf16[128,512]{1,0:T(8,128)(2,1)S(1)} %get-tuple-element.45), channel_id=1, source_target_pairs={{0,6},{1,7},{2,4},{3,5},{4,2},{5,3},{6,0},{7,1},{8,14},{9,15},{10,... | collective-permute-start | bytes 393224 | tf_op jit(solution)/shard_map/ppermute | solution.py:620
  63.3 4.0 %collective-permute-start.16 = (bf16[32,512]{1,0:T(8,128)(2,1)S(1)}, bf16[32,512]{1,0:T(8,128)(2,1)S(1)}, u32[]{:S(2)}, u32[]{:S(2)}) collective-permute-start(bf16[32,512]{1,0:T(8,128)(2,1)S(1)} %get-tuple-element.47), channel_id=1, source_target_pairs={{0,8},{4,12},{8,0},{12,4},{16,24},{20,28},{24,16},{28,20},{1,9},{5... | collective-permute-start | bytes 98312 | tf_op jit(solution)/shard_map/ppermute | solution.py:551
  64.2 5.7 %collective-permute-start.18 = (bf16[32,512]{1,0:T(8,128)(2,1)S(1)}, bf16[32,512]{1,0:T(8,128)(2,1)S(1)}, u32[]{:S(2)}, u32[]{:S(2)}) collective-permute-start(bf16[32,512]{1,0:T(8,128)(2,1)S(1)} %get-tuple-element.48), channel_id=1, source_target_pairs={{0,24},{4,28},{8,16},{12,20},{16,8},{20,12},{24,0},{28,4},{1,25},{... | collective-permute-start | bytes 98312 | tf_op jit(solution)/shard_map/ppermute | solution.py:551
  66.0 4.8 %collective-permute-start.17 = (bf16[32,512]{1,0:T(8,128)(2,1)S(1)}, bf16[32,512]{1,0:T(8,128)(2,1)S(1)}, u32[]{:S(2)}, u32[]{:S(2)}) collective-permute-start(bf16[32,512]{1,0:T(8,128)(2,1)S(1)} %get-tuple-element.49), channel_id=1, source_target_pairs={{0,16},{4,20},{8,24},{12,28},{16,0},{20,4},{24,8},{28,12},{1,17},{... | collective-permute-start | bytes 98312 | tf_op jit(solution)/shard_map/ppermute | solution.py:551

commit v7 on v6

--- a/solution.py
+++ b/solution.py
@@ -32,7 +32,10 @@
     return pl.multiple_of((length + 7) // 8 * (8 * heads_local), 8 * heads_local)
 
 
-def fetch_kernel(lengths_ref, me_ref, own_ref, w_ref, own_out_ref, w_out_ref, blank_ref, sem, own_sem):
+def fetch_kernel(
+    lengths_ref, me_ref, freqs_ref, own_ref, w_ref,
+    own_out_ref, w_out_ref, blank_ref, cos_ref, sin_ref, angle_s, sem, own_sem,
+):
     head_count, cols = w_out_ref.shape[1:3]
     chunk_rows = CHUNK * cols // LANES
     me = me_ref[0]
@@ -52,23 +55,34 @@
     def _(r):
         last = pl.multiple_of((lengths_ref[r] - 1) // CHUNK * chunk_rows, chunk_rows)
         blank_ref[r, pl.ds(last, chunk_rows)] = jnp.zeros((chunk_rows, LANES), jnp.bfloat16)
-
+        angle_s[pl.ds(r, 1), :] = lengths_ref[r].astype(jnp.float32) * freqs_ref[...]
+
+    cos_ref[...] = jnp.cos(angle_s[...])
+    lane = lax.broadcasted_iota(jnp.int32, sin_ref.shape, 1)
+    sine = jnp.sin(angle_s[...])
+    sin_ref[...] = jnp.where(lane < LANES // 2, -sine, sine)
     for copy in copies:
         copy.wait()
 
 
 def fetch(me, lengths, hidden, w_qkv, v_shape, head_count):
     cols = w_qkv.shape[2]
+    rows = hidden.shape[0]
+    exponents = jnp.arange(LANES, dtype=jnp.float32) % (LANES // 2) / (LANES // 2)
+    freqs = (rope_theta**-exponents)[None, :]
     return pl.pallas_call(
         fetch_kernel,
         out_shape=(
             pltpu.VMEM(hidden.shape, jnp.bfloat16),
             pltpu.VMEM((w_qkv.shape[0], head_count, cols, cols), jnp.bfloat16),
             pltpu.VMEM(v_shape, jnp.bfloat16),
-        ),
-        in_specs=[SMEM, SMEM, ANY, ANY],
-        out_specs=(VMEM, VMEM, VMEM),
+            pltpu.VMEM((rows, LANES), jnp.float32),
+            pltpu.VMEM((rows, LANES), jnp.float32),
+        ),
+        in_specs=[SMEM, SMEM, VMEM, ANY, ANY],
+        out_specs=[VMEM] * 5,
         scratch_shapes=[
+            pltpu.VMEM((rows, LANES), jnp.float32),
             pltpu.SemaphoreType.DMA((w_qkv.shape[0], head_count)),
             pltpu.SemaphoreType.DMA(()),
         ],
@@ -77,7 +91,7 @@
             flops=0, bytes_accessed=4 * w_qkv.size, transcendentals=0
         ),
         name="fetch",
-    )(in_hbm(lengths), me, in_hbm(hidden), in_hbm(w_qkv))
+    )(in_hbm(lengths), me, freqs, in_hbm(hidden), in_hbm(w_qkv))
 
 
 def attention_kernel(head_count, lengths_ref, me_ref, cos_ref, sin_ref, *refs):
@@ -273,10 +287,14 @@
 RELAYOUT_ROWS = 128
 RELAYOUT_STEP = 16
 
+def slot_of(j, head_count):
+    return j // 2 + j % 2 * (head_count // 2)
+
+
 def relayout_kernel(js, me_ref, w_ref, *refs):
     out_ref, token_ref, in_s, in_sem = refs[-4:]
     token_ref[...] = jnp.zeros_like(token_ref)
-    experts, _, cols, _ = out_ref.shape
+    experts, head_count, cols, _ = out_ref.shape
     step = in_s.shape[1]
     per_block = cols // step
     copies = []
@@ -297,7 +315,7 @@
         copy.wait()
         for s in range(step // RELAYOUT_STEP):
             part = in_s[slot, pl.ds(s * RELAYOUT_STEP, RELAYOUT_STEP)]
-            out_ref[:, j, pl.ds(i * step + s * RELAYOUT_STEP, RELAYOUT_STEP), :] = jnp.swapaxes(
+            out_ref[:, slot_of(j, head_count), pl.ds(i * step + s * RELAYOUT_STEP, RELAYOUT_STEP), :] = jnp.swapaxes(
                 part, 0, 1
             )
 
@@ -412,6 +430,156 @@
     )(me, in_hbm(w_down), after)
 
 
+def expert_products(states, w_ref, first, p, per_step):
+    columns = w_ref.shape[3]
+    depth = states.shape[1]
+    taken = pl.ds(first, depth // w_ref.shape[2])
+    products = [
+        jnp.dot(
+            states,
+            w_ref[p * per_step + i, taken].reshape(depth, columns),
+            preferred_element_type=jnp.float32,
+        )
+        for i in range(per_step)
+    ]
+    return products[0] if per_step == 1 else jnp.concatenate(products, axis=1)
+
+
+def steps_of(w_shape):
+    per_step = max(1, 2 * LANES // w_shape[3])
+    return w_shape[0] // per_step, per_step
+
+
+def square_sum(ref, depth):
+    return jnp.sum(jnp.square(ref[:, :depth].astype(jnp.float32)), axis=1, keepdims=True)
+
+
+def units_step(me, p, per_step, experts, product, scale, shares):
+    tokens = product.shape[0]
+    first_half = lax.broadcasted_iota(jnp.int32, (tokens, LANES), 1) < LANES // 2
+    source = lax.broadcasted_iota(jnp.int32, (LANES, LANES), 0)
+    lane = lax.broadcasted_iota(jnp.int32, (LANES, LANES), 1)
+    expert = me * experts + p * per_step + lane * per_step // LANES
+    share = jnp.dot(
+        shares, (source == expert).astype(jnp.bfloat16), preferred_element_type=jnp.float32
+    )
+    a, b = product[:, :LANES], product[:, LANES:]
+    gate = jnp.where(first_half, a, pltpu.roll(b, LANES // 2, 1)) * scale
+    upward = jnp.where(first_half, pltpu.roll(a, LANES // 2, 1), b) * scale
+    return (share * (gate / (1.0 + jnp.exp(-gate)) * upward)).astype(jnp.bfloat16)
+
+
+def part_of(p):
+    return pl.ds(pl.multiple_of(p * LANES, LANES), LANES)
+
+
+def whole_kernel(me_ref, mine_ref, other_ref, w_ref, _, units_ref, states_s):
+    experts, head_count, cols, _ = w_ref.shape
+    depth = head_count // 2 * cols
+    states_s[:, :depth] = mine_ref[:, :depth]
+    states_s[:, depth:] = other_ref[:, :depth]
+    square = square_sum(mine_ref, depth) + square_sum(other_ref, depth)
+    scale = lax.rsqrt(square / (2 * depth) + norm_eps)
+    shares = mine_ref[:, depth:]
+    steps, per_step = steps_of(w_ref.shape)
+
+    @pl.loop(0, steps, unroll=4)
+    def _(p):
+        product = expert_products(states_s[...], w_ref, 0, p, per_step)
+        units_ref[:, part_of(p)] = units_step(
+            me_ref[0], p, per_step, experts, product, scale, shares
+        )
+
+
+def first_kernel(mine_ref, w_ref, _, product_ref):
+    _, head_count, cols, _ = w_ref.shape
+    steps, per_step = steps_of(w_ref.shape)
+
+    @pl.loop(0, steps, unroll=4)
+    def _(p):
+        states = mine_ref[:, : head_count // 2 * cols]
+        product_ref[p] = expert_products(states, w_ref, 0, p, per_step)
+
+
+def second_kernel(me_ref, mine_ref, other_ref, product_ref, w_ref, w_down_ref, units_ref, send_ref):
+    experts, head_count, cols, _ = w_ref.shape
+    depth = head_count // 2 * cols
+    square = square_sum(mine_ref, depth) + square_sum(other_ref, depth)
+    scale = lax.rsqrt(square / (2 * depth) + norm_eps)
+    shares = mine_ref[:, depth:]
+    steps, per_step = steps_of(w_ref.shape)
+
+    @pl.loop(0, steps, unroll=4)
+    def _(p):
+        product = product_ref[p] + expert_products(
+            other_ref[:, :depth], w_ref, head_count // 2, p, per_step
+        )
+        units_ref[:, part_of(p)] = units_step(
+            me_ref[0], p, per_step, experts, product, scale, shares
+        )
+
+    down_blocks(units_ref[...], w_down_ref, 1, send_ref)
+
+
+def experts_whole(me, mine, other, weights, after, total_units):
+    experts, head_count, cols, columns = weights.shape
+    tokens = mine.shape[0]
+    return pl.pallas_call(
+        whole_kernel,
+        out_shape=jax.ShapeDtypeStruct((tokens, total_units), jnp.bfloat16),
+        in_specs=[SMEM] + [VMEM] * 3 + [ANY],
+        out_specs=VMEM,
+        scratch_shapes=[pltpu.VMEM((tokens, head_count * cols), jnp.bfloat16)],
+        compiler_params=pltpu.CompilerParams(vmem_limit_bytes=12 * 2**20),
+        cost_estimate=pl.CostEstimate(
+            flops=2 * tokens * head_count * cols * experts * columns,
+            bytes_accessed=2 * head_count * cols * experts * columns,
+            transcendentals=0,
+        ),
+        name="experts_whole",
+    )(me, mine, other, in_vmem(weights), after)
+
+
+def experts_first(mine, weights, after):
+    experts, head_count, cols, columns = weights.shape
+    tokens = mine.shape[0]
+    steps, per_step = steps_of(weights.shape)
+    return pl.pallas_call(
+        first_kernel,
+        out_shape=jax.ShapeDtypeStruct((steps, tokens, per_step * columns), jnp.float32),
+        in_specs=[VMEM] * 2 + [ANY],
+        out_specs=VMEM,
+        compiler_params=pltpu.CompilerParams(vmem_limit_bytes=12 * 2**20),
+        cost_estimate=pl.CostEstimate(
+            flops=tokens * head_count * cols * experts * columns,
+            bytes_accessed=head_count * cols * experts * columns,
+            transcendentals=0,
+        ),
+        name="experts_first",
+    )(mine, in_vmem(weights), after)
+
+
+def experts_second(me, mine, other, products, weights, w_down):
+    experts, head_count, cols, columns = weights.shape
+    tokens = mine.shape[0]
+    return pl.pallas_call(
+        second_kernel,
+        out_shape=(
+            jax.ShapeDtypeStruct((tokens, w_down.shape[1]), jnp.bfloat16),
+            jax.ShapeDtypeStruct((tokens, head_count // 2 * cols), jnp.bfloat16),
+        ),
+        in_specs=[SMEM] + [VMEM] * 5,
+        out_specs=(VMEM, VMEM),
+        compiler_params=pltpu.CompilerParams(vmem_limit_bytes=12 * 2**20),
+        cost_estimate=pl.CostEstimate(
+            flops=tokens * head_count * cols * experts * columns,
+            bytes_accessed=head_count * cols * experts * columns,
+            transcendentals=0,
+        ),
+        name="experts_second",
+    )(me, mine, other, products, in_vmem(weights), in_vmem(w_down))
+
+
 def down_blocks(units, w_ref, first, out_ref):
     cols = w_ref.shape[2]
     for t in range(w_ref.shape[0] // 2):
@@ -420,87 +588,24 @@
         ).astype(jnp.bfloat16)
 
 
-def experts_kernel(me_ref, mine_ref, other_ref, w_ref, w_down_ref, _, units_ref, send_ref, states_s):
-    me = me_ref[0]
-    experts, head_count, cols, columns = w_ref.shape
-    blocks = head_count // 2
-    tokens = states_s.shape[0]
-    square = 0.0
-    for j in range(head_count):
-        part = (mine_ref, other_ref)[j % 2][:, j // 2 * cols : (j // 2 + 1) * cols]
-        states_s[:, j * cols : (j + 1) * cols] = part
-        square += jnp.sum(jnp.square(part.astype(jnp.float32)), axis=1, keepdims=True)
-    scale = lax.rsqrt(square / (head_count * cols) + norm_eps)
-    shares = mine_ref[:, blocks * cols :]
-    per_step = max(1, 2 * LANES // columns)
-    first_half = lax.broadcasted_iota(jnp.int32, (tokens, LANES), 1) < LANES // 2
-    source = lax.broadcasted_iota(jnp.int32, (LANES, LANES), 0)
-    lane = lax.broadcasted_iota(jnp.int32, (LANES, LANES), 1)
-
-    @pl.loop(0, experts // per_step, unroll=4)
-    def _(p):
-        states = states_s[...]
-        products = [
-            jnp.dot(
-                states,
-                w_ref[p * per_step + i].reshape(head_count * cols, columns),
-                preferred_element_type=jnp.float32,
-            )
-            for i in range(per_step)
-        ]
-        product = products[0] if per_step == 1 else jnp.concatenate(products, axis=1)
-        expert = me * experts + p * per_step + lane * per_step // LANES
-        share = jnp.dot(
-            shares, (source == expert).astype(jnp.bfloat16), preferred_element_type=jnp.float32
-        )
-        a, b = product[:, :LANES], product[:, LANES:]
-        gate = jnp.where(first_half, a, pltpu.roll(b, LANES // 2, 1)) * scale
-        upward = jnp.where(first_half, pltpu.roll(a, LANES // 2, 1), b) * scale
-        units = share * (gate / (1.0 + jnp.exp(-gate)) * upward)
-        units_ref[:, pl.ds(pl.multiple_of(p * LANES, LANES), LANES)] = units.astype(jnp.bfloat16)
-
-    down_blocks(units_ref[...], w_down_ref, 1, send_ref)
-
-
-def experts_part(me, mine, other, weights, w_down, after):
-    experts, head_count, cols, columns = weights.shape
-    tokens = mine.shape[0]
-    total_units = w_down.shape[1]
-    return pl.pallas_call(
-        experts_kernel,
-        out_shape=(
-            jax.ShapeDtypeStruct((tokens, total_units), jnp.bfloat16),
-            jax.ShapeDtypeStruct((tokens, head_count // 2 * cols), jnp.bfloat16),
-        ),
-        in_specs=[SMEM] + [VMEM] * 4 + [ANY],
-        out_specs=(VMEM, VMEM),
-        scratch_shapes=[pltpu.VMEM((tokens, head_count * cols), jnp.bfloat16)],
-        compiler_params=pltpu.CompilerParams(vmem_limit_bytes=16 * 2**20),
-        cost_estimate=pl.CostEstimate(
-            flops=2 * tokens * head_count * cols * experts * columns,
-            bytes_accessed=2 * head_count * cols * experts * columns,
-            transcendentals=0,
-        ),
-        name="experts",
-    )(me, mine, other, in_vmem(weights), in_vmem(w_down), after)
-
-
-def down_kernel(units_ref, w_ref, keep_ref):
-    down_blocks(units_ref[...], w_ref, 0, keep_ref)
-
-
-def down_part(units, w_down):
+def down_kernel(firsts, units_ref, w_ref, *outs):
+    for first, out_ref in zip(firsts, outs):
+        down_blocks(units_ref[...], w_ref, first, out_ref)
+
+
+def down_part(units, w_down, firsts):
     head_count, total_units, cols = w_down.shape
     tokens = units.shape[0]
-    return pl.pallas_call(
-        down_kernel,
-        out_shape=jax.ShapeDtypeStruct((tokens, head_count // 2 * cols), jnp.bfloat16),
+    half = jax.ShapeDtypeStruct((tokens, head_count // 2 * cols), jnp.bfloat16)
+    return pl.pallas_call(
+        functools.partial(down_kernel, firsts),
+        out_shape=[half] * len(firsts),
         in_specs=[VMEM, VMEM],
-        out_specs=VMEM,
-        compiler_params=pltpu.CompilerParams(vmem_limit_bytes=16 * 2**20),
+        out_specs=[VMEM] * len(firsts),
+        compiler_params=pltpu.CompilerParams(vmem_limit_bytes=12 * 2**20),
         cost_estimate=pl.CostEstimate(
-            flops=2 * tokens * total_units * head_count // 2 * cols,
-            bytes_accessed=2 * total_units * head_count // 2 * cols,
+            flops=len(firsts) * tokens * total_units * head_count * cols,
+            bytes_accessed=len(firsts) * total_units * head_count * cols,
             transcendentals=0,
         ),
         name="down",
@@ -563,18 +668,14 @@
     even = range(0, head_size, 2)
 
     pieces = [hidden] + [swap(hidden, "head", head_size, j) for j in range(1, head_size)]
-    half_dim = k_cache.shape[3] // 2
-    freqs = rope_theta ** (-jnp.arange(half_dim, dtype=jnp.float32) / half_dim)
-    angles = lengths.astype(jnp.float32)[:, None] * freqs[None, :]
-    cosine, sine = jnp.cos(angles), jnp.sin(angles)
     flat = (rows, k_cache.shape[1] * k_cache.shape[2], k_cache.shape[3])
-    own, w_near, room = fetch(me_ref, lengths, hidden, w_qkv, flat, head_size)
+    own, w_near, room, cosine, sine = fetch(me_ref, lengths, hidden, w_qkv, flat, head_size)
     keep, send = attention(
         [own] + pieces[1:],
         me_ref,
         lengths,
-        jnp.concatenate([cosine, cosine], axis=1),
-        jnp.concatenate([-sine, sine], axis=1),
+        cosine,
+        sine,
         w_near,
         room,
         w_out,
@@ -597,19 +698,20 @@
     line = [payload] + [swap(payload, "req", req_size, k) for k in steps]
     w_down_flat = w_down.reshape(experts_local * units_local, width)
     buffer, token = by_expert(tuple(late), me_ref, w_in, head_size, buffer, payload)
-    w_down_near, token = fetch_down(me_ref, w_down_flat, head_size, token)
     line = stack_part(line, token)
     crossed = swap(line, "req", req_size, 1)
     line_other = swap(line, "head", head_size, 1)
-    units, send = experts_part(me_ref, line, line_other, buffer, w_down_near, token)
+    units = experts_whole(me_ref, line, line_other, buffer, token, w_down_flat.shape[0])
+    w_down_near, _ = fetch_down(me_ref, w_down_flat, head_size, units)
+    keep, send = down_part(units, w_down_near, (0, 1))
     crossed = hold(crossed, send)
     crossed_other = swap(crossed, "head", head_size, 1)
-    keep = down_part(units, w_down_near)
     line_sums = sum_part(keep, swap(send, "head", head_size, 1), cols, jnp.float32)
     total = line_sums[0]
     got = [swap(line_sums[j // 2], "head", head_size, j) for j in even if j]
-    units, send = experts_part(me_ref, crossed, crossed_other, buffer, w_down_near, line_sums[-1])
-    keep = down_part(units, w_down_near)
+    products = experts_first(crossed, buffer, line_sums[-1])
+    units, send = experts_second(me_ref, crossed, crossed_other, products, buffer, w_down_near)
+    (keep,) = down_part(units, w_down_near, (0,))
     crossed_sums = sum_part(keep, swap(send, "head", head_size, 1), cols, jnp.bfloat16)
     for j in even:
         pairs = [

time: 72.3 us -> 70.1 us (0.970)
  waiting for transfers between devices: 16.6 us -> 15.1 us
  other arithmetic: 1.77 us -> 0.89 us
    ppermute x17, waiting for transfers between devices: 11.7 us -> 10.3 us  [swap(): return lax.ppermute(value, axis, [(i, i ^ mask) for i in range(size)])]
    pallas_call x1, Pallas kernels: 9.8 us -> 8.51 us  [attention(): pl.pallas_call(functools.partial(attention_kernel, head_count), out_shape...]
    pallas_call x4 -> x5, Pallas kernels: 10.4 us -> 10.8 us  [the longest x1 3.76 us: experts_whole(): pl.pallas_call(whole_kernel, out_shape=jax.ShapeDtypeStruct((tokens, tota...]
  transfers between devices with their start and end apart: 19 -> 19, of which waited for: 11 -> 11; matrix products, arithmetic and copies ran while one was open for 2% -> 0% of each run, Pallas kernels for 29% -> 33%
where the time goes in v7:
time: 70.1 us; the launch traced here: 69.5 us
  Pallas kernels  34.7 us (50%)
  starting transfers between devices  18.3 us (26%)
  waiting for transfers between devices  15.1 us (22%)
  other arithmetic  0.89 us (1%)
    ppermute x17, starting transfers between devices, swap(): return lax.ppermute(value, axis, [(i, i ^ mask) for i in range(size)])  15.4 us
    ppermute x17, waiting for transfers between devices, swap(): return lax.ppermute(value, axis, [(i, i ^ mask) for i in range(size)])  10.3 us
    pallas_call x1, Pallas kernels, attention(): pl.pallas_call(functools.partial(attention_kernel, head_count), out_shape...  8.51 us
    pallas_call x2, Pallas kernels, by_expert(): pl.pallas_call(functools.partial(relayout_kernel, js), out_shape=(pltpu.V...  7.44 us
    ppermute x2, waiting for transfers between devices, per_device(): got.append(lax.ppermute(crossed_sums[j // 2], ('req', 'head'), pairs))  4.87 us
    pallas_call x1, Pallas kernels, fetch_down(): pl.pallas_call(fetch_down_kernel, out_shape=(pltpu.VMEM((head_count, tota...  4.15 us
    pallas_call x1, Pallas kernels, experts_whole(): pl.pallas_call(whole_kernel, out_shape=jax.ShapeDtypeStruct((tokens, tota...  3.76 us
    pallas_call x1, Pallas kernels, fetch(): pl.pallas_call(fetch_kernel, out_shape=(pltpu.VMEM(hidden.shape, jnp.bflo...  3.57 us
  transfers between devices with their start and end apart: 19, of which 11 were waited for; matrix products, arithmetic and copies ran while one was open for 0% of the time, Pallas kernels for 33%

profile of v7, /device:TPU:0, one launch (start us, length us, event | category | flops | bytes accessed | tf_op | source)
XLA Modules:
  0.0 69.5 jit_solution(9110308893209368757)
XLA Ops:
  0.0 0.5 collective-permute-start.1
  0.5 2.5 %collective-permute-start = (bf16[32,512]{1,0:T(8,128)(2,1)}, bf16[32,512]{1,0:T(8,128)(2,1)S(1)}, u32[]{:S(2)}, u32[]{:S(2)}) collective-permute-start(bf16[32,512]{1,0:T(8,128)(2,1)} %refs_0_.1), channel_id=1, source_target_pairs={{0,2},{1,3},{2,0},{3,1},{4,6},{5,7},{6,4},{7,5},{8,10},{9,11},{10,... | collective-permute-start | bytes 98312 | tf_op jit(solution)/shard_map/ppermute | solution.py:656
  3.0 0.1 collective-permute-start.2
  3.1 3.6 %fetch.1 = (bf16[32,512]{1,0:T(8,128)(2,1)S(1)}, bf16[3,4,512,512]{3,2,1,0:T(8,128)(2,1)S(1)}, bf16[32,1536,128]{2,1,0:T(8,128)(2,1)S(1)}, f32[32,128]{1,0:T(8,128)S(1)}, f32[32,128]{1,0:T(8,128)S(1)}) custom-call(s32[32]{0:T(128)} %lengths_ref.3, s32[1]{0:T(128)} %bitcast.me_ref, f32[1,128]{1,0:T(1,128)S(1)} %fusion.2.freqs_ref, bf16[32,512]{1,0:T(8,128)(2,1)} %refs_0_.1, ...), custom_call_target="tpu_custom_call" | custom-call | bytes 12582912 | tf_op jit(solution)/shard_map/fetch/pallas_call | solution.py:73
  6.7 0.0 collective-permute-done.1.refs_1_
  6.7 0.0 collective-permute-done.refs_2_.refs_1_
  6.7 0.0 collective-permute-done.2.refs_3_
  6.7 0.0 copy-start.1
  6.8 0.0 copy-start.2
  6.8 8.5 %attention.1 = (bf16[32,1024]{1,0:T(8,128)(2,1)S(1)}, bf16[32,1024]{1,0:T(8,128)(2,1)S(1)}, bf16[32,1536,128]{2,1,0:T(8,128)(2,1)S(1)}) custom-call(s32[32]{0:T(128)} %lengths_ref.3, s32[1]{0:T(128)} %bitcast.me_ref, f32[32,128]{1,0:T(8,128)S(1)} %get-tuple-element.27.cos_ref, ...), custom_call_target="tpu_custom_call", output_to_operand_aliasing={{2}: (9, {})} | custom-call | flops 268435456 | bytes 5242880 | tf_op jit(solution)/shard_map/attention/pallas_call | solution.py:258
  15.3 0.0 copy-start
  15.3 0.2 collective-permute-start.3
  15.5 0.0 copy-done.1
  15.5 0.1 copy.16
  15.5 0.0 copy-done.2
  15.5 0.1 copy.17
  15.6 1.0 %collective-permute-done.3 = bf16[32,1024]{1,0:T(8,128)(2,1)S(1)} collective-permute-done((bf16[32,1024]{1,0:T(8,128)(2,1)S(1)}, bf16[32,1024]{1,0:T(8,128)(2,1)S(1)}, u32[]{:S(2)}, u32[]{:S(2)}) %collective-permute-start.3) | collective-permute-done | bytes 65568 | tf_op jit(solution)/shard_map/ppermute | solution.py:656
  16.6 1.8 %collective-permute-start.4 = (bf16[32,1024]{1,0:T(8,128)(2,1)S(1)}, bf16[32,1024]{1,0:T(8,128)(2,1)S(1)}, u32[]{:S(2)}, u32[]{:S(2)}) collective-permute-start(bf16[32,1024]{1,0:T(8,128)(2,1)S(1)} %add_convert_fusion.1.refs_0_.refs_2_), channel_id=1, source_target_pairs={{0,2},{1,3},{2,0},{3,1},{4,6},{5,7},{6,4},{7,5},{8,10},{9,11},{10,... | collective-permute-start | bytes 196616 | tf_op jit(solution)/shard_map/ppermute | solution.py:656
  18.4 0.2 select_reduce_fusion
  18.6 3.7 %by_expert_0.1 = (bf16[16,4,512,256]{3,2,1,0:T(8,128)(2,1)S(1)}, f32[8,128]{1,0:T(8,128)S(1)}) custom-call(s32[1]{0:T(128)} %bitcast.me_ref, bf16[2048,16,256]{2,1,0:T(8,128)(2,1)} %w_ref.5, bf16[32,1024]{1,0:T(8,128)(2,1)S(1)} %add_convert_fusion.1.refs_0_.refs_2_), custom_call_target="tpu_custom_call" | custom-call | bytes 16777216 | tf_op jit(solution)/shard_map/by_expert_0/pallas_call | solution.py:329
  22.3 0.0 collective-permute-done.4.refs_3_
  22.3 0.0 copy-done
  22.4 3.7 %collective-permute-start.7 = (bf16[32,1152]{1,0:T(8,128)(2,1)S(1)}, bf16[32,1152]{1,0:T(8,128)(2,1)S(1)}, u32[]{:S(2)}, u32[]{:S(2)}) collective-permute-start(bf16[32,1152]{1,0:T(8,128)(2,1)S(1)} %get-tuple-element.35.refs_1_.refs_0_), channel_id=1, source_target_pairs={{0,24},{4,28},{8,16},{12,20},{16,8},{20,12},{24,0},{28,4},{1,25},{... | collective-permute-start | bytes 221192 | tf_op jit(solution)/shard_map/ppermute | solution.py:656
  26.0 0.0 collective-permute-start.6
  26.0 0.8 %collective-permute-start.5 = (bf16[32,1152]{1,0:T(8,128)(2,1)S(1)}, bf16[32,1152]{1,0:T(8,128)(2,1)S(1)}, u32[]{:S(2)}, u32[]{:S(2)}) collective-permute-start(bf16[32,1152]{1,0:T(8,128)(2,1)S(1)} %get-tuple-element.35.refs_1_.refs_0_), channel_id=1, source_target_pairs={{0,8},{4,12},{8,0},{12,4},{16,24},{20,28},{24,16},{28,20},{1,9},{5... | collective-permute-start | bytes 221192 | tf_op jit(solution)/shard_map/ppermute | solution.py:656
  26.8 3.7 %by_expert_2.1 = (bf16[16,4,512,256]{3,2,1,0:T(8,128)(2,1)S(1)}, f32[8,128]{1,0:T(8,128)S(1)}) custom-call(s32[1]{0:T(128)} %bitcast.me_ref, bf16[2048,16,256]{2,1,0:T(8,128)(2,1)} %w_ref.5, bf16[16,4,512,256]{3,2,1,0:T(8,128)(2,1)S(1)} %get-tuple-element.36.refs_0_, ...), custom_call_target="tpu_custom_call", output_to_operand_aliasing={{0}: (2, {})} | custom-call | bytes 16777216 | tf_op jit(solution)/shard_map/by_expert_2/pallas_call | solution.py:329
  30.6 0.0 collective-permute-done.7.refs_3_
  30.6 2.2 %collective-permute-done.6.refs_2_ = bf16[32,1152]{1,0:T(8,128)(2,1)S(1)} collective-permute-done((bf16[32,1152]{1,0:T(8,128)(2,1)S(1)}, bf16[32,1152]{1,0:T(8,128)(2,1)S(1)}, u32[]{:S(2)}, u32[]{:S(2)}) %collective-permute-start.6) | collective-permute-done | bytes 73760 | tf_op jit(solution)/shard_map/ppermute | solution.py:656
  32.7 0.0 collective-permute-done.5.refs_1_
  32.8 0.1 collective-permute-start.8
  32.8 1.0 %collective-permute-start.11 = (bf16[128,1152]{1,0:T(8,128)(2,1)S(1)}, bf16[128,1152]{1,0:T(8,128)(2,1)S(1)}, u32[]{:S(2)}, u32[]{:S(2)}) collective-permute-start(bf16[128,1152]{1,0:T(8,128)(2,1)S(1)} %stack.1.mine_ref), channel_id=1, source_target_pairs={{0,4},{4,0},{8,12},{12,8},{16,20},{20,16},{24,28},{28,24},{1,5},{5... | collective-permute-start | bytes 884744 | tf_op jit(solution)/shard_map/ppermute | solution.py:656
  33.8 0.6 collective-permute-done.8.other_ref
  34.4 3.8 %experts_whole.1._.units_ref = bf16[128,2048]{1,0:T(8,128)(2,1)S(1)} custom-call(s32[1]{0:T(128)} %bitcast.me_ref, bf16[128,1152]{1,0:T(8,128)(2,1)S(1)} %stack.1.mine_ref, bf16[128,1152]{1,0:T(8,128)(2,1)S(1)} %collective-permute-done.8.other_ref, bf16[16,4,512,256]{3,2,1,0:T(8,128)(2,1)S(1)} %get-tuple-element.38.w_ref, ...), custom_call_target="tpu_custom_call" | custom-call | flops 2147483648 | bytes 16777216 | tf_op jit(solution)/shard_map/experts_whole/pallas_call | solution.py:527
  38.2 4.1 %fetch_down.1 = (bf16[4,2048,512]{2,1,0:T(8,128)(2,1)S(1)}, f32[8,128]{1,0:T(8,128)}) custom-call(s32[1]{0:T(128)} %bitcast.me_ref, bf16[2048,2048]{1,0:T(8,128)(2,1)} %bitcast.6, bf16[128,2048]{1,0:T(8,128)(2,1)S(1)} %experts_whole.1._.units_ref), custom_call_target="tpu_custom_call" | custom-call | bytes 16777216 | tf_op jit(solution)/shard_map/fetch_down/pallas_call | solution.py:416
  42.3 1.3 %down.2 = (bf16[128,1024]{1,0:T(8,128)(2,1)S(1)}, bf16[128,1024]{1,0:T(8,128)(2,1)S(1)}) custom-call(bf16[128,2048]{1,0:T(8,128)(2,1)S(1)} %experts_whole.1._.units_ref, bf16[4,2048,512]{2,1,0:T(8,128)(2,1)S(1)} %get-tuple-element.39.w_ref.w_down_ref), custom_call_target="tpu_custom_call" | custom-call | flops 1073741824 | bytes 8388608 | tf_op jit(solution)/shard_map/down/pallas_call | solution.py:600
  43.6 0.2 collective-permute-start.9
  43.8 0.0 collective-permute-done.11.value_ref
  43.8 0.4 collective-permute-start.12
  44.2 1.0 %collective-permute-done.9.sent_ref = bf16[128,1024]{1,0:T(8,128)(2,1)S(1)} collective-permute-done((bf16[128,1024]{1,0:T(8,128)(2,1)S(1)}, bf16[128,1024]{1,0:T(8,128)(2,1)S(1)}, u32[]{:S(2)}, u32[]{:S(2)}) %collective-permute-start.9) | collective-permute-done | bytes 262176 | tf_op jit(solution)/shard_map/ppermute | solution.py:656
  45.2 0.1 sum.2
  45.3 1.8 %experts_first.1.product_ref = f32[16,128,256]{2,1,0:T(8,128)S(1)} custom-call(bf16[128,1152]{1,0:T(8,128)(2,1)S(1)} %hold.1.mine_ref, bf16[16,4,512,256]{3,2,1,0:T(8,128)(2,1)S(1)} %get-tuple-element.38.w_ref, bf16[128,512]{1,0:T(8,128)(2,1)S(1)} %get-tuple-element.43._), custom_call_target="tpu_custom_call" | custom-call | flops 1073741824 | bytes 8388608 | tf_op jit(solution)/shard_map/experts_first/pallas_call | solution.py:547
  47.1 0.0 collective-permute-done.12.other_ref
  47.1 3.3 %experts_second.1 = (bf16[128,2048]{1,0:T(8,128)(2,1)S(1)}, bf16[128,1024]{1,0:T(8,128)(2,1)S(1)}) custom-call(s32[1]{0:T(128)} %bitcast.me_ref, bf16[128,1152]{1,0:T(8,128)(2,1)S(1)} %hold.1.mine_ref, bf16[128,1152]{1,0:T(8,128)(2,1)S(1)} %collective-permute-done.12.other_ref, f32[16,128,256]{2,1,0:T(8,128)S(1)} %experts_first.1.product_ref, ...), custom_call_target="tpu_custom_call" | custom-call | flops 1073741824 | bytes 8388608 | tf_op jit(solution)/shard_map/experts_second/pallas_call | solution.py:565
  50.4 0.2 collective-permute-start.13
  50.6 0.5 collective-permute-start.10
  51.1 0.7 %down.3.keep_ref = bf16[128,1024]{1,0:T(8,128)(2,1)S(1)} custom-call(bf16[128,2048]{1,0:T(8,128)(2,1)S(1)} %get-tuple-element.44.units_ref, bf16[4,2048,512]{2,1,0:T(8,128)(2,1)S(1)} %get-tuple-element.39.w_ref.w_down_ref), custom_call_target="tpu_custom_call" | custom-call | flops 536870912 | bytes 4194304 | tf_op jit(solution)/shard_map/down/pallas_call | solution.py:600
  51.8 0.2 collective-permute-done.13.sent_ref
  52.0 0.1 sum.3
  52.1 1.0 %collective-permute-start.14 = (bf16[128,512]{1,0:T(8,128)(2,1)S(1)}, bf16[128,512]{1,0:T(8,128)(2,1)S(1)}, u32[]{:S(2)}, u32[]{:S(2)}) collective-permute-start(bf16[128,512]{1,0:T(8,128)(2,1)S(1)} %get-tuple-element.46), channel_id=1, source_target_pairs={{0,4},{1,5},{2,6},{3,7},{4,0},{5,1},{6,2},{7,3},{8,12},{9,13},{10,... | collective-permute-start | bytes 393224 | tf_op jit(solution)/shard_map/ppermute | solution.py:722
  53.1 1.9 %collective-permute-start.15 = (bf16[128,512]{1,0:T(8,128)(2,1)S(1)}, bf16[128,512]{1,0:T(8,128)(2,1)S(1)}, u32[]{:S(2)}, u32[]{:S(2)}) collective-permute-start(bf16[128,512]{1,0:T(8,128)(2,1)S(1)} %get-tuple-element.47), channel_id=1, source_target_pairs={{0,6},{1,7},{2,4},{3,5},{4,2},{5,3},{6,0},{7,1},{8,14},{9,15},{10,... | collective-permute-start | bytes 393224 | tf_op jit(solution)/shard_map/ppermute | solution.py:722
  55.0 1.4 %collective-permute-done.10 = bf16[128,512]{1,0:T(8,128)(2,1)S(1)} collective-permute-done((bf16[128,512]{1,0:T(8,128)(2,1)S(1)}, bf16[128,512]{1,0:T(8,128)(2,1)S(1)}, u32[]{:S(2)}, u32[]{:S(2)}) %collective-permute-start.10) | collective-permute-done | bytes 131104 | tf_op jit(solution)/shard_map/ppermute | solution.py:656
  56.4 2.1 %collective-permute-done.14 = bf16[128,512]{1,0:T(8,128)(2,1)S(1)} collective-permute-done((bf16[128,512]{1,0:T(8,128)(2,1)S(1)}, bf16[128,512]{1,0:T(8,128)(2,1)S(1)}, u32[]{:S(2)}, u32[]{:S(2)}) %collective-permute-start.14) | collective-permute-done | bytes 131104 | tf_op jit(solution)/shard_map/ppermute | solution.py:722
  58.5 2.8 %collective-permute-done.15 = bf16[128,512]{1,0:T(8,128)(2,1)S(1)} collective-permute-done((bf16[128,512]{1,0:T(8,128)(2,1)S(1)}, bf16[128,512]{1,0:T(8,128)(2,1)S(1)}, u32[]{:S(2)}, u32[]{:S(2)}) %collective-permute-start.15) | collective-permute-done | bytes 131104 | tf_op jit(solution)/shard_map/ppermute | solution.py:722
  61.2 0.1 add_convert_fusion
  61.3 0.8 %collective-permute-start.16 = (bf16[32,512]{1,0:T(8,128)(2,1)S(1)}, bf16[32,512]{1,0:T(8,128)(2,1)S(1)}, u32[]{:S(2)}, u32[]{:S(2)}) collective-permute-start(bf16[32,512]{1,0:T(8,128)(2,1)S(1)} %get-tuple-element.49), channel_id=1, source_target_pairs={{0,8},{4,12},{8,0},{12,4},{16,24},{20,28},{24,16},{28,20},{1,9},{5... | collective-permute-start | bytes 98312 | tf_op jit(solution)/shard_map/ppermute | solution.py:656
  62.1 1.6 %collective-permute-start.18 = (bf16[32,512]{1,0:T(8,128)(2,1)S(1)}, bf16[32,512]{1,0:T(8,128)(2,1)S(1)}, u32[]{:S(2)}, u32[]{:S(2)}) collective-permute-start(bf16[32,512]{1,0:T(8,128)(2,1)S(1)} %get-tuple-element.50), channel_id=1, source_target_pairs={{0,24},{4,28},{8,16},{12,20},{16,8},{20,12},{24,0},{28,4},{1,25},{... | collective-permute-start | bytes 98312 | tf_op jit(solution)/shard_map/ppermute | solution.py:656
  63.7 1.2 %collective-permute-start.17 = (bf16[32,512]{1,0:T(8,128)(2,1)S(1)}, bf16[32,512]{1,0:T(8,128)(2,1)S(1)}, u32[]{:S(2)}, u32[]{:S(2)}) collective-permute-start(bf16[32,512]{1,0:T(8,128)(2,1)S(1)} %get-tuple-element.51), channel_id=1, source_target_pairs={{0,16},{4,20},{8,24},{12,28},{16,0},{20,4},{24,8},{28,12},{1,17},{... | collective-permute-start | bytes 98312 | tf_op jit(solution)/shard_map/ppermute | solution.py:656
  64.9 0.4 collective-permute-done.16
  65.3 2.5 %collective-permute-done.18 = bf16[32,512]{1,0:T(8,128)(2,1)S(1)} collective-permute-done((bf16[32,512]{1,0:T(8,128)(2,1)S(1)}, bf16[32,512]{1,0:T(8,128)(2,1)S(1)}, u32[]{:S(2)}, u32[]{:S(2)}) %collective-permute-start.18) | collective-permute-done | bytes 32800 | tf_op jit(solution)/shard_map/ppermute | solution.py:656
  67.8 1.0 %collective-permute-done.17 = bf16[32,512]{1,0:T(8,128)(2,1)S(1)} collective-permute-done((bf16[32,512]{1,0:T(8,128)(2,1)S(1)}, bf16[32,512]{1,0:T(8,128)(2,1)S(1)}, u32[]{:S(2)}, u32[]{:S(2)}) %collective-permute-start.17) | collective-permute-done | bytes 32800 | tf_op jit(solution)/shard_map/ppermute | solution.py:656
  68.8 0.6 add_convert_fusion.2
  (7 shorter events, 0.1 us)
Async XLA Ops:
  0.0 6.7 %collective-permute-start.1 = (bf16[32,512]{1,0:T(8,128)(2,1)}, bf16[32,512]{1,0:T(8,128)(2,1)S(1)}, u32[]{:S(2)}, u32[]{:S(2)}) collective-permute-start(bf16[32,512]{1,0:T(8,128)(2,1)} %refs_0_.1), channel_id=1, source_target_pairs={{0,1},{1,0},{2,3},{3,2},{4,5},{5,4},{6,7},{7,6},{8,9},{9,8},{10,11... | collective-permute-start | bytes 98312 | tf_op jit(solution)/shard_map/ppermute | solution.py:656
  0.5 6.3 %collective-permute-start = (bf16[32,512]{1,0:T(8,128)(2,1)}, bf16[32,512]{1,0:T(8,128)(2,1)S(1)}, u32[]{:S(2)}, u32[]{:S(2)}) collective-permute-start(bf16[32,512]{1,0:T(8,128)(2,1)} %refs_0_.1), channel_id=1, source_target_pairs={{0,2},{1,3},{2,0},{3,1},{4,6},{5,7},{6,4},{7,5},{8,10},{9,11},{10,... | collective-permute-start | bytes 98312 | tf_op jit(solution)/shard_map/ppermute | solution.py:656
  3.0 3.8 %collective-permute-start.2 = (bf16[32,512]{1,0:T(8,128)(2,1)}, bf16[32,512]{1,0:T(8,128)(2,1)S(1)}, u32[]{:S(2)}, u32[]{:S(2)}) collective-permute-start(bf16[32,512]{1,0:T(8,128)(2,1)} %refs_0_.1), channel_id=1, source_target_pairs={{0,3},{1,2},{2,1},{3,0},{4,7},{5,6},{6,5},{7,4},{8,11},{9,10},{10,... | collective-permute-start | bytes 98312 | tf_op jit(solution)/shard_map/ppermute | solution.py:656
  6.7 8.7 %copy-start.1 = (s32[32,8]{0,1:T(8,128)S(1)}, s32[32,8]{0,1:T(8,128)}, u32[]{:S(2)}) copy-start(s32[32,8]{0,1:T(8,128)} %param.12) | copy-start | bytes 3076
  6.8 8.8 %copy-start.2 = (f32[32,8]{0,1:T(8,128)S(1)}, f32[32,8]{0,1:T(8,128)}, u32[]{:S(2)}) copy-start(f32[32,8]{0,1:T(8,128)} %param.13) | copy-start | bytes 3076
  15.3 7.0 %copy-start = (bf16[32,512]{1,0:T(8,128)(2,1)S(1)}, bf16[32,512]{1,0:T(8,128)(2,1)}, u32[]{:S(2)}) copy-start(bf16[32,512]{1,0:T(8,128)(2,1)} %refs_0_.1) | copy-start | bytes 98308
  15.3 1.3 %collective-permute-start.3 = (bf16[32,1024]{1,0:T(8,128)(2,1)S(1)}, bf16[32,1024]{1,0:T(8,128)(2,1)S(1)}, u32[]{:S(2)}, u32[]{:S(2)}) collective-permute-start(bf16[32,1024]{1,0:T(8,128)(2,1)S(1)} %get-tuple-element.33), channel_id=1, source_target_pairs={{0,1},{1,0},{2,3},{3,2},{4,5},{5,4},{6,7},{7,6},{8,9},{9,8},{10,11... | collective-permute-start | bytes 196616 | tf_op jit(solution)/shard_map/ppermute | solution.py:656
  16.6 5.7 %collective-permute-start.4 = (bf16[32,1024]{1,0:T(8,128)(2,1)S(1)}, bf16[32,1024]{1,0:T(8,128)(2,1)S(1)}, u32[]{:S(2)}, u32[]{:S(2)}) collective-permute-start(bf16[32,1024]{1,0:T(8,128)(2,1)S(1)} %add_convert_fusion.1.refs_0_.refs_2_), channel_id=1, source_target_pairs={{0,2},{1,3},{2,0},{3,1},{4,6},{5,7},{6,4},{7,5},{8,10},{9,11},{10,... | collective-permute-start | bytes 196616 | tf_op jit(solution)/shard_map/ppermute | solution.py:656
  22.4 8.2 %collective-permute-start.7 = (bf16[32,1152]{1,0:T(8,128)(2,1)S(1)}, bf16[32,1152]{1,0:T(8,128)(2,1)S(1)}, u32[]{:S(2)}, u32[]{:S(2)}) collective-permute-start(bf16[32,1152]{1,0:T(8,128)(2,1)S(1)} %get-tuple-element.35.refs_1_.refs_0_), channel_id=1, source_target_pairs={{0,24},{4,28},{8,16},{12,20},{16,8},{20,12},{24,0},{28,4},{1,25},{... | collective-permute-start | bytes 221192 | tf_op jit(solution)/shard_map/ppermute | solution.py:656
  26.0 6.7 %collective-permute-start.6 = (bf16[32,1152]{1,0:T(8,128)(2,1)S(1)}, bf16[32,1152]{1,0:T(8,128)(2,1)S(1)}, u32[]{:S(2)}, u32[]{:S(2)}) collective-permute-start(bf16[32,1152]{1,0:T(8,128)(2,1)S(1)} %get-tuple-element.35.refs_1_.refs_0_), channel_id=1, source_target_pairs={{0,16},{4,20},{8,24},{12,28},{16,0},{20,4},{24,8},{28,12},{1,17},{... | collective-permute-start | bytes 221192 | tf_op jit(solution)/shard_map/ppermute | solution.py:656
  26.0 6.7 %collective-permute-start.5 = (bf16[32,1152]{1,0:T(8,128)(2,1)S(1)}, bf16[32,1152]{1,0:T(8,128)(2,1)S(1)}, u32[]{:S(2)}, u32[]{:S(2)}) collective-permute-start(bf16[32,1152]{1,0:T(8,128)(2,1)S(1)} %get-tuple-element.35.refs_1_.refs_0_), channel_id=1, source_target_pairs={{0,8},{4,12},{8,0},{12,4},{16,24},{20,28},{24,16},{28,20},{1,9},{5... | collective-permute-start | bytes 221192 | tf_op jit(solution)/shard_map/ppermute | solution.py:656
  32.8 1.6 %collective-permute-start.8 = (bf16[128,1152]{1,0:T(8,128)(2,1)S(1)}, bf16[128,1152]{1,0:T(8,128)(2,1)S(1)}, u32[]{:S(2)}, u32[]{:S(2)}) collective-permute-start(bf16[128,1152]{1,0:T(8,128)(2,1)S(1)} %stack.1.mine_ref), channel_id=1, source_target_pairs={{0,1},{1,0},{2,3},{3,2},{4,5},{5,4},{6,7},{7,6},{8,9},{9,8},{10,11... | collective-permute-start | bytes 884744 | tf_op jit(solution)/shard_map/ppermute | solution.py:656
  32.8 11.0 %collective-permute-start.11 = (bf16[128,1152]{1,0:T(8,128)(2,1)S(1)}, bf16[128,1152]{1,0:T(8,128)(2,1)S(1)}, u32[]{:S(2)}, u32[]{:S(2)}) collective-permute-start(bf16[128,1152]{1,0:T(8,128)(2,1)S(1)} %stack.1.mine_ref), channel_id=1, source_target_pairs={{0,4},{4,0},{8,12},{12,8},{16,20},{20,16},{24,28},{28,24},{1,5},{5... | collective-permute-start | bytes 884744 | tf_op jit(solution)/shard_map/ppermute | solution.py:656
  43.6 1.6 %collective-permute-start.9 = (bf16[128,1024]{1,0:T(8,128)(2,1)S(1)}, bf16[128,1024]{1,0:T(8,128)(2,1)S(1)}, u32[]{:S(2)}, u32[]{:S(2)}) collective-permute-start(bf16[128,1024]{1,0:T(8,128)(2,1)S(1)} %get-tuple-element.41.after_ref), channel_id=1, source_target_pairs={{0,1},{1,0},{2,3},{3,2},{4,5},{5,4},{6,7},{7,6},{8,9},{9,8},{10,11... | collective-permute-start | bytes 786440 | tf_op jit(solution)/shard_map/ppermute | solution.py:656
  43.8 3.3 %collective-permute-start.12 = (bf16[128,1152]{1,0:T(8,128)(2,1)S(1)}, bf16[128,1152]{1,0:T(8,128)(2,1)S(1)}, u32[]{:S(2)}, u32[]{:S(2)}) collective-permute-start(bf16[128,1152]{1,0:T(8,128)(2,1)S(1)} %hold.1.mine_ref), channel_id=1, source_target_pairs={{0,1},{1,0},{2,3},{3,2},{4,5},{5,4},{6,7},{7,6},{8,9},{9,8},{10,11... | collective-permute-start | bytes 884744 | tf_op jit(solution)/shard_map/ppermute | solution.py:656
  50.4 1.6 %collective-permute-start.13 = (bf16[128,1024]{1,0:T(8,128)(2,1)S(1)}, bf16[128,1024]{1,0:T(8,128)(2,1)S(1)}, u32[]{:S(2)}, u32[]{:S(2)}) collective-permute-start(bf16[128,1024]{1,0:T(8,128)(2,1)S(1)} %get-tuple-element.45), channel_id=1, source_target_pairs={{0,1},{1,0},{2,3},{3,2},{4,5},{5,4},{6,7},{7,6},{8,9},{9,8},{10,11... | collective-permute-start | bytes 786440 | tf_op jit(solution)/shard_map/ppermute | solution.py:656
  50.6 5.8 %collective-permute-start.10 = (bf16[128,512]{1,0:T(8,128)(2,1)S(1)}, bf16[128,512]{1,0:T(8,128)(2,1)S(1)}, u32[]{:S(2)}, u32[]{:S(2)}) collective-permute-start(bf16[128,512]{1,0:T(8,128)(2,1)S(1)} %get-tuple-element.43._), channel_id=1, source_target_pairs={{0,2},{1,3},{2,0},{3,1},{4,6},{5,7},{6,4},{7,5},{8,10},{9,11},{10,... | collective-permute-start | bytes 393224 | tf_op jit(solution)/shard_map/ppermute | solution.py:656
  52.1 6.4 %collective-permute-start.14 = (bf16[128,512]{1,0:T(8,128)(2,1)S(1)}, bf16[128,512]{1,0:T(8,128)(2,1)S(1)}, u32[]{:S(2)}, u32[]{:S(2)}) collective-permute-start(bf16[128,512]{1,0:T(8,128)(2,1)S(1)} %get-tuple-element.46), channel_id=1, source_target_pairs={{0,4},{1,5},{2,6},{3,7},{4,0},{5,1},{6,2},{7,3},{8,12},{9,13},{10,... | collective-permute-start | bytes 393224 | tf_op jit(solution)/shard_map/ppermute | solution.py:722
  53.1 8.2 %collective-permute-start.15 = (bf16[128,512]{1,0:T(8,128)(2,1)S(1)}, bf16[128,512]{1,0:T(8,128)(2,1)S(1)}, u32[]{:S(2)}, u32[]{:S(2)}) collective-permute-start(bf16[128,512]{1,0:T(8,128)(2,1)S(1)} %get-tuple-element.47), channel_id=1, source_target_pairs={{0,6},{1,7},{2,4},{3,5},{4,2},{5,3},{6,0},{7,1},{8,14},{9,15},{10,... | collective-permute-start | bytes 393224 | tf_op jit(solution)/shard_map/ppermute | solution.py:722
  61.3 4.0 %collective-permute-start.16 = (bf16[32,512]{1,0:T(8,128)(2,1)S(1)}, bf16[32,512]{1,0:T(8,128)(2,1)S(1)}, u32[]{:S(2)}, u32[]{:S(2)}) collective-permute-start(bf16[32,512]{1,0:T(8,128)(2,1)S(1)} %get-tuple-element.49), channel_id=1, source_target_pairs={{0,8},{4,12},{8,0},{12,4},{16,24},{20,28},{24,16},{28,20},{1,9},{5... | collective-permute-start | bytes 98312 | tf_op jit(solution)/shard_map/ppermute | solution.py:656
  62.1 5.7 %collective-permute-start.18 = (bf16[32,512]{1,0:T(8,128)(2,1)S(1)}, bf16[32,512]{1,0:T(8,128)(2,1)S(1)}, u32[]{:S(2)}, u32[]{:S(2)}) collective-permute-start(bf16[32,512]{1,0:T(8,128)(2,1)S(1)} %get-tuple-element.50), channel_id=1, source_target_pairs={{0,24},{4,28},{8,16},{12,20},{16,8},{20,12},{24,0},{28,4},{1,25},{... | collective-permute-start | bytes 98312 | tf_op jit(solution)/shard_map/ppermute | solution.py:656
  63.7 5.2 %collective-permute-start.17 = (bf16[32,512]{1,0:T(8,128)(2,1)S(1)}, bf16[32,512]{1,0:T(8,128)(2,1)S(1)}, u32[]{:S(2)}, u32[]{:S(2)}) collective-permute-start(bf16[32,512]{1,0:T(8,128)(2,1)S(1)} %get-tuple-element.51), channel_id=1, source_target_pairs={{0,16},{4,20},{8,24},{12,28},{16,0},{20,4},{24,8},{28,12},{1,17},{... | collective-permute-start | bytes 98312 | tf_op jit(solution)/shard_map/ppermute | solution.py:656

commit v8 on v7

--- a/solution.py
+++ b/solution.py
@@ -33,8 +33,8 @@
 
 
 def fetch_kernel(
-    lengths_ref, me_ref, freqs_ref, own_ref, w_ref,
-    own_out_ref, w_out_ref, blank_ref, cos_ref, sin_ref, angle_s, sem, own_sem,
+    lengths_hbm, me_ref, freqs_ref, own_ref, w_ref,
+    own_out_ref, w_out_ref, blank_ref, cos_ref, sin_ref, lengths_ref, angle_s, sem, own_sem, len_sem,
 ):
     head_count, cols = w_out_ref.shape[1:3]
     chunk_rows = CHUNK * cols // LANES
@@ -48,13 +48,21 @@
                     w_ref.at[c, pl.ds(first, cols)], w_out_ref.at[c, j], sem.at[c, j]
                 )
             )
+    lengths_copy = pltpu.make_async_copy(lengths_hbm, lengths_ref, len_sem)
+    lengths_copy.start()
     for copy in copies:
         copy.start()
-
-    @pl.loop(0, blank_ref.shape[0])
+    lengths_copy.wait()
+
+    rows = angle_s.shape[0]
+    cache_rows = blank_ref.shape[0] // rows
+
+    @pl.loop(0, rows)
     def _(r):
-        last = pl.multiple_of((lengths_ref[r] - 1) // CHUNK * chunk_rows, chunk_rows)
-        blank_ref[r, pl.ds(last, chunk_rows)] = jnp.zeros((chunk_rows, LANES), jnp.bfloat16)
+        last = r * cache_rows + (lengths_ref[r] - 1) // CHUNK * chunk_rows
+        blank_ref[pl.ds(pl.multiple_of(last, chunk_rows), chunk_rows)] = jnp.zeros(
+            (chunk_rows, LANES), jnp.bfloat16
+        )
         angle_s[pl.ds(r, 1), :] = lengths_ref[r].astype(jnp.float32) * freqs_ref[...]
 
     cos_ref[...] = jnp.cos(angle_s[...])
@@ -78,12 +86,14 @@
             pltpu.VMEM(v_shape, jnp.bfloat16),
             pltpu.VMEM((rows, LANES), jnp.float32),
             pltpu.VMEM((rows, LANES), jnp.float32),
-        ),
-        in_specs=[SMEM, SMEM, VMEM, ANY, ANY],
-        out_specs=[VMEM] * 5,
+            pltpu.SMEM(lengths.shape, lengths.dtype),
+        ),
+        in_specs=[ANY, SMEM, VMEM, ANY, ANY],
+        out_specs=[VMEM] * 5 + [SMEM],
         scratch_shapes=[
             pltpu.VMEM((rows, LANES), jnp.float32),
             pltpu.SemaphoreType.DMA((w_qkv.shape[0], head_count)),
+            pltpu.SemaphoreType.DMA(()),
             pltpu.SemaphoreType.DMA(()),
         ],
         compiler_params=pltpu.CompilerParams(vmem_limit_bytes=8 * 2**20),
@@ -97,8 +107,8 @@
 def attention_kernel(head_count, lengths_ref, me_ref, cos_ref, sin_ref, *refs):
     pieces = refs[:head_count]
     (
-        w_qkv_ref, _, w_out_ref, k_ref, v_ref, keep_ref, send_ref, v_s,
-        w_out_s, k_s, query_s, key_s, value_s, attended_s, out_sem, k_sem, v_sem,
+        w_qkv_ref, _, w_out_ref, k_ref, v_ref, w_down_ref, keep_ref, send_ref, v_s, down_ref,
+        w_out_s, k_s, query_s, key_s, value_s, attended_s, out_sem, k_sem, v_sem, down_sem,
     ) = refs[head_count:]
     rows, cols = pieces[0].shape
     heads_local = cols // LANES
@@ -111,19 +121,30 @@
             w_out_ref.at[:, pl.ds(first, cols)], w_out_s.at[j], out_sem.at[j]
         )
 
-    def cache_copy(source, target, sem, r):
-        used = used_rows(lengths_ref[r], heads_local)
+    cache_rows = k_s.shape[0] // rows
+
+    def cache_copy(source, target, sem, r, used):
+        taken = pl.ds(pl.multiple_of(r * cache_rows, cache_rows), used)
         return pltpu.make_async_copy(
-            source.at[r, pl.ds(0, used)], target.at[r, pl.ds(0, used)], sem.at[r]
+            source.at[taken], target.at[taken], sem.at[r // GROUP]
         )
 
     @pl.loop(0, rows, unroll=4)
     def _(r):
-        cache_copy(k_ref, k_s, k_sem, r).start()
-        cache_copy(v_ref, v_s, v_sem, r).start()
+        used = used_rows(lengths_ref[r], heads_local)
+        cache_copy(k_ref, k_s, k_sem, r, used).start()
+        cache_copy(v_ref, v_s, v_sem, r, used).start()
+
+    def down_copy(j):
+        first = pl.multiple_of((me ^ j) * cols, cols)
+        return pltpu.make_async_copy(
+            w_down_ref.at[:, pl.ds(first, cols)], down_ref.at[j], down_sem.at[j]
+        )
 
     for j in range(head_count):
         out_copy(j).start()
+    for j in range(head_count):
+        down_copy(j).start()
 
     if heads_local < SUBLANES:
         query_s[...] = jnp.zeros_like(query_s)
@@ -170,16 +191,17 @@
         own = [jnp.concatenate([a, b], axis=0) for a, b in zip(own[::2], own[1::2])]
         values = [diagonal(value_s[a], value_s[b]) for a, b in pairs]
         longest = functools.reduce(jnp.maximum, lengths)
-        for r in requests:
-            cache_copy(k_ref, k_s, k_sem, r).wait()
-            cache_copy(v_ref, v_s, v_sem, r).wait()
+        used = used_rows(sum((length + 7) // 8 * 8 for length in lengths), heads_local)
+        cache_copy(k_ref, k_s, k_sem, g * GROUP, used).wait()
+        cache_copy(v_ref, v_s, v_sem, g * GROUP, used).wait()
 
         def with_chunks(count):
             def both(ref, c, pair, span):
                 parts = []
                 for r, length in zip(pair, span):
                     first = jnp.minimum(c, (length - 1) // CHUNK) * chunk_rows if c else 0
-                    parts.append(ref[r, pl.ds(pl.multiple_of(first, chunk_rows), chunk_rows)])
+                    first = pl.multiple_of(r * cache_rows + first, chunk_rows)
+                    parts.append(ref[pl.ds(first, chunk_rows)])
                 return jnp.concatenate(parts, axis=1)
 
             scores = [
@@ -235,7 +257,7 @@
                 attended_s[a] = summed[:SUBLANES, :LANES]
                 attended_s[b] = summed[SUBLANES:, LANES:]
 
-        for count in range(1, k_s.shape[1] // chunk_rows + 1):
+        for count in range(1, cache_rows // chunk_rows + 1):
             pl.when((longest + CHUNK - 1) // CHUNK == count)(
                 functools.partial(with_chunks, count)
             )
@@ -249,17 +271,24 @@
         target[:, j // 2 * cols : (j // 2 + 1) * cols] = jnp.dot(
             attended, w_out_s[j], preferred_element_type=jnp.float32
         ).astype(jnp.bfloat16)
-
-
-def attention(pieces, me, lengths, cosine, sine, w_qkv, room, w_out, k_cache, v_cache):
+    for j in range(head_count):
+        down_copy(j).wait()
+
+
+def attention(pieces, me, lengths, cosine, sine, w_qkv, room, w_out, k_cache, v_cache, w_down):
     head_count = len(pieces)
     rows, cols = pieces[0].shape
     half = jax.ShapeDtypeStruct((rows, head_count // 2 * cols), jnp.bfloat16)
     return pl.pallas_call(
         functools.partial(attention_kernel, head_count),
-        out_shape=(half, half, pltpu.VMEM(room.shape, jnp.bfloat16)),
-        in_specs=[SMEM, SMEM] + [VMEM] * (head_count + 4) + [ANY] * 3,
-        out_specs=(VMEM, VMEM, VMEM),
+        out_shape=(
+            half,
+            half,
+            pltpu.VMEM(room.shape, jnp.bfloat16),
+            pltpu.VMEM((head_count, w_down.shape[0], cols), jnp.bfloat16),
+        ),
+        in_specs=[SMEM, SMEM] + [VMEM] * (head_count + 4) + [ANY] * 4,
+        out_specs=(VMEM, VMEM, VMEM, VMEM),
         input_output_aliases={head_count + 5: 2},
         scratch_shapes=[
             pltpu.VMEM((head_count, cols, cols), jnp.bfloat16),
@@ -268,20 +297,21 @@
         + [pltpu.VMEM((rows, SUBLANES, LANES), jnp.float32)] * 4
         + [
             pltpu.SemaphoreType.DMA((head_count,)),
-            pltpu.SemaphoreType.DMA((rows,)),
-            pltpu.SemaphoreType.DMA((rows,)),
+            pltpu.SemaphoreType.DMA((rows // GROUP,)),
+            pltpu.SemaphoreType.DMA((rows // GROUP,)),
+            pltpu.SemaphoreType.DMA((head_count,)),
         ],
         compiler_params=pltpu.CompilerParams(vmem_limit_bytes=20 * 2**20),
         cost_estimate=pl.CostEstimate(
             flops=2 * rows * 4 * cols * head_count * cols,
-            bytes_accessed=2 * cols * cols * head_count + k_cache.size // 2,
+            bytes_accessed=2 * w_down.size + k_cache.size // 2,
             transcendentals=0,
         ),
         name="attention",
     )(
-        in_hbm(lengths), me, cosine, sine, *map(in_vmem, pieces), in_vmem(w_qkv), in_vmem(room),
-        in_hbm(w_out), in_hbm(k_cache), in_hbm(v_cache),
-    )[:2]
+        pltpu.with_memory_space_constraint(lengths, pltpu.SMEM), me, in_vmem(cosine), in_vmem(sine), *map(in_vmem, pieces), in_vmem(w_qkv), in_vmem(room),
+        in_hbm(w_out), in_hbm(k_cache), in_hbm(v_cache), in_hbm(w_down),
+    )
 
 
 RELAYOUT_ROWS = 128
@@ -397,39 +427,6 @@
     )(*parts, after)
 
 
-def fetch_down_kernel(me_ref, w_ref, _, out_ref, token_ref, sem):
-    token_ref[...] = jnp.zeros_like(token_ref)
-    head_count, _, cols = out_ref.shape
-    copies = []
-    for j in range(head_count):
-        first = pl.multiple_of((me_ref[0] ^ j) * cols, cols)
-        copies.append(
-            pltpu.make_async_copy(w_ref.at[:, pl.ds(first, cols)], out_ref.at[j], sem.at[j])
-        )
-        copies[-1].start()
-    for copy in copies:
-        copy.wait()
-
-
-def fetch_down(me, w_down, head_count, after):
-    total_units, width = w_down.shape
-    return pl.pallas_call(
-        fetch_down_kernel,
-        out_shape=(
-            pltpu.VMEM((head_count, total_units, width // head_count), jnp.bfloat16),
-            jax.ShapeDtypeStruct((SUBLANES, LANES), jnp.float32),
-        ),
-        in_specs=[SMEM, ANY, ANY],
-        out_specs=(VMEM, VMEM),
-        scratch_shapes=[pltpu.SemaphoreType.DMA((head_count,))],
-        compiler_params=pltpu.CompilerParams(vmem_limit_bytes=8 * 2**20),
-        cost_estimate=pl.CostEstimate(
-            flops=0, bytes_accessed=4 * w_down.size, transcendentals=0
-        ),
-        name="fetch_down",
-    )(me, in_hbm(w_down), after)
-
-
 def expert_products(states, w_ref, first, p, per_step):
     columns = w_ref.shape[3]
     depth = states.shape[1]
@@ -668,12 +665,12 @@
     even = range(0, head_size, 2)
 
     pieces = [hidden] + [swap(hidden, "head", head_size, j) for j in range(1, head_size)]
-    flat = (rows, k_cache.shape[1] * k_cache.shape[2], k_cache.shape[3])
-    own, w_near, room, cosine, sine = fetch(me_ref, lengths, hidden, w_qkv, flat, head_size)
-    keep, send = attention(
+    flat = (rows * k_cache.shape[1] * k_cache.shape[2], k_cache.shape[3])
+    own, w_near, room, cosine, sine, lengths_near = fetch(me_ref, lengths, hidden, w_qkv, flat, head_size)
+    keep, send, _, w_down_near = attention(
         [own] + pieces[1:],
         me_ref,
-        lengths,
+        lengths_near,
         cosine,
         sine,
         w_near,
@@ -681,6 +678,7 @@
         w_out,
         k_cache.reshape(flat),
         v_cache.reshape(flat),
+        w_down.reshape(experts_local * units_local, width),
     )
     half = keep.astype(jnp.float32) + swap(send, "head", head_size, 1).astype(jnp.float32)
     half = half.astype(jnp.bfloat16)
@@ -696,23 +694,23 @@
 
     steps = range(2, req_size, 2)
     line = [payload] + [swap(payload, "req", req_size, k) for k in steps]
-    w_down_flat = w_down.reshape(experts_local * units_local, width)
     buffer, token = by_expert(tuple(late), me_ref, w_in, head_size, buffer, payload)
     line = stack_part(line, token)
     crossed = swap(line, "req", req_size, 1)
     line_other = swap(line, "head", head_size, 1)
-    units = experts_whole(me_ref, line, line_other, buffer, token, w_down_flat.shape[0])
-    w_down_near, _ = fetch_down(me_ref, w_down_flat, head_size, units)
+    units = experts_whole(me_ref, line, line_other, buffer, token, w_down_near.shape[1])
     keep, send = down_part(units, w_down_near, (0, 1))
     crossed = hold(crossed, send)
     crossed_other = swap(crossed, "head", head_size, 1)
     line_sums = sum_part(keep, swap(send, "head", head_size, 1), cols, jnp.float32)
     total = line_sums[0]
-    got = [swap(line_sums[j // 2], "head", head_size, j) for j in even if j]
     products = experts_first(crossed, buffer, line_sums[-1])
     units, send = experts_second(me_ref, crossed, crossed_other, products, buffer, w_down_near)
     (keep,) = down_part(units, w_down_near, (0,))
     crossed_sums = sum_part(keep, swap(send, "head", head_size, 1), cols, jnp.bfloat16)
+    got = [
+        swap(hold(line_sums[j // 2], crossed_sums[0]), "head", head_size, j) for j in even if j
+    ]
     for j in even:
         pairs = [
             (r * head_size + h, (r ^ 1) * head_size + (h ^ j))

time: 70.1 us -> 68.3 us (0.974)
  Pallas kernels: 34.7 us -> 28.6 us
  local copies, waits for them, and re-layouts: 0.19 us -> 3.45 us
  starting transfers between devices: 18.3 us -> 19.5 us
    pallas_call x1 -> x0, Pallas kernels: 4.15 us -> none  [fetch_down(): pl.pallas_call(fetch_down_kernel, out_shape=(pltpu.VMEM((head_count, tota...]
    ppermute x17, waiting for transfers between devices: 10.3 us -> 14.4 us  [swap(): return lax.ppermute(value, axis, [(i, i ^ mask) for i in range(size)])]
    ppermute x2, waiting for transfers between devices: 4.87 us -> 1.23 us  [per_device(): got.append(lax.ppermute(crossed_sums[j // 2], ('req', 'head'), pairs))]
    unnamed x8 -> x14, local copies, waits for them, and re-layouts: 0.17 us -> 3.43 us
    pallas_call x1, Pallas kernels: 8.51 us -> 7.22 us  [attention(): pl.pallas_call(functools.partial(attention_kernel, head_count), out_shape...]
    ppermute x17, starting transfers between devices: 15.4 us -> 16.6 us  [swap(): return lax.ppermute(value, axis, [(i, i ^ mask) for i in range(size)])]
  transfers between devices with their start and end apart: 19 -> 19, of which waited for: 11 -> 11; matrix products, arithmetic and copies ran while one was open for 0% -> 0% of each run, Pallas kernels for 33% -> 26%
where the time goes in v8:
time: 68.3 us
  Pallas kernels  28.6 us (42%)
  starting transfers between devices  19.5 us (29%)
  waiting for transfers between devices  15.6 us (23%)
  local copies, waits for them, and re-layouts  3.45 us (5%)
  other arithmetic  0.9 us (1%)
    ppermute x17, starting transfers between devices, swap(): return lax.ppermute(value, axis, [(i, i ^ mask) for i in range(size)])  16.6 us
    ppermute x17, waiting for transfers between devices, swap(): return lax.ppermute(value, axis, [(i, i ^ mask) for i in range(size)])  14.4 us
    pallas_call x2, Pallas kernels, by_expert(): pl.pallas_call(functools.partial(relayout_kernel, js), out_shape=(pltpu.V...  7.44 us
    pallas_call x1, Pallas kernels, attention(): pl.pallas_call(functools.partial(attention_kernel, head_count), out_shape...  7.22 us
    pallas_call x1, Pallas kernels, experts_whole(): pl.pallas_call(whole_kernel, out_shape=jax.ShapeDtypeStruct((tokens, tota...  3.77 us
    unnamed x14, local copies, waits for them, and re-layouts  3.43 us
    pallas_call x1, Pallas kernels, experts_second(): pl.pallas_call(second_kernel, out_shape=(jax.ShapeDtypeStruct((tokens, w_...  3.28 us
    pallas_call x1, Pallas kernels, fetch(): pl.pallas_call(fetch_kernel, out_shape=(pltpu.VMEM(hidden.shape, jnp.bflo...  2.91 us
  transfers between devices with their start and end apart: 19, of which 11 were waited for; matrix products, arithmetic and copies ran while one was open for 0% of the time, Pallas kernels for 26%

profile of v8, /device:TPU:0, one launch (start us, length us, event | category | flops | bytes accessed | tf_op | source)
XLA Modules:
  0.0 68.3 jit_solution(9717958641080037116)
XLA Ops:
  0.0 0.5 collective-permute-start.1
  0.5 2.5 %collective-permute-start = (bf16[32,512]{1,0:T(8,128)(2,1)}, bf16[32,512]{1,0:T(8,128)(2,1)S(1)}, u32[]{:S(2)}, u32[]{:S(2)}) collective-permute-start(bf16[32,512]{1,0:T(8,128)(2,1)} %refs_0_.1), channel_id=1, source_target_pairs={{0,2},{1,3},{2,0},{3,1},{4,6},{5,7},{6,4},{7,5},{8,10},{9,11},{10,... | collective-permute-start | bytes 98312 | tf_op jit(solution)/shard_map/ppermute | solution.py:653
  3.0 0.1 collective-permute-start.2
  3.1 2.9 %fetch.1 = (bf16[32,512]{1,0:T(8,128)(2,1)S(1)}, bf16[3,4,512,512]{3,2,1,0:T(8,128)(2,1)S(1)}, bf16[49152,128]{1,0:T(8,128)(2,1)S(1)}, f32[32,128]{1,0:T(8,128)S...) custom-call(s32[32]{0:T(128)} %lengths_hbm.1, s32[1]{0:T(128)} %bitcast.me_ref, f32[1,128]{1,0:T(1,128)S(1)} %fusion.2.freqs_ref, ...), custom_call_target="tpu_custom_call" | custom-call | bytes 12582912 | tf_op jit(solution)/shard_map/fetch/pallas_call | solution.py:81
  6.1 0.0 collective-permute-done.1.refs_1_
  6.1 0.0 collective-permute-done.refs_2_.refs_1_
  6.1 0.4 collective-permute-done.2.refs_3_
  6.5 0.0 copy-start.2
  6.5 0.0 copy-start.3
  6.5 7.2 %attention.1 = (bf16[32,1024]{1,0:T(8,128)(2,1)S(1)}, bf16[32,1024]{1,0:T(8,128)(2,1)S(1)}, bf16[49152,128]{1,0:T(8,128)(2,1)S(1)}, bf16[4,2048,512]{2,1,0:T(8,128)(2,1)S(1)}) custom-call(s32[32]{0:T(128)S(4)} %get-tuple-element.28.lengths_ref, s32[1]{0:T(128)} %bitcast.me_ref, ...), custom_call_target="tpu_custom_call", output_to_operand_aliasing={{2}: (9, {})} | custom-call | flops 268435456 | bytes 11534336 | tf_op jit(solution)/shard_map/attention/pallas_call | solution.py:282
  13.7 0.0 copy-start
  13.8 3.3 %copy-done = bf16[4,2048,512]{2,1,0:T(8,128)(2,1)} copy-done((bf16[4,2048,512]{2,1,0:T(8,128)(2,1)}, bf16[4,2048,512]{2,1,0:T(8,128)(2,1)S(1)}, u32[]{:S(2)}) %copy-start) | copy-done | bytes 8388632
  17.0 0.2 collective-permute-start.3
  17.3 0.0 copy-done.2
  17.3 0.1 copy.17
  17.3 0.0 copy-done.3
  17.3 0.1 copy.18
  17.4 0.9 %collective-permute-done.3 = bf16[32,1024]{1,0:T(8,128)(2,1)S(1)} collective-permute-done((bf16[32,1024]{1,0:T(8,128)(2,1)S(1)}, bf16[32,1024]{1,0:T(8,128)(2,1)S(1)}, u32[]{:S(2)}, u32[]{:S(2)}) %collective-permute-start.3) | collective-permute-done | bytes 65568 | tf_op jit(solution)/shard_map/ppermute | solution.py:653
  18.3 1.4 %collective-permute-start.4 = (bf16[32,1024]{1,0:T(8,128)(2,1)S(1)}, bf16[32,1024]{1,0:T(8,128)(2,1)S(1)}, u32[]{:S(2)}, u32[]{:S(2)}) collective-permute-start(bf16[32,1024]{1,0:T(8,128)(2,1)S(1)} %add_convert_fusion.1.refs_0_.refs_2_), channel_id=1, source_target_pairs={{0,2},{1,3},{2,0},{3,1},{4,6},{5,7},{6,4},{7,5},{8,10},{9,11},{10,... | collective-permute-start | bytes 196616 | tf_op jit(solution)/shard_map/ppermute | solution.py:653
  19.7 0.2 select_reduce_fusion
  19.9 3.7 %by_expert_0.1 = (bf16[16,4,512,256]{3,2,1,0:T(8,128)(2,1)S(1)}, f32[8,128]{1,0:T(8,128)S(1)}) custom-call(s32[1]{0:T(128)} %bitcast.me_ref, bf16[2048,16,256]{2,1,0:T(8,128)(2,1)} %w_ref.5, bf16[32,1024]{1,0:T(8,128)(2,1)S(1)} %add_convert_fusion.1.refs_0_.refs_2_), custom_call_target="tpu_custom_call" | custom-call | bytes 16777216 | tf_op jit(solution)/shard_map/by_expert_0/pallas_call | solution.py:359
  23.6 0.0 collective-permute-done.4.refs_3_
  23.6 0.0 copy-done.1
  23.7 3.3 %collective-permute-start.7 = (bf16[32,1152]{1,0:T(8,128)(2,1)S(1)}, bf16[32,1152]{1,0:T(8,128)(2,1)S(1)}, u32[]{:S(2)}, u32[]{:S(2)}) collective-permute-start(bf16[32,1152]{1,0:T(8,128)(2,1)S(1)} %get-tuple-element.37.refs_1_.refs_0_), channel_id=1, source_target_pairs={{0,24},{4,28},{8,16},{12,20},{16,8},{20,12},{24,0},{28,4},{1,25},{... | collective-permute-start | bytes 221192 | tf_op jit(solution)/shard_map/ppermute | solution.py:653
  27.0 0.0 collective-permute-start.6
  27.0 1.1 %collective-permute-start.5 = (bf16[32,1152]{1,0:T(8,128)(2,1)S(1)}, bf16[32,1152]{1,0:T(8,128)(2,1)S(1)}, u32[]{:S(2)}, u32[]{:S(2)}) collective-permute-start(bf16[32,1152]{1,0:T(8,128)(2,1)S(1)} %get-tuple-element.37.refs_1_.refs_0_), channel_id=1, source_target_pairs={{0,8},{4,12},{8,0},{12,4},{16,24},{20,28},{24,16},{28,20},{1,9},{5... | collective-permute-start | bytes 221192 | tf_op jit(solution)/shard_map/ppermute | solution.py:653
  28.1 3.7 %by_expert_2.1 = (bf16[16,4,512,256]{3,2,1,0:T(8,128)(2,1)S(1)}, f32[8,128]{1,0:T(8,128)S(1)}) custom-call(s32[1]{0:T(128)} %bitcast.me_ref, bf16[2048,16,256]{2,1,0:T(8,128)(2,1)} %w_ref.5, bf16[16,4,512,256]{3,2,1,0:T(8,128)(2,1)S(1)} %get-tuple-element.38.refs_0_, ...), custom_call_target="tpu_custom_call", output_to_operand_aliasing={{0}: (2, {})} | custom-call | bytes 16777216 | tf_op jit(solution)/shard_map/by_expert_2/pallas_call | solution.py:359
  31.9 0.0 slice-start
  31.9 0.0 collective-permute-done.7.refs_3_
  31.9 1.1 %collective-permute-done.6.refs_2_ = bf16[32,1152]{1,0:T(8,128)(2,1)S(1)} collective-permute-done((bf16[32,1152]{1,0:T(8,128)(2,1)S(1)}, bf16[32,1152]{1,0:T(8,128)(2,1)S(1)}, u32[]{:S(2)}, u32[]{:S(2)}) %collective-permute-start.6) | collective-permute-done | bytes 73760 | tf_op jit(solution)/shard_map/ppermute | solution.py:653
  32.9 0.2 collective-permute-done.5.refs_1_
  33.2 0.1 collective-permute-start.8
  33.3 2.3 %collective-permute-start.10 = (bf16[128,1152]{1,0:T(8,128)(2,1)S(1)}, bf16[128,1152]{1,0:T(8,128)(2,1)S(1)}, u32[]{:S(2)}, u32[]{:S(2)}) collective-permute-start(bf16[128,1152]{1,0:T(8,128)(2,1)S(1)} %stack.1.mine_ref), channel_id=1, source_target_pairs={{0,4},{4,0},{8,12},{12,8},{16,20},{20,16},{24,28},{28,24},{1,5},{5... | collective-permute-start | bytes 884744 | tf_op jit(solution)/shard_map/ppermute | solution.py:653
  35.5 0.0 collective-permute-done.8.other_ref
  35.5 3.8 %experts_whole.1.units_ref = bf16[128,2048]{1,0:T(8,128)(2,1)S(1)} custom-call(s32[1]{0:T(128)} %bitcast.me_ref, bf16[128,1152]{1,0:T(8,128)(2,1)S(1)} %stack.1.mine_ref, bf16[128,1152]{1,0:T(8,128)(2,1)S(1)} %collective-permute-done.8.other_ref, bf16[16,4,512,256]{3,2,1,0:T(8,128)(2,1)S(1)} %get-tuple-element.40.w_ref, f32[8,128]{1,0:T(8,128)S(1)} %get-tuple-element.39.refs_4_._), custom_call_target="tpu_custom_call" | custom-call | flops 2147483648 | bytes 16777216 | tf_op jit(solution)/shard_map/experts_whole/pallas_call | solution.py:524
  39.3 0.0 slice-done
  39.3 0.0 slice-done.1
  39.4 1.3 %down.2 = (bf16[128,1024]{1,0:T(8,128)(2,1)S(1)}, bf16[128,1024]{1,0:T(8,128)(2,1)S(1)}) custom-call(bf16[128,2048]{1,0:T(8,128)(2,1)S(1)} %experts_whole.1.units_ref, bf16[4,2048,512]{2,1,0:T(8,128)(2,1)S(1)} %bitcast.5), custom_call_target="tpu_custom_call" | custom-call | flops 1073741824 | bytes 8388608 | tf_op jit(solution)/shard_map/down/pallas_call | solution.py:597
  40.6 0.2 collective-permute-start.9
  40.9 2.3 %collective-permute-done.10.value_ref = bf16[128,1152]{1,0:T(8,128)(2,1)S(1)} collective-permute-done((bf16[128,1152]{1,0:T(8,128)(2,1)S(1)}, bf16[128,1152]{1,0:T(8,128)(2,1)S(1)}, u32[]{:S(2)}, u32[]{:S(2)}) %collective-permute-start.10) | collective-permute-done | bytes 294944 | tf_op jit(solution)/shard_map/ppermute | solution.py:653
  43.1 0.0 collective-permute-start.11
  43.1 0.0 collective-permute-done.9.sent_ref
  43.2 0.1 sum.2
  43.2 1.8 %experts_first.1.product_ref = f32[16,128,256]{2,1,0:T(8,128)S(1)} custom-call(bf16[128,1152]{1,0:T(8,128)(2,1)S(1)} %hold.2.mine_ref, bf16[16,4,512,256]{3,2,1,0:T(8,128)(2,1)S(1)} %get-tuple-element.40.w_ref, bf16[128,512]{1,0:T(8,128)(2,1)S(1)} %get-tuple-element.45._.value_ref), custom_call_target="tpu_custom_call" | custom-call | flops 1073741824 | bytes 8388608 | tf_op jit(solution)/shard_map/experts_first/pallas_call | solution.py:544
  45.0 0.0 collective-permute-done.11.other_ref
  45.0 3.3 %experts_second.1 = (bf16[128,2048]{1,0:T(8,128)(2,1)S(1)}, bf16[128,1024]{1,0:T(8,128)(2,1)S(1)}) custom-call(s32[1]{0:T(128)} %bitcast.me_ref, bf16[128,1152]{1,0:T(8,128)(2,1)S(1)} %hold.2.mine_ref, bf16[128,1152]{1,0:T(8,128)(2,1)S(1)} %collective-permute-done.11.other_ref, f32[16,128,256]{2,1,0:T(8,128)S(1)} %experts_first.1.product_ref, ...), custom_call_target="tpu_custom_call" | custom-call | flops 1073741824 | bytes 8388608 | tf_op jit(solution)/shard_map/experts_second/pallas_call | solution.py:562
  48.3 0.6 collective-permute-start.12
  48.9 0.7 %down.3.keep_ref = bf16[128,1024]{1,0:T(8,128)(2,1)S(1)} custom-call(bf16[128,2048]{1,0:T(8,128)(2,1)S(1)} %get-tuple-element.46.units_ref, bf16[4,2048,512]{2,1,0:T(8,128)(2,1)S(1)} %bitcast.5), custom_call_target="tpu_custom_call" | custom-call | flops 536870912 | bytes 4194304 | tf_op jit(solution)/shard_map/down/pallas_call | solution.py:597
  49.6 0.4 collective-permute-done.12.sent_ref
  50.1 0.1 sum.3
  50.2 0.7 %collective-permute-start.13 = (bf16[128,512]{1,0:T(8,128)(2,1)S(1)}, bf16[128,512]{1,0:T(8,128)(2,1)S(1)}, u32[]{:S(2)}, u32[]{:S(2)}) collective-permute-start(bf16[128,512]{1,0:T(8,128)(2,1)S(1)} %hold.3), channel_id=1, source_target_pairs={{0,2},{1,3},{2,0},{3,1},{4,6},{5,7},{6,4},{7,5},{8,10},{9,11},{10,... | collective-permute-start | bytes 393224 | tf_op jit(solution)/shard_map/ppermute | solution.py:653
  50.8 2.6 %collective-permute-start.15 = (bf16[128,512]{1,0:T(8,128)(2,1)S(1)}, bf16[128,512]{1,0:T(8,128)(2,1)S(1)}, u32[]{:S(2)}, u32[]{:S(2)}) collective-permute-start(bf16[128,512]{1,0:T(8,128)(2,1)S(1)} %get-tuple-element.49), channel_id=1, source_target_pairs={{0,6},{1,7},{2,4},{3,5},{4,2},{5,3},{6,0},{7,1},{8,14},{9,15},{10,... | collective-permute-start | bytes 393224 | tf_op jit(solution)/shard_map/ppermute | solution.py:720
  53.5 0.3 collective-permute-start.14
  53.7 5.1 %collective-permute-done.13 = bf16[128,512]{1,0:T(8,128)(2,1)S(1)} collective-permute-done((bf16[128,512]{1,0:T(8,128)(2,1)S(1)}, bf16[128,512]{1,0:T(8,128)(2,1)S(1)}, u32[]{:S(2)}, u32[]{:S(2)}) %collective-permute-start.13) | collective-permute-done | bytes 131104 | tf_op jit(solution)/shard_map/ppermute | solution.py:653
  58.8 0.0 collective-permute-done.15
  58.8 1.2 %collective-permute-done.14 = bf16[128,512]{1,0:T(8,128)(2,1)S(1)} collective-permute-done((bf16[128,512]{1,0:T(8,128)(2,1)S(1)}, bf16[128,512]{1,0:T(8,128)(2,1)S(1)}, u32[]{:S(2)}, u32[]{:S(2)}) %collective-permute-start.14) | collective-permute-done | bytes 131104 | tf_op jit(solution)/shard_map/ppermute | solution.py:720
  60.0 0.1 add_convert_fusion
  60.1 0.8 %collective-permute-start.16 = (bf16[32,512]{1,0:T(8,128)(2,1)S(1)}, bf16[32,512]{1,0:T(8,128)(2,1)S(1)}, u32[]{:S(2)}, u32[]{:S(2)}) collective-permute-start(bf16[32,512]{1,0:T(8,128)(2,1)S(1)} %get-tuple-element.51), channel_id=1, source_target_pairs={{0,8},{4,12},{8,0},{12,4},{16,24},{20,28},{24,16},{28,20},{1,9},{5... | collective-permute-start | bytes 98312 | tf_op jit(solution)/shard_map/ppermute | solution.py:653
  61.0 1.6 %collective-permute-start.18 = (bf16[32,512]{1,0:T(8,128)(2,1)S(1)}, bf16[32,512]{1,0:T(8,128)(2,1)S(1)}, u32[]{:S(2)}, u32[]{:S(2)}) collective-permute-start(bf16[32,512]{1,0:T(8,128)(2,1)S(1)} %get-tuple-element.52), channel_id=1, source_target_pairs={{0,24},{4,28},{8,16},{12,20},{16,8},{20,12},{24,0},{28,4},{1,25},{... | collective-permute-start | bytes 98312 | tf_op jit(solution)/shard_map/ppermute | solution.py:653
  62.5 1.2 %collective-permute-start.17 = (bf16[32,512]{1,0:T(8,128)(2,1)S(1)}, bf16[32,512]{1,0:T(8,128)(2,1)S(1)}, u32[]{:S(2)}, u32[]{:S(2)}) collective-permute-start(bf16[32,512]{1,0:T(8,128)(2,1)S(1)} %get-tuple-element.53), channel_id=1, source_target_pairs={{0,16},{4,20},{8,24},{12,28},{16,0},{20,4},{24,8},{28,12},{1,17},{... | collective-permute-start | bytes 98312 | tf_op jit(solution)/shard_map/ppermute | solution.py:653
  63.7 0.4 collective-permute-done.16
  64.1 2.6 %collective-permute-done.18 = bf16[32,512]{1,0:T(8,128)(2,1)S(1)} collective-permute-done((bf16[32,512]{1,0:T(8,128)(2,1)S(1)}, bf16[32,512]{1,0:T(8,128)(2,1)S(1)}, u32[]{:S(2)}, u32[]{:S(2)}) %collective-permute-start.18) | collective-permute-done | bytes 32800 | tf_op jit(solution)/shard_map/ppermute | solution.py:653
  66.7 1.0 %collective-permute-done.17 = bf16[32,512]{1,0:T(8,128)(2,1)S(1)} collective-permute-done((bf16[32,512]{1,0:T(8,128)(2,1)S(1)}, bf16[32,512]{1,0:T(8,128)(2,1)S(1)}, u32[]{:S(2)}, u32[]{:S(2)}) %collective-permute-start.17) | collective-permute-done | bytes 32800 | tf_op jit(solution)/shard_map/ppermute | solution.py:653
  67.7 0.6 add_convert_fusion.2
  (11 shorter events, 0.1 us)
Async XLA Ops:
  0.0 6.1 %collective-permute-start.1 = (bf16[32,512]{1,0:T(8,128)(2,1)}, bf16[32,512]{1,0:T(8,128)(2,1)S(1)}, u32[]{:S(2)}, u32[]{:S(2)}) collective-permute-start(bf16[32,512]{1,0:T(8,128)(2,1)} %refs_0_.1), channel_id=1, source_target_pairs={{0,1},{1,0},{2,3},{3,2},{4,5},{5,4},{6,7},{7,6},{8,9},{9,8},{10,11... | collective-permute-start | bytes 98312 | tf_op jit(solution)/shard_map/ppermute | solution.py:653
  0.5 5.6 %collective-permute-start = (bf16[32,512]{1,0:T(8,128)(2,1)}, bf16[32,512]{1,0:T(8,128)(2,1)S(1)}, u32[]{:S(2)}, u32[]{:S(2)}) collective-permute-start(bf16[32,512]{1,0:T(8,128)(2,1)} %refs_0_.1), channel_id=1, source_target_pairs={{0,2},{1,3},{2,0},{3,1},{4,6},{5,7},{6,4},{7,5},{8,10},{9,11},{10,... | collective-permute-start | bytes 98312 | tf_op jit(solution)/shard_map/ppermute | solution.py:653
  3.0 3.6 %collective-permute-start.2 = (bf16[32,512]{1,0:T(8,128)(2,1)}, bf16[32,512]{1,0:T(8,128)(2,1)S(1)}, u32[]{:S(2)}, u32[]{:S(2)}) collective-permute-start(bf16[32,512]{1,0:T(8,128)(2,1)} %refs_0_.1), channel_id=1, source_target_pairs={{0,3},{1,2},{2,1},{3,0},{4,7},{5,6},{6,5},{7,4},{8,11},{9,10},{10,... | collective-permute-start | bytes 98312 | tf_op jit(solution)/shard_map/ppermute | solution.py:653
  6.5 10.7 %copy-start.2 = (s32[32,8]{0,1:T(8,128)S(1)}, s32[32,8]{0,1:T(8,128)}, u32[]{:S(2)}) copy-start(s32[32,8]{0,1:T(8,128)} %param.12) | copy-start | bytes 3076
  6.5 10.8 %copy-start.3 = (f32[32,8]{0,1:T(8,128)S(1)}, f32[32,8]{0,1:T(8,128)}, u32[]{:S(2)}) copy-start(f32[32,8]{0,1:T(8,128)} %param.13) | copy-start | bytes 3076
  13.7 3.3 %copy-start = (bf16[4,2048,512]{2,1,0:T(8,128)(2,1)}, bf16[4,2048,512]{2,1,0:T(8,128)(2,1)S(1)}, u32[]{:S(2)}) copy-start(bf16[4,2048,512]{2,1,0:T(8,128)(2,1)S(1)} %get-tuple-element.41.w_ref.w_down_ref) | copy-start | bytes 25165828
  17.0 6.6 %copy-start.1 = (bf16[32,512]{1,0:T(8,128)(2,1)S(1)}, bf16[32,512]{1,0:T(8,128)(2,1)}, u32[]{:S(2)}) copy-start(bf16[32,512]{1,0:T(8,128)(2,1)} %refs_0_.1) | copy-start | bytes 98308
  17.0 1.3 %collective-permute-start.3 = (bf16[32,1024]{1,0:T(8,128)(2,1)S(1)}, bf16[32,1024]{1,0:T(8,128)(2,1)S(1)}, u32[]{:S(2)}, u32[]{:S(2)}) collective-permute-start(bf16[32,1024]{1,0:T(8,128)(2,1)S(1)} %get-tuple-element.35), channel_id=1, source_target_pairs={{0,1},{1,0},{2,3},{3,2},{4,5},{5,4},{6,7},{7,6},{8,9},{9,8},{10,11... | collective-permute-start | bytes 196616 | tf_op jit(solution)/shard_map/ppermute | solution.py:653
  18.3 5.3 %collective-permute-start.4 = (bf16[32,1024]{1,0:T(8,128)(2,1)S(1)}, bf16[32,1024]{1,0:T(8,128)(2,1)S(1)}, u32[]{:S(2)}, u32[]{:S(2)}) collective-permute-start(bf16[32,1024]{1,0:T(8,128)(2,1)S(1)} %add_convert_fusion.1.refs_0_.refs_2_), channel_id=1, source_target_pairs={{0,2},{1,3},{2,0},{3,1},{4,6},{5,7},{6,4},{7,5},{8,10},{9,11},{10,... | collective-permute-start | bytes 196616 | tf_op jit(solution)/shard_map/ppermute | solution.py:653
  23.7 8.2 %collective-permute-start.7 = (bf16[32,1152]{1,0:T(8,128)(2,1)S(1)}, bf16[32,1152]{1,0:T(8,128)(2,1)S(1)}, u32[]{:S(2)}, u32[]{:S(2)}) collective-permute-start(bf16[32,1152]{1,0:T(8,128)(2,1)S(1)} %get-tuple-element.37.refs_1_.refs_0_), channel_id=1, source_target_pairs={{0,24},{4,28},{8,16},{12,20},{16,8},{20,12},{24,0},{28,4},{1,25},{... | collective-permute-start | bytes 221192 | tf_op jit(solution)/shard_map/ppermute | solution.py:653
  27.0 6.0 %collective-permute-start.6 = (bf16[32,1152]{1,0:T(8,128)(2,1)S(1)}, bf16[32,1152]{1,0:T(8,128)(2,1)S(1)}, u32[]{:S(2)}, u32[]{:S(2)}) collective-permute-start(bf16[32,1152]{1,0:T(8,128)(2,1)S(1)} %get-tuple-element.37.refs_1_.refs_0_), channel_id=1, source_target_pairs={{0,16},{4,20},{8,24},{12,28},{16,0},{20,4},{24,8},{28,12},{1,17},{... | collective-permute-start | bytes 221192 | tf_op jit(solution)/shard_map/ppermute | solution.py:653
  27.0 6.2 %collective-permute-start.5 = (bf16[32,1152]{1,0:T(8,128)(2,1)S(1)}, bf16[32,1152]{1,0:T(8,128)(2,1)S(1)}, u32[]{:S(2)}, u32[]{:S(2)}) collective-permute-start(bf16[32,1152]{1,0:T(8,128)(2,1)S(1)} %get-tuple-element.37.refs_1_.refs_0_), channel_id=1, source_target_pairs={{0,8},{4,12},{8,0},{12,4},{16,24},{20,28},{24,16},{28,20},{1,9},{5... | collective-permute-start | bytes 221192 | tf_op jit(solution)/shard_map/ppermute | solution.py:653
  31.9 7.5 %slice-start = ((s8[8388608]{0:T(1024)(128)(4,1)}), s8[4194304]{0:T(1024)(128)(4,1)S(1)}, s32[]{:S(2)}) async-start(s8[8388608]{0:T(1024)(128)(4,1)} %bitcast.4), calls=%async_computation | async-start | bytes 8388608
  33.2 2.4 %collective-permute-start.8 = (bf16[128,1152]{1,0:T(8,128)(2,1)S(1)}, bf16[128,1152]{1,0:T(8,128)(2,1)S(1)}, u32[]{:S(2)}, u32[]{:S(2)}) collective-permute-start(bf16[128,1152]{1,0:T(8,128)(2,1)S(1)} %stack.1.mine_ref), channel_id=1, source_target_pairs={{0,1},{1,0},{2,3},{3,2},{4,5},{5,4},{6,7},{7,6},{8,9},{9,8},{10,11... | collective-permute-start | bytes 884744 | tf_op jit(solution)/shard_map/ppermute | solution.py:653
  33.3 9.9 %collective-permute-start.10 = (bf16[128,1152]{1,0:T(8,128)(2,1)S(1)}, bf16[128,1152]{1,0:T(8,128)(2,1)S(1)}, u32[]{:S(2)}, u32[]{:S(2)}) collective-permute-start(bf16[128,1152]{1,0:T(8,128)(2,1)S(1)} %stack.1.mine_ref), channel_id=1, source_target_pairs={{0,4},{4,0},{8,12},{12,8},{16,20},{20,16},{24,28},{28,24},{1,5},{5... | collective-permute-start | bytes 884744 | tf_op jit(solution)/shard_map/ppermute | solution.py:653
  35.5 3.8 %slice-start.1 = ((s8[8388608]{0:T(1024)(128)(4,1)}), s8[4194304]{0:T(1024)(128)(4,1)S(1)}, s32[]{:S(2)}) async-start(s8[8388608]{0:T(1024)(128)(4,1)} %bitcast.4), calls=%async_computation.1 | async-start | bytes 8388608
  40.6 2.5 %collective-permute-start.9 = (bf16[128,1024]{1,0:T(8,128)(2,1)S(1)}, bf16[128,1024]{1,0:T(8,128)(2,1)S(1)}, u32[]{:S(2)}, u32[]{:S(2)}) collective-permute-start(bf16[128,1024]{1,0:T(8,128)(2,1)S(1)} %get-tuple-element.43.after_ref), channel_id=1, source_target_pairs={{0,1},{1,0},{2,3},{3,2},{4,5},{5,4},{6,7},{7,6},{8,9},{9,8},{10,11... | collective-permute-start | bytes 786440 | tf_op jit(solution)/shard_map/ppermute | solution.py:653
  43.1 1.9 %collective-permute-start.11 = (bf16[128,1152]{1,0:T(8,128)(2,1)S(1)}, bf16[128,1152]{1,0:T(8,128)(2,1)S(1)}, u32[]{:S(2)}, u32[]{:S(2)}) collective-permute-start(bf16[128,1152]{1,0:T(8,128)(2,1)S(1)} %hold.2.mine_ref), channel_id=1, source_target_pairs={{0,1},{1,0},{2,3},{3,2},{4,5},{5,4},{6,7},{7,6},{8,9},{9,8},{10,11... | collective-permute-start | bytes 884744 | tf_op jit(solution)/shard_map/ppermute | solution.py:653
  48.3 1.7 %collective-permute-start.12 = (bf16[128,1024]{1,0:T(8,128)(2,1)S(1)}, bf16[128,1024]{1,0:T(8,128)(2,1)S(1)}, u32[]{:S(2)}, u32[]{:S(2)}) collective-permute-start(bf16[128,1024]{1,0:T(8,128)(2,1)S(1)} %get-tuple-element.47), channel_id=1, source_target_pairs={{0,1},{1,0},{2,3},{3,2},{4,5},{5,4},{6,7},{7,6},{8,9},{9,8},{10,11... | collective-permute-start | bytes 786440 | tf_op jit(solution)/shard_map/ppermute | solution.py:653
  50.2 8.7 %collective-permute-start.13 = (bf16[128,512]{1,0:T(8,128)(2,1)S(1)}, bf16[128,512]{1,0:T(8,128)(2,1)S(1)}, u32[]{:S(2)}, u32[]{:S(2)}) collective-permute-start(bf16[128,512]{1,0:T(8,128)(2,1)S(1)} %hold.3), channel_id=1, source_target_pairs={{0,2},{1,3},{2,0},{3,1},{4,6},{5,7},{6,4},{7,5},{8,10},{9,11},{10,... | collective-permute-start | bytes 393224 | tf_op jit(solution)/shard_map/ppermute | solution.py:653
  50.8 8.0 %collective-permute-start.15 = (bf16[128,512]{1,0:T(8,128)(2,1)S(1)}, bf16[128,512]{1,0:T(8,128)(2,1)S(1)}, u32[]{:S(2)}, u32[]{:S(2)}) collective-permute-start(bf16[128,512]{1,0:T(8,128)(2,1)S(1)} %get-tuple-element.49), channel_id=1, source_target_pairs={{0,6},{1,7},{2,4},{3,5},{4,2},{5,3},{6,0},{7,1},{8,14},{9,15},{10,... | collective-permute-start | bytes 393224 | tf_op jit(solution)/shard_map/ppermute | solution.py:720
  53.5 6.6 %collective-permute-start.14 = (bf16[128,512]{1,0:T(8,128)(2,1)S(1)}, bf16[128,512]{1,0:T(8,128)(2,1)S(1)}, u32[]{:S(2)}, u32[]{:S(2)}) collective-permute-start(bf16[128,512]{1,0:T(8,128)(2,1)S(1)} %get-tuple-element.48.after_ref), channel_id=1, source_target_pairs={{0,4},{1,5},{2,6},{3,7},{4,0},{5,1},{6,2},{7,3},{8,12},{9,13},{10,... | collective-permute-start | bytes 393224 | tf_op jit(solution)/shard_map/ppermute | solution.py:720
  60.1 4.0 %collective-permute-start.16 = (bf16[32,512]{1,0:T(8,128)(2,1)S(1)}, bf16[32,512]{1,0:T(8,128)(2,1)S(1)}, u32[]{:S(2)}, u32[]{:S(2)}) collective-permute-start(bf16[32,512]{1,0:T(8,128)(2,1)S(1)} %get-tuple-element.51), channel_id=1, source_target_pairs={{0,8},{4,12},{8,0},{12,4},{16,24},{20,28},{24,16},{28,20},{1,9},{5... | collective-permute-start | bytes 98312 | tf_op jit(solution)/shard_map/ppermute | solution.py:653
  61.0 5.7 %collective-permute-start.18 = (bf16[32,512]{1,0:T(8,128)(2,1)S(1)}, bf16[32,512]{1,0:T(8,128)(2,1)S(1)}, u32[]{:S(2)}, u32[]{:S(2)}) collective-permute-start(bf16[32,512]{1,0:T(8,128)(2,1)S(1)} %get-tuple-element.52), channel_id=1, source_target_pairs={{0,24},{4,28},{8,16},{12,20},{16,8},{20,12},{24,0},{28,4},{1,25},{... | collective-permute-start | bytes 98312 | tf_op jit(solution)/shard_map/ppermute | solution.py:653
  62.5 5.2 %collective-permute-start.17 = (bf16[32,512]{1,0:T(8,128)(2,1)S(1)}, bf16[32,512]{1,0:T(8,128)(2,1)S(1)}, u32[]{:S(2)}, u32[]{:S(2)}) collective-permute-start(bf16[32,512]{1,0:T(8,128)(2,1)S(1)} %get-tuple-element.53), channel_id=1, source_target_pairs={{0,16},{4,20},{8,24},{12,28},{16,0},{20,4},{24,8},{28,12},{1,17},{... | collective-permute-start | bytes 98312 | tf_op jit(solution)/shard_map/ppermute | solution.py:653

commit v9 on v8

--- a/solution.py
+++ b/solution.py
@@ -33,13 +33,25 @@
 
 
 def fetch_kernel(
-    lengths_hbm, me_ref, freqs_ref, own_ref, w_ref,
-    own_out_ref, w_out_ref, blank_ref, cos_ref, sin_ref, lengths_ref, angle_s, sem, own_sem, len_sem,
+    lengths_hbm, me_ref, freqs_ref, own_ref, w_ref, ids_ref, route_ref,
+    own_out_ref, w_out_ref, blank_ref, cos_ref, sin_ref, lengths_ref, shares_ref,
+    angle_s, ids_s, route_s, sem, small_sem,
 ):
     head_count, cols = w_out_ref.shape[1:3]
     chunk_rows = CHUNK * cols // LANES
     me = me_ref[0]
-    copies = [pltpu.make_async_copy(own_ref, own_out_ref, own_sem)]
+    lengths_copy, *copies = [
+        pltpu.make_async_copy(source, target, small_sem.at[i])
+        for i, (source, target) in enumerate(
+            (
+                (lengths_hbm, lengths_ref),
+                (ids_ref, ids_s),
+                (route_ref, route_s),
+                (own_ref, own_out_ref),
+            )
+        )
+    ]
+    small = copies[:2]
     for c in range(w_ref.shape[0]):
         for j in range(head_count):
             first = pl.multiple_of((me ^ j) * cols, cols)
@@ -48,7 +60,6 @@
                     w_ref.at[c, pl.ds(first, cols)], w_out_ref.at[c, j], sem.at[c, j]
                 )
             )
-    lengths_copy = pltpu.make_async_copy(lengths_hbm, lengths_ref, len_sem)
     lengths_copy.start()
     for copy in copies:
         copy.start()
@@ -69,11 +80,18 @@
     lane = lax.broadcasted_iota(jnp.int32, sin_ref.shape, 1)
     sine = jnp.sin(angle_s[...])
     sin_ref[...] = jnp.where(lane < LANES // 2, -sine, sine)
-    for copy in copies:
+    for copy in small:
         copy.wait()
-
-
-def fetch(me, lengths, hidden, w_qkv, v_shape, head_count):
+    expert = lax.broadcasted_iota(jnp.int32, (shares_ref.shape[1], rows), 0)
+    shares = jnp.zeros(expert.shape, jnp.float32)
+    for k in range(ids_s.shape[0]):
+        shares += jnp.where(expert == ids_s[k : k + 1, :], route_s[k : k + 1, :], 0.0)
+    shares_ref[...] = jnp.transpose(shares, (1, 0)).astype(jnp.bfloat16)
+    for copy in copies[2:]:
+        copy.wait()
+
+
+def fetch(me, lengths, hidden, w_qkv, v_shape, head_count, expert_ids, route_weights, experts):
     cols = w_qkv.shape[2]
     rows = hidden.shape[0]
     exponents = jnp.arange(LANES, dtype=jnp.float32) % (LANES // 2) / (LANES // 2)
@@ -87,21 +105,26 @@
             pltpu.VMEM((rows, LANES), jnp.float32),
             pltpu.VMEM((rows, LANES), jnp.float32),
             pltpu.SMEM(lengths.shape, lengths.dtype),
-        ),
-        in_specs=[ANY, SMEM, VMEM, ANY, ANY],
-        out_specs=[VMEM] * 5 + [SMEM],
+            pltpu.VMEM((rows, -(-experts // LANES) * LANES), jnp.bfloat16),
+        ),
+        in_specs=[ANY, SMEM, VMEM] + [ANY] * 4,
+        out_specs=[VMEM] * 5 + [SMEM, VMEM],
         scratch_shapes=[
             pltpu.VMEM((rows, LANES), jnp.float32),
+            pltpu.VMEM(expert_ids.shape[::-1], expert_ids.dtype),
+            pltpu.VMEM(route_weights.shape[::-1], route_weights.dtype),
             pltpu.SemaphoreType.DMA((w_qkv.shape[0], head_count)),
-            pltpu.SemaphoreType.DMA(()),
-            pltpu.SemaphoreType.DMA(()),
+            pltpu.SemaphoreType.DMA((4,)),
         ],
         compiler_params=pltpu.CompilerParams(vmem_limit_bytes=8 * 2**20),
         cost_estimate=pl.CostEstimate(
             flops=0, bytes_accessed=4 * w_qkv.size, transcendentals=0
         ),
         name="fetch",
-    )(in_hbm(lengths), me, freqs, in_hbm(hidden), in_hbm(w_qkv))
+    )(
+        in_hbm(lengths), me, freqs, in_hbm(hidden), in_hbm(w_qkv), in_hbm(expert_ids.T),
+        in_hbm(route_weights.T),
+    )
 
 
 def attention_kernel(head_count, lengths_ref, me_ref, cos_ref, sin_ref, *refs):
@@ -451,23 +474,22 @@
     return jnp.sum(jnp.square(ref[:, :depth].astype(jnp.float32)), axis=1, keepdims=True)
 
 
-def units_step(me, p, per_step, experts, product, scale, shares):
+def local_shares(me, shares, experts):
+    lanes = shares.shape[1]
+    return pltpu.roll(shares.astype(jnp.float32), lax.rem(lanes - me * experts, lanes), 1)
+
+
+def units_step(p, per_step, product, scale, shares):
     tokens = product.shape[0]
     first_half = lax.broadcasted_iota(jnp.int32, (tokens, LANES), 1) < LANES // 2
-    source = lax.broadcasted_iota(jnp.int32, (LANES, LANES), 0)
-    lane = lax.broadcasted_iota(jnp.int32, (LANES, LANES), 1)
-    expert = me * experts + p * per_step + lane * per_step // LANES
-    share = jnp.dot(
-        shares, (source == expert).astype(jnp.bfloat16), preferred_element_type=jnp.float32
-    )
+    expert = p * per_step
+    share = shares[:, expert : expert + 1]
+    if per_step == 2:
+        share = jnp.where(first_half, share, shares[:, expert + 1 : expert + 2])
     a, b = product[:, :LANES], product[:, LANES:]
     gate = jnp.where(first_half, a, pltpu.roll(b, LANES // 2, 1)) * scale
-    upward = jnp.where(first_half, pltpu.roll(a, LANES // 2, 1), b) * scale
-    return (share * (gate / (1.0 + jnp.exp(-gate)) * upward)).astype(jnp.bfloat16)
-
-
-def part_of(p):
-    return pl.ds(pl.multiple_of(p * LANES, LANES), LANES)
+    upward = jnp.where(first_half, pltpu.roll(a, LANES // 2, 1), b) * (scale * 0.5)
+    return (share * (gate * (1.0 + jnp.tanh(gate * 0.5)) * upward)).astype(jnp.bfloat16)
 
 
 def whole_kernel(me_ref, mine_ref, other_ref, w_ref, _, units_ref, states_s):
@@ -477,14 +499,12 @@
     states_s[:, depth:] = other_ref[:, :depth]
     square = square_sum(mine_ref, depth) + square_sum(other_ref, depth)
     scale = lax.rsqrt(square / (2 * depth) + norm_eps)
-    shares = mine_ref[:, depth:]
+    shares = local_shares(me_ref[0], mine_ref[:, depth:], experts)
     steps, per_step = steps_of(w_ref.shape)
-
-    @pl.loop(0, steps, unroll=4)
-    def _(p):
+    for p in range(steps):
         product = expert_products(states_s[...], w_ref, 0, p, per_step)
-        units_ref[:, part_of(p)] = units_step(
-            me_ref[0], p, per_step, experts, product, scale, shares
+        units_ref[:, p * LANES : (p + 1) * LANES] = units_step(
+            p, per_step, product, scale, shares
         )
 
 
@@ -503,16 +523,14 @@
     depth = head_count // 2 * cols
     square = square_sum(mine_ref, depth) + square_sum(other_ref, depth)
     scale = lax.rsqrt(square / (2 * depth) + norm_eps)
-    shares = mine_ref[:, depth:]
+    shares = local_shares(me_ref[0], mine_ref[:, depth:], experts)
     steps, per_step = steps_of(w_ref.shape)
-
-    @pl.loop(0, steps, unroll=4)
-    def _(p):
+    for p in range(steps):
         product = product_ref[p] + expert_products(
             other_ref[:, :depth], w_ref, head_count // 2, p, per_step
         )
-        units_ref[:, part_of(p)] = units_step(
-            me_ref[0], p, per_step, experts, product, scale, shares
+        units_ref[:, p * LANES : (p + 1) * LANES] = units_step(
+            p, per_step, product, scale, shares
         )
 
     down_blocks(units_ref[...], w_down_ref, 1, send_ref)
@@ -666,9 +684,13 @@
 
     pieces = [hidden] + [swap(hidden, "head", head_size, j) for j in range(1, head_size)]
     flat = (rows * k_cache.shape[1] * k_cache.shape[2], k_cache.shape[3])
-    own, w_near, room, cosine, sine, lengths_near = fetch(me_ref, lengths, hidden, w_qkv, flat, head_size)
+    own, w_near, room, cosine, sine, lengths_near, shares = fetch(
+        me_ref, lengths, hidden, w_qkv, flat, head_size, expert_ids, route_weights,
+        head_size * experts_local,
+    )
+    pieces[0] = own
     keep, send, _, w_down_near = attention(
-        [own] + pieces[1:],
+        pieces,
         me_ref,
         lengths_near,
         cosine,
@@ -680,24 +702,21 @@
         v_cache.reshape(flat),
         w_down.reshape(experts_local * units_local, width),
     )
-    half = keep.astype(jnp.float32) + swap(send, "head", head_size, 1).astype(jnp.float32)
-    half = half.astype(jnp.bfloat16)
+    (half,) = sum_part(keep, swap(send, "head", head_size, 1), keep.shape[1], jnp.bfloat16)
     others = [swap(half, "head", head_size, j) for j in even if j]
     early, late = range(head_size // 2), range(head_size // 2, head_size)
     buffer, token = by_expert(tuple(early), me_ref, w_in, head_size, None, half)
 
-    every = jnp.arange(head_size * experts_local, dtype=jnp.int32)
-    matches = (expert_ids[:, :, None] == every[None, None, :]).astype(jnp.float32)
-    shares = jnp.sum(route_weights[:, :, None] * matches, axis=1).astype(jnp.bfloat16)
-    shares = jnp.pad(shares, ((0, 0), (0, -shares.shape[1] % LANES)))
-    payload, resid = payload_part([pieces[j] for j in even], half, others, shares, token)
+    payload, resid = payload_part(
+        [pieces[j] for j in even], half, others, shares, token
+    )
 
     steps = range(2, req_size, 2)
     line = [payload] + [swap(payload, "req", req_size, k) for k in steps]
     buffer, token = by_expert(tuple(late), me_ref, w_in, head_size, buffer, payload)
     line = stack_part(line, token)
+    line_other = swap(line, "head", head_size, 1)
     crossed = swap(line, "req", req_size, 1)
-    line_other = swap(line, "head", head_size, 1)
     units = experts_whole(me_ref, line, line_other, buffer, token, w_down_near.shape[1])
     keep, send = down_part(units, w_down_near, (0, 1))
     crossed = hold(crossed, send)

time: 68.3 us -> 64.2 us (0.940)
  local copies, waits for them, and re-layouts: 3.45 us -> 0.01 us
  Pallas kernels: 28.6 us -> 26.2 us
  waiting for transfers between devices: 15.6 us -> 17.2 us
    unnamed x14 -> x0, local copies, waits for them, and re-layouts: 3.43 us -> none
    ppermute x17, waiting for transfers between devices: 14.4 us -> 16 us  [swap(): return lax.ppermute(value, axis, [(i, i ^ mask) for i in range(size)])]
    pallas_call x1, Pallas kernels: 3.28 us -> 2.09 us  [experts_second(): pl.pallas_call(second_kernel, out_shape=(jax.ShapeDtypeStruct((tokens, w_...]
    pallas_call x1, Pallas kernels: 3.77 us -> 2.69 us  [experts_whole(): pl.pallas_call(whole_kernel, out_shape=jax.ShapeDtypeStruct((tokens, tota...]
  transfers between devices with their start and end apart: 19 -> 19, of which waited for: 11 -> 10; matrix products, arithmetic and copies ran while one was open for 0% -> 0% of each run, Pallas kernels for 26% -> 27%
where the time goes in v9:
time: 64.2 us; the launch traced here: 63.7 us
  Pallas kernels  26.2 us (41%)
  starting transfers between devices  19.4 us (30%)
  waiting for transfers between devices  17.2 us (27%)
  other arithmetic  0.73 us (1%)
    ppermute x17, starting transfers between devices, swap(): return lax.ppermute(value, axis, [(i, i ^ mask) for i in range(size)])  16.4 us
    ppermute x17, waiting for transfers between devices, swap(): return lax.ppermute(value, axis, [(i, i ^ mask) for i in range(size)])  16 us
    pallas_call x2, Pallas kernels, by_expert(): pl.pallas_call(functools.partial(relayout_kernel, js), out_shape=(pltpu.V...  7.43 us
    pallas_call x1, Pallas kernels, attention(): pl.pallas_call(functools.partial(attention_kernel, head_count), out_shape...  6.9 us
    ppermute x2, starting transfers between devices, per_device(): got.append(lax.ppermute(crossed_sums[j // 2], ('req', 'head'), pairs))  2.98 us
    pallas_call x1, Pallas kernels, fetch(): pl.pallas_call(fetch_kernel, out_shape=(pltpu.VMEM(hidden.shape, jnp.bflo...  2.94 us
    pallas_call x1, Pallas kernels, experts_whole(): pl.pallas_call(whole_kernel, out_shape=jax.ShapeDtypeStruct((tokens, tota...  2.69 us
    pallas_call x1, Pallas kernels, experts_second(): pl.pallas_call(second_kernel, out_shape=(jax.ShapeDtypeStruct((tokens, w_...  2.09 us
  transfers between devices with their start and end apart: 19, of which 10 were waited for; matrix products, arithmetic and copies ran while one was open for 0% of the time, Pallas kernels for 27%

profile of v9, /device:TPU:0, one launch (start us, length us, event | category | flops | bytes accessed | tf_op | source)
XLA Modules:
  0.0 63.7 jit_solution(7471229198688124929)
XLA Ops:
  0.0 3.0 %collective-permute-start = (bf16[32,512]{1,0:T(8,128)(2,1)}, bf16[32,512]{1,0:T(8,128)(2,1)S(1)}, u32[]{:S(2)}, u32[]{:S(2)}) collective-permute-start(bf16[32,512]{1,0:T(8,128)(2,1)} %own_ref.1), channel_id=1, source_target_pairs={{0,2},{1,3},{2,0},{3,1},{4,6},{5,7},{6,4},{7,5},{8,10},{9,11},{10,... | collective-permute-start | bytes 98312 | tf_op jit(solution)/shard_map/ppermute | solution.py:671
  3.0 0.0 collective-permute-start.2
  3.0 0.1 collective-permute-start.1
  3.1 2.9 %fetch.1 = (bf16[32,512]{1,0:T(8,128)(2,1)S(1)}, bf16[3,4,512,512]{3,2,1,0:T(8,128)(2,1)S(1)}, bf16[49152,128]{1,0:T(8,128)(2,1)S(1)}, f32[32,128]{1,0:T(8,128)S...) custom-call(s32[32]{0:T(128)} %lengths_hbm.1, s32[1]{0:T(128)} %bitcast.me_ref, ...), custom_call_target="tpu_custom_call" | custom-call | bytes 12582912 | tf_op jit(solution)/shard_map/fetch/pallas_call | solution.py:99
  6.1 0.0 collective-permute-done.refs_2_.refs_1_
  6.1 0.5 collective-permute-done.2.refs_3_
  6.6 0.0 collective-permute-done.1.refs_1_
  6.6 6.9 %attention.1 = (bf16[32,1024]{1,0:T(8,128)(2,1)S(1)}, bf16[32,1024]{1,0:T(8,128)(2,1)S(1)}, bf16[49152,128]{1,0:T(8,128)(2,1)S(1)}, bf16[4,2048,512]{2,1,0:T(8,128)(2,1)S(1)}) custom-call(s32[32]{0:T(128)S(4)} %get-tuple-element.30.lengths_ref, s32[1]{0:T(128)} %bitcast.me_ref, ...), custom_call_target="tpu_custom_call", output_to_operand_aliasing={{2}: (9, {})} | custom-call | flops 268435456 | bytes 11534336 | tf_op jit(solution)/shard_map/attention/pallas_call | solution.py:305
  13.5 0.1 collective-permute-start.3
  13.6 1.2 %collective-permute-done.3.sent_ref = bf16[32,1024]{1,0:T(8,128)(2,1)S(1)} collective-permute-done((bf16[32,1024]{1,0:T(8,128)(2,1)S(1)}, bf16[32,1024]{1,0:T(8,128)(2,1)S(1)}, u32[]{:S(2)}, u32[]{:S(2)}) %collective-permute-start.3) | collective-permute-done | bytes 65568 | tf_op jit(solution)/shard_map/ppermute | solution.py:671
  14.9 1.6 %collective-permute-start.4 = (bf16[32,1024]{1,0:T(8,128)(2,1)S(1)}, bf16[32,1024]{1,0:T(8,128)(2,1)S(1)}, u32[]{:S(2)}, u32[]{:S(2)}) collective-permute-start(bf16[32,1024]{1,0:T(8,128)(2,1)S(1)} %sum.3.refs_0_.refs_2_), channel_id=1, source_target_pairs={{0,2},{1,3},{2,0},{3,1},{4,6},{5,7},{6,4},{7,5},{8,10},{9,11},{10,... | collective-permute-start | bytes 196616 | tf_op jit(solution)/shard_map/ppermute | solution.py:671
  16.5 3.7 %by_expert_0.1 = (bf16[16,4,512,256]{3,2,1,0:T(8,128)(2,1)S(1)}, f32[8,128]{1,0:T(8,128)S(1)}) custom-call(s32[1]{0:T(128)} %bitcast.me_ref, bf16[2048,16,256]{2,1,0:T(8,128)(2,1)} %w_ref.5, bf16[32,1024]{1,0:T(8,128)(2,1)S(1)} %sum.3.refs_0_.refs_2_), custom_call_target="tpu_custom_call" | custom-call | bytes 16777216 | tf_op jit(solution)/shard_map/by_expert_0/pallas_call | solution.py:382
  20.2 0.0 collective-permute-done.4.refs_3_
  20.2 3.6 %collective-permute-start.7 = (bf16[32,1152]{1,0:T(8,128)(2,1)S(1)}, bf16[32,1152]{1,0:T(8,128)(2,1)S(1)}, u32[]{:S(2)}, u32[]{:S(2)}) collective-permute-start(bf16[32,1152]{1,0:T(8,128)(2,1)S(1)} %get-tuple-element.39.refs_1_.refs_0_), channel_id=1, source_target_pairs={{0,24},{4,28},{8,16},{12,20},{16,8},{20,12},{24,0},{28,4},{1,25},{... | collective-permute-start | bytes 221192 | tf_op jit(solution)/shard_map/ppermute | solution.py:671
  23.9 0.0 collective-permute-start.6
  23.9 0.8 %collective-permute-start.5 = (bf16[32,1152]{1,0:T(8,128)(2,1)S(1)}, bf16[32,1152]{1,0:T(8,128)(2,1)S(1)}, u32[]{:S(2)}, u32[]{:S(2)}) collective-permute-start(bf16[32,1152]{1,0:T(8,128)(2,1)S(1)} %get-tuple-element.39.refs_1_.refs_0_), channel_id=1, source_target_pairs={{0,8},{4,12},{8,0},{12,4},{16,24},{20,28},{24,16},{28,20},{1,9},{5... | collective-permute-start | bytes 221192 | tf_op jit(solution)/shard_map/ppermute | solution.py:671
  24.7 3.7 %by_expert_2.1 = (bf16[16,4,512,256]{3,2,1,0:T(8,128)(2,1)S(1)}, f32[8,128]{1,0:T(8,128)S(1)}) custom-call(s32[1]{0:T(128)} %bitcast.me_ref, bf16[2048,16,256]{2,1,0:T(8,128)(2,1)} %w_ref.5, bf16[16,4,512,256]{3,2,1,0:T(8,128)(2,1)S(1)} %get-tuple-element.40.refs_0_, ...), custom_call_target="tpu_custom_call", output_to_operand_aliasing={{0}: (2, {})} | custom-call | bytes 16777216 | tf_op jit(solution)/shard_map/by_expert_2/pallas_call | solution.py:382
  28.4 0.0 collective-permute-done.7.refs_3_
  28.4 1.4 %collective-permute-done.6.refs_2_ = bf16[32,1152]{1,0:T(8,128)(2,1)S(1)} collective-permute-done((bf16[32,1152]{1,0:T(8,128)(2,1)S(1)}, bf16[32,1152]{1,0:T(8,128)(2,1)S(1)}, u32[]{:S(2)}, u32[]{:S(2)}) %collective-permute-start.6) | collective-permute-done | bytes 73760 | tf_op jit(solution)/shard_map/ppermute | solution.py:671
  29.8 0.0 collective-permute-done.5.refs_1_
  29.9 0.1 collective-permute-start.8
  29.9 2.1 %collective-permute-start.10 = (bf16[128,1152]{1,0:T(8,128)(2,1)S(1)}, bf16[128,1152]{1,0:T(8,128)(2,1)S(1)}, u32[]{:S(2)}, u32[]{:S(2)}) collective-permute-start(bf16[128,1152]{1,0:T(8,128)(2,1)S(1)} %stack.1.mine_ref), channel_id=1, source_target_pairs={{0,4},{4,0},{8,12},{12,8},{16,20},{20,16},{24,28},{28,24},{1,5},{5... | collective-permute-start | bytes 884744 | tf_op jit(solution)/shard_map/ppermute | solution.py:671
  32.1 0.0 collective-permute-done.8.other_ref
  32.1 2.7 %experts_whole.1.units_ref = bf16[128,2048]{1,0:T(8,128)(2,1)S(1)} custom-call(s32[1]{0:T(128)} %bitcast.me_ref, bf16[128,1152]{1,0:T(8,128)(2,1)S(1)} %stack.1.mine_ref, bf16[128,1152]{1,0:T(8,128)(2,1)S(1)} %collective-permute-done.8.other_ref, bf16[16,4,512,256]{3,2,1,0:T(8,128)(2,1)S(1)} %get-tuple-element.42.w_ref, f32[8,128]{1,0:T(8,128)S(1)} %get-tuple-element.41.refs_4_._), custom_call_target="tpu_custom_call" | custom-call | flops 2147483648 | bytes 16777216 | tf_op jit(solution)/shard_map/experts_whole/pallas_call | solution.py:542
  34.8 1.3 %down.2 = (bf16[128,1024]{1,0:T(8,128)(2,1)S(1)}, bf16[128,1024]{1,0:T(8,128)(2,1)S(1)}) custom-call(bf16[128,2048]{1,0:T(8,128)(2,1)S(1)} %experts_whole.1.units_ref, bf16[4,2048,512]{2,1,0:T(8,128)(2,1)S(1)} %get-tuple-element.43.w_ref.w_down_ref), custom_call_target="tpu_custom_call" | custom-call | flops 1073741824 | bytes 8388608 | tf_op jit(solution)/shard_map/down/pallas_call | solution.py:615
  36.0 0.2 collective-permute-start.9
  36.3 3.4 %collective-permute-done.10.value_ref = bf16[128,1152]{1,0:T(8,128)(2,1)S(1)} collective-permute-done((bf16[128,1152]{1,0:T(8,128)(2,1)S(1)}, bf16[128,1152]{1,0:T(8,128)(2,1)S(1)}, u32[]{:S(2)}, u32[]{:S(2)}) %collective-permute-start.10) | collective-permute-done | bytes 294944 | tf_op jit(solution)/shard_map/ppermute | solution.py:671
  39.7 0.0 collective-permute-start.11
  39.7 0.0 collective-permute-done.9.sent_ref
  39.7 0.1 sum.4
  39.7 2.0 %experts_first.1.product_ref = f32[16,128,256]{2,1,0:T(8,128)S(1)} custom-call(bf16[128,1152]{1,0:T(8,128)(2,1)S(1)} %hold.2.mine_ref, bf16[16,4,512,256]{3,2,1,0:T(8,128)(2,1)S(1)} %get-tuple-element.42.w_ref, bf16[128,512]{1,0:T(8,128)(2,1)S(1)} %get-tuple-element.47._.value_ref), custom_call_target="tpu_custom_call" | custom-call | flops 1073741824 | bytes 8388608 | tf_op jit(solution)/shard_map/experts_first/pallas_call | solution.py:562
  41.7 0.0 collective-permute-done.11.other_ref
  41.7 2.1 %experts_second.1 = (bf16[128,2048]{1,0:T(8,128)(2,1)S(1)}, bf16[128,1024]{1,0:T(8,128)(2,1)S(1)}) custom-call(s32[1]{0:T(128)} %bitcast.me_ref, bf16[128,1152]{1,0:T(8,128)(2,1)S(1)} %hold.2.mine_ref, bf16[128,1152]{1,0:T(8,128)(2,1)S(1)} %collective-permute-done.11.other_ref, f32[16,128,256]{2,1,0:T(8,128)S(1)} %experts_first.1.product_ref, ...), custom_call_target="tpu_custom_call" | custom-call | flops 1073741824 | bytes 8388608 | tf_op jit(solution)/shard_map/experts_second/pallas_call | solution.py:580
  43.8 0.6 collective-permute-start.12
  44.4 0.7 %down.3.keep_ref = bf16[128,1024]{1,0:T(8,128)(2,1)S(1)} custom-call(bf16[128,2048]{1,0:T(8,128)(2,1)S(1)} %get-tuple-element.48.units_ref, bf16[4,2048,512]{2,1,0:T(8,128)(2,1)S(1)} %get-tuple-element.43.w_ref.w_down_ref), custom_call_target="tpu_custom_call" | custom-call | flops 536870912 | bytes 4194304 | tf_op jit(solution)/shard_map/down/pallas_call | solution.py:615
  45.1 0.4 collective-permute-done.12.sent_ref
  45.6 0.1 sum.5
  45.6 0.6 collective-permute-start.13
  46.2 2.7 %collective-permute-start.15 = (bf16[128,512]{1,0:T(8,128)(2,1)S(1)}, bf16[128,512]{1,0:T(8,128)(2,1)S(1)}, u32[]{:S(2)}, u32[]{:S(2)}) collective-permute-start(bf16[128,512]{1,0:T(8,128)(2,1)S(1)} %get-tuple-element.51), channel_id=1, source_target_pairs={{0,6},{1,7},{2,4},{3,5},{4,2},{5,3},{6,0},{7,1},{8,14},{9,15},{10,... | collective-permute-start | bytes 393224 | tf_op jit(solution)/shard_map/ppermute | solution.py:739
  49.0 0.3 collective-permute-start.14
  49.2 5.1 %collective-permute-done.13 = bf16[128,512]{1,0:T(8,128)(2,1)S(1)} collective-permute-done((bf16[128,512]{1,0:T(8,128)(2,1)S(1)}, bf16[128,512]{1,0:T(8,128)(2,1)S(1)}, u32[]{:S(2)}, u32[]{:S(2)}) %collective-permute-start.13) | collective-permute-done | bytes 131104 | tf_op jit(solution)/shard_map/ppermute | solution.py:671
  54.3 0.0 collective-permute-done.15
  54.3 1.2 %collective-permute-done.14 = bf16[128,512]{1,0:T(8,128)(2,1)S(1)} collective-permute-done((bf16[128,512]{1,0:T(8,128)(2,1)S(1)}, bf16[128,512]{1,0:T(8,128)(2,1)S(1)}, u32[]{:S(2)}, u32[]{:S(2)}) %collective-permute-start.14) | collective-permute-done | bytes 131104 | tf_op jit(solution)/shard_map/ppermute | solution.py:739
  55.5 0.1 add_convert_fusion
  55.6 1.1 %collective-permute-start.16 = (bf16[32,512]{1,0:T(8,128)(2,1)S(1)}, bf16[32,512]{1,0:T(8,128)(2,1)S(1)}, u32[]{:S(2)}, u32[]{:S(2)}) collective-permute-start(bf16[32,512]{1,0:T(8,128)(2,1)S(1)} %get-tuple-element.53), channel_id=1, source_target_pairs={{0,8},{4,12},{8,0},{12,4},{16,24},{20,28},{24,16},{28,20},{1,9},{5... | collective-permute-start | bytes 98312 | tf_op jit(solution)/shard_map/ppermute | solution.py:671
  56.7 1.6 %collective-permute-start.18 = (bf16[32,512]{1,0:T(8,128)(2,1)S(1)}, bf16[32,512]{1,0:T(8,128)(2,1)S(1)}, u32[]{:S(2)}, u32[]{:S(2)}) collective-permute-start(bf16[32,512]{1,0:T(8,128)(2,1)S(1)} %get-tuple-element.54), channel_id=1, source_target_pairs={{0,24},{4,28},{8,16},{12,20},{16,8},{20,12},{24,0},{28,4},{1,25},{... | collective-permute-start | bytes 98312 | tf_op jit(solution)/shard_map/ppermute | solution.py:671
  58.3 0.9 %collective-permute-start.17 = (bf16[32,512]{1,0:T(8,128)(2,1)S(1)}, bf16[32,512]{1,0:T(8,128)(2,1)S(1)}, u32[]{:S(2)}, u32[]{:S(2)}) collective-permute-start(bf16[32,512]{1,0:T(8,128)(2,1)S(1)} %get-tuple-element.55), channel_id=1, source_target_pairs={{0,16},{4,20},{8,24},{12,28},{16,0},{20,4},{24,8},{28,12},{1,17},{... | collective-permute-start | bytes 98312 | tf_op jit(solution)/shard_map/ppermute | solution.py:671
  59.2 0.4 collective-permute-done.16
  59.6 2.8 %collective-permute-done.18 = bf16[32,512]{1,0:T(8,128)(2,1)S(1)} collective-permute-done((bf16[32,512]{1,0:T(8,128)(2,1)S(1)}, bf16[32,512]{1,0:T(8,128)(2,1)S(1)}, u32[]{:S(2)}, u32[]{:S(2)}) %collective-permute-start.18) | collective-permute-done | bytes 32800 | tf_op jit(solution)/shard_map/ppermute | solution.py:671
  62.4 0.7 %collective-permute-done.17 = bf16[32,512]{1,0:T(8,128)(2,1)S(1)} collective-permute-done((bf16[32,512]{1,0:T(8,128)(2,1)S(1)}, bf16[32,512]{1,0:T(8,128)(2,1)S(1)}, u32[]{:S(2)}, u32[]{:S(2)}) %collective-permute-start.17) | collective-permute-done | bytes 32800 | tf_op jit(solution)/shard_map/ppermute | solution.py:671
  63.1 0.6 %add_convert_fusion.1 = bf16[32,512]{1,0:T(8,128)(2,1)} fusion(f32[32,512]{1,0:T(8,128)S(1)} %get-tuple-element.52, bf16[32,512]{1,0:T(8,128)(2,1)S(1)} %collective-permute-done.18, bf16[32,512]{1,0:T(8,128)(2,1)S(1)} %collective-permute-done.17, bf16[32,512]{1,0:T(8,128)(2,1)S(1)} %collective-permute-done.16, bf16[128,512]{1,0:T(8,128)(2,1)S(1)} %add_convert_fusion), kind=kLoop, calls=%fused_computation.1 | loop fusion | flops 147456 | bytes 229376 | tf_op jit(solution)/shard_map/convert_element_type | solution.py:746
  (7 shorter events, 0.1 us)
Async XLA Ops:
  0.0 6.1 %collective-permute-start = (bf16[32,512]{1,0:T(8,128)(2,1)}, bf16[32,512]{1,0:T(8,128)(2,1)S(1)}, u32[]{:S(2)}, u32[]{:S(2)}) collective-permute-start(bf16[32,512]{1,0:T(8,128)(2,1)} %own_ref.1), channel_id=1, source_target_pairs={{0,2},{1,3},{2,0},{3,1},{4,6},{5,7},{6,4},{7,5},{8,10},{9,11},{10,... | collective-permute-start | bytes 98312 | tf_op jit(solution)/shard_map/ppermute | solution.py:671
  3.0 3.6 %collective-permute-start.2 = (bf16[32,512]{1,0:T(8,128)(2,1)}, bf16[32,512]{1,0:T(8,128)(2,1)S(1)}, u32[]{:S(2)}, u32[]{:S(2)}) collective-permute-start(bf16[32,512]{1,0:T(8,128)(2,1)} %own_ref.1), channel_id=1, source_target_pairs={{0,3},{1,2},{2,1},{3,0},{4,7},{5,6},{6,5},{7,4},{8,11},{9,10},{10,... | collective-permute-start | bytes 98312 | tf_op jit(solution)/shard_map/ppermute | solution.py:671
  3.0 3.6 %collective-permute-start.1 = (bf16[32,512]{1,0:T(8,128)(2,1)}, bf16[32,512]{1,0:T(8,128)(2,1)S(1)}, u32[]{:S(2)}, u32[]{:S(2)}) collective-permute-start(bf16[32,512]{1,0:T(8,128)(2,1)} %own_ref.1), channel_id=1, source_target_pairs={{0,1},{1,0},{2,3},{3,2},{4,5},{5,4},{6,7},{7,6},{8,9},{9,8},{10,11... | collective-permute-start | bytes 98312 | tf_op jit(solution)/shard_map/ppermute | solution.py:671
  13.5 1.3 %collective-permute-start.3 = (bf16[32,1024]{1,0:T(8,128)(2,1)S(1)}, bf16[32,1024]{1,0:T(8,128)(2,1)S(1)}, u32[]{:S(2)}, u32[]{:S(2)}) collective-permute-start(bf16[32,1024]{1,0:T(8,128)(2,1)S(1)} %get-tuple-element.36), channel_id=1, source_target_pairs={{0,1},{1,0},{2,3},{3,2},{4,5},{5,4},{6,7},{7,6},{8,9},{9,8},{10,11... | collective-permute-start | bytes 196616 | tf_op jit(solution)/shard_map/ppermute | solution.py:671
  14.9 5.3 %collective-permute-start.4 = (bf16[32,1024]{1,0:T(8,128)(2,1)S(1)}, bf16[32,1024]{1,0:T(8,128)(2,1)S(1)}, u32[]{:S(2)}, u32[]{:S(2)}) collective-permute-start(bf16[32,1024]{1,0:T(8,128)(2,1)S(1)} %sum.3.refs_0_.refs_2_), channel_id=1, source_target_pairs={{0,2},{1,3},{2,0},{3,1},{4,6},{5,7},{6,4},{7,5},{8,10},{9,11},{10,... | collective-permute-start | bytes 196616 | tf_op jit(solution)/shard_map/ppermute | solution.py:671
  20.2 8.2 %collective-permute-start.7 = (bf16[32,1152]{1,0:T(8,128)(2,1)S(1)}, bf16[32,1152]{1,0:T(8,128)(2,1)S(1)}, u32[]{:S(2)}, u32[]{:S(2)}) collective-permute-start(bf16[32,1152]{1,0:T(8,128)(2,1)S(1)} %get-tuple-element.39.refs_1_.refs_0_), channel_id=1, source_target_pairs={{0,24},{4,28},{8,16},{12,20},{16,8},{20,12},{24,0},{28,4},{1,25},{... | collective-permute-start | bytes 221192 | tf_op jit(solution)/shard_map/ppermute | solution.py:671
  23.9 6.0 %collective-permute-start.6 = (bf16[32,1152]{1,0:T(8,128)(2,1)S(1)}, bf16[32,1152]{1,0:T(8,128)(2,1)S(1)}, u32[]{:S(2)}, u32[]{:S(2)}) collective-permute-start(bf16[32,1152]{1,0:T(8,128)(2,1)S(1)} %get-tuple-element.39.refs_1_.refs_0_), channel_id=1, source_target_pairs={{0,16},{4,20},{8,24},{12,28},{16,0},{20,4},{24,8},{28,12},{1,17},{... | collective-permute-start | bytes 221192 | tf_op jit(solution)/shard_map/ppermute | solution.py:671
  23.9 6.0 %collective-permute-start.5 = (bf16[32,1152]{1,0:T(8,128)(2,1)S(1)}, bf16[32,1152]{1,0:T(8,128)(2,1)S(1)}, u32[]{:S(2)}, u32[]{:S(2)}) collective-permute-start(bf16[32,1152]{1,0:T(8,128)(2,1)S(1)} %get-tuple-element.39.refs_1_.refs_0_), channel_id=1, source_target_pairs={{0,8},{4,12},{8,0},{12,4},{16,24},{20,28},{24,16},{28,20},{1,9},{5... | collective-permute-start | bytes 221192 | tf_op jit(solution)/shard_map/ppermute | solution.py:671
  29.9 2.2 %collective-permute-start.8 = (bf16[128,1152]{1,0:T(8,128)(2,1)S(1)}, bf16[128,1152]{1,0:T(8,128)(2,1)S(1)}, u32[]{:S(2)}, u32[]{:S(2)}) collective-permute-start(bf16[128,1152]{1,0:T(8,128)(2,1)S(1)} %stack.1.mine_ref), channel_id=1, source_target_pairs={{0,1},{1,0},{2,3},{3,2},{4,5},{5,4},{6,7},{7,6},{8,9},{9,8},{10,11... | collective-permute-start | bytes 884744 | tf_op jit(solution)/shard_map/ppermute | solution.py:671
  29.9 9.7 %collective-permute-start.10 = (bf16[128,1152]{1,0:T(8,128)(2,1)S(1)}, bf16[128,1152]{1,0:T(8,128)(2,1)S(1)}, u32[]{:S(2)}, u32[]{:S(2)}) collective-permute-start(bf16[128,1152]{1,0:T(8,128)(2,1)S(1)} %stack.1.mine_ref), channel_id=1, source_target_pairs={{0,4},{4,0},{8,12},{12,8},{16,20},{20,16},{24,28},{28,24},{1,5},{5... | collective-permute-start | bytes 884744 | tf_op jit(solution)/shard_map/ppermute | solution.py:671
  36.0 3.6 %collective-permute-start.9 = (bf16[128,1024]{1,0:T(8,128)(2,1)S(1)}, bf16[128,1024]{1,0:T(8,128)(2,1)S(1)}, u32[]{:S(2)}, u32[]{:S(2)}) collective-permute-start(bf16[128,1024]{1,0:T(8,128)(2,1)S(1)} %get-tuple-element.45.after_ref), channel_id=1, source_target_pairs={{0,1},{1,0},{2,3},{3,2},{4,5},{5,4},{6,7},{7,6},{8,9},{9,8},{10,11... | collective-permute-start | bytes 786440 | tf_op jit(solution)/shard_map/ppermute | solution.py:671
  39.7 2.1 %collective-permute-start.11 = (bf16[128,1152]{1,0:T(8,128)(2,1)S(1)}, bf16[128,1152]{1,0:T(8,128)(2,1)S(1)}, u32[]{:S(2)}, u32[]{:S(2)}) collective-permute-start(bf16[128,1152]{1,0:T(8,128)(2,1)S(1)} %hold.2.mine_ref), channel_id=1, source_target_pairs={{0,1},{1,0},{2,3},{3,2},{4,5},{5,4},{6,7},{7,6},{8,9},{9,8},{10,11... | collective-permute-start | bytes 884744 | tf_op jit(solution)/shard_map/ppermute | solution.py:671
  43.8 1.7 %collective-permute-start.12 = (bf16[128,1024]{1,0:T(8,128)(2,1)S(1)}, bf16[128,1024]{1,0:T(8,128)(2,1)S(1)}, u32[]{:S(2)}, u32[]{:S(2)}) collective-permute-start(bf16[128,1024]{1,0:T(8,128)(2,1)S(1)} %get-tuple-element.49), channel_id=1, source_target_pairs={{0,1},{1,0},{2,3},{3,2},{4,5},{5,4},{6,7},{7,6},{8,9},{9,8},{10,11... | collective-permute-start | bytes 786440 | tf_op jit(solution)/shard_map/ppermute | solution.py:671
  45.6 8.7 %collective-permute-start.13 = (bf16[128,512]{1,0:T(8,128)(2,1)S(1)}, bf16[128,512]{1,0:T(8,128)(2,1)S(1)}, u32[]{:S(2)}, u32[]{:S(2)}) collective-permute-start(bf16[128,512]{1,0:T(8,128)(2,1)S(1)} %hold.3), channel_id=1, source_target_pairs={{0,2},{1,3},{2,0},{3,1},{4,6},{5,7},{6,4},{7,5},{8,10},{9,11},{10,... | collective-permute-start | bytes 393224 | tf_op jit(solution)/shard_map/ppermute | solution.py:671
  46.2 8.1 %collective-permute-start.15 = (bf16[128,512]{1,0:T(8,128)(2,1)S(1)}, bf16[128,512]{1,0:T(8,128)(2,1)S(1)}, u32[]{:S(2)}, u32[]{:S(2)}) collective-permute-start(bf16[128,512]{1,0:T(8,128)(2,1)S(1)} %get-tuple-element.51), channel_id=1, source_target_pairs={{0,6},{1,7},{2,4},{3,5},{4,2},{5,3},{6,0},{7,1},{8,14},{9,15},{10,... | collective-permute-start | bytes 393224 | tf_op jit(solution)/shard_map/ppermute | solution.py:739
  49.0 6.6 %collective-permute-start.14 = (bf16[128,512]{1,0:T(8,128)(2,1)S(1)}, bf16[128,512]{1,0:T(8,128)(2,1)S(1)}, u32[]{:S(2)}, u32[]{:S(2)}) collective-permute-start(bf16[128,512]{1,0:T(8,128)(2,1)S(1)} %get-tuple-element.50.after_ref), channel_id=1, source_target_pairs={{0,4},{1,5},{2,6},{3,7},{4,0},{5,1},{6,2},{7,3},{8,12},{9,13},{10,... | collective-permute-start | bytes 393224 | tf_op jit(solution)/shard_map/ppermute | solution.py:739
  55.6 4.0 %collective-permute-start.16 = (bf16[32,512]{1,0:T(8,128)(2,1)S(1)}, bf16[32,512]{1,0:T(8,128)(2,1)S(1)}, u32[]{:S(2)}, u32[]{:S(2)}) collective-permute-start(bf16[32,512]{1,0:T(8,128)(2,1)S(1)} %get-tuple-element.53), channel_id=1, source_target_pairs={{0,8},{4,12},{8,0},{12,4},{16,24},{20,28},{24,16},{28,20},{1,9},{5... | collective-permute-start | bytes 98312 | tf_op jit(solution)/shard_map/ppermute | solution.py:671
  56.7 5.7 %collective-permute-start.18 = (bf16[32,512]{1,0:T(8,128)(2,1)S(1)}, bf16[32,512]{1,0:T(8,128)(2,1)S(1)}, u32[]{:S(2)}, u32[]{:S(2)}) collective-permute-start(bf16[32,512]{1,0:T(8,128)(2,1)S(1)} %get-tuple-element.54), channel_id=1, source_target_pairs={{0,24},{4,28},{8,16},{12,20},{16,8},{20,12},{24,0},{28,4},{1,25},{... | collective-permute-start | bytes 98312 | tf_op jit(solution)/shard_map/ppermute | solution.py:671
  58.3 4.8 %collective-permute-start.17 = (bf16[32,512]{1,0:T(8,128)(2,1)S(1)}, bf16[32,512]{1,0:T(8,128)(2,1)S(1)}, u32[]{:S(2)}, u32[]{:S(2)}) collective-permute-start(bf16[32,512]{1,0:T(8,128)(2,1)S(1)} %get-tuple-element.55), channel_id=1, source_target_pairs={{0,16},{4,20},{8,24},{12,28},{16,0},{20,4},{24,8},{28,12},{1,17},{... | collective-permute-start | bytes 98312 | tf_op jit(solution)/shard_map/ppermute | solution.py:671

commit v10 on v9

--- a/solution.py
+++ b/solution.py
@@ -1,4 +1,5 @@
 import functools
+import itertools
 import jax
 import jax.numpy as jnp
 from jax import lax
@@ -10,8 +11,9 @@
 norm_eps = 1e-05
 LANES = 128
 SUBLANES = 8
-CHUNK = 128
+CHUNK = 96
 GROUP = 8
+TOGETHER = 1
 MASKED = -1e30
 
 
@@ -201,9 +203,9 @@
             [jnp.concatenate([a, blank], axis=1), jnp.concatenate([blank, b], axis=1)], axis=0
         )
 
-    @pl.loop(0, rows // GROUP)
-    def _(g):
-        requests = [g * GROUP + i for i in range(GROUP)]
+    @pl.loop(0, rows // (GROUP * TOGETHER))
+    def _(step):
+        requests = [step * GROUP * TOGETHER + i for i in range(GROUP * TOGETHER)]
         pairs = list(zip(requests[::2], requests[1::2]))
         lengths = [lengths_ref[r] for r in requests]
         spans = list(zip(lengths[::2], lengths[1::2]))
@@ -213,12 +215,18 @@
         ]
         own = [jnp.concatenate([a, b], axis=0) for a, b in zip(own[::2], own[1::2])]
         values = [diagonal(value_s[a], value_s[b]) for a, b in pairs]
-        longest = functools.reduce(jnp.maximum, lengths)
-        used = used_rows(sum((length + 7) // 8 * 8 for length in lengths), heads_local)
-        cache_copy(k_ref, k_s, k_sem, g * GROUP, used).wait()
-        cache_copy(v_ref, v_s, v_sem, g * GROUP, used).wait()
-
-        def with_chunks(count):
+        needed = []
+        for i in range(TOGETHER):
+            part = lengths[i * GROUP : (i + 1) * GROUP]
+            needed.append((functools.reduce(jnp.maximum, part) + CHUNK - 1) // CHUNK)
+            used = used_rows(sum((length + 7) // 8 * 8 for length in part), heads_local)
+            first = requests[i * GROUP]
+            cache_copy(k_ref, k_s, k_sem, first, used).wait()
+            cache_copy(v_ref, v_s, v_sem, first, used).wait()
+
+        def with_chunks(counts):
+            counts = [count for count in counts for _ in range(GROUP // 2)]
+
             def both(ref, c, pair, span):
                 parts = []
                 for r, length in zip(pair, span):
@@ -237,7 +245,7 @@
                     )
                     for c in range(count)
                 ]
-                for query, pair, span in zip(queries, pairs, spans)
+                for count, query, pair, span in zip(counts, queries, pairs, spans)
             ]
             limits = [
                 jnp.where(upper, span[0] * heads_local, span[1] * heads_local) for span in spans
@@ -280,10 +288,12 @@
                 attended_s[a] = summed[:SUBLANES, :LANES]
                 attended_s[b] = summed[SUBLANES:, LANES:]
 
-        for count in range(1, cache_rows // chunk_rows + 1):
-            pl.when((longest + CHUNK - 1) // CHUNK == count)(
-                functools.partial(with_chunks, count)
+        most = cache_rows // chunk_rows
+        for counts in itertools.product(range(1, most + 1), repeat=TOGETHER):
+            chosen = functools.reduce(
+                jnp.logical_and, [have == count for have, count in zip(needed, counts)]
             )
+            pl.when(chosen)(functools.partial(with_chunks, counts))
 
     attended = jnp.concatenate(
         [attended_s[:, h, :] for h in range(heads_local)], axis=1
@@ -511,9 +521,7 @@
 def first_kernel(mine_ref, w_ref, _, product_ref):
     _, head_count, cols, _ = w_ref.shape
     steps, per_step = steps_of(w_ref.shape)
-
-    @pl.loop(0, steps, unroll=4)
-    def _(p):
+    for p in range(steps):
         states = mine_ref[:, : head_count // 2 * cols]
         product_ref[p] = expert_products(states, w_ref, 0, p, per_step)
 
@@ -603,19 +611,19 @@
         ).astype(jnp.bfloat16)
 
 
-def down_kernel(firsts, units_ref, w_ref, *outs):
+def down_kernel(firsts, units_ref, w_ref, _, *outs):
     for first, out_ref in zip(firsts, outs):
         down_blocks(units_ref[...], w_ref, first, out_ref)
 
 
-def down_part(units, w_down, firsts):
+def down_part(units, w_down, firsts, after):
     head_count, total_units, cols = w_down.shape
     tokens = units.shape[0]
     half = jax.ShapeDtypeStruct((tokens, head_count // 2 * cols), jnp.bfloat16)
     return pl.pallas_call(
         functools.partial(down_kernel, firsts),
         out_shape=[half] * len(firsts),
-        in_specs=[VMEM, VMEM],
+        in_specs=[VMEM, VMEM, ANY],
         out_specs=[VMEM] * len(firsts),
         compiler_params=pltpu.CompilerParams(vmem_limit_bytes=12 * 2**20),
         cost_estimate=pl.CostEstimate(
@@ -624,7 +632,7 @@
             transcendentals=0,
         ),
         name="down",
-    )(units, in_vmem(w_down))
+    )(units, in_vmem(w_down), after)
 
 
 def hold_kernel(value_ref, after_ref, out_ref):
@@ -718,18 +726,16 @@
     line_other = swap(line, "head", head_size, 1)
     crossed = swap(line, "req", req_size, 1)
     units = experts_whole(me_ref, line, line_other, buffer, token, w_down_near.shape[1])
-    keep, send = down_part(units, w_down_near, (0, 1))
+    keep, send = down_part(units, w_down_near, (0, 1), token)
+    line_sums = sum_part(keep, swap(send, "head", head_size, 1), cols, jnp.float32)
     crossed = hold(crossed, send)
     crossed_other = swap(crossed, "head", head_size, 1)
-    line_sums = sum_part(keep, swap(send, "head", head_size, 1), cols, jnp.float32)
-    total = line_sums[0]
     products = experts_first(crossed, buffer, line_sums[-1])
     units, send = experts_second(me_ref, crossed, crossed_other, products, buffer, w_down_near)
-    (keep,) = down_part(units, w_down_near, (0,))
+    (keep,) = down_part(units, w_down_near, (0,), send)
     crossed_sums = sum_part(keep, swap(send, "head", head_size, 1), cols, jnp.bfloat16)
-    got = [
-        swap(hold(line_sums[j // 2], crossed_sums[0]), "head", head_size, j) for j in even if j
-    ]
+    total = line_sums[0]
+    got = [swap(hold(line_sums[j // 2], keep), "head", head_size, j) for j in even if j]
     for j in even:
         pairs = [
             (r * head_size + h, (r ^ 1) * head_size + (h ^ j))

time: 64.2 us -> 62.9 us (0.980)
  Pallas kernels: 26.2 us -> 24.8 us
  starting transfers between devices: 19.4 us -> 18.5 us
    ppermute x2, waiting for transfers between devices: 1.23 us -> 4.12 us  [per_device(): got.append(lax.ppermute(crossed_sums[j // 2], ('req', 'head'), pairs))]
    ppermute x17, waiting for transfers between devices: 16 us -> 13.7 us  [swap(): return lax.ppermute(value, axis, [(i, i ^ mask) for i in range(size)])]
    ppermute x17, starting transfers between devices: 16.4 us -> 15.5 us  [swap(): return lax.ppermute(value, axis, [(i, i ^ mask) for i in range(size)])]
    pallas_call x1, Pallas kernels: 6.9 us -> 6.2 us  [attention(): pl.pallas_call(functools.partial(attention_kernel, head_count), out_shape...]
    pallas_call x1, Pallas kernels: 1.99 us -> 1.3 us  [experts_first(): pl.pallas_call(first_kernel, out_shape=jax.ShapeDtypeStruct((steps, token...]
  transfers between devices with their start and end apart: 19 -> 19, of which waited for: 10 -> 12; matrix products, arithmetic and copies ran while one was open for 0% -> 0% of each run, Pallas kernels for 27% -> 27%
where the time goes in v10:
time: 62.9 us; the launch traced here: 62 us
  Pallas kernels  24.8 us (39%)
  starting transfers between devices  18.5 us (29%)
  waiting for transfers between devices  17.8 us (28%)
  other arithmetic  0.73 us (1%)
    ppermute x17, starting transfers between devices, swap(): return lax.ppermute(value, axis, [(i, i ^ mask) for i in range(size)])  15.5 us
    ppermute x17, waiting for transfers between devices, swap(): return lax.ppermute(value, axis, [(i, i ^ mask) for i in range(size)])  13.7 us
    pallas_call x2, Pallas kernels, by_expert(): pl.pallas_call(functools.partial(relayout_kernel, js), out_shape=(pltpu.V...  7.43 us
    pallas_call x1, Pallas kernels, attention(): pl.pallas_call(functools.partial(attention_kernel, head_count), out_shape...  6.2 us
    ppermute x2, waiting for transfers between devices, per_device(): got.append(lax.ppermute(crossed_sums[j // 2], ('req', 'head'), pairs))  4.12 us
    ppermute x2, starting transfers between devices, per_device(): got.append(lax.ppermute(crossed_sums[j // 2], ('req', 'head'), pairs))  3.04 us
    pallas_call x1, Pallas kernels, fetch(): pl.pallas_call(fetch_kernel, out_shape=(pltpu.VMEM(hidden.shape, jnp.bflo...  2.94 us
    pallas_call x1, Pallas kernels, experts_whole(): pl.pallas_call(whole_kernel, out_shape=jax.ShapeDtypeStruct((tokens, tota...  2.68 us
  transfers between devices with their start and end apart: 19, of which 12 were waited for; matrix products, arithmetic and copies ran while one was open for 0% of the time, Pallas kernels for 27%

profile of v10, /device:TPU:0, one launch (start us, length us, event | category | flops | bytes accessed | tf_op | source)
XLA Modules:
  0.0 62.0 jit_solution(12204799636564407705)
XLA Ops:
  0.0 3.0 %collective-permute-start = (bf16[32,512]{1,0:T(8,128)(2,1)}, bf16[32,512]{1,0:T(8,128)(2,1)S(1)}, u32[]{:S(2)}, u32[]{:S(2)}) collective-permute-start(bf16[32,512]{1,0:T(8,128)(2,1)} %own_ref.1), channel_id=1, source_target_pairs={{0,2},{1,3},{2,0},{3,1},{4,6},{5,7},{6,4},{7,5},{8,10},{9,11},{10,... | collective-permute-start | bytes 98312 | tf_op jit(solution)/shard_map/ppermute | solution.py:679
  3.0 0.0 collective-permute-start.2
  3.0 0.1 collective-permute-start.1
  3.1 2.9 %fetch.1 = (bf16[32,512]{1,0:T(8,128)(2,1)S(1)}, bf16[3,4,512,512]{3,2,1,0:T(8,128)(2,1)S(1)}, bf16[49152,128]{1,0:T(8,128)(2,1)S(1)}, f32[32,128]{1,0:T(8,128)S...) custom-call(s32[32]{0:T(128)} %lengths_hbm.1, s32[1]{0:T(128)} %bitcast.me_ref, ...), custom_call_target="tpu_custom_call" | custom-call | bytes 12582912 | tf_op jit(solution)/shard_map/fetch/pallas_call | solution.py:101
  6.1 0.0 collective-permute-done.refs_2_.refs_1_
  6.1 0.5 collective-permute-done.2.refs_3_
  6.6 0.0 collective-permute-done.1.refs_1_
  6.6 6.2 %attention.1 = (bf16[32,1024]{1,0:T(8,128)(2,1)S(1)}, bf16[32,1024]{1,0:T(8,128)(2,1)S(1)}, bf16[49152,128]{1,0:T(8,128)(2,1)S(1)}, bf16[4,2048,512]{2,1,0:T(8,128)(2,1)S(1)}) custom-call(s32[32]{0:T(128)S(4)} %get-tuple-element.30.lengths_ref, s32[1]{0:T(128)} %bitcast.me_ref, ...), custom_call_target="tpu_custom_call", output_to_operand_aliasing={{2}: (9, {})} | custom-call | flops 268435456 | bytes 11534336 | tf_op jit(solution)/shard_map/attention/pallas_call | solution.py:315
  12.8 0.1 collective-permute-start.3
  12.9 1.2 %collective-permute-done.3.sent_ref = bf16[32,1024]{1,0:T(8,128)(2,1)S(1)} collective-permute-done((bf16[32,1024]{1,0:T(8,128)(2,1)S(1)}, bf16[32,1024]{1,0:T(8,128)(2,1)S(1)}, u32[]{:S(2)}, u32[]{:S(2)}) %collective-permute-start.3) | collective-permute-done | bytes 65568 | tf_op jit(solution)/shard_map/ppermute | solution.py:679
  14.2 1.6 %collective-permute-start.4 = (bf16[32,1024]{1,0:T(8,128)(2,1)S(1)}, bf16[32,1024]{1,0:T(8,128)(2,1)S(1)}, u32[]{:S(2)}, u32[]{:S(2)}) collective-permute-start(bf16[32,1024]{1,0:T(8,128)(2,1)S(1)} %sum.3.refs_0_.refs_2_), channel_id=1, source_target_pairs={{0,2},{1,3},{2,0},{3,1},{4,6},{5,7},{6,4},{7,5},{8,10},{9,11},{10,... | collective-permute-start | bytes 196616 | tf_op jit(solution)/shard_map/ppermute | solution.py:679
  15.8 3.7 %by_expert_0.1 = (bf16[16,4,512,256]{3,2,1,0:T(8,128)(2,1)S(1)}, f32[8,128]{1,0:T(8,128)S(1)}) custom-call(s32[1]{0:T(128)} %bitcast.me_ref, bf16[2048,16,256]{2,1,0:T(8,128)(2,1)} %w_ref.5, bf16[32,1024]{1,0:T(8,128)(2,1)S(1)} %sum.3.refs_0_.refs_2_), custom_call_target="tpu_custom_call" | custom-call | bytes 16777216 | tf_op jit(solution)/shard_map/by_expert_0/pallas_call | solution.py:392
  19.5 0.0 collective-permute-done.4.refs_3_
  19.6 3.4 %collective-permute-start.7 = (bf16[32,1152]{1,0:T(8,128)(2,1)S(1)}, bf16[32,1152]{1,0:T(8,128)(2,1)S(1)}, u32[]{:S(2)}, u32[]{:S(2)}) collective-permute-start(bf16[32,1152]{1,0:T(8,128)(2,1)S(1)} %get-tuple-element.39.refs_1_.refs_0_), channel_id=1, source_target_pairs={{0,24},{4,28},{8,16},{12,20},{16,8},{20,12},{24,0},{28,4},{1,25},{... | collective-permute-start | bytes 221192 | tf_op jit(solution)/shard_map/ppermute | solution.py:679
  23.0 0.2 collective-permute-start.6
  23.2 0.8 %collective-permute-start.5 = (bf16[32,1152]{1,0:T(8,128)(2,1)S(1)}, bf16[32,1152]{1,0:T(8,128)(2,1)S(1)}, u32[]{:S(2)}, u32[]{:S(2)}) collective-permute-start(bf16[32,1152]{1,0:T(8,128)(2,1)S(1)} %get-tuple-element.39.refs_1_.refs_0_), channel_id=1, source_target_pairs={{0,8},{4,12},{8,0},{12,4},{16,24},{20,28},{24,16},{28,20},{1,9},{5... | collective-permute-start | bytes 221192 | tf_op jit(solution)/shard_map/ppermute | solution.py:679
  24.0 3.7 %by_expert_2.1 = (bf16[16,4,512,256]{3,2,1,0:T(8,128)(2,1)S(1)}, f32[8,128]{1,0:T(8,128)S(1)}) custom-call(s32[1]{0:T(128)} %bitcast.me_ref, bf16[2048,16,256]{2,1,0:T(8,128)(2,1)} %w_ref.5, bf16[16,4,512,256]{3,2,1,0:T(8,128)(2,1)S(1)} %get-tuple-element.40.refs_0_, ...), custom_call_target="tpu_custom_call", output_to_operand_aliasing={{0}: (2, {})} | custom-call | bytes 16777216 | tf_op jit(solution)/shard_map/by_expert_2/pallas_call | solution.py:392
  27.8 0.0 collective-permute-done.7.refs_3_
  27.8 2.2 %collective-permute-done.6.refs_2_ = bf16[32,1152]{1,0:T(8,128)(2,1)S(1)} collective-permute-done((bf16[32,1152]{1,0:T(8,128)(2,1)S(1)}, bf16[32,1152]{1,0:T(8,128)(2,1)S(1)}, u32[]{:S(2)}, u32[]{:S(2)}) %collective-permute-start.6) | collective-permute-done | bytes 73760 | tf_op jit(solution)/shard_map/ppermute | solution.py:679
  29.9 0.0 collective-permute-done.5.refs_1_
  30.0 0.1 collective-permute-start.8
  30.1 1.4 %collective-permute-start.10 = (bf16[128,1152]{1,0:T(8,128)(2,1)S(1)}, bf16[128,1152]{1,0:T(8,128)(2,1)S(1)}, u32[]{:S(2)}, u32[]{:S(2)}) collective-permute-start(bf16[128,1152]{1,0:T(8,128)(2,1)S(1)} %stack.1.mine_ref), channel_id=1, source_target_pairs={{0,4},{4,0},{8,12},{12,8},{16,20},{20,16},{24,28},{28,24},{1,5},{5... | collective-permute-start | bytes 884744 | tf_op jit(solution)/shard_map/ppermute | solution.py:679
  31.4 0.2 collective-permute-done.8.other_ref
  31.6 2.7 %experts_whole.1.units_ref = bf16[128,2048]{1,0:T(8,128)(2,1)S(1)} custom-call(s32[1]{0:T(128)} %bitcast.me_ref, bf16[128,1152]{1,0:T(8,128)(2,1)S(1)} %stack.1.mine_ref, bf16[128,1152]{1,0:T(8,128)(2,1)S(1)} %collective-permute-done.8.other_ref, bf16[16,4,512,256]{3,2,1,0:T(8,128)(2,1)S(1)} %get-tuple-element.42.w_ref, f32[8,128]{1,0:T(8,128)S(1)} %get-tuple-element.41.refs_4_._), custom_call_target="tpu_custom_call" | custom-call | flops 2147483648 | bytes 16777216 | tf_op jit(solution)/shard_map/experts_whole/pallas_call | solution.py:550
  34.3 1.3 %down.2 = (bf16[128,1024]{1,0:T(8,128)(2,1)S(1)}, bf16[128,1024]{1,0:T(8,128)(2,1)S(1)}) custom-call(bf16[128,2048]{1,0:T(8,128)(2,1)S(1)} %experts_whole.1.units_ref, bf16[4,2048,512]{2,1,0:T(8,128)(2,1)S(1)} %get-tuple-element.43.w_ref.w_down_ref, f32[8,128]{1,0:T(8,128)S(1)} %get-tuple-element.41.refs_4_._), custom_call_target="tpu_custom_call" | custom-call | flops 1073741824 | bytes 8388608 | tf_op jit(solution)/shard_map/down/pallas_call | solution.py:623
  35.6 0.2 collective-permute-start.9
  35.8 3.7 %collective-permute-done.10.value_ref = bf16[128,1152]{1,0:T(8,128)(2,1)S(1)} collective-permute-done((bf16[128,1152]{1,0:T(8,128)(2,1)S(1)}, bf16[128,1152]{1,0:T(8,128)(2,1)S(1)}, u32[]{:S(2)}, u32[]{:S(2)}) %collective-permute-start.10) | collective-permute-done | bytes 294944 | tf_op jit(solution)/shard_map/ppermute | solution.py:679
  39.5 0.0 collective-permute-start.11
  39.5 0.0 collective-permute-done.9.sent_ref
  39.5 0.1 sum.4
  39.6 1.3 %experts_first.1.product_ref = f32[16,128,256]{2,1,0:T(8,128)S(1)} custom-call(bf16[128,1152]{1,0:T(8,128)(2,1)S(1)} %hold.2.mine_ref, bf16[16,4,512,256]{3,2,1,0:T(8,128)(2,1)S(1)} %get-tuple-element.42.w_ref, bf16[128,512]{1,0:T(8,128)(2,1)S(1)} %get-tuple-element.47._.value_ref), custom_call_target="tpu_custom_call" | custom-call | flops 1073741824 | bytes 8388608 | tf_op jit(solution)/shard_map/experts_first/pallas_call | solution.py:570
  40.9 0.2 collective-permute-done.11.other_ref
  41.1 2.1 %experts_second.1 = (bf16[128,2048]{1,0:T(8,128)(2,1)S(1)}, bf16[128,1024]{1,0:T(8,128)(2,1)S(1)}) custom-call(s32[1]{0:T(128)} %bitcast.me_ref, bf16[128,1152]{1,0:T(8,128)(2,1)S(1)} %hold.2.mine_ref, bf16[128,1152]{1,0:T(8,128)(2,1)S(1)} %collective-permute-done.11.other_ref, f32[16,128,256]{2,1,0:T(8,128)S(1)} %experts_first.1.product_ref, ...), custom_call_target="tpu_custom_call" | custom-call | flops 1073741824 | bytes 8388608 | tf_op jit(solution)/shard_map/experts_second/pallas_call | solution.py:588
  43.2 0.4 collective-permute-start.13
  43.5 0.7 %down.3.after_ref.keep_ref = bf16[128,1024]{1,0:T(8,128)(2,1)S(1)} custom-call(bf16[128,2048]{1,0:T(8,128)(2,1)S(1)} %get-tuple-element.48.units_ref, bf16[4,2048,512]{2,1,0:T(8,128)(2,1)S(1)} %get-tuple-element.43.w_ref.w_down_ref, bf16[128,1024]{1,0:T(8,128)(2,1)S(1)} %get-tuple-element.49._), custom_call_target="tpu_custom_call" | custom-call | flops 536870912 | bytes 4194304 | tf_op jit(solution)/shard_map/down/pallas_call | solution.py:623
  44.3 0.6 collective-permute-start.12
  44.8 0.0 collective-permute-done.13.sent_ref
  44.8 0.1 sum.5
  44.9 1.4 %collective-permute-start.14 = (bf16[128,512]{1,0:T(8,128)(2,1)S(1)}, bf16[128,512]{1,0:T(8,128)(2,1)S(1)}, u32[]{:S(2)}, u32[]{:S(2)}) collective-permute-start(bf16[128,512]{1,0:T(8,128)(2,1)S(1)} %get-tuple-element.50), channel_id=1, source_target_pairs={{0,4},{1,5},{2,6},{3,7},{4,0},{5,1},{6,2},{7,3},{8,12},{9,13},{10,... | collective-permute-start | bytes 393224 | tf_op jit(solution)/shard_map/ppermute | solution.py:745
  46.3 1.7 %collective-permute-start.15 = (bf16[128,512]{1,0:T(8,128)(2,1)S(1)}, bf16[128,512]{1,0:T(8,128)(2,1)S(1)}, u32[]{:S(2)}, u32[]{:S(2)}) collective-permute-start(bf16[128,512]{1,0:T(8,128)(2,1)S(1)} %get-tuple-element.51), channel_id=1, source_target_pairs={{0,6},{1,7},{2,4},{3,5},{4,2},{5,3},{6,0},{7,1},{8,14},{9,15},{10,... | collective-permute-start | bytes 393224 | tf_op jit(solution)/shard_map/ppermute | solution.py:745
  48.0 2.0 %collective-permute-done.12 = bf16[128,512]{1,0:T(8,128)(2,1)S(1)} collective-permute-done((bf16[128,512]{1,0:T(8,128)(2,1)S(1)}, bf16[128,512]{1,0:T(8,128)(2,1)S(1)}, u32[]{:S(2)}, u32[]{:S(2)}) %collective-permute-start.12) | collective-permute-done | bytes 131104 | tf_op jit(solution)/shard_map/ppermute | solution.py:679
  49.9 1.4 %collective-permute-done.14 = bf16[128,512]{1,0:T(8,128)(2,1)S(1)} collective-permute-done((bf16[128,512]{1,0:T(8,128)(2,1)S(1)}, bf16[128,512]{1,0:T(8,128)(2,1)S(1)}, u32[]{:S(2)}, u32[]{:S(2)}) %collective-permute-start.14) | collective-permute-done | bytes 131104 | tf_op jit(solution)/shard_map/ppermute | solution.py:745
  51.3 2.8 %collective-permute-done.15 = bf16[128,512]{1,0:T(8,128)(2,1)S(1)} collective-permute-done((bf16[128,512]{1,0:T(8,128)(2,1)S(1)}, bf16[128,512]{1,0:T(8,128)(2,1)S(1)}, u32[]{:S(2)}, u32[]{:S(2)}) %collective-permute-start.15) | collective-permute-done | bytes 131104 | tf_op jit(solution)/shard_map/ppermute | solution.py:745
  54.1 0.1 add_convert_fusion
  54.2 0.4 collective-permute-start.16
  54.5 2.0 %collective-permute-start.18 = (bf16[32,512]{1,0:T(8,128)(2,1)S(1)}, bf16[32,512]{1,0:T(8,128)(2,1)S(1)}, u32[]{:S(2)}, u32[]{:S(2)}) collective-permute-start(bf16[32,512]{1,0:T(8,128)(2,1)S(1)} %get-tuple-element.54), channel_id=1, source_target_pairs={{0,24},{4,28},{8,16},{12,20},{16,8},{20,12},{24,0},{28,4},{1,25},{... | collective-permute-start | bytes 98312 | tf_op jit(solution)/shard_map/ppermute | solution.py:679
  56.6 1.1 %collective-permute-start.17 = (bf16[32,512]{1,0:T(8,128)(2,1)S(1)}, bf16[32,512]{1,0:T(8,128)(2,1)S(1)}, u32[]{:S(2)}, u32[]{:S(2)}) collective-permute-start(bf16[32,512]{1,0:T(8,128)(2,1)S(1)} %get-tuple-element.55), channel_id=1, source_target_pairs={{0,16},{4,20},{8,24},{12,28},{16,0},{20,4},{24,8},{28,12},{1,17},{... | collective-permute-start | bytes 98312 | tf_op jit(solution)/shard_map/ppermute | solution.py:679
  57.7 0.7 %collective-permute-done.16 = bf16[32,512]{1,0:T(8,128)(2,1)S(1)} collective-permute-done((bf16[32,512]{1,0:T(8,128)(2,1)S(1)}, bf16[32,512]{1,0:T(8,128)(2,1)S(1)}, u32[]{:S(2)}, u32[]{:S(2)}) %collective-permute-start.16) | collective-permute-done | bytes 32800 | tf_op jit(solution)/shard_map/ppermute | solution.py:679
  58.4 1.8 %collective-permute-done.18 = bf16[32,512]{1,0:T(8,128)(2,1)S(1)} collective-permute-done((bf16[32,512]{1,0:T(8,128)(2,1)S(1)}, bf16[32,512]{1,0:T(8,128)(2,1)S(1)}, u32[]{:S(2)}, u32[]{:S(2)}) %collective-permute-start.18) | collective-permute-done | bytes 32800 | tf_op jit(solution)/shard_map/ppermute | solution.py:679
  60.3 1.1 %collective-permute-done.17 = bf16[32,512]{1,0:T(8,128)(2,1)S(1)} collective-permute-done((bf16[32,512]{1,0:T(8,128)(2,1)S(1)}, bf16[32,512]{1,0:T(8,128)(2,1)S(1)}, u32[]{:S(2)}, u32[]{:S(2)}) %collective-permute-start.17) | collective-permute-done | bytes 32800 | tf_op jit(solution)/shard_map/ppermute | solution.py:679
  61.4 0.6 %add_convert_fusion.1 = bf16[32,512]{1,0:T(8,128)(2,1)} fusion(f32[32,512]{1,0:T(8,128)S(1)} %get-tuple-element.52, bf16[32,512]{1,0:T(8,128)(2,1)S(1)} %collective-permute-done.18, bf16[32,512]{1,0:T(8,128)(2,1)S(1)} %collective-permute-done.17, bf16[32,512]{1,0:T(8,128)(2,1)S(1)} %collective-permute-done.16, bf16[128,512]{1,0:T(8,128)(2,1)S(1)} %add_convert_fusion), kind=kLoop, calls=%fused_computation.1 | loop fusion | flops 147456 | bytes 229376 | tf_op jit(solution)/shard_map/convert_element_type | solution.py:752
  (7 shorter events, 0.1 us)
Async XLA Ops:
  0.0 6.1 %collective-permute-start = (bf16[32,512]{1,0:T(8,128)(2,1)}, bf16[32,512]{1,0:T(8,128)(2,1)S(1)}, u32[]{:S(2)}, u32[]{:S(2)}) collective-permute-start(bf16[32,512]{1,0:T(8,128)(2,1)} %own_ref.1), channel_id=1, source_target_pairs={{0,2},{1,3},{2,0},{3,1},{4,6},{5,7},{6,4},{7,5},{8,10},{9,11},{10,... | collective-permute-start | bytes 98312 | tf_op jit(solution)/shard_map/ppermute | solution.py:679
  3.0 3.6 %collective-permute-start.2 = (bf16[32,512]{1,0:T(8,128)(2,1)}, bf16[32,512]{1,0:T(8,128)(2,1)S(1)}, u32[]{:S(2)}, u32[]{:S(2)}) collective-permute-start(bf16[32,512]{1,0:T(8,128)(2,1)} %own_ref.1), channel_id=1, source_target_pairs={{0,3},{1,2},{2,1},{3,0},{4,7},{5,6},{6,5},{7,4},{8,11},{9,10},{10,... | collective-permute-start | bytes 98312 | tf_op jit(solution)/shard_map/ppermute | solution.py:679
  3.0 3.6 %collective-permute-start.1 = (bf16[32,512]{1,0:T(8,128)(2,1)}, bf16[32,512]{1,0:T(8,128)(2,1)S(1)}, u32[]{:S(2)}, u32[]{:S(2)}) collective-permute-start(bf16[32,512]{1,0:T(8,128)(2,1)} %own_ref.1), channel_id=1, source_target_pairs={{0,1},{1,0},{2,3},{3,2},{4,5},{5,4},{6,7},{7,6},{8,9},{9,8},{10,11... | collective-permute-start | bytes 98312 | tf_op jit(solution)/shard_map/ppermute | solution.py:679
  12.8 1.3 %collective-permute-start.3 = (bf16[32,1024]{1,0:T(8,128)(2,1)S(1)}, bf16[32,1024]{1,0:T(8,128)(2,1)S(1)}, u32[]{:S(2)}, u32[]{:S(2)}) collective-permute-start(bf16[32,1024]{1,0:T(8,128)(2,1)S(1)} %get-tuple-element.36), channel_id=1, source_target_pairs={{0,1},{1,0},{2,3},{3,2},{4,5},{5,4},{6,7},{7,6},{8,9},{9,8},{10,11... | collective-permute-start | bytes 196616 | tf_op jit(solution)/shard_map/ppermute | solution.py:679
  14.2 5.4 %collective-permute-start.4 = (bf16[32,1024]{1,0:T(8,128)(2,1)S(1)}, bf16[32,1024]{1,0:T(8,128)(2,1)S(1)}, u32[]{:S(2)}, u32[]{:S(2)}) collective-permute-start(bf16[32,1024]{1,0:T(8,128)(2,1)S(1)} %sum.3.refs_0_.refs_2_), channel_id=1, source_target_pairs={{0,2},{1,3},{2,0},{3,1},{4,6},{5,7},{6,4},{7,5},{8,10},{9,11},{10,... | collective-permute-start | bytes 196616 | tf_op jit(solution)/shard_map/ppermute | solution.py:679
  19.6 8.2 %collective-permute-start.7 = (bf16[32,1152]{1,0:T(8,128)(2,1)S(1)}, bf16[32,1152]{1,0:T(8,128)(2,1)S(1)}, u32[]{:S(2)}, u32[]{:S(2)}) collective-permute-start(bf16[32,1152]{1,0:T(8,128)(2,1)S(1)} %get-tuple-element.39.refs_1_.refs_0_), channel_id=1, source_target_pairs={{0,24},{4,28},{8,16},{12,20},{16,8},{20,12},{24,0},{28,4},{1,25},{... | collective-permute-start | bytes 221192 | tf_op jit(solution)/shard_map/ppermute | solution.py:679
  23.0 6.9 %collective-permute-start.6 = (bf16[32,1152]{1,0:T(8,128)(2,1)S(1)}, bf16[32,1152]{1,0:T(8,128)(2,1)S(1)}, u32[]{:S(2)}, u32[]{:S(2)}) collective-permute-start(bf16[32,1152]{1,0:T(8,128)(2,1)S(1)} %get-tuple-element.39.refs_1_.refs_0_), channel_id=1, source_target_pairs={{0,16},{4,20},{8,24},{12,28},{16,0},{20,4},{24,8},{28,12},{1,17},{... | collective-permute-start | bytes 221192 | tf_op jit(solution)/shard_map/ppermute | solution.py:679
  23.2 6.8 %collective-permute-start.5 = (bf16[32,1152]{1,0:T(8,128)(2,1)S(1)}, bf16[32,1152]{1,0:T(8,128)(2,1)S(1)}, u32[]{:S(2)}, u32[]{:S(2)}) collective-permute-start(bf16[32,1152]{1,0:T(8,128)(2,1)S(1)} %get-tuple-element.39.refs_1_.refs_0_), channel_id=1, source_target_pairs={{0,8},{4,12},{8,0},{12,4},{16,24},{20,28},{24,16},{28,20},{1,9},{5... | collective-permute-start | bytes 221192 | tf_op jit(solution)/shard_map/ppermute | solution.py:679
  30.0 1.6 %collective-permute-start.8 = (bf16[128,1152]{1,0:T(8,128)(2,1)S(1)}, bf16[128,1152]{1,0:T(8,128)(2,1)S(1)}, u32[]{:S(2)}, u32[]{:S(2)}) collective-permute-start(bf16[128,1152]{1,0:T(8,128)(2,1)S(1)} %stack.1.mine_ref), channel_id=1, source_target_pairs={{0,1},{1,0},{2,3},{3,2},{4,5},{5,4},{6,7},{7,6},{8,9},{9,8},{10,11... | collective-permute-start | bytes 884744 | tf_op jit(solution)/shard_map/ppermute | solution.py:679
  30.1 9.4 %collective-permute-start.10 = (bf16[128,1152]{1,0:T(8,128)(2,1)S(1)}, bf16[128,1152]{1,0:T(8,128)(2,1)S(1)}, u32[]{:S(2)}, u32[]{:S(2)}) collective-permute-start(bf16[128,1152]{1,0:T(8,128)(2,1)S(1)} %stack.1.mine_ref), channel_id=1, source_target_pairs={{0,4},{4,0},{8,12},{12,8},{16,20},{20,16},{24,28},{28,24},{1,5},{5... | collective-permute-start | bytes 884744 | tf_op jit(solution)/shard_map/ppermute | solution.py:679
  35.6 3.9 %collective-permute-start.9 = (bf16[128,1024]{1,0:T(8,128)(2,1)S(1)}, bf16[128,1024]{1,0:T(8,128)(2,1)S(1)}, u32[]{:S(2)}, u32[]{:S(2)}) collective-permute-start(bf16[128,1024]{1,0:T(8,128)(2,1)S(1)} %get-tuple-element.45.after_ref), channel_id=1, source_target_pairs={{0,1},{1,0},{2,3},{3,2},{4,5},{5,4},{6,7},{7,6},{8,9},{9,8},{10,11... | collective-permute-start | bytes 786440 | tf_op jit(solution)/shard_map/ppermute | solution.py:679
  39.5 1.6 %collective-permute-start.11 = (bf16[128,1152]{1,0:T(8,128)(2,1)S(1)}, bf16[128,1152]{1,0:T(8,128)(2,1)S(1)}, u32[]{:S(2)}, u32[]{:S(2)}) collective-permute-start(bf16[128,1152]{1,0:T(8,128)(2,1)S(1)} %hold.2.mine_ref), channel_id=1, source_target_pairs={{0,1},{1,0},{2,3},{3,2},{4,5},{5,4},{6,7},{7,6},{8,9},{9,8},{10,11... | collective-permute-start | bytes 884744 | tf_op jit(solution)/shard_map/ppermute | solution.py:679
  43.2 1.7 %collective-permute-start.13 = (bf16[128,1024]{1,0:T(8,128)(2,1)S(1)}, bf16[128,1024]{1,0:T(8,128)(2,1)S(1)}, u32[]{:S(2)}, u32[]{:S(2)}) collective-permute-start(bf16[128,1024]{1,0:T(8,128)(2,1)S(1)} %get-tuple-element.49._), channel_id=1, source_target_pairs={{0,1},{1,0},{2,3},{3,2},{4,5},{5,4},{6,7},{7,6},{8,9},{9,8},{10,11... | collective-permute-start | bytes 786440 | tf_op jit(solution)/shard_map/ppermute | solution.py:679
  44.3 5.7 %collective-permute-start.12 = (bf16[128,512]{1,0:T(8,128)(2,1)S(1)}, bf16[128,512]{1,0:T(8,128)(2,1)S(1)}, u32[]{:S(2)}, u32[]{:S(2)}) collective-permute-start(bf16[128,512]{1,0:T(8,128)(2,1)S(1)} %hold.3), channel_id=1, source_target_pairs={{0,2},{1,3},{2,0},{3,1},{4,6},{5,7},{6,4},{7,5},{8,10},{9,11},{10,... | collective-permute-start | bytes 393224 | tf_op jit(solution)/shard_map/ppermute | solution.py:679
  44.9 6.4 %collective-permute-start.14 = (bf16[128,512]{1,0:T(8,128)(2,1)S(1)}, bf16[128,512]{1,0:T(8,128)(2,1)S(1)}, u32[]{:S(2)}, u32[]{:S(2)}) collective-permute-start(bf16[128,512]{1,0:T(8,128)(2,1)S(1)} %get-tuple-element.50), channel_id=1, source_target_pairs={{0,4},{1,5},{2,6},{3,7},{4,0},{5,1},{6,2},{7,3},{8,12},{9,13},{10,... | collective-permute-start | bytes 393224 | tf_op jit(solution)/shard_map/ppermute | solution.py:745
  46.3 7.8 %collective-permute-start.15 = (bf16[128,512]{1,0:T(8,128)(2,1)S(1)}, bf16[128,512]{1,0:T(8,128)(2,1)S(1)}, u32[]{:S(2)}, u32[]{:S(2)}) collective-permute-start(bf16[128,512]{1,0:T(8,128)(2,1)S(1)} %get-tuple-element.51), channel_id=1, source_target_pairs={{0,6},{1,7},{2,4},{3,5},{4,2},{5,3},{6,0},{7,1},{8,14},{9,15},{10,... | collective-permute-start | bytes 393224 | tf_op jit(solution)/shard_map/ppermute | solution.py:745
  54.2 4.3 %collective-permute-start.16 = (bf16[32,512]{1,0:T(8,128)(2,1)S(1)}, bf16[32,512]{1,0:T(8,128)(2,1)S(1)}, u32[]{:S(2)}, u32[]{:S(2)}) collective-permute-start(bf16[32,512]{1,0:T(8,128)(2,1)S(1)} %get-tuple-element.53), channel_id=1, source_target_pairs={{0,8},{4,12},{8,0},{12,4},{16,24},{20,28},{24,16},{28,20},{1,9},{5... | collective-permute-start | bytes 98312 | tf_op jit(solution)/shard_map/ppermute | solution.py:679
  54.5 5.7 %collective-permute-start.18 = (bf16[32,512]{1,0:T(8,128)(2,1)S(1)}, bf16[32,512]{1,0:T(8,128)(2,1)S(1)}, u32[]{:S(2)}, u32[]{:S(2)}) collective-permute-start(bf16[32,512]{1,0:T(8,128)(2,1)S(1)} %get-tuple-element.54), channel_id=1, source_target_pairs={{0,24},{4,28},{8,16},{12,20},{16,8},{20,12},{24,0},{28,4},{1,25},{... | collective-permute-start | bytes 98312 | tf_op jit(solution)/shard_map/ppermute | solution.py:679
  56.6 4.8 %collective-permute-start.17 = (bf16[32,512]{1,0:T(8,128)(2,1)S(1)}, bf16[32,512]{1,0:T(8,128)(2,1)S(1)}, u32[]{:S(2)}, u32[]{:S(2)}) collective-permute-start(bf16[32,512]{1,0:T(8,128)(2,1)S(1)} %get-tuple-element.55), channel_id=1, source_target_pairs={{0,16},{4,20},{8,24},{12,28},{16,0},{20,4},{24,8},{28,12},{1,17},{... | collective-permute-start | bytes 98312 | tf_op jit(solution)/shard_map/ppermute | solution.py:679

commit v11 on v10

--- a/solution.py
+++ b/solution.py
@@ -443,18 +443,23 @@
 
 
 def stack_kernel(count, *refs):
+    all_ref, states_ref = refs[-2:]
     rows = refs[0].shape[0]
     for i in range(count):
-        refs[-1][i * rows : (i + 1) * rows, :] = refs[i][...]
-
-
-def stack_part(parts, after):
+        part = slice(i * rows, (i + 1) * rows)
+        all_ref[part, :] = refs[i][...]
+        states_ref[part, :] = refs[i][:, : states_ref.shape[1]]
+
+
+def stack_part(parts, width, after):
     rows, columns = parts[0].shape
     return pl.pallas_call(
         functools.partial(stack_kernel, len(parts)),
-        out_shape=jax.ShapeDtypeStruct((len(parts) * rows, columns), jnp.bfloat16),
+        out_shape=[
+            jax.ShapeDtypeStruct((len(parts) * rows, n), jnp.bfloat16) for n in (columns, width)
+        ],
         in_specs=[VMEM] * len(parts) + [ANY],
-        out_specs=VMEM,
+        out_specs=[VMEM] * 2,
         compiler_params=pltpu.CompilerParams(vmem_limit_bytes=8 * 2**20),
         name="stack",
     )(*parts, after)
@@ -554,11 +559,7 @@
         out_specs=VMEM,
         scratch_shapes=[pltpu.VMEM((tokens, head_count * cols), jnp.bfloat16)],
         compiler_params=pltpu.CompilerParams(vmem_limit_bytes=12 * 2**20),
-        cost_estimate=pl.CostEstimate(
-            flops=2 * tokens * head_count * cols * experts * columns,
-            bytes_accessed=2 * head_count * cols * experts * columns,
-            transcendentals=0,
-        ),
+        cost_estimate=pl.CostEstimate(flops=0, bytes_accessed=0, transcendentals=0),
         name="experts_whole",
     )(me, mine, other, in_vmem(weights), after)
 
@@ -626,11 +627,7 @@
         in_specs=[VMEM, VMEM, ANY],
         out_specs=[VMEM] * len(firsts),
         compiler_params=pltpu.CompilerParams(vmem_limit_bytes=12 * 2**20),
-        cost_estimate=pl.CostEstimate(
-            flops=len(firsts) * tokens * total_units * head_count * cols,
-            bytes_accessed=len(firsts) * total_units * head_count * cols,
-            transcendentals=0,
-        ),
+        cost_estimate=pl.CostEstimate(flops=0, bytes_accessed=0, transcendentals=0),
         name="down",
     )(units, in_vmem(w_down), after)
 
@@ -652,6 +649,8 @@
 
 
 def sum_kernel(keep_ref, sent_ref, *outs):
+    *outs, token_ref = outs
+    token_ref[...] = jnp.zeros_like(token_ref)
     cols = outs[0].shape[1]
     for t, out in enumerate(outs):
         part = slice(t * cols, (t + 1) * cols)
@@ -667,9 +666,10 @@
         out_shape=[
             jax.ShapeDtypeStruct((tokens, cols), jnp.bfloat16 if t else first_type)
             for t in range(blocks)
-        ],
+        ]
+        + [jax.ShapeDtypeStruct((SUBLANES, LANES), jnp.float32)],
         in_specs=[VMEM, VMEM],
-        out_specs=[VMEM] * blocks,
+        out_specs=[VMEM] * (blocks + 1),
         compiler_params=pltpu.CompilerParams(vmem_limit_bytes=8 * 2**20),
         name="sum",
     )(keep, sent)
@@ -710,7 +710,7 @@
         v_cache.reshape(flat),
         w_down.reshape(experts_local * units_local, width),
     )
-    (half,) = sum_part(keep, swap(send, "head", head_size, 1), keep.shape[1], jnp.bfloat16)
+    half, _ = sum_part(keep, swap(send, "head", head_size, 1), keep.shape[1], jnp.bfloat16)
     others = [swap(half, "head", head_size, j) for j in even if j]
     early, late = range(head_size // 2), range(head_size // 2, head_size)
     buffer, token = by_expert(tuple(early), me_ref, w_in, head_size, None, half)
@@ -722,27 +722,30 @@
     steps = range(2, req_size, 2)
     line = [payload] + [swap(payload, "req", req_size, k) for k in steps]
     buffer, token = by_expert(tuple(late), me_ref, w_in, head_size, buffer, payload)
-    line = stack_part(line, token)
-    line_other = swap(line, "head", head_size, 1)
+    line, line_states = stack_part(line, head_size // 2 * cols, token)
+    line_other = swap(line_states, "head", head_size, 1)
     crossed = swap(line, "req", req_size, 1)
     units = experts_whole(me_ref, line, line_other, buffer, token, w_down_near.shape[1])
     keep, send = down_part(units, w_down_near, (0, 1), token)
-    line_sums = sum_part(keep, swap(send, "head", head_size, 1), cols, jnp.float32)
+    *line_sums, token = sum_part(keep, swap(send, "head", head_size, 1), cols, jnp.float32)
     crossed = hold(crossed, send)
     crossed_other = swap(crossed, "head", head_size, 1)
-    products = experts_first(crossed, buffer, line_sums[-1])
+    products = experts_first(crossed, buffer, token)
     units, send = experts_second(me_ref, crossed, crossed_other, products, buffer, w_down_near)
     (keep,) = down_part(units, w_down_near, (0,), send)
-    crossed_sums = sum_part(keep, swap(send, "head", head_size, 1), cols, jnp.bfloat16)
+    *crossed_sums, token = sum_part(keep, swap(send, "head", head_size, 1), cols, jnp.bfloat16)
     total = line_sums[0]
-    got = [swap(hold(line_sums[j // 2], keep), "head", head_size, j) for j in even if j]
+    got = []
     for j in even:
         pairs = [
             (r * head_size + h, (r ^ 1) * head_size + (h ^ j))
             for r in range(req_size)
             for h in range(head_size)
         ]
-        got.append(lax.ppermute(crossed_sums[j // 2], ("req", "head"), pairs))
+        got.append(lax.ppermute(hold(crossed_sums[j // 2], token), ("req", "head"), pairs))
+    got += [
+        swap(hold(line_sums[j // 2], token), "head", head_size, j) for j in even if j
+    ]
     for part in got:
         total = total + part.astype(jnp.float32)
     chunks = total.astype(jnp.bfloat16).reshape(req_size // 2, rows, cols)

time: 62.9 us -> 64.1 us (1.019); the launches traced: 62 us -> 64.3 us
  Pallas kernels: 24.8 us -> 25.9 us
  starting transfers between devices: 18.5 us -> 19.5 us
    ppermute x17, starting transfers between devices: 15.5 us -> 17.5 us  [swap(): return lax.ppermute(value, axis, [(i, i ^ mask) for i in range(size)])]
    ppermute x2, starting transfers between devices: 3.04 us -> 2.05 us  [per_device(): lax.ppermute(hold(crossed_sums[j // 2], token), ('req', 'head'), pairs)]
    ppermute x2, waiting for transfers between devices: 4.12 us -> 5.06 us  [per_device(): lax.ppermute(hold(crossed_sums[j // 2], token), ('req', 'head'), pairs)]
    ppermute x17, waiting for transfers between devices: 13.7 us -> 12.9 us  [swap(): return lax.ppermute(value, axis, [(i, i ^ mask) for i in range(size)])]
  transfers between devices with their start and end apart: 19 -> 19, of which waited for: 12 -> 12; matrix products, arithmetic and copies ran while one was open for 0% -> 0% of each run, Pallas kernels for 27% -> 26%
where the time goes in v11:
time: 64.1 us; the launch traced here: 64.3 us
  Pallas kernels  25.9 us (40%)
  starting transfers between devices  19.5 us (30%)
  waiting for transfers between devices  18 us (28%)
  other arithmetic  0.72 us (1%)
    ppermute x17, starting transfers between devices, swap(): return lax.ppermute(value, axis, [(i, i ^ mask) for i in range(size)])  17.5 us
    ppermute x17, waiting for transfers between devices, swap(): return lax.ppermute(value, axis, [(i, i ^ mask) for i in range(size)])  12.9 us
    pallas_call x2, Pallas kernels, by_expert(): pl.pallas_call(functools.partial(relayout_kernel, js), out_shape=(pltpu.V...  7.43 us
    pallas_call x1, Pallas kernels, attention(): pl.pallas_call(functools.partial(attention_kernel, head_count), out_shape...  6.7 us
    ppermute x2, waiting for transfers between devices, per_device(): lax.ppermute(hold(crossed_sums[j // 2], token), ('req', 'head'), pairs)  5.06 us
    pallas_call x1, Pallas kernels, fetch(): pl.pallas_call(fetch_kernel, out_shape=(pltpu.VMEM(hidden.shape, jnp.bflo...  2.94 us
    pallas_call x1, Pallas kernels, experts_whole(): pl.pallas_call(whole_kernel, out_shape=jax.ShapeDtypeStruct((tokens, tota...  2.69 us
    ppermute x2, starting transfers between devices, per_device(): lax.ppermute(hold(crossed_sums[j // 2], token), ('req', 'head'), pairs)  2.05 us
  transfers between devices with their start and end apart: 19, of which 12 were waited for; matrix products, arithmetic and copies ran while one was open for 0% of the time, Pallas kernels for 26%

profile of v11, /device:TPU:0, one launch (start us, length us, event | category | flops | bytes accessed | tf_op | source)
XLA Modules:
  0.0 64.3 jit_solution(7895625829697025331)
XLA Ops:
  0.0 3.0 %collective-permute-start = (bf16[32,512]{1,0:T(8,128)(2,1)}, bf16[32,512]{1,0:T(8,128)(2,1)S(1)}, u32[]{:S(2)}, u32[]{:S(2)}) collective-permute-start(bf16[32,512]{1,0:T(8,128)(2,1)} %own_ref.1), channel_id=1, source_target_pairs={{0,2},{1,3},{2,0},{3,1},{4,6},{5,7},{6,4},{7,5},{8,10},{9,11},{10,... | collective-permute-start | bytes 98312 | tf_op jit(solution)/shard_map/ppermute | solution.py:679
  3.0 0.0 collective-permute-start.2
  3.0 0.1 collective-permute-start.1
  3.1 2.9 %fetch.1 = (bf16[32,512]{1,0:T(8,128)(2,1)S(1)}, bf16[3,4,512,512]{3,2,1,0:T(8,128)(2,1)S(1)}, bf16[49152,128]{1,0:T(8,128)(2,1)S(1)}, f32[32,128]{1,0:T(8,128)S...) custom-call(s32[32]{0:T(128)} %lengths_hbm.1, s32[1]{0:T(128)} %bitcast.me_ref, ...), custom_call_target="tpu_custom_call" | custom-call | bytes 12582912 | tf_op jit(solution)/shard_map/fetch/pallas_call | solution.py:101
  6.1 0.0 collective-permute-done.refs_2_.refs_1_
  6.1 0.5 collective-permute-done.2.refs_3_
  6.6 0.0 collective-permute-done.1.refs_1_
  6.6 6.7 %attention.1 = (bf16[32,1024]{1,0:T(8,128)(2,1)S(1)}, bf16[32,1024]{1,0:T(8,128)(2,1)S(1)}, bf16[49152,128]{1,0:T(8,128)(2,1)S(1)}, bf16[4,2048,512]{2,1,0:T(8,128)(2,1)S(1)}) custom-call(s32[32]{0:T(128)S(4)} %get-tuple-element.35.lengths_ref, s32[1]{0:T(128)} %bitcast.me_ref, ...), custom_call_target="tpu_custom_call", output_to_operand_aliasing={{2}: (9, {})} | custom-call | flops 268435456 | bytes 11534336 | tf_op jit(solution)/shard_map/attention/pallas_call | solution.py:315
  13.3 0.1 collective-permute-start.3
  13.4 1.2 %collective-permute-done.3.sent_ref = bf16[32,1024]{1,0:T(8,128)(2,1)S(1)} collective-permute-done((bf16[32,1024]{1,0:T(8,128)(2,1)S(1)}, bf16[32,1024]{1,0:T(8,128)(2,1)S(1)}, u32[]{:S(2)}, u32[]{:S(2)}) %collective-permute-start.3) | collective-permute-done | bytes 65568 | tf_op jit(solution)/shard_map/ppermute | solution.py:679
  14.6 0.6 sum.3
  15.2 1.6 %collective-permute-start.4 = (bf16[32,1024]{1,0:T(8,128)(2,1)S(1)}, bf16[32,1024]{1,0:T(8,128)(2,1)S(1)}, u32[]{:S(2)}, u32[]{:S(2)}) collective-permute-start(bf16[32,1024]{1,0:T(8,128)(2,1)S(1)} %get-tuple-element.42.refs_0_.refs_2_), channel_id=1, source_target_pairs={{0,2},{1,3},{2,0},{3,1},{4,6},{5,7},{6,4},{7,5},{8,10},{9,11},{10,... | collective-permute-start | bytes 196616 | tf_op jit(solution)/shard_map/ppermute | solution.py:679
  16.8 3.7 %by_expert_0.1 = (bf16[16,4,512,256]{3,2,1,0:T(8,128)(2,1)S(1)}, f32[8,128]{1,0:T(8,128)S(1)}) custom-call(s32[1]{0:T(128)} %bitcast.me_ref, bf16[2048,16,256]{2,1,0:T(8,128)(2,1)} %w_ref.5, bf16[32,1024]{1,0:T(8,128)(2,1)S(1)} %get-tuple-element.42.refs_0_.refs_2_), custom_call_target="tpu_custom_call" | custom-call | bytes 16777216 | tf_op jit(solution)/shard_map/by_expert_0/pallas_call | solution.py:392
  20.5 0.0 collective-permute-done.4.refs_3_
  20.6 3.2 %collective-permute-start.7 = (bf16[32,1152]{1,0:T(8,128)(2,1)S(1)}, bf16[32,1152]{1,0:T(8,128)(2,1)S(1)}, u32[]{:S(2)}, u32[]{:S(2)}) collective-permute-start(bf16[32,1152]{1,0:T(8,128)(2,1)S(1)} %get-tuple-element.45.refs_1_.refs_0_), channel_id=1, source_target_pairs={{0,24},{4,28},{8,16},{12,20},{16,8},{20,12},{24,0},{28,4},{1,25},{... | collective-permute-start | bytes 221192 | tf_op jit(solution)/shard_map/ppermute | solution.py:679
  23.8 0.0 collective-permute-start.6
  23.8 1.3 %collective-permute-start.5 = (bf16[32,1152]{1,0:T(8,128)(2,1)S(1)}, bf16[32,1152]{1,0:T(8,128)(2,1)S(1)}, u32[]{:S(2)}, u32[]{:S(2)}) collective-permute-start(bf16[32,1152]{1,0:T(8,128)(2,1)S(1)} %get-tuple-element.45.refs_1_.refs_0_), channel_id=1, source_target_pairs={{0,8},{4,12},{8,0},{12,4},{16,24},{20,28},{24,16},{28,20},{1,9},{5... | collective-permute-start | bytes 221192 | tf_op jit(solution)/shard_map/ppermute | solution.py:679
  25.0 3.7 %by_expert_2.1 = (bf16[16,4,512,256]{3,2,1,0:T(8,128)(2,1)S(1)}, f32[8,128]{1,0:T(8,128)S(1)}) custom-call(s32[1]{0:T(128)} %bitcast.me_ref, bf16[2048,16,256]{2,1,0:T(8,128)(2,1)} %w_ref.5, bf16[16,4,512,256]{3,2,1,0:T(8,128)(2,1)S(1)} %get-tuple-element.46.refs_0_, ...), custom_call_target="tpu_custom_call", output_to_operand_aliasing={{0}: (2, {})} | custom-call | bytes 16777216 | tf_op jit(solution)/shard_map/by_expert_2/pallas_call | solution.py:392
  28.8 0.0 collective-permute-done.7.refs_3_
  28.8 1.7 %collective-permute-done.6.refs_2_ = bf16[32,1152]{1,0:T(8,128)(2,1)S(1)} collective-permute-done((bf16[32,1152]{1,0:T(8,128)(2,1)S(1)}, bf16[32,1152]{1,0:T(8,128)(2,1)S(1)}, u32[]{:S(2)}, u32[]{:S(2)}) %collective-permute-start.6) | collective-permute-done | bytes 73760 | tf_op jit(solution)/shard_map/ppermute | solution.py:679
  30.5 0.0 collective-permute-done.5.refs_1_
  30.5 0.1 collective-permute-start.8
  30.6 2.5 %collective-permute-start.10 = (bf16[128,1152]{1,0:T(8,128)(2,1)S(1)}, bf16[128,1152]{1,0:T(8,128)(2,1)S(1)}, u32[]{:S(2)}, u32[]{:S(2)}) collective-permute-start(bf16[128,1152]{1,0:T(8,128)(2,1)S(1)} %get-tuple-element.48.mine_ref), channel_id=1, source_target_pairs={{0,4},{4,0},{8,12},{12,8},{16,20},{20,16},{24,28},{28,24},{1,5},{5... | collective-permute-start | bytes 884744 | tf_op jit(solution)/shard_map/ppermute | solution.py:679
  33.1 0.0 collective-permute-done.8.other_ref
  33.1 2.7 %experts_whole.1.units_ref = bf16[128,2048]{1,0:T(8,128)(2,1)S(1)} custom-call(s32[1]{0:T(128)} %bitcast.me_ref, bf16[128,1152]{1,0:T(8,128)(2,1)S(1)} %get-tuple-element.48.mine_ref, bf16[128,1024]{1,0:T(8,128)(2,1)S(1)} %collective-permute-done.8.other_ref, bf16[16,4,512,256]{3,2,1,0:T(8,128)(2,1)S(1)} %get-tuple-element.50.w_ref, ...), custom_call_target="tpu_custom_call" | custom-call | tf_op jit(solution)/shard_map/experts_whole/pallas_call | solution.py:555
  35.8 1.3 %down.2 = (bf16[128,1024]{1,0:T(8,128)(2,1)S(1)}, bf16[128,1024]{1,0:T(8,128)(2,1)S(1)}) custom-call(bf16[128,2048]{1,0:T(8,128)(2,1)S(1)} %experts_whole.1.units_ref, bf16[4,2048,512]{2,1,0:T(8,128)(2,1)S(1)} %get-tuple-element.51.w_ref.w_down_ref, f32[8,128]{1,0:T(8,128)S(1)} %get-tuple-element.47.refs_4_._), custom_call_target="tpu_custom_call" | custom-call | tf_op jit(solution)/shard_map/down/pallas_call | solution.py:624
  37.1 0.2 collective-permute-start.9
  37.3 3.4 %collective-permute-done.10.value_ref = bf16[128,1152]{1,0:T(8,128)(2,1)S(1)} collective-permute-done((bf16[128,1152]{1,0:T(8,128)(2,1)S(1)}, bf16[128,1152]{1,0:T(8,128)(2,1)S(1)}, u32[]{:S(2)}, u32[]{:S(2)}) %collective-permute-start.10) | collective-permute-done | bytes 294944 | tf_op jit(solution)/shard_map/ppermute | solution.py:679
  40.7 0.0 collective-permute-start.11
  40.7 0.0 collective-permute-done.9.sent_ref
  40.7 0.1 sum.4
  40.8 1.3 %experts_first.1.product_ref = f32[16,128,256]{2,1,0:T(8,128)S(1)} custom-call(bf16[128,1152]{1,0:T(8,128)(2,1)S(1)} %hold.4.mine_ref, bf16[16,4,512,256]{3,2,1,0:T(8,128)(2,1)S(1)} %get-tuple-element.50.w_ref, f32[8,128]{1,0:T(8,128)S(1)} %get-tuple-element.55._), custom_call_target="tpu_custom_call" | custom-call | flops 1073741824 | bytes 8388608 | tf_op jit(solution)/shard_map/experts_first/pallas_call | solution.py:571
  42.1 0.2 collective-permute-done.11.other_ref
  42.3 2.0 %experts_second.1 = (bf16[128,2048]{1,0:T(8,128)(2,1)S(1)}, bf16[128,1024]{1,0:T(8,128)(2,1)S(1)}) custom-call(s32[1]{0:T(128)} %bitcast.me_ref, bf16[128,1152]{1,0:T(8,128)(2,1)S(1)} %hold.4.mine_ref, bf16[128,1152]{1,0:T(8,128)(2,1)S(1)} %collective-permute-done.11.other_ref, f32[16,128,256]{2,1,0:T(8,128)S(1)} %experts_first.1.product_ref, ...), custom_call_target="tpu_custom_call" | custom-call | flops 1073741824 | bytes 8388608 | tf_op jit(solution)/shard_map/experts_second/pallas_call | solution.py:589
  44.3 0.4 collective-permute-start.12
  44.7 0.7 %down.3.keep_ref = bf16[128,1024]{1,0:T(8,128)(2,1)S(1)} custom-call(bf16[128,2048]{1,0:T(8,128)(2,1)S(1)} %get-tuple-element.56.units_ref, bf16[4,2048,512]{2,1,0:T(8,128)(2,1)S(1)} %get-tuple-element.51.w_ref.w_down_ref, bf16[128,1024]{1,0:T(8,128)(2,1)S(1)} %get-tuple-element.57._), custom_call_target="tpu_custom_call" | custom-call | tf_op jit(solution)/shard_map/down/pallas_call | solution.py:624
  45.4 0.5 collective-permute-done.12.sent_ref
  45.9 0.1 sum.5
  46.0 1.8 %collective-permute-start.14 = (bf16[128,512]{1,0:T(8,128)(2,1)S(1)}, bf16[128,512]{1,0:T(8,128)(2,1)S(1)}, u32[]{:S(2)}, u32[]{:S(2)}) collective-permute-start(bf16[128,512]{1,0:T(8,128)(2,1)S(1)} %hold.6), channel_id=1, source_target_pairs={{0,6},{1,7},{2,4},{3,5},{4,2},{5,3},{6,0},{7,1},{8,14},{9,15},{10,... | collective-permute-start | bytes 393224 | tf_op jit(solution)/shard_map/ppermute | solution.py:745
  47.8 0.3 collective-permute-start.13
  48.1 1.5 %collective-permute-start.15 = (bf16[128,512]{1,0:T(8,128)(2,1)S(1)}, bf16[128,512]{1,0:T(8,128)(2,1)S(1)}, u32[]{:S(2)}, u32[]{:S(2)}) collective-permute-start(bf16[128,512]{1,0:T(8,128)(2,1)S(1)} %hold.7), channel_id=1, source_target_pairs={{0,2},{1,3},{2,0},{3,1},{4,6},{5,7},{6,4},{7,5},{8,10},{9,11},{10,... | collective-permute-start | bytes 393224 | tf_op jit(solution)/shard_map/ppermute | solution.py:679
  49.6 3.7 %collective-permute-done.14 = bf16[128,512]{1,0:T(8,128)(2,1)S(1)} collective-permute-done((bf16[128,512]{1,0:T(8,128)(2,1)S(1)}, bf16[128,512]{1,0:T(8,128)(2,1)S(1)}, u32[]{:S(2)}, u32[]{:S(2)}) %collective-permute-start.14) | collective-permute-done | bytes 131104 | tf_op jit(solution)/shard_map/ppermute | solution.py:745
  53.3 1.3 %collective-permute-done.13 = bf16[128,512]{1,0:T(8,128)(2,1)S(1)} collective-permute-done((bf16[128,512]{1,0:T(8,128)(2,1)S(1)}, bf16[128,512]{1,0:T(8,128)(2,1)S(1)}, u32[]{:S(2)}, u32[]{:S(2)}) %collective-permute-start.13) | collective-permute-done | bytes 131104 | tf_op jit(solution)/shard_map/ppermute | solution.py:745
  54.6 0.9 %collective-permute-done.15 = bf16[128,512]{1,0:T(8,128)(2,1)S(1)} collective-permute-done((bf16[128,512]{1,0:T(8,128)(2,1)S(1)}, bf16[128,512]{1,0:T(8,128)(2,1)S(1)}, u32[]{:S(2)}, u32[]{:S(2)}) %collective-permute-start.15) | collective-permute-done | bytes 131104 | tf_op jit(solution)/shard_map/ppermute | solution.py:679
  55.5 0.1 add_convert_fusion
  55.6 1.4 %collective-permute-start.16 = (bf16[32,512]{1,0:T(8,128)(2,1)S(1)}, bf16[32,512]{1,0:T(8,128)(2,1)S(1)}, u32[]{:S(2)}, u32[]{:S(2)}) collective-permute-start(bf16[32,512]{1,0:T(8,128)(2,1)S(1)} %get-tuple-element.63), channel_id=1, source_target_pairs={{0,8},{4,12},{8,0},{12,4},{16,24},{20,28},{24,16},{28,20},{1,9},{5... | collective-permute-start | bytes 98312 | tf_op jit(solution)/shard_map/ppermute | solution.py:679
  56.9 1.6 %collective-permute-start.18 = (bf16[32,512]{1,0:T(8,128)(2,1)S(1)}, bf16[32,512]{1,0:T(8,128)(2,1)S(1)}, u32[]{:S(2)}, u32[]{:S(2)}) collective-permute-start(bf16[32,512]{1,0:T(8,128)(2,1)S(1)} %get-tuple-element.64), channel_id=1, source_target_pairs={{0,24},{4,28},{8,16},{12,20},{16,8},{20,12},{24,0},{28,4},{1,25},{... | collective-permute-start | bytes 98312 | tf_op jit(solution)/shard_map/ppermute | solution.py:679
  58.5 0.6 collective-permute-start.17
  59.1 0.4 collective-permute-done.16
  59.6 3.1 %collective-permute-done.18 = bf16[32,512]{1,0:T(8,128)(2,1)S(1)} collective-permute-done((bf16[32,512]{1,0:T(8,128)(2,1)S(1)}, bf16[32,512]{1,0:T(8,128)(2,1)S(1)}, u32[]{:S(2)}, u32[]{:S(2)}) %collective-permute-start.18) | collective-permute-done | bytes 32800 | tf_op jit(solution)/shard_map/ppermute | solution.py:679
  62.7 1.0 %collective-permute-done.17 = bf16[32,512]{1,0:T(8,128)(2,1)S(1)} collective-permute-done((bf16[32,512]{1,0:T(8,128)(2,1)S(1)}, bf16[32,512]{1,0:T(8,128)(2,1)S(1)}, u32[]{:S(2)}, u32[]{:S(2)}) %collective-permute-start.17) | collective-permute-done | bytes 32800 | tf_op jit(solution)/shard_map/ppermute | solution.py:679
  63.7 0.6 add_convert_fusion.1
  (8 shorter events, 0.1 us)
Async XLA Ops:
  0.0 6.1 %collective-permute-start = (bf16[32,512]{1,0:T(8,128)(2,1)}, bf16[32,512]{1,0:T(8,128)(2,1)S(1)}, u32[]{:S(2)}, u32[]{:S(2)}) collective-permute-start(bf16[32,512]{1,0:T(8,128)(2,1)} %own_ref.1), channel_id=1, source_target_pairs={{0,2},{1,3},{2,0},{3,1},{4,6},{5,7},{6,4},{7,5},{8,10},{9,11},{10,... | collective-permute-start | bytes 98312 | tf_op jit(solution)/shard_map/ppermute | solution.py:679
  3.0 3.6 %collective-permute-start.2 = (bf16[32,512]{1,0:T(8,128)(2,1)}, bf16[32,512]{1,0:T(8,128)(2,1)S(1)}, u32[]{:S(2)}, u32[]{:S(2)}) collective-permute-start(bf16[32,512]{1,0:T(8,128)(2,1)} %own_ref.1), channel_id=1, source_target_pairs={{0,3},{1,2},{2,1},{3,0},{4,7},{5,6},{6,5},{7,4},{8,11},{9,10},{10,... | collective-permute-start | bytes 98312 | tf_op jit(solution)/shard_map/ppermute | solution.py:679
  3.0 3.6 %collective-permute-start.1 = (bf16[32,512]{1,0:T(8,128)(2,1)}, bf16[32,512]{1,0:T(8,128)(2,1)S(1)}, u32[]{:S(2)}, u32[]{:S(2)}) collective-permute-start(bf16[32,512]{1,0:T(8,128)(2,1)} %own_ref.1), channel_id=1, source_target_pairs={{0,1},{1,0},{2,3},{3,2},{4,5},{5,4},{6,7},{7,6},{8,9},{9,8},{10,11... | collective-permute-start | bytes 98312 | tf_op jit(solution)/shard_map/ppermute | solution.py:679
  13.3 1.3 %collective-permute-start.3 = (bf16[32,1024]{1,0:T(8,128)(2,1)S(1)}, bf16[32,1024]{1,0:T(8,128)(2,1)S(1)}, u32[]{:S(2)}, u32[]{:S(2)}) collective-permute-start(bf16[32,1024]{1,0:T(8,128)(2,1)S(1)} %get-tuple-element.41), channel_id=1, source_target_pairs={{0,1},{1,0},{2,3},{3,2},{4,5},{5,4},{6,7},{7,6},{8,9},{9,8},{10,11... | collective-permute-start | bytes 196616 | tf_op jit(solution)/shard_map/ppermute | solution.py:679
  15.2 5.3 %collective-permute-start.4 = (bf16[32,1024]{1,0:T(8,128)(2,1)S(1)}, bf16[32,1024]{1,0:T(8,128)(2,1)S(1)}, u32[]{:S(2)}, u32[]{:S(2)}) collective-permute-start(bf16[32,1024]{1,0:T(8,128)(2,1)S(1)} %get-tuple-element.42.refs_0_.refs_2_), channel_id=1, source_target_pairs={{0,2},{1,3},{2,0},{3,1},{4,6},{5,7},{6,4},{7,5},{8,10},{9,11},{10,... | collective-permute-start | bytes 196616 | tf_op jit(solution)/shard_map/ppermute | solution.py:679
  20.6 8.2 %collective-permute-start.7 = (bf16[32,1152]{1,0:T(8,128)(2,1)S(1)}, bf16[32,1152]{1,0:T(8,128)(2,1)S(1)}, u32[]{:S(2)}, u32[]{:S(2)}) collective-permute-start(bf16[32,1152]{1,0:T(8,128)(2,1)S(1)} %get-tuple-element.45.refs_1_.refs_0_), channel_id=1, source_target_pairs={{0,24},{4,28},{8,16},{12,20},{16,8},{20,12},{24,0},{28,4},{1,25},{... | collective-permute-start | bytes 221192 | tf_op jit(solution)/shard_map/ppermute | solution.py:679
  23.8 6.7 %collective-permute-start.6 = (bf16[32,1152]{1,0:T(8,128)(2,1)S(1)}, bf16[32,1152]{1,0:T(8,128)(2,1)S(1)}, u32[]{:S(2)}, u32[]{:S(2)}) collective-permute-start(bf16[32,1152]{1,0:T(8,128)(2,1)S(1)} %get-tuple-element.45.refs_1_.refs_0_), channel_id=1, source_target_pairs={{0,16},{4,20},{8,24},{12,28},{16,0},{20,4},{24,8},{28,12},{1,17},{... | collective-permute-start | bytes 221192 | tf_op jit(solution)/shard_map/ppermute | solution.py:679
  23.8 6.7 %collective-permute-start.5 = (bf16[32,1152]{1,0:T(8,128)(2,1)S(1)}, bf16[32,1152]{1,0:T(8,128)(2,1)S(1)}, u32[]{:S(2)}, u32[]{:S(2)}) collective-permute-start(bf16[32,1152]{1,0:T(8,128)(2,1)S(1)} %get-tuple-element.45.refs_1_.refs_0_), channel_id=1, source_target_pairs={{0,8},{4,12},{8,0},{12,4},{16,24},{20,28},{24,16},{28,20},{1,9},{5... | collective-permute-start | bytes 221192 | tf_op jit(solution)/shard_map/ppermute | solution.py:679
  30.5 2.6 %collective-permute-start.8 = (bf16[128,1024]{1,0:T(8,128)(2,1)S(1)}, bf16[128,1024]{1,0:T(8,128)(2,1)S(1)}, u32[]{:S(2)}, u32[]{:S(2)}) collective-permute-start(bf16[128,1024]{1,0:T(8,128)(2,1)S(1)} %get-tuple-element.49), channel_id=1, source_target_pairs={{0,1},{1,0},{2,3},{3,2},{4,5},{5,4},{6,7},{7,6},{8,9},{9,8},{10,11... | collective-permute-start | bytes 786440 | tf_op jit(solution)/shard_map/ppermute | solution.py:679
  30.6 10.1 %collective-permute-start.10 = (bf16[128,1152]{1,0:T(8,128)(2,1)S(1)}, bf16[128,1152]{1,0:T(8,128)(2,1)S(1)}, u32[]{:S(2)}, u32[]{:S(2)}) collective-permute-start(bf16[128,1152]{1,0:T(8,128)(2,1)S(1)} %get-tuple-element.48.mine_ref), channel_id=1, source_target_pairs={{0,4},{4,0},{8,12},{12,8},{16,20},{20,16},{24,28},{28,24},{1,5},{5... | collective-permute-start | bytes 884744 | tf_op jit(solution)/shard_map/ppermute | solution.py:679
  37.1 3.6 %collective-permute-start.9 = (bf16[128,1024]{1,0:T(8,128)(2,1)S(1)}, bf16[128,1024]{1,0:T(8,128)(2,1)S(1)}, u32[]{:S(2)}, u32[]{:S(2)}) collective-permute-start(bf16[128,1024]{1,0:T(8,128)(2,1)S(1)} %get-tuple-element.53.after_ref), channel_id=1, source_target_pairs={{0,1},{1,0},{2,3},{3,2},{4,5},{5,4},{6,7},{7,6},{8,9},{9,8},{10,11... | collective-permute-start | bytes 786440 | tf_op jit(solution)/shard_map/ppermute | solution.py:679
  40.7 1.6 %collective-permute-start.11 = (bf16[128,1152]{1,0:T(8,128)(2,1)S(1)}, bf16[128,1152]{1,0:T(8,128)(2,1)S(1)}, u32[]{:S(2)}, u32[]{:S(2)}) collective-permute-start(bf16[128,1152]{1,0:T(8,128)(2,1)S(1)} %hold.4.mine_ref), channel_id=1, source_target_pairs={{0,1},{1,0},{2,3},{3,2},{4,5},{5,4},{6,7},{7,6},{8,9},{9,8},{10,11... | collective-permute-start | bytes 884744 | tf_op jit(solution)/shard_map/ppermute | solution.py:679
  44.3 1.6 %collective-permute-start.12 = (bf16[128,1024]{1,0:T(8,128)(2,1)S(1)}, bf16[128,1024]{1,0:T(8,128)(2,1)S(1)}, u32[]{:S(2)}, u32[]{:S(2)}) collective-permute-start(bf16[128,1024]{1,0:T(8,128)(2,1)S(1)} %get-tuple-element.57._), channel_id=1, source_target_pairs={{0,1},{1,0},{2,3},{3,2},{4,5},{5,4},{6,7},{7,6},{8,9},{9,8},{10,11... | collective-permute-start | bytes 786440 | tf_op jit(solution)/shard_map/ppermute | solution.py:679
  46.0 7.3 %collective-permute-start.14 = (bf16[128,512]{1,0:T(8,128)(2,1)S(1)}, bf16[128,512]{1,0:T(8,128)(2,1)S(1)}, u32[]{:S(2)}, u32[]{:S(2)}) collective-permute-start(bf16[128,512]{1,0:T(8,128)(2,1)S(1)} %hold.6), channel_id=1, source_target_pairs={{0,6},{1,7},{2,4},{3,5},{4,2},{5,3},{6,0},{7,1},{8,14},{9,15},{10,... | collective-permute-start | bytes 393224 | tf_op jit(solution)/shard_map/ppermute | solution.py:745
  47.8 6.8 %collective-permute-start.13 = (bf16[128,512]{1,0:T(8,128)(2,1)S(1)}, bf16[128,512]{1,0:T(8,128)(2,1)S(1)}, u32[]{:S(2)}, u32[]{:S(2)}) collective-permute-start(bf16[128,512]{1,0:T(8,128)(2,1)S(1)} %hold.5), channel_id=1, source_target_pairs={{0,4},{1,5},{2,6},{3,7},{4,0},{5,1},{6,2},{7,3},{8,12},{9,13},{10,... | collective-permute-start | bytes 393224 | tf_op jit(solution)/shard_map/ppermute | solution.py:745
  48.1 7.4 %collective-permute-start.15 = (bf16[128,512]{1,0:T(8,128)(2,1)S(1)}, bf16[128,512]{1,0:T(8,128)(2,1)S(1)}, u32[]{:S(2)}, u32[]{:S(2)}) collective-permute-start(bf16[128,512]{1,0:T(8,128)(2,1)S(1)} %hold.7), channel_id=1, source_target_pairs={{0,2},{1,3},{2,0},{3,1},{4,6},{5,7},{6,4},{7,5},{8,10},{9,11},{10,... | collective-permute-start | bytes 393224 | tf_op jit(solution)/shard_map/ppermute | solution.py:679
  55.6 4.0 %collective-permute-start.16 = (bf16[32,512]{1,0:T(8,128)(2,1)S(1)}, bf16[32,512]{1,0:T(8,128)(2,1)S(1)}, u32[]{:S(2)}, u32[]{:S(2)}) collective-permute-start(bf16[32,512]{1,0:T(8,128)(2,1)S(1)} %get-tuple-element.63), channel_id=1, source_target_pairs={{0,8},{4,12},{8,0},{12,4},{16,24},{20,28},{24,16},{28,20},{1,9},{5... | collective-permute-start | bytes 98312 | tf_op jit(solution)/shard_map/ppermute | solution.py:679
  56.9 5.7 %collective-permute-start.18 = (bf16[32,512]{1,0:T(8,128)(2,1)S(1)}, bf16[32,512]{1,0:T(8,128)(2,1)S(1)}, u32[]{:S(2)}, u32[]{:S(2)}) collective-permute-start(bf16[32,512]{1,0:T(8,128)(2,1)S(1)} %get-tuple-element.64), channel_id=1, source_target_pairs={{0,24},{4,28},{8,16},{12,20},{16,8},{20,12},{24,0},{28,4},{1,25},{... | collective-permute-start | bytes 98312 | tf_op jit(solution)/shard_map/ppermute | solution.py:679
  58.5 5.1 %collective-permute-start.17 = (bf16[32,512]{1,0:T(8,128)(2,1)S(1)}, bf16[32,512]{1,0:T(8,128)(2,1)S(1)}, u32[]{:S(2)}, u32[]{:S(2)}) collective-permute-start(bf16[32,512]{1,0:T(8,128)(2,1)S(1)} %get-tuple-element.65), channel_id=1, source_target_pairs={{0,16},{4,20},{8,24},{12,28},{16,0},{20,4},{24,8},{28,12},{1,17},{... | collective-permute-start | bytes 98312 | tf_op jit(solution)/shard_map/ppermute | solution.py:679

commit v12 on v10

--- a/solution.py
+++ b/solution.py
@@ -11,9 +11,8 @@
 norm_eps = 1e-05
 LANES = 128
 SUBLANES = 8
-CHUNK = 96
+CHUNK = 128
 GROUP = 8
-TOGETHER = 1
 MASKED = -1e30
 
 
@@ -34,10 +33,33 @@
     return pl.multiple_of((length + 7) // 8 * (8 * heads_local), 8 * heads_local)
 
 
+def exchanges(count):
+    steps = []
+    size = 1
+    while size < count:
+        gap = size
+        while gap >= 1:
+            for start in range(gap % size, count - gap, 2 * gap):
+                for i in range(min(gap, count - start - gap)):
+                    if (start + i) // (2 * size) == (start + i + gap) // (2 * size):
+                        steps.append((start + i, start + i + gap))
+            gap //= 2
+        size *= 2
+    return steps
+
+
+def packed(length, request):
+    return (length << 16) + request
+
+
+def unpacked(key):
+    return key >> 16, key & 0xFFFF
+
+
 def fetch_kernel(
     lengths_hbm, me_ref, freqs_ref, own_ref, w_ref, ids_ref, route_ref,
-    own_out_ref, w_out_ref, blank_ref, cos_ref, sin_ref, lengths_ref, shares_ref,
-    angle_s, ids_s, route_s, sem, small_sem,
+    own_out_ref, w_out_ref, blank_ref, cos_ref, sin_ref, keys_ref, shares_ref,
+    lengths_ref, angle_s, ids_s, route_s, sem, small_sem,
 ):
     head_count, cols = w_out_ref.shape[1:3]
     chunk_rows = CHUNK * cols // LANES
@@ -82,6 +104,15 @@
     lane = lax.broadcasted_iota(jnp.int32, sin_ref.shape, 1)
     sine = jnp.sin(angle_s[...])
     sin_ref[...] = jnp.where(lane < LANES // 2, -sine, sine)
+    @pl.loop(0, rows // GROUP)
+    def _(g):
+        keys = [packed(lengths_ref[g * GROUP + i], g * GROUP + i) for i in range(GROUP)]
+        for low, high in exchanges(GROUP):
+            larger, smaller = jnp.maximum(keys[low], keys[high]), jnp.minimum(keys[low], keys[high])
+            keys[low], keys[high] = larger, smaller
+        for i in range(GROUP):
+            keys_ref[g * GROUP + i] = keys[i]
+
     for copy in small:
         copy.wait()
     expert = lax.broadcasted_iota(jnp.int32, (shares_ref.shape[1], rows), 0)
@@ -112,6 +143,7 @@
         in_specs=[ANY, SMEM, VMEM] + [ANY] * 4,
         out_specs=[VMEM] * 5 + [SMEM, VMEM],
         scratch_shapes=[
+            pltpu.SMEM(lengths.shape, lengths.dtype),
             pltpu.VMEM((rows, LANES), jnp.float32),
             pltpu.VMEM(expert_ids.shape[::-1], expert_ids.dtype),
             pltpu.VMEM(route_weights.shape[::-1], route_weights.dtype),
@@ -129,7 +161,7 @@
     )
 
 
-def attention_kernel(head_count, lengths_ref, me_ref, cos_ref, sin_ref, *refs):
+def attention_kernel(head_count, keys_ref, me_ref, cos_ref, sin_ref, *refs):
     pieces = refs[:head_count]
     (
         w_qkv_ref, _, w_out_ref, k_ref, v_ref, w_down_ref, keep_ref, send_ref, v_s, down_ref,
@@ -155,8 +187,9 @@
         )
 
     @pl.loop(0, rows, unroll=4)
-    def _(r):
-        used = used_rows(lengths_ref[r], heads_local)
+    def _(i):
+        length, r = unpacked(keys_ref[i])
+        used = used_rows(length, heads_local)
         cache_copy(k_ref, k_s, k_sem, r, used).start()
         cache_copy(v_ref, v_s, v_sem, r, used).start()
 
@@ -203,11 +236,10 @@
             [jnp.concatenate([a, blank], axis=1), jnp.concatenate([blank, b], axis=1)], axis=0
         )
 
-    @pl.loop(0, rows // (GROUP * TOGETHER))
-    def _(step):
-        requests = [step * GROUP * TOGETHER + i for i in range(GROUP * TOGETHER)]
+    @pl.loop(0, rows // GROUP)
+    def _(g):
+        lengths, requests = zip(*[unpacked(keys_ref[g * GROUP + i]) for i in range(GROUP)])
         pairs = list(zip(requests[::2], requests[1::2]))
-        lengths = [lengths_ref[r] for r in requests]
         spans = list(zip(lengths[::2], lengths[1::2]))
         queries = [diagonal(query_s[a], query_s[b]).astype(jnp.bfloat16) for a, b in pairs]
         own = [
@@ -215,17 +247,13 @@
         ]
         own = [jnp.concatenate([a, b], axis=0) for a, b in zip(own[::2], own[1::2])]
         values = [diagonal(value_s[a], value_s[b]) for a, b in pairs]
-        needed = []
-        for i in range(TOGETHER):
-            part = lengths[i * GROUP : (i + 1) * GROUP]
-            needed.append((functools.reduce(jnp.maximum, part) + CHUNK - 1) // CHUNK)
-            used = used_rows(sum((length + 7) // 8 * 8 for length in part), heads_local)
-            first = requests[i * GROUP]
-            cache_copy(k_ref, k_s, k_sem, first, used).wait()
-            cache_copy(v_ref, v_s, v_sem, first, used).wait()
+        used = used_rows(sum((length + 7) // 8 * 8 for length in lengths), heads_local)
+        cache_copy(k_ref, k_s, k_sem, g * GROUP, used).wait()
+        cache_copy(v_ref, v_s, v_sem, g * GROUP, used).wait()
+        needed = [(lengths[i] + CHUNK - 1) // CHUNK for i in (0, GROUP // 2)]
 
         def with_chunks(counts):
-            counts = [count for count in counts for _ in range(GROUP // 2)]
+            counts = [count for count in counts for _ in range(GROUP // 4)]
 
             def both(ref, c, pair, span):
                 parts = []
@@ -289,11 +317,11 @@
                 attended_s[b] = summed[SUBLANES:, LANES:]
 
         most = cache_rows // chunk_rows
-        for counts in itertools.product(range(1, most + 1), repeat=TOGETHER):
-            chosen = functools.reduce(
-                jnp.logical_and, [have == count for have, count in zip(needed, counts)]
-            )
-            pl.when(chosen)(functools.partial(with_chunks, counts))
+        for longer, shorter in itertools.product(range(1, most + 1), repeat=2):
+            if longer >= shorter:
+                pl.when((needed[0] == longer) & (needed[1] == shorter))(
+                    functools.partial(with_chunks, (longer, shorter))
+                )
 
     attended = jnp.concatenate(
         [attended_s[:, h, :] for h in range(heads_local)], axis=1
@@ -308,7 +336,7 @@
         down_copy(j).wait()
 
 
-def attention(pieces, me, lengths, cosine, sine, w_qkv, room, w_out, k_cache, v_cache, w_down):
+def attention(pieces, me, keys, cosine, sine, w_qkv, room, w_out, k_cache, v_cache, w_down):
     head_count = len(pieces)
     rows, cols = pieces[0].shape
     half = jax.ShapeDtypeStruct((rows, head_count // 2 * cols), jnp.bfloat16)
@@ -342,7 +370,7 @@
         ),
         name="attention",
     )(
-        pltpu.with_memory_space_constraint(lengths, pltpu.SMEM), me, in_vmem(cosine), in_vmem(sine), *map(in_vmem, pieces), in_vmem(w_qkv), in_vmem(room),
+        pltpu.with_memory_space_constraint(keys, pltpu.SMEM), me, in_vmem(cosine), in_vmem(sine), *map(in_vmem, pieces), in_vmem(w_qkv), in_vmem(room),
         in_hbm(w_out), in_hbm(k_cache), in_hbm(v_cache), in_hbm(w_down),
     )
 
@@ -692,7 +720,7 @@
 
     pieces = [hidden] + [swap(hidden, "head", head_size, j) for j in range(1, head_size)]
     flat = (rows * k_cache.shape[1] * k_cache.shape[2], k_cache.shape[3])
-    own, w_near, room, cosine, sine, lengths_near, shares = fetch(
+    own, w_near, room, cosine, sine, keys, shares = fetch(
         me_ref, lengths, hidden, w_qkv, flat, head_size, expert_ids, route_weights,
         head_size * experts_local,
     )
@@ -700,7 +728,7 @@
     keep, send, _, w_down_near = attention(
         pieces,
         me_ref,
-        lengths_near,
+        keys,
         cosine,
         sine,
         w_near,

time: 62.9 us -> 63.3 us (level); the launches traced: 62 us -> 63.6 us
  starting transfers between devices: 18.5 us -> 19.8 us
  Pallas kernels: 24.8 us -> 25.5 us
    ppermute x17, starting transfers between devices: 15.5 us -> 16.7 us  [swap(): return lax.ppermute(value, axis, [(i, i ^ mask) for i in range(size)])]
    pallas_call x1, Pallas kernels: 6.2 us -> 6.85 us  [attention(): pl.pallas_call(functools.partial(attention_kernel, head_count), out_shape...]
  transfers between devices with their start and end apart: 19 -> 19, of which waited for: 12 -> 11; matrix products, arithmetic and copies ran while one was open for 0% -> 0% of each run, Pallas kernels for 27% -> 26%
where the time goes in v12:
time: 63.3 us; the launch traced here: 63.6 us
  Pallas kernels  25.5 us (40%)
  starting transfers between devices  19.8 us (31%)
  waiting for transfers between devices  17.5 us (28%)
  other arithmetic  0.73 us (1%)
    ppermute x17, starting transfers between devices, swap(): return lax.ppermute(value, axis, [(i, i ^ mask) for i in range(size)])  16.7 us
    ppermute x17, waiting for transfers between devices, swap(): return lax.ppermute(value, axis, [(i, i ^ mask) for i in range(size)])  13.3 us
    pallas_call x2, Pallas kernels, by_expert(): pl.pallas_call(functools.partial(relayout_kernel, js), out_shape=(pltpu.V...  7.43 us
    pallas_call x1, Pallas kernels, attention(): pl.pallas_call(functools.partial(attention_kernel, head_count), out_shape...  6.85 us
    ppermute x2, waiting for transfers between devices, per_device(): got.append(lax.ppermute(crossed_sums[j // 2], ('req', 'head'), pairs))  4.14 us
    ppermute x2, starting transfers between devices, per_device(): got.append(lax.ppermute(crossed_sums[j // 2], ('req', 'head'), pairs))  3.03 us
    pallas_call x1, Pallas kernels, fetch(): pl.pallas_call(fetch_kernel, out_shape=(pltpu.VMEM(hidden.shape, jnp.bflo...  2.94 us
    pallas_call x1, Pallas kernels, experts_whole(): pl.pallas_call(whole_kernel, out_shape=jax.ShapeDtypeStruct((tokens, tota...  2.68 us
  transfers between devices with their start and end apart: 19, of which 11 were waited for; matrix products, arithmetic and copies ran while one was open for 0% of the time, Pallas kernels for 26%

profile of v12, /device:TPU:0, one launch (start us, length us, event | category | flops | bytes accessed | tf_op | source)
XLA Modules:
  0.0 63.6 jit_solution(18106587477932912932)
XLA Ops:
  0.0 3.0 %collective-permute-start = (bf16[32,512]{1,0:T(8,128)(2,1)}, bf16[32,512]{1,0:T(8,128)(2,1)S(1)}, u32[]{:S(2)}, u32[]{:S(2)}) collective-permute-start(bf16[32,512]{1,0:T(8,128)(2,1)} %own_ref.1), channel_id=1, source_target_pairs={{0,2},{1,3},{2,0},{3,1},{4,6},{5,7},{6,4},{7,5},{8,10},{9,11},{10,... | collective-permute-start | bytes 98312 | tf_op jit(solution)/shard_map/ppermute | solution.py:707
  3.0 0.0 collective-permute-start.2
  3.0 0.1 collective-permute-start.1
  3.1 2.9 %fetch.1 = (bf16[32,512]{1,0:T(8,128)(2,1)S(1)}, bf16[3,4,512,512]{3,2,1,0:T(8,128)(2,1)S(1)}, bf16[49152,128]{1,0:T(8,128)(2,1)S(1)}, f32[32,128]{1,0:T(8,128)S...) custom-call(s32[32]{0:T(128)} %lengths_hbm.1, s32[1]{0:T(128)} %bitcast.me_ref, ...), custom_call_target="tpu_custom_call" | custom-call | bytes 12582912 | tf_op jit(solution)/shard_map/fetch/pallas_call | solution.py:132
  6.1 0.0 collective-permute-done.refs_2_.refs_1_
  6.1 0.5 collective-permute-done.2.refs_3_
  6.6 0.0 collective-permute-done.1.refs_1_
  6.6 6.8 %attention.1 = (bf16[32,1024]{1,0:T(8,128)(2,1)S(1)}, bf16[32,1024]{1,0:T(8,128)(2,1)S(1)}, bf16[49152,128]{1,0:T(8,128)(2,1)S(1)}, bf16[4,2048,512]{2,1,0:T(8,128)(2,1)S(1)}) custom-call(s32[32]{0:T(128)S(4)} %get-tuple-element.30.keys_ref, s32[1]{0:T(128)} %bitcast.me_ref, ...), custom_call_target="tpu_custom_call", output_to_operand_aliasing={{2}: (9, {})} | custom-call | flops 268435456 | bytes 11534336 | tf_op jit(solution)/shard_map/attention/pallas_call | solution.py:343
  13.5 0.1 collective-permute-start.3
  13.5 1.2 %collective-permute-done.3.sent_ref = bf16[32,1024]{1,0:T(8,128)(2,1)S(1)} collective-permute-done((bf16[32,1024]{1,0:T(8,128)(2,1)S(1)}, bf16[32,1024]{1,0:T(8,128)(2,1)S(1)}, u32[]{:S(2)}, u32[]{:S(2)}) %collective-permute-start.3) | collective-permute-done | bytes 65568 | tf_op jit(solution)/shard_map/ppermute | solution.py:707
  14.8 1.6 %collective-permute-start.4 = (bf16[32,1024]{1,0:T(8,128)(2,1)S(1)}, bf16[32,1024]{1,0:T(8,128)(2,1)S(1)}, u32[]{:S(2)}, u32[]{:S(2)}) collective-permute-start(bf16[32,1024]{1,0:T(8,128)(2,1)S(1)} %sum.3.refs_0_.refs_2_), channel_id=1, source_target_pairs={{0,2},{1,3},{2,0},{3,1},{4,6},{5,7},{6,4},{7,5},{8,10},{9,11},{10,... | collective-permute-start | bytes 196616 | tf_op jit(solution)/shard_map/ppermute | solution.py:707
  16.4 3.7 %by_expert_0.1 = (bf16[16,4,512,256]{3,2,1,0:T(8,128)(2,1)S(1)}, f32[8,128]{1,0:T(8,128)S(1)}) custom-call(s32[1]{0:T(128)} %bitcast.me_ref, bf16[2048,16,256]{2,1,0:T(8,128)(2,1)} %w_ref.5, bf16[32,1024]{1,0:T(8,128)(2,1)S(1)} %sum.3.refs_0_.refs_2_), custom_call_target="tpu_custom_call" | custom-call | bytes 16777216 | tf_op jit(solution)/shard_map/by_expert_0/pallas_call | solution.py:420
  20.2 0.0 collective-permute-done.4.refs_3_
  20.2 3.4 %collective-permute-start.7 = (bf16[32,1152]{1,0:T(8,128)(2,1)S(1)}, bf16[32,1152]{1,0:T(8,128)(2,1)S(1)}, u32[]{:S(2)}, u32[]{:S(2)}) collective-permute-start(bf16[32,1152]{1,0:T(8,128)(2,1)S(1)} %get-tuple-element.39.refs_1_.refs_0_), channel_id=1, source_target_pairs={{0,24},{4,28},{8,16},{12,20},{16,8},{20,12},{24,0},{28,4},{1,25},{... | collective-permute-start | bytes 221192 | tf_op jit(solution)/shard_map/ppermute | solution.py:707
  23.6 0.0 collective-permute-start.6
  23.6 1.1 %collective-permute-start.5 = (bf16[32,1152]{1,0:T(8,128)(2,1)S(1)}, bf16[32,1152]{1,0:T(8,128)(2,1)S(1)}, u32[]{:S(2)}, u32[]{:S(2)}) collective-permute-start(bf16[32,1152]{1,0:T(8,128)(2,1)S(1)} %get-tuple-element.39.refs_1_.refs_0_), channel_id=1, source_target_pairs={{0,8},{4,12},{8,0},{12,4},{16,24},{20,28},{24,16},{28,20},{1,9},{5... | collective-permute-start | bytes 221192 | tf_op jit(solution)/shard_map/ppermute | solution.py:707
  24.7 3.7 %by_expert_2.1 = (bf16[16,4,512,256]{3,2,1,0:T(8,128)(2,1)S(1)}, f32[8,128]{1,0:T(8,128)S(1)}) custom-call(s32[1]{0:T(128)} %bitcast.me_ref, bf16[2048,16,256]{2,1,0:T(8,128)(2,1)} %w_ref.5, bf16[16,4,512,256]{3,2,1,0:T(8,128)(2,1)S(1)} %get-tuple-element.40.refs_0_, ...), custom_call_target="tpu_custom_call", output_to_operand_aliasing={{0}: (2, {})} | custom-call | bytes 16777216 | tf_op jit(solution)/shard_map/by_expert_2/pallas_call | solution.py:420
  28.4 0.0 collective-permute-done.7.refs_3_
  28.4 1.4 %collective-permute-done.6.refs_2_ = bf16[32,1152]{1,0:T(8,128)(2,1)S(1)} collective-permute-done((bf16[32,1152]{1,0:T(8,128)(2,1)S(1)}, bf16[32,1152]{1,0:T(8,128)(2,1)S(1)}, u32[]{:S(2)}, u32[]{:S(2)}) %collective-permute-start.6) | collective-permute-done | bytes 73760 | tf_op jit(solution)/shard_map/ppermute | solution.py:707
  29.8 0.0 collective-permute-done.5.refs_1_
  29.9 0.1 collective-permute-start.8
  30.0 2.6 %collective-permute-start.10 = (bf16[128,1152]{1,0:T(8,128)(2,1)S(1)}, bf16[128,1152]{1,0:T(8,128)(2,1)S(1)}, u32[]{:S(2)}, u32[]{:S(2)}) collective-permute-start(bf16[128,1152]{1,0:T(8,128)(2,1)S(1)} %stack.1.mine_ref), channel_id=1, source_target_pairs={{0,4},{4,0},{8,12},{12,8},{16,20},{20,16},{24,28},{28,24},{1,5},{5... | collective-permute-start | bytes 884744 | tf_op jit(solution)/shard_map/ppermute | solution.py:707
  32.6 0.0 collective-permute-done.8.other_ref
  32.6 2.7 %experts_whole.1.units_ref = bf16[128,2048]{1,0:T(8,128)(2,1)S(1)} custom-call(s32[1]{0:T(128)} %bitcast.me_ref, bf16[128,1152]{1,0:T(8,128)(2,1)S(1)} %stack.1.mine_ref, bf16[128,1152]{1,0:T(8,128)(2,1)S(1)} %collective-permute-done.8.other_ref, bf16[16,4,512,256]{3,2,1,0:T(8,128)(2,1)S(1)} %get-tuple-element.42.w_ref, f32[8,128]{1,0:T(8,128)S(1)} %get-tuple-element.41.refs_4_._), custom_call_target="tpu_custom_call" | custom-call | flops 2147483648 | bytes 16777216 | tf_op jit(solution)/shard_map/experts_whole/pallas_call | solution.py:578
  35.3 1.3 %down.2 = (bf16[128,1024]{1,0:T(8,128)(2,1)S(1)}, bf16[128,1024]{1,0:T(8,128)(2,1)S(1)}) custom-call(bf16[128,2048]{1,0:T(8,128)(2,1)S(1)} %experts_whole.1.units_ref, bf16[4,2048,512]{2,1,0:T(8,128)(2,1)S(1)} %get-tuple-element.43.w_ref.w_down_ref, f32[8,128]{1,0:T(8,128)S(1)} %get-tuple-element.41.refs_4_._), custom_call_target="tpu_custom_call" | custom-call | flops 1073741824 | bytes 8388608 | tf_op jit(solution)/shard_map/down/pallas_call | solution.py:651
  36.5 0.2 collective-permute-start.9
  36.8 3.4 %collective-permute-done.10.value_ref = bf16[128,1152]{1,0:T(8,128)(2,1)S(1)} collective-permute-done((bf16[128,1152]{1,0:T(8,128)(2,1)S(1)}, bf16[128,1152]{1,0:T(8,128)(2,1)S(1)}, u32[]{:S(2)}, u32[]{:S(2)}) %collective-permute-start.10) | collective-permute-done | bytes 294944 | tf_op jit(solution)/shard_map/ppermute | solution.py:707
  40.2 0.0 collective-permute-start.11
  40.2 0.0 collective-permute-done.9.sent_ref
  40.2 0.1 sum.4
  40.2 1.3 %experts_first.1.product_ref = f32[16,128,256]{2,1,0:T(8,128)S(1)} custom-call(bf16[128,1152]{1,0:T(8,128)(2,1)S(1)} %hold.2.mine_ref, bf16[16,4,512,256]{3,2,1,0:T(8,128)(2,1)S(1)} %get-tuple-element.42.w_ref, bf16[128,512]{1,0:T(8,128)(2,1)S(1)} %get-tuple-element.47._.value_ref), custom_call_target="tpu_custom_call" | custom-call | flops 1073741824 | bytes 8388608 | tf_op jit(solution)/shard_map/experts_first/pallas_call | solution.py:598
  41.6 0.2 collective-permute-done.11.other_ref
  41.8 2.1 %experts_second.1 = (bf16[128,2048]{1,0:T(8,128)(2,1)S(1)}, bf16[128,1024]{1,0:T(8,128)(2,1)S(1)}) custom-call(s32[1]{0:T(128)} %bitcast.me_ref, bf16[128,1152]{1,0:T(8,128)(2,1)S(1)} %hold.2.mine_ref, bf16[128,1152]{1,0:T(8,128)(2,1)S(1)} %collective-permute-done.11.other_ref, f32[16,128,256]{2,1,0:T(8,128)S(1)} %experts_first.1.product_ref, ...), custom_call_target="tpu_custom_call" | custom-call | flops 1073741824 | bytes 8388608 | tf_op jit(solution)/shard_map/experts_second/pallas_call | solution.py:616
  43.8 0.4 collective-permute-start.13
  44.2 0.7 %down.3.after_ref.keep_ref = bf16[128,1024]{1,0:T(8,128)(2,1)S(1)} custom-call(bf16[128,2048]{1,0:T(8,128)(2,1)S(1)} %get-tuple-element.48.units_ref, bf16[4,2048,512]{2,1,0:T(8,128)(2,1)S(1)} %get-tuple-element.43.w_ref.w_down_ref, bf16[128,1024]{1,0:T(8,128)(2,1)S(1)} %get-tuple-element.49._), custom_call_target="tpu_custom_call" | custom-call | flops 536870912 | bytes 4194304 | tf_op jit(solution)/shard_map/down/pallas_call | solution.py:651
  45.0 0.6 collective-permute-start.12
  45.5 0.0 collective-permute-done.13.sent_ref
  45.6 0.1 sum.5
  45.6 1.8 %collective-permute-start.14 = (bf16[128,512]{1,0:T(8,128)(2,1)S(1)}, bf16[128,512]{1,0:T(8,128)(2,1)S(1)}, u32[]{:S(2)}, u32[]{:S(2)}) collective-permute-start(bf16[128,512]{1,0:T(8,128)(2,1)S(1)} %get-tuple-element.50), channel_id=1, source_target_pairs={{0,4},{1,5},{2,6},{3,7},{4,0},{5,1},{6,2},{7,3},{8,12},{9,13},{10,... | collective-permute-start | bytes 393224 | tf_op jit(solution)/shard_map/ppermute | solution.py:773
  47.4 1.2 %collective-permute-start.15 = (bf16[128,512]{1,0:T(8,128)(2,1)S(1)}, bf16[128,512]{1,0:T(8,128)(2,1)S(1)}, u32[]{:S(2)}, u32[]{:S(2)}) collective-permute-start(bf16[128,512]{1,0:T(8,128)(2,1)S(1)} %get-tuple-element.51), channel_id=1, source_target_pairs={{0,6},{1,7},{2,4},{3,5},{4,2},{5,3},{6,0},{7,1},{8,14},{9,15},{10,... | collective-permute-start | bytes 393224 | tf_op jit(solution)/shard_map/ppermute | solution.py:773
  48.6 2.0 %collective-permute-done.12 = bf16[128,512]{1,0:T(8,128)(2,1)S(1)} collective-permute-done((bf16[128,512]{1,0:T(8,128)(2,1)S(1)}, bf16[128,512]{1,0:T(8,128)(2,1)S(1)}, u32[]{:S(2)}, u32[]{:S(2)}) %collective-permute-start.12) | collective-permute-done | bytes 131104 | tf_op jit(solution)/shard_map/ppermute | solution.py:707
  50.6 1.3 %collective-permute-done.14 = bf16[128,512]{1,0:T(8,128)(2,1)S(1)} collective-permute-done((bf16[128,512]{1,0:T(8,128)(2,1)S(1)}, bf16[128,512]{1,0:T(8,128)(2,1)S(1)}, u32[]{:S(2)}, u32[]{:S(2)}) %collective-permute-start.14) | collective-permute-done | bytes 131104 | tf_op jit(solution)/shard_map/ppermute | solution.py:773
  52.0 2.8 %collective-permute-done.15 = bf16[128,512]{1,0:T(8,128)(2,1)S(1)} collective-permute-done((bf16[128,512]{1,0:T(8,128)(2,1)S(1)}, bf16[128,512]{1,0:T(8,128)(2,1)S(1)}, u32[]{:S(2)}, u32[]{:S(2)}) %collective-permute-start.15) | collective-permute-done | bytes 131104 | tf_op jit(solution)/shard_map/ppermute | solution.py:773
  54.8 0.1 add_convert_fusion
  54.9 1.4 %collective-permute-start.16 = (bf16[32,512]{1,0:T(8,128)(2,1)S(1)}, bf16[32,512]{1,0:T(8,128)(2,1)S(1)}, u32[]{:S(2)}, u32[]{:S(2)}) collective-permute-start(bf16[32,512]{1,0:T(8,128)(2,1)S(1)} %get-tuple-element.53), channel_id=1, source_target_pairs={{0,8},{4,12},{8,0},{12,4},{16,24},{20,28},{24,16},{28,20},{1,9},{5... | collective-permute-start | bytes 98312 | tf_op jit(solution)/shard_map/ppermute | solution.py:707
  56.2 1.6 %collective-permute-start.18 = (bf16[32,512]{1,0:T(8,128)(2,1)S(1)}, bf16[32,512]{1,0:T(8,128)(2,1)S(1)}, u32[]{:S(2)}, u32[]{:S(2)}) collective-permute-start(bf16[32,512]{1,0:T(8,128)(2,1)S(1)} %get-tuple-element.54), channel_id=1, source_target_pairs={{0,24},{4,28},{8,16},{12,20},{16,8},{20,12},{24,0},{28,4},{1,25},{... | collective-permute-start | bytes 98312 | tf_op jit(solution)/shard_map/ppermute | solution.py:707
  57.8 0.6 collective-permute-start.17
  58.4 0.4 collective-permute-done.16
  58.8 3.1 %collective-permute-done.18 = bf16[32,512]{1,0:T(8,128)(2,1)S(1)} collective-permute-done((bf16[32,512]{1,0:T(8,128)(2,1)S(1)}, bf16[32,512]{1,0:T(8,128)(2,1)S(1)}, u32[]{:S(2)}, u32[]{:S(2)}) %collective-permute-start.18) | collective-permute-done | bytes 32800 | tf_op jit(solution)/shard_map/ppermute | solution.py:707
  61.9 1.0 %collective-permute-done.17 = bf16[32,512]{1,0:T(8,128)(2,1)S(1)} collective-permute-done((bf16[32,512]{1,0:T(8,128)(2,1)S(1)}, bf16[32,512]{1,0:T(8,128)(2,1)S(1)}, u32[]{:S(2)}, u32[]{:S(2)}) %collective-permute-start.17) | collective-permute-done | bytes 32800 | tf_op jit(solution)/shard_map/ppermute | solution.py:707
  62.9 0.6 %add_convert_fusion.1 = bf16[32,512]{1,0:T(8,128)(2,1)} fusion(f32[32,512]{1,0:T(8,128)S(1)} %get-tuple-element.52, bf16[32,512]{1,0:T(8,128)(2,1)S(1)} %collective-permute-done.18, bf16[32,512]{1,0:T(8,128)(2,1)S(1)} %collective-permute-done.17, bf16[32,512]{1,0:T(8,128)(2,1)S(1)} %collective-permute-done.16, bf16[128,512]{1,0:T(8,128)(2,1)S(1)} %add_convert_fusion), kind=kLoop, calls=%fused_computation.1 | loop fusion | flops 147456 | bytes 229376 | tf_op jit(solution)/shard_map/convert_element_type | solution.py:780
  (7 shorter events, 0.1 us)
Async XLA Ops:
  0.0 6.1 %collective-permute-start = (bf16[32,512]{1,0:T(8,128)(2,1)}, bf16[32,512]{1,0:T(8,128)(2,1)S(1)}, u32[]{:S(2)}, u32[]{:S(2)}) collective-permute-start(bf16[32,512]{1,0:T(8,128)(2,1)} %own_ref.1), channel_id=1, source_target_pairs={{0,2},{1,3},{2,0},{3,1},{4,6},{5,7},{6,4},{7,5},{8,10},{9,11},{10,... | collective-permute-start | bytes 98312 | tf_op jit(solution)/shard_map/ppermute | solution.py:707
  3.0 3.6 %collective-permute-start.2 = (bf16[32,512]{1,0:T(8,128)(2,1)}, bf16[32,512]{1,0:T(8,128)(2,1)S(1)}, u32[]{:S(2)}, u32[]{:S(2)}) collective-permute-start(bf16[32,512]{1,0:T(8,128)(2,1)} %own_ref.1), channel_id=1, source_target_pairs={{0,3},{1,2},{2,1},{3,0},{4,7},{5,6},{6,5},{7,4},{8,11},{9,10},{10,... | collective-permute-start | bytes 98312 | tf_op jit(solution)/shard_map/ppermute | solution.py:707
  3.0 3.6 %collective-permute-start.1 = (bf16[32,512]{1,0:T(8,128)(2,1)}, bf16[32,512]{1,0:T(8,128)(2,1)S(1)}, u32[]{:S(2)}, u32[]{:S(2)}) collective-permute-start(bf16[32,512]{1,0:T(8,128)(2,1)} %own_ref.1), channel_id=1, source_target_pairs={{0,1},{1,0},{2,3},{3,2},{4,5},{5,4},{6,7},{7,6},{8,9},{9,8},{10,11... | collective-permute-start | bytes 98312 | tf_op jit(solution)/shard_map/ppermute | solution.py:707
  13.5 1.3 %collective-permute-start.3 = (bf16[32,1024]{1,0:T(8,128)(2,1)S(1)}, bf16[32,1024]{1,0:T(8,128)(2,1)S(1)}, u32[]{:S(2)}, u32[]{:S(2)}) collective-permute-start(bf16[32,1024]{1,0:T(8,128)(2,1)S(1)} %get-tuple-element.36), channel_id=1, source_target_pairs={{0,1},{1,0},{2,3},{3,2},{4,5},{5,4},{6,7},{7,6},{8,9},{9,8},{10,11... | collective-permute-start | bytes 196616 | tf_op jit(solution)/shard_map/ppermute | solution.py:707
  14.8 5.4 %collective-permute-start.4 = (bf16[32,1024]{1,0:T(8,128)(2,1)S(1)}, bf16[32,1024]{1,0:T(8,128)(2,1)S(1)}, u32[]{:S(2)}, u32[]{:S(2)}) collective-permute-start(bf16[32,1024]{1,0:T(8,128)(2,1)S(1)} %sum.3.refs_0_.refs_2_), channel_id=1, source_target_pairs={{0,2},{1,3},{2,0},{3,1},{4,6},{5,7},{6,4},{7,5},{8,10},{9,11},{10,... | collective-permute-start | bytes 196616 | tf_op jit(solution)/shard_map/ppermute | solution.py:707
  20.2 8.2 %collective-permute-start.7 = (bf16[32,1152]{1,0:T(8,128)(2,1)S(1)}, bf16[32,1152]{1,0:T(8,128)(2,1)S(1)}, u32[]{:S(2)}, u32[]{:S(2)}) collective-permute-start(bf16[32,1152]{1,0:T(8,128)(2,1)S(1)} %get-tuple-element.39.refs_1_.refs_0_), channel_id=1, source_target_pairs={{0,24},{4,28},{8,16},{12,20},{16,8},{20,12},{24,0},{28,4},{1,25},{... | collective-permute-start | bytes 221192 | tf_op jit(solution)/shard_map/ppermute | solution.py:707
  23.6 6.3 %collective-permute-start.6 = (bf16[32,1152]{1,0:T(8,128)(2,1)S(1)}, bf16[32,1152]{1,0:T(8,128)(2,1)S(1)}, u32[]{:S(2)}, u32[]{:S(2)}) collective-permute-start(bf16[32,1152]{1,0:T(8,128)(2,1)S(1)} %get-tuple-element.39.refs_1_.refs_0_), channel_id=1, source_target_pairs={{0,16},{4,20},{8,24},{12,28},{16,0},{20,4},{24,8},{28,12},{1,17},{... | collective-permute-start | bytes 221192 | tf_op jit(solution)/shard_map/ppermute | solution.py:707
  23.6 6.3 %collective-permute-start.5 = (bf16[32,1152]{1,0:T(8,128)(2,1)S(1)}, bf16[32,1152]{1,0:T(8,128)(2,1)S(1)}, u32[]{:S(2)}, u32[]{:S(2)}) collective-permute-start(bf16[32,1152]{1,0:T(8,128)(2,1)S(1)} %get-tuple-element.39.refs_1_.refs_0_), channel_id=1, source_target_pairs={{0,8},{4,12},{8,0},{12,4},{16,24},{20,28},{24,16},{28,20},{1,9},{5... | collective-permute-start | bytes 221192 | tf_op jit(solution)/shard_map/ppermute | solution.py:707
  29.9 2.7 %collective-permute-start.8 = (bf16[128,1152]{1,0:T(8,128)(2,1)S(1)}, bf16[128,1152]{1,0:T(8,128)(2,1)S(1)}, u32[]{:S(2)}, u32[]{:S(2)}) collective-permute-start(bf16[128,1152]{1,0:T(8,128)(2,1)S(1)} %stack.1.mine_ref), channel_id=1, source_target_pairs={{0,1},{1,0},{2,3},{3,2},{4,5},{5,4},{6,7},{7,6},{8,9},{9,8},{10,11... | collective-permute-start | bytes 884744 | tf_op jit(solution)/shard_map/ppermute | solution.py:707
  30.0 10.2 %collective-permute-start.10 = (bf16[128,1152]{1,0:T(8,128)(2,1)S(1)}, bf16[128,1152]{1,0:T(8,128)(2,1)S(1)}, u32[]{:S(2)}, u32[]{:S(2)}) collective-permute-start(bf16[128,1152]{1,0:T(8,128)(2,1)S(1)} %stack.1.mine_ref), channel_id=1, source_target_pairs={{0,4},{4,0},{8,12},{12,8},{16,20},{20,16},{24,28},{28,24},{1,5},{5... | collective-permute-start | bytes 884744 | tf_op jit(solution)/shard_map/ppermute | solution.py:707
  36.5 3.6 %collective-permute-start.9 = (bf16[128,1024]{1,0:T(8,128)(2,1)S(1)}, bf16[128,1024]{1,0:T(8,128)(2,1)S(1)}, u32[]{:S(2)}, u32[]{:S(2)}) collective-permute-start(bf16[128,1024]{1,0:T(8,128)(2,1)S(1)} %get-tuple-element.45.after_ref), channel_id=1, source_target_pairs={{0,1},{1,0},{2,3},{3,2},{4,5},{5,4},{6,7},{7,6},{8,9},{9,8},{10,11... | collective-permute-start | bytes 786440 | tf_op jit(solution)/shard_map/ppermute | solution.py:707
  40.2 1.6 %collective-permute-start.11 = (bf16[128,1152]{1,0:T(8,128)(2,1)S(1)}, bf16[128,1152]{1,0:T(8,128)(2,1)S(1)}, u32[]{:S(2)}, u32[]{:S(2)}) collective-permute-start(bf16[128,1152]{1,0:T(8,128)(2,1)S(1)} %hold.2.mine_ref), channel_id=1, source_target_pairs={{0,1},{1,0},{2,3},{3,2},{4,5},{5,4},{6,7},{7,6},{8,9},{9,8},{10,11... | collective-permute-start | bytes 884744 | tf_op jit(solution)/shard_map/ppermute | solution.py:707
  43.8 1.7 %collective-permute-start.13 = (bf16[128,1024]{1,0:T(8,128)(2,1)S(1)}, bf16[128,1024]{1,0:T(8,128)(2,1)S(1)}, u32[]{:S(2)}, u32[]{:S(2)}) collective-permute-start(bf16[128,1024]{1,0:T(8,128)(2,1)S(1)} %get-tuple-element.49._), channel_id=1, source_target_pairs={{0,1},{1,0},{2,3},{3,2},{4,5},{5,4},{6,7},{7,6},{8,9},{9,8},{10,11... | collective-permute-start | bytes 786440 | tf_op jit(solution)/shard_map/ppermute | solution.py:707
  45.0 5.7 %collective-permute-start.12 = (bf16[128,512]{1,0:T(8,128)(2,1)S(1)}, bf16[128,512]{1,0:T(8,128)(2,1)S(1)}, u32[]{:S(2)}, u32[]{:S(2)}) collective-permute-start(bf16[128,512]{1,0:T(8,128)(2,1)S(1)} %hold.3), channel_id=1, source_target_pairs={{0,2},{1,3},{2,0},{3,1},{4,6},{5,7},{6,4},{7,5},{8,10},{9,11},{10,... | collective-permute-start | bytes 393224 | tf_op jit(solution)/shard_map/ppermute | solution.py:707
  45.6 6.3 %collective-permute-start.14 = (bf16[128,512]{1,0:T(8,128)(2,1)S(1)}, bf16[128,512]{1,0:T(8,128)(2,1)S(1)}, u32[]{:S(2)}, u32[]{:S(2)}) collective-permute-start(bf16[128,512]{1,0:T(8,128)(2,1)S(1)} %get-tuple-element.50), channel_id=1, source_target_pairs={{0,4},{1,5},{2,6},{3,7},{4,0},{5,1},{6,2},{7,3},{8,12},{9,13},{10,... | collective-permute-start | bytes 393224 | tf_op jit(solution)/shard_map/ppermute | solution.py:773
  47.4 7.3 %collective-permute-start.15 = (bf16[128,512]{1,0:T(8,128)(2,1)S(1)}, bf16[128,512]{1,0:T(8,128)(2,1)S(1)}, u32[]{:S(2)}, u32[]{:S(2)}) collective-permute-start(bf16[128,512]{1,0:T(8,128)(2,1)S(1)} %get-tuple-element.51), channel_id=1, source_target_pairs={{0,6},{1,7},{2,4},{3,5},{4,2},{5,3},{6,0},{7,1},{8,14},{9,15},{10,... | collective-permute-start | bytes 393224 | tf_op jit(solution)/shard_map/ppermute | solution.py:773
  54.9 4.0 %collective-permute-start.16 = (bf16[32,512]{1,0:T(8,128)(2,1)S(1)}, bf16[32,512]{1,0:T(8,128)(2,1)S(1)}, u32[]{:S(2)}, u32[]{:S(2)}) collective-permute-start(bf16[32,512]{1,0:T(8,128)(2,1)S(1)} %get-tuple-element.53), channel_id=1, source_target_pairs={{0,8},{4,12},{8,0},{12,4},{16,24},{20,28},{24,16},{28,20},{1,9},{5... | collective-permute-start | bytes 98312 | tf_op jit(solution)/shard_map/ppermute | solution.py:707
  56.2 5.7 %collective-permute-start.18 = (bf16[32,512]{1,0:T(8,128)(2,1)S(1)}, bf16[32,512]{1,0:T(8,128)(2,1)S(1)}, u32[]{:S(2)}, u32[]{:S(2)}) collective-permute-start(bf16[32,512]{1,0:T(8,128)(2,1)S(1)} %get-tuple-element.54), channel_id=1, source_target_pairs={{0,24},{4,28},{8,16},{12,20},{16,8},{20,12},{24,0},{28,4},{1,25},{... | collective-permute-start | bytes 98312 | tf_op jit(solution)/shard_map/ppermute | solution.py:707
  57.8 5.1 %collective-permute-start.17 = (bf16[32,512]{1,0:T(8,128)(2,1)S(1)}, bf16[32,512]{1,0:T(8,128)(2,1)S(1)}, u32[]{:S(2)}, u32[]{:S(2)}) collective-permute-start(bf16[32,512]{1,0:T(8,128)(2,1)S(1)} %get-tuple-element.55), channel_id=1, source_target_pairs={{0,16},{4,20},{8,24},{12,28},{16,0},{20,4},{24,8},{28,12},{1,17},{... | collective-permute-start | bytes 98312 | tf_op jit(solution)/shard_map/ppermute | solution.py:707

commit v13 on v12

--- a/solution.py
+++ b/solution.py
@@ -58,7 +58,7 @@
 
 def fetch_kernel(
     lengths_hbm, me_ref, freqs_ref, own_ref, w_ref, ids_ref, route_ref,
-    own_out_ref, w_out_ref, blank_ref, cos_ref, sin_ref, keys_ref, shares_ref,
+    own_out_ref, w_out_ref, blank_ref, cos_ref, sin_ref, keys_ref, shares_ref, part_ref,
     lengths_ref, angle_s, ids_s, route_s, sem, small_sem,
 ):
     head_count, cols = w_out_ref.shape[1:3]
@@ -76,8 +76,8 @@
         )
     ]
     small = copies[:2]
-    for c in range(w_ref.shape[0]):
-        for j in range(head_count):
+    for j in range(head_count):
+        for c in range(w_ref.shape[0]):
             first = pl.multiple_of((me ^ j) * cols, cols)
             copies.append(
                 pltpu.make_async_copy(
@@ -120,7 +120,14 @@
     for k in range(ids_s.shape[0]):
         shares += jnp.where(expert == ids_s[k : k + 1, :], route_s[k : k + 1, :], 0.0)
     shares_ref[...] = jnp.transpose(shares, (1, 0)).astype(jnp.bfloat16)
-    for copy in copies[2:]:
+    kinds = w_ref.shape[0]
+    for copy in copies[2 : 3 + kinds]:
+        copy.wait()
+    for c in range(kinds):
+        part_ref[c] = jnp.dot(
+            own_out_ref[...], w_out_ref[c, 0], preferred_element_type=jnp.float32
+        )
+    for copy in copies[3 + kinds :]:
         copy.wait()
 
 
@@ -139,9 +146,10 @@
             pltpu.VMEM((rows, LANES), jnp.float32),
             pltpu.SMEM(lengths.shape, lengths.dtype),
             pltpu.VMEM((rows, -(-experts // LANES) * LANES), jnp.bfloat16),
+            pltpu.VMEM((w_qkv.shape[0], rows, cols), jnp.float32),
         ),
         in_specs=[ANY, SMEM, VMEM] + [ANY] * 4,
-        out_specs=[VMEM] * 5 + [SMEM, VMEM],
+        out_specs=[VMEM] * 5 + [SMEM, VMEM, VMEM],
         scratch_shapes=[
             pltpu.SMEM(lengths.shape, lengths.dtype),
             pltpu.VMEM((rows, LANES), jnp.float32),
@@ -161,7 +169,7 @@
     )
 
 
-def attention_kernel(head_count, keys_ref, me_ref, cos_ref, sin_ref, *refs):
+def attention_kernel(head_count, keys_ref, me_ref, cos_ref, sin_ref, part_ref, *refs):
     pieces = refs[:head_count]
     (
         w_qkv_ref, _, w_out_ref, k_ref, v_ref, w_down_ref, keep_ref, send_ref, v_s, down_ref,
@@ -213,10 +221,13 @@
     scale = lax.rsqrt(square / (cols * head_count) + norm_eps)
     cosine, sine = cos_ref[...], sin_ref[...]
     for c, target in enumerate((query_s, key_s, value_s)):
-        projected = scale * jnp.dot(
-            states,
-            w_qkv_ref[c].reshape(head_count * cols, cols),
-            preferred_element_type=jnp.float32,
+        projected = scale * (
+            part_ref[c]
+            + jnp.dot(
+                states[:, cols:],
+                w_qkv_ref[c, pl.ds(1, head_count - 1)].reshape((head_count - 1) * cols, cols),
+                preferred_element_type=jnp.float32,
+            )
         )
         for h in range(heads_local):
             part = projected[:, h * LANES : (h + 1) * LANES]
@@ -336,7 +347,7 @@
         down_copy(j).wait()
 
 
-def attention(pieces, me, keys, cosine, sine, w_qkv, room, w_out, k_cache, v_cache, w_down):
+def attention(pieces, me, keys, cosine, sine, part, w_qkv, room, w_out, k_cache, v_cache, w_down):
     head_count = len(pieces)
     rows, cols = pieces[0].shape
     half = jax.ShapeDtypeStruct((rows, head_count // 2 * cols), jnp.bfloat16)
@@ -348,9 +359,9 @@
             pltpu.VMEM(room.shape, jnp.bfloat16),
             pltpu.VMEM((head_count, w_down.shape[0], cols), jnp.bfloat16),
         ),
-        in_specs=[SMEM, SMEM] + [VMEM] * (head_count + 4) + [ANY] * 4,
+        in_specs=[SMEM, SMEM] + [VMEM] * (head_count + 5) + [ANY] * 4,
         out_specs=(VMEM, VMEM, VMEM, VMEM),
-        input_output_aliases={head_count + 5: 2},
+        input_output_aliases={head_count + 6: 2},
         scratch_shapes=[
             pltpu.VMEM((head_count, cols, cols), jnp.bfloat16),
             pltpu.VMEM(k_cache.shape, jnp.bfloat16),
@@ -370,7 +381,7 @@
         ),
         name="attention",
     )(
-        pltpu.with_memory_space_constraint(keys, pltpu.SMEM), me, in_vmem(cosine), in_vmem(sine), *map(in_vmem, pieces), in_vmem(w_qkv), in_vmem(room),
+        pltpu.with_memory_space_constraint(keys, pltpu.SMEM), me, in_vmem(cosine), in_vmem(sine), in_vmem(part), *map(in_vmem, pieces), in_vmem(w_qkv), in_vmem(room),
         in_hbm(w_out), in_hbm(k_cache), in_hbm(v_cache), in_hbm(w_down),
     )
 
@@ -720,7 +731,7 @@
 
     pieces = [hidden] + [swap(hidden, "head", head_size, j) for j in range(1, head_size)]
     flat = (rows * k_cache.shape[1] * k_cache.shape[2], k_cache.shape[3])
-    own, w_near, room, cosine, sine, keys, shares = fetch(
+    own, w_near, room, cosine, sine, keys, shares, part = fetch(
         me_ref, lengths, hidden, w_qkv, flat, head_size, expert_ids, route_weights,
         head_size * experts_local,
     )
@@ -731,6 +742,7 @@
         keys,
         cosine,
         sine,
+        part,
         w_near,
         room,
         w_out,

time: 63.3 us -> 62.9 us (level)
  starting transfers between devices: 19.8 us -> 18.7 us
    ppermute x17, starting transfers between devices: 16.7 us -> 15.7 us  [swap(): return lax.ppermute(value, axis, [(i, i ^ mask) for i in range(size)])]
  transfers between devices with their start and end apart: 19 -> 19, of which waited for: 11 -> 12; matrix products, arithmetic and copies ran while one was open for 0% -> 0% of each run, Pallas kernels for 26% -> 26%
where the time goes in v13:
time: 62.9 us; the launch traced here: 62.6 us
  Pallas kernels  25.2 us (40%)
  starting transfers between devices  18.7 us (30%)
  waiting for transfers between devices  17.7 us (28%)
  other arithmetic  0.73 us (1%)
    ppermute x17, starting transfers between devices, swap(): return lax.ppermute(value, axis, [(i, i ^ mask) for i in range(size)])  15.7 us
    ppermute x17, waiting for transfers between devices, swap(): return lax.ppermute(value, axis, [(i, i ^ mask) for i in range(size)])  13.6 us
    pallas_call x2, Pallas kernels, by_expert(): pl.pallas_call(functools.partial(relayout_kernel, js), out_shape=(pltpu.V...  7.43 us
    pallas_call x1, Pallas kernels, attention(): pl.pallas_call(functools.partial(attention_kernel, head_count), out_shape...  6.44 us
    ppermute x2, waiting for transfers between devices, per_device(): got.append(lax.ppermute(crossed_sums[j // 2], ('req', 'head'), pairs))  4.12 us
    ppermute x2, starting transfers between devices, per_device(): got.append(lax.ppermute(crossed_sums[j // 2], ('req', 'head'), pairs))  3.05 us
    pallas_call x1, Pallas kernels, fetch(): pl.pallas_call(fetch_kernel, out_shape=(pltpu.VMEM(hidden.shape, jnp.bflo...  3.04 us
    pallas_call x1, Pallas kernels, experts_whole(): pl.pallas_call(whole_kernel, out_shape=jax.ShapeDtypeStruct((tokens, tota...  2.68 us
  transfers between devices with their start and end apart: 19, of which 12 were waited for; matrix products, arithmetic and copies ran while one was open for 0% of the time, Pallas kernels for 26%

profile of v13, /device:TPU:0, one launch (start us, length us, event | category | flops | bytes accessed | tf_op | source)
XLA Modules:
  0.0 62.6 jit_solution(3614125193698433337)
XLA Ops:
  0.0 3.0 %collective-permute-start = (bf16[32,512]{1,0:T(8,128)(2,1)}, bf16[32,512]{1,0:T(8,128)(2,1)S(1)}, u32[]{:S(2)}, u32[]{:S(2)}) collective-permute-start(bf16[32,512]{1,0:T(8,128)(2,1)} %own_ref.1), channel_id=1, source_target_pairs={{0,2},{1,3},{2,0},{3,1},{4,6},{5,7},{6,4},{7,5},{8,10},{9,11},{10,... | collective-permute-start | bytes 98312 | tf_op jit(solution)/shard_map/ppermute | solution.py:718
  3.0 0.0 collective-permute-start.2
  3.0 0.1 collective-permute-start.1
  3.1 3.0 %fetch.1 = (bf16[32,512]{1,0:T(8,128)(2,1)S(1)}, bf16[3,4,512,512]{3,2,1,0:T(8,128)(2,1)S(1)}, bf16[49152,128]{1,0:T(8,128)(2,1)S(1)}, f32[32,128]{1,0:T(8,128)S...) custom-call(s32[32]{0:T(128)} %lengths_hbm.1, ...), custom_call_target="tpu_custom_call" | custom-call | bytes 12582912 | tf_op jit(solution)/shard_map/fetch/pallas_call | solution.py:139
  6.2 0.0 collective-permute-done.refs_2_.refs_1_
  6.2 0.4 collective-permute-done.2.refs_3_
  6.6 0.0 collective-permute-done.1.refs_1_
  6.6 6.4 %attention.1 = (bf16[32,1024]{1,0:T(8,128)(2,1)S(1)}, bf16[32,1024]{1,0:T(8,128)(2,1)S(1)}, bf16[49152,128]{1,0:T(8,128)(2,1)S(1)}, bf16[4,2048,512]{2,1,0:T(8,128)(2,1)S(1)}) custom-call(s32[32]{0:T(128)S(4)} %get-tuple-element.31.keys_ref, s32[1]{0:T(128)} %bitcast.me_ref, ...), custom_call_target="tpu_custom_call", output_to_operand_aliasing={{2}: (10, {})} | custom-call | flops 268435456 | bytes 11534336 | tf_op jit(solution)/shard_map/attention/pallas_call | solution.py:354
  13.1 0.1 collective-permute-start.3
  13.2 1.2 %collective-permute-done.3.sent_ref = bf16[32,1024]{1,0:T(8,128)(2,1)S(1)} collective-permute-done((bf16[32,1024]{1,0:T(8,128)(2,1)S(1)}, bf16[32,1024]{1,0:T(8,128)(2,1)S(1)}, u32[]{:S(2)}, u32[]{:S(2)}) %collective-permute-start.3) | collective-permute-done | bytes 65568 | tf_op jit(solution)/shard_map/ppermute | solution.py:718
  14.4 1.7 %collective-permute-start.4 = (bf16[32,1024]{1,0:T(8,128)(2,1)S(1)}, bf16[32,1024]{1,0:T(8,128)(2,1)S(1)}, u32[]{:S(2)}, u32[]{:S(2)}) collective-permute-start(bf16[32,1024]{1,0:T(8,128)(2,1)S(1)} %sum.3.refs_0_.refs_2_), channel_id=1, source_target_pairs={{0,2},{1,3},{2,0},{3,1},{4,6},{5,7},{6,4},{7,5},{8,10},{9,11},{10,... | collective-permute-start | bytes 196616 | tf_op jit(solution)/shard_map/ppermute | solution.py:718
  16.1 3.7 %by_expert_0.1 = (bf16[16,4,512,256]{3,2,1,0:T(8,128)(2,1)S(1)}, f32[8,128]{1,0:T(8,128)S(1)}) custom-call(s32[1]{0:T(128)} %bitcast.me_ref, bf16[2048,16,256]{2,1,0:T(8,128)(2,1)} %w_ref.5, bf16[32,1024]{1,0:T(8,128)(2,1)S(1)} %sum.3.refs_0_.refs_2_), custom_call_target="tpu_custom_call" | custom-call | bytes 16777216 | tf_op jit(solution)/shard_map/by_expert_0/pallas_call | solution.py:431
  19.9 0.0 collective-permute-done.4.refs_3_
  19.9 3.8 %collective-permute-start.7 = (bf16[32,1152]{1,0:T(8,128)(2,1)S(1)}, bf16[32,1152]{1,0:T(8,128)(2,1)S(1)}, u32[]{:S(2)}, u32[]{:S(2)}) collective-permute-start(bf16[32,1152]{1,0:T(8,128)(2,1)S(1)} %get-tuple-element.41.refs_1_.refs_0_), channel_id=1, source_target_pairs={{0,24},{4,28},{8,16},{12,20},{16,8},{20,12},{24,0},{28,4},{1,25},{... | collective-permute-start | bytes 221192 | tf_op jit(solution)/shard_map/ppermute | solution.py:718
  23.7 0.0 collective-permute-start.6
  23.7 0.7 %collective-permute-start.5 = (bf16[32,1152]{1,0:T(8,128)(2,1)S(1)}, bf16[32,1152]{1,0:T(8,128)(2,1)S(1)}, u32[]{:S(2)}, u32[]{:S(2)}) collective-permute-start(bf16[32,1152]{1,0:T(8,128)(2,1)S(1)} %get-tuple-element.41.refs_1_.refs_0_), channel_id=1, source_target_pairs={{0,8},{4,12},{8,0},{12,4},{16,24},{20,28},{24,16},{28,20},{1,9},{5... | collective-permute-start | bytes 221192 | tf_op jit(solution)/shard_map/ppermute | solution.py:718
  24.4 3.7 %by_expert_2.1 = (bf16[16,4,512,256]{3,2,1,0:T(8,128)(2,1)S(1)}, f32[8,128]{1,0:T(8,128)S(1)}) custom-call(s32[1]{0:T(128)} %bitcast.me_ref, bf16[2048,16,256]{2,1,0:T(8,128)(2,1)} %w_ref.5, bf16[16,4,512,256]{3,2,1,0:T(8,128)(2,1)S(1)} %get-tuple-element.42.refs_0_, ...), custom_call_target="tpu_custom_call", output_to_operand_aliasing={{0}: (2, {})} | custom-call | bytes 16777216 | tf_op jit(solution)/shard_map/by_expert_2/pallas_call | solution.py:431
  28.1 0.0 collective-permute-done.7.refs_3_
  28.1 2.0 %collective-permute-done.6.refs_2_ = bf16[32,1152]{1,0:T(8,128)(2,1)S(1)} collective-permute-done((bf16[32,1152]{1,0:T(8,128)(2,1)S(1)}, bf16[32,1152]{1,0:T(8,128)(2,1)S(1)}, u32[]{:S(2)}, u32[]{:S(2)}) %collective-permute-start.6) | collective-permute-done | bytes 73760 | tf_op jit(solution)/shard_map/ppermute | solution.py:718
  30.1 0.0 collective-permute-done.5.refs_1_
  30.1 0.1 collective-permute-start.8
  30.2 1.5 %collective-permute-start.10 = (bf16[128,1152]{1,0:T(8,128)(2,1)S(1)}, bf16[128,1152]{1,0:T(8,128)(2,1)S(1)}, u32[]{:S(2)}, u32[]{:S(2)}) collective-permute-start(bf16[128,1152]{1,0:T(8,128)(2,1)S(1)} %stack.1.mine_ref), channel_id=1, source_target_pairs={{0,4},{4,0},{8,12},{12,8},{16,20},{20,16},{24,28},{28,24},{1,5},{5... | collective-permute-start | bytes 884744 | tf_op jit(solution)/shard_map/ppermute | solution.py:718
  31.7 0.1 collective-permute-done.8.other_ref
  31.8 2.7 %experts_whole.1.units_ref = bf16[128,2048]{1,0:T(8,128)(2,1)S(1)} custom-call(s32[1]{0:T(128)} %bitcast.me_ref, bf16[128,1152]{1,0:T(8,128)(2,1)S(1)} %stack.1.mine_ref, bf16[128,1152]{1,0:T(8,128)(2,1)S(1)} %collective-permute-done.8.other_ref, bf16[16,4,512,256]{3,2,1,0:T(8,128)(2,1)S(1)} %get-tuple-element.44.w_ref, f32[8,128]{1,0:T(8,128)S(1)} %get-tuple-element.43.refs_4_._), custom_call_target="tpu_custom_call" | custom-call | flops 2147483648 | bytes 16777216 | tf_op jit(solution)/shard_map/experts_whole/pallas_call | solution.py:589
  34.5 1.3 %down.2 = (bf16[128,1024]{1,0:T(8,128)(2,1)S(1)}, bf16[128,1024]{1,0:T(8,128)(2,1)S(1)}) custom-call(bf16[128,2048]{1,0:T(8,128)(2,1)S(1)} %experts_whole.1.units_ref, bf16[4,2048,512]{2,1,0:T(8,128)(2,1)S(1)} %get-tuple-element.45.w_ref.w_down_ref, f32[8,128]{1,0:T(8,128)S(1)} %get-tuple-element.43.refs_4_._), custom_call_target="tpu_custom_call" | custom-call | flops 1073741824 | bytes 8388608 | tf_op jit(solution)/shard_map/down/pallas_call | solution.py:662
  35.8 0.2 collective-permute-start.9
  36.0 3.7 %collective-permute-done.10.value_ref = bf16[128,1152]{1,0:T(8,128)(2,1)S(1)} collective-permute-done((bf16[128,1152]{1,0:T(8,128)(2,1)S(1)}, bf16[128,1152]{1,0:T(8,128)(2,1)S(1)}, u32[]{:S(2)}, u32[]{:S(2)}) %collective-permute-start.10) | collective-permute-done | bytes 294944 | tf_op jit(solution)/shard_map/ppermute | solution.py:718
  39.7 0.0 collective-permute-start.11
  39.7 0.0 collective-permute-done.9.sent_ref
  39.7 0.1 sum.4
  39.7 1.3 %experts_first.1.product_ref = f32[16,128,256]{2,1,0:T(8,128)S(1)} custom-call(bf16[128,1152]{1,0:T(8,128)(2,1)S(1)} %hold.2.mine_ref, bf16[16,4,512,256]{3,2,1,0:T(8,128)(2,1)S(1)} %get-tuple-element.44.w_ref, bf16[128,512]{1,0:T(8,128)(2,1)S(1)} %get-tuple-element.49._.value_ref), custom_call_target="tpu_custom_call" | custom-call | flops 1073741824 | bytes 8388608 | tf_op jit(solution)/shard_map/experts_first/pallas_call | solution.py:609
  41.0 0.2 collective-permute-done.11.other_ref
  41.2 2.1 %experts_second.1 = (bf16[128,2048]{1,0:T(8,128)(2,1)S(1)}, bf16[128,1024]{1,0:T(8,128)(2,1)S(1)}) custom-call(s32[1]{0:T(128)} %bitcast.me_ref, bf16[128,1152]{1,0:T(8,128)(2,1)S(1)} %hold.2.mine_ref, bf16[128,1152]{1,0:T(8,128)(2,1)S(1)} %collective-permute-done.11.other_ref, f32[16,128,256]{2,1,0:T(8,128)S(1)} %experts_first.1.product_ref, ...), custom_call_target="tpu_custom_call" | custom-call | flops 1073741824 | bytes 8388608 | tf_op jit(solution)/shard_map/experts_second/pallas_call | solution.py:627
  43.3 0.4 collective-permute-start.13
  43.7 0.7 %down.3.after_ref.keep_ref = bf16[128,1024]{1,0:T(8,128)(2,1)S(1)} custom-call(bf16[128,2048]{1,0:T(8,128)(2,1)S(1)} %get-tuple-element.50.units_ref, bf16[4,2048,512]{2,1,0:T(8,128)(2,1)S(1)} %get-tuple-element.45.w_ref.w_down_ref, bf16[128,1024]{1,0:T(8,128)(2,1)S(1)} %get-tuple-element.51._), custom_call_target="tpu_custom_call" | custom-call | flops 536870912 | bytes 4194304 | tf_op jit(solution)/shard_map/down/pallas_call | solution.py:662
  44.4 0.6 collective-permute-start.12
  45.0 0.0 collective-permute-done.13.sent_ref
  45.0 0.1 sum.5
  45.1 1.5 %collective-permute-start.14 = (bf16[128,512]{1,0:T(8,128)(2,1)S(1)}, bf16[128,512]{1,0:T(8,128)(2,1)S(1)}, u32[]{:S(2)}, u32[]{:S(2)}) collective-permute-start(bf16[128,512]{1,0:T(8,128)(2,1)S(1)} %get-tuple-element.52), channel_id=1, source_target_pairs={{0,4},{1,5},{2,6},{3,7},{4,0},{5,1},{6,2},{7,3},{8,12},{9,13},{10,... | collective-permute-start | bytes 393224 | tf_op jit(solution)/shard_map/ppermute | solution.py:785
  46.6 1.5 %collective-permute-start.15 = (bf16[128,512]{1,0:T(8,128)(2,1)S(1)}, bf16[128,512]{1,0:T(8,128)(2,1)S(1)}, u32[]{:S(2)}, u32[]{:S(2)}) collective-permute-start(bf16[128,512]{1,0:T(8,128)(2,1)S(1)} %get-tuple-element.53), channel_id=1, source_target_pairs={{0,6},{1,7},{2,4},{3,5},{4,2},{5,3},{6,0},{7,1},{8,14},{9,15},{10,... | collective-permute-start | bytes 393224 | tf_op jit(solution)/shard_map/ppermute | solution.py:785
  48.1 2.0 %collective-permute-done.12 = bf16[128,512]{1,0:T(8,128)(2,1)S(1)} collective-permute-done((bf16[128,512]{1,0:T(8,128)(2,1)S(1)}, bf16[128,512]{1,0:T(8,128)(2,1)S(1)}, u32[]{:S(2)}, u32[]{:S(2)}) %collective-permute-start.12) | collective-permute-done | bytes 131104 | tf_op jit(solution)/shard_map/ppermute | solution.py:718
  50.1 1.4 %collective-permute-done.14 = bf16[128,512]{1,0:T(8,128)(2,1)S(1)} collective-permute-done((bf16[128,512]{1,0:T(8,128)(2,1)S(1)}, bf16[128,512]{1,0:T(8,128)(2,1)S(1)}, u32[]{:S(2)}, u32[]{:S(2)}) %collective-permute-start.14) | collective-permute-done | bytes 131104 | tf_op jit(solution)/shard_map/ppermute | solution.py:785
  51.5 2.8 %collective-permute-done.15 = bf16[128,512]{1,0:T(8,128)(2,1)S(1)} collective-permute-done((bf16[128,512]{1,0:T(8,128)(2,1)S(1)}, bf16[128,512]{1,0:T(8,128)(2,1)S(1)}, u32[]{:S(2)}, u32[]{:S(2)}) %collective-permute-start.15) | collective-permute-done | bytes 131104 | tf_op jit(solution)/shard_map/ppermute | solution.py:785
  54.2 0.1 add_convert_fusion
  54.3 1.0 %collective-permute-start.16 = (bf16[32,512]{1,0:T(8,128)(2,1)S(1)}, bf16[32,512]{1,0:T(8,128)(2,1)S(1)}, u32[]{:S(2)}, u32[]{:S(2)}) collective-permute-start(bf16[32,512]{1,0:T(8,128)(2,1)S(1)} %get-tuple-element.55), channel_id=1, source_target_pairs={{0,8},{4,12},{8,0},{12,4},{16,24},{20,28},{24,16},{28,20},{1,9},{5... | collective-permute-start | bytes 98312 | tf_op jit(solution)/shard_map/ppermute | solution.py:718
  55.3 1.8 %collective-permute-start.18 = (bf16[32,512]{1,0:T(8,128)(2,1)S(1)}, bf16[32,512]{1,0:T(8,128)(2,1)S(1)}, u32[]{:S(2)}, u32[]{:S(2)}) collective-permute-start(bf16[32,512]{1,0:T(8,128)(2,1)S(1)} %get-tuple-element.56), channel_id=1, source_target_pairs={{0,24},{4,28},{8,16},{12,20},{16,8},{20,12},{24,0},{28,4},{1,25},{... | collective-permute-start | bytes 98312 | tf_op jit(solution)/shard_map/ppermute | solution.py:718
  57.1 0.8 %collective-permute-start.17 = (bf16[32,512]{1,0:T(8,128)(2,1)S(1)}, bf16[32,512]{1,0:T(8,128)(2,1)S(1)}, u32[]{:S(2)}, u32[]{:S(2)}) collective-permute-start(bf16[32,512]{1,0:T(8,128)(2,1)S(1)} %get-tuple-element.57), channel_id=1, source_target_pairs={{0,16},{4,20},{8,24},{12,28},{16,0},{20,4},{24,8},{28,12},{1,17},{... | collective-permute-start | bytes 98312 | tf_op jit(solution)/shard_map/ppermute | solution.py:718
  57.9 0.4 collective-permute-done.16
  58.3 2.7 %collective-permute-done.18 = bf16[32,512]{1,0:T(8,128)(2,1)S(1)} collective-permute-done((bf16[32,512]{1,0:T(8,128)(2,1)S(1)}, bf16[32,512]{1,0:T(8,128)(2,1)S(1)}, u32[]{:S(2)}, u32[]{:S(2)}) %collective-permute-start.18) | collective-permute-done | bytes 32800 | tf_op jit(solution)/shard_map/ppermute | solution.py:718
  61.0 0.9 %collective-permute-done.17 = bf16[32,512]{1,0:T(8,128)(2,1)S(1)} collective-permute-done((bf16[32,512]{1,0:T(8,128)(2,1)S(1)}, bf16[32,512]{1,0:T(8,128)(2,1)S(1)}, u32[]{:S(2)}, u32[]{:S(2)}) %collective-permute-start.17) | collective-permute-done | bytes 32800 | tf_op jit(solution)/shard_map/ppermute | solution.py:718
  61.9 0.6 %add_convert_fusion.1 = bf16[32,512]{1,0:T(8,128)(2,1)} fusion(f32[32,512]{1,0:T(8,128)S(1)} %get-tuple-element.54, bf16[32,512]{1,0:T(8,128)(2,1)S(1)} %collective-permute-done.18, bf16[32,512]{1,0:T(8,128)(2,1)S(1)} %collective-permute-done.17, bf16[32,512]{1,0:T(8,128)(2,1)S(1)} %collective-permute-done.16, bf16[128,512]{1,0:T(8,128)(2,1)S(1)} %add_convert_fusion), kind=kLoop, calls=%fused_computation.1 | loop fusion | flops 147456 | bytes 229376 | tf_op jit(solution)/shard_map/convert_element_type | solution.py:792
  (7 shorter events, 0.1 us)
Async XLA Ops:
  0.0 6.2 %collective-permute-start = (bf16[32,512]{1,0:T(8,128)(2,1)}, bf16[32,512]{1,0:T(8,128)(2,1)S(1)}, u32[]{:S(2)}, u32[]{:S(2)}) collective-permute-start(bf16[32,512]{1,0:T(8,128)(2,1)} %own_ref.1), channel_id=1, source_target_pairs={{0,2},{1,3},{2,0},{3,1},{4,6},{5,7},{6,4},{7,5},{8,10},{9,11},{10,... | collective-permute-start | bytes 98312 | tf_op jit(solution)/shard_map/ppermute | solution.py:718
  3.0 3.6 %collective-permute-start.2 = (bf16[32,512]{1,0:T(8,128)(2,1)}, bf16[32,512]{1,0:T(8,128)(2,1)S(1)}, u32[]{:S(2)}, u32[]{:S(2)}) collective-permute-start(bf16[32,512]{1,0:T(8,128)(2,1)} %own_ref.1), channel_id=1, source_target_pairs={{0,3},{1,2},{2,1},{3,0},{4,7},{5,6},{6,5},{7,4},{8,11},{9,10},{10,... | collective-permute-start | bytes 98312 | tf_op jit(solution)/shard_map/ppermute | solution.py:718
  3.0 3.6 %collective-permute-start.1 = (bf16[32,512]{1,0:T(8,128)(2,1)}, bf16[32,512]{1,0:T(8,128)(2,1)S(1)}, u32[]{:S(2)}, u32[]{:S(2)}) collective-permute-start(bf16[32,512]{1,0:T(8,128)(2,1)} %own_ref.1), channel_id=1, source_target_pairs={{0,1},{1,0},{2,3},{3,2},{4,5},{5,4},{6,7},{7,6},{8,9},{9,8},{10,11... | collective-permute-start | bytes 98312 | tf_op jit(solution)/shard_map/ppermute | solution.py:718
  13.1 1.3 %collective-permute-start.3 = (bf16[32,1024]{1,0:T(8,128)(2,1)S(1)}, bf16[32,1024]{1,0:T(8,128)(2,1)S(1)}, u32[]{:S(2)}, u32[]{:S(2)}) collective-permute-start(bf16[32,1024]{1,0:T(8,128)(2,1)S(1)} %get-tuple-element.38), channel_id=1, source_target_pairs={{0,1},{1,0},{2,3},{3,2},{4,5},{5,4},{6,7},{7,6},{8,9},{9,8},{10,11... | collective-permute-start | bytes 196616 | tf_op jit(solution)/shard_map/ppermute | solution.py:718
  14.4 5.5 %collective-permute-start.4 = (bf16[32,1024]{1,0:T(8,128)(2,1)S(1)}, bf16[32,1024]{1,0:T(8,128)(2,1)S(1)}, u32[]{:S(2)}, u32[]{:S(2)}) collective-permute-start(bf16[32,1024]{1,0:T(8,128)(2,1)S(1)} %sum.3.refs_0_.refs_2_), channel_id=1, source_target_pairs={{0,2},{1,3},{2,0},{3,1},{4,6},{5,7},{6,4},{7,5},{8,10},{9,11},{10,... | collective-permute-start | bytes 196616 | tf_op jit(solution)/shard_map/ppermute | solution.py:718
  19.9 8.2 %collective-permute-start.7 = (bf16[32,1152]{1,0:T(8,128)(2,1)S(1)}, bf16[32,1152]{1,0:T(8,128)(2,1)S(1)}, u32[]{:S(2)}, u32[]{:S(2)}) collective-permute-start(bf16[32,1152]{1,0:T(8,128)(2,1)S(1)} %get-tuple-element.41.refs_1_.refs_0_), channel_id=1, source_target_pairs={{0,24},{4,28},{8,16},{12,20},{16,8},{20,12},{24,0},{28,4},{1,25},{... | collective-permute-start | bytes 221192 | tf_op jit(solution)/shard_map/ppermute | solution.py:718
  23.7 6.4 %collective-permute-start.6 = (bf16[32,1152]{1,0:T(8,128)(2,1)S(1)}, bf16[32,1152]{1,0:T(8,128)(2,1)S(1)}, u32[]{:S(2)}, u32[]{:S(2)}) collective-permute-start(bf16[32,1152]{1,0:T(8,128)(2,1)S(1)} %get-tuple-element.41.refs_1_.refs_0_), channel_id=1, source_target_pairs={{0,16},{4,20},{8,24},{12,28},{16,0},{20,4},{24,8},{28,12},{1,17},{... | collective-permute-start | bytes 221192 | tf_op jit(solution)/shard_map/ppermute | solution.py:718
  23.7 6.4 %collective-permute-start.5 = (bf16[32,1152]{1,0:T(8,128)(2,1)S(1)}, bf16[32,1152]{1,0:T(8,128)(2,1)S(1)}, u32[]{:S(2)}, u32[]{:S(2)}) collective-permute-start(bf16[32,1152]{1,0:T(8,128)(2,1)S(1)} %get-tuple-element.41.refs_1_.refs_0_), channel_id=1, source_target_pairs={{0,8},{4,12},{8,0},{12,4},{16,24},{20,28},{24,16},{28,20},{1,9},{5... | collective-permute-start | bytes 221192 | tf_op jit(solution)/shard_map/ppermute | solution.py:718
  30.1 1.6 %collective-permute-start.8 = (bf16[128,1152]{1,0:T(8,128)(2,1)S(1)}, bf16[128,1152]{1,0:T(8,128)(2,1)S(1)}, u32[]{:S(2)}, u32[]{:S(2)}) collective-permute-start(bf16[128,1152]{1,0:T(8,128)(2,1)S(1)} %stack.1.mine_ref), channel_id=1, source_target_pairs={{0,1},{1,0},{2,3},{3,2},{4,5},{5,4},{6,7},{7,6},{8,9},{9,8},{10,11... | collective-permute-start | bytes 884744 | tf_op jit(solution)/shard_map/ppermute | solution.py:718
  30.2 9.4 %collective-permute-start.10 = (bf16[128,1152]{1,0:T(8,128)(2,1)S(1)}, bf16[128,1152]{1,0:T(8,128)(2,1)S(1)}, u32[]{:S(2)}, u32[]{:S(2)}) collective-permute-start(bf16[128,1152]{1,0:T(8,128)(2,1)S(1)} %stack.1.mine_ref), channel_id=1, source_target_pairs={{0,4},{4,0},{8,12},{12,8},{16,20},{20,16},{24,28},{28,24},{1,5},{5... | collective-permute-start | bytes 884744 | tf_op jit(solution)/shard_map/ppermute | solution.py:718
  35.8 3.9 %collective-permute-start.9 = (bf16[128,1024]{1,0:T(8,128)(2,1)S(1)}, bf16[128,1024]{1,0:T(8,128)(2,1)S(1)}, u32[]{:S(2)}, u32[]{:S(2)}) collective-permute-start(bf16[128,1024]{1,0:T(8,128)(2,1)S(1)} %get-tuple-element.47.after_ref), channel_id=1, source_target_pairs={{0,1},{1,0},{2,3},{3,2},{4,5},{5,4},{6,7},{7,6},{8,9},{9,8},{10,11... | collective-permute-start | bytes 786440 | tf_op jit(solution)/shard_map/ppermute | solution.py:718
  39.7 1.6 %collective-permute-start.11 = (bf16[128,1152]{1,0:T(8,128)(2,1)S(1)}, bf16[128,1152]{1,0:T(8,128)(2,1)S(1)}, u32[]{:S(2)}, u32[]{:S(2)}) collective-permute-start(bf16[128,1152]{1,0:T(8,128)(2,1)S(1)} %hold.2.mine_ref), channel_id=1, source_target_pairs={{0,1},{1,0},{2,3},{3,2},{4,5},{5,4},{6,7},{7,6},{8,9},{9,8},{10,11... | collective-permute-start | bytes 884744 | tf_op jit(solution)/shard_map/ppermute | solution.py:718
  43.3 1.7 %collective-permute-start.13 = (bf16[128,1024]{1,0:T(8,128)(2,1)S(1)}, bf16[128,1024]{1,0:T(8,128)(2,1)S(1)}, u32[]{:S(2)}, u32[]{:S(2)}) collective-permute-start(bf16[128,1024]{1,0:T(8,128)(2,1)S(1)} %get-tuple-element.51._), channel_id=1, source_target_pairs={{0,1},{1,0},{2,3},{3,2},{4,5},{5,4},{6,7},{7,6},{8,9},{9,8},{10,11... | collective-permute-start | bytes 786440 | tf_op jit(solution)/shard_map/ppermute | solution.py:718
  44.4 5.7 %collective-permute-start.12 = (bf16[128,512]{1,0:T(8,128)(2,1)S(1)}, bf16[128,512]{1,0:T(8,128)(2,1)S(1)}, u32[]{:S(2)}, u32[]{:S(2)}) collective-permute-start(bf16[128,512]{1,0:T(8,128)(2,1)S(1)} %hold.3), channel_id=1, source_target_pairs={{0,2},{1,3},{2,0},{3,1},{4,6},{5,7},{6,4},{7,5},{8,10},{9,11},{10,... | collective-permute-start | bytes 393224 | tf_op jit(solution)/shard_map/ppermute | solution.py:718
  45.1 6.4 %collective-permute-start.14 = (bf16[128,512]{1,0:T(8,128)(2,1)S(1)}, bf16[128,512]{1,0:T(8,128)(2,1)S(1)}, u32[]{:S(2)}, u32[]{:S(2)}) collective-permute-start(bf16[128,512]{1,0:T(8,128)(2,1)S(1)} %get-tuple-element.52), channel_id=1, source_target_pairs={{0,4},{1,5},{2,6},{3,7},{4,0},{5,1},{6,2},{7,3},{8,12},{9,13},{10,... | collective-permute-start | bytes 393224 | tf_op jit(solution)/shard_map/ppermute | solution.py:785
  46.6 7.6 %collective-permute-start.15 = (bf16[128,512]{1,0:T(8,128)(2,1)S(1)}, bf16[128,512]{1,0:T(8,128)(2,1)S(1)}, u32[]{:S(2)}, u32[]{:S(2)}) collective-permute-start(bf16[128,512]{1,0:T(8,128)(2,1)S(1)} %get-tuple-element.53), channel_id=1, source_target_pairs={{0,6},{1,7},{2,4},{3,5},{4,2},{5,3},{6,0},{7,1},{8,14},{9,15},{10,... | collective-permute-start | bytes 393224 | tf_op jit(solution)/shard_map/ppermute | solution.py:785
  54.3 4.0 %collective-permute-start.16 = (bf16[32,512]{1,0:T(8,128)(2,1)S(1)}, bf16[32,512]{1,0:T(8,128)(2,1)S(1)}, u32[]{:S(2)}, u32[]{:S(2)}) collective-permute-start(bf16[32,512]{1,0:T(8,128)(2,1)S(1)} %get-tuple-element.55), channel_id=1, source_target_pairs={{0,8},{4,12},{8,0},{12,4},{16,24},{20,28},{24,16},{28,20},{1,9},{5... | collective-permute-start | bytes 98312 | tf_op jit(solution)/shard_map/ppermute | solution.py:718
  55.3 5.7 %collective-permute-start.18 = (bf16[32,512]{1,0:T(8,128)(2,1)S(1)}, bf16[32,512]{1,0:T(8,128)(2,1)S(1)}, u32[]{:S(2)}, u32[]{:S(2)}) collective-permute-start(bf16[32,512]{1,0:T(8,128)(2,1)S(1)} %get-tuple-element.56), channel_id=1, source_target_pairs={{0,24},{4,28},{8,16},{12,20},{16,8},{20,12},{24,0},{28,4},{1,25},{... | collective-permute-start | bytes 98312 | tf_op jit(solution)/shard_map/ppermute | solution.py:718
  57.1 4.8 %collective-permute-start.17 = (bf16[32,512]{1,0:T(8,128)(2,1)S(1)}, bf16[32,512]{1,0:T(8,128)(2,1)S(1)}, u32[]{:S(2)}, u32[]{:S(2)}) collective-permute-start(bf16[32,512]{1,0:T(8,128)(2,1)S(1)} %get-tuple-element.57), channel_id=1, source_target_pairs={{0,16},{4,20},{8,24},{12,28},{16,0},{20,4},{24,8},{28,12},{1,17},{... | collective-permute-start | bytes 98312 | tf_op jit(solution)/shard_map/ppermute | solution.py:718
